TPU v7x, 32 devices: a whole 2x2x4 slice. The times are simulated.
32 devices in a mesh: replica: 2 (over x), section: 16 (over z, y, core).
Axes of the slice: x: 2, y: 2, z: 4, core: 2. Of those that a mesh axis runs over, the one named last changes fastest.
Arguments:
- prompt_states: bfloat16 [16384, 8192], P(('replica', 'section')), parts along dimension 0, may hold values from -60 to 60
- kv_weight: bfloat16 [8192, 1024], P('section'), may hold values from -0.0625 to 0.0625
- image_owner: int32 [256], P(('replica', 'section')), parts along dimension 0, may hold values from 0 to 15, as said below
- image_row: int32 [256], P(('replica', 'section')), parts along dimension 0, may hold values from 0 to 7
- queries: bfloat16 [256, 4096], P(('replica', 'section')), parts along dimension 0, may hold values from -100 to 100
- cache: bfloat16 [256, 256, 1024], P(('replica', 'section')), parts along dimension 0, may hold values from -6 to 6
- context_length: int32 [256], P(('replica', 'section')), parts along dimension 0, may hold values from 2 to 256, as said below
Outputs:
- attended: bfloat16 [256, 4096], P(('replica', 'section')), parts along dimension 0
There are 2 independent parts, one for each index of `replica`. A program takes and returns all parts, laid end to end along the dimension named above; an argument that names none is the same for every part. Nothing has to cross between parts.
Inputs may be any that keep to these rules, and one draw needn't show every extreme that they name: `image_owner`: the images of one device go to distinct owners; some owner receives one image from every device. `context_length`: every device holds a row with all 256 positions live.
All inputs are finite; a program needn't handle non-finite values.
Results may differ from a plain program's by a relative error of at most 0.005.
Values may be sent and summed in bfloat16 or wider, within the bound.
No kernel may reach another device: no remote copies, remote signals or barrier semaphores. Data moves between devices by JAX's collectives and lax.ppermute only.
A program may use at most 128 MiB of HBM per device.

v0:
```python
import math

import jax
import jax.numpy as jnp
from jax import lax
from jax.sharding import PartitionSpec as P

HD = 128
KVH = 4
QH = 32
IMG_TOK = 64


masked_score = -1e30


def normalize_rows(states):
    values = states.astype(jnp.float32)
    return values * lax.rsqrt(jnp.mean(values * values, axis=-1, keepdims=True) + 1e-05)


def per_device(prompt_states, kv_weight, image_owner, image_row, queries, cache, context_length):
    peer_count = lax.axis_size("section")
    image_count = image_owner.shape[0]
    kv_width = kv_weight.shape[1]
    rows_dev = queries.shape[0]
    context = cache.shape[1]
    key_width = kv_width // 2
    group_size = QH // KVH
    score_scale = 1.0 / math.sqrt(HD)
    normed = normalize_rows(prompt_states).astype(jnp.bfloat16)
    new_kv = jnp.dot(
        normed,
        lax.all_gather(kv_weight, "section", axis=0, tiled=True),
        preferred_element_type=jnp.float32,
    ).astype(jnp.bfloat16)
    image_kv = new_kv.reshape(image_count, IMG_TOK, kv_width)
    local_queries = queries.reshape(rows_dev, KVH, group_size, HD)
    res_keys = cache[:, :, :key_width].reshape(rows_dev, context, KVH, HD)
    res_vals = cache[:, :, key_width:].reshape(rows_dev, context, KVH, HD)
    res_scores = (
        jnp.einsum("rkgd,rtkd->rkgt", local_queries, res_keys, preferred_element_type=jnp.float32)
        * score_scale
    )
    res_live = (jnp.arange(context)[None, :] < context_length[:, None])[:, None, None, :]
    res_scores = jnp.where(res_live, res_scores, masked_score)
    res_max = jnp.max(res_scores, axis=-1)
    placement = jnp.arange(peer_count)[:, None] == image_owner[None, :]
    kv_slots = jnp.dot(
        placement.astype(jnp.bfloat16),
        image_kv.reshape(image_count, IMG_TOK * kv_width),
        preferred_element_type=jnp.float32,
    ).astype(jnp.bfloat16)
    row_slots = jnp.where(
        jnp.any(placement, axis=1),
        jnp.sum(jnp.where(placement, image_row[None, :], 0), axis=1),
        rows_dev,
    )
    got_kv, got_rows = (
        lax.all_to_all(
            kv_slots.reshape(peer_count, IMG_TOK, kv_width),
            "section",
            split_axis=0,
            concat_axis=0,
            tiled=True,
        ),
        lax.all_to_all(
            row_slots.reshape(peer_count, 1), "section", split_axis=0, concat_axis=0, tiled=True
        ),
    )
    got_keys = got_kv[:, :, :key_width].reshape(peer_count, IMG_TOK, KVH, HD)
    got_vals = got_kv[:, :, key_width:].reshape(peer_count, IMG_TOK, KVH, HD)
    new_scores = (
        jnp.einsum("rkgd,smkd->rkgsm", local_queries, got_keys, preferred_element_type=jnp.float32)
        * score_scale
    )
    new_live = (got_rows[:, 0][None, :] == jnp.arange(rows_dev)[:, None])[:, None, None, :, None]
    new_scores = jnp.where(new_live, new_scores, masked_score)
    row_top = jnp.maximum(res_max, jnp.max(new_scores, axis=(-2, -1)))
    res_w = jnp.where(res_live, jnp.exp(res_scores - row_top[..., None]), 0.0)
    new_w = jnp.where(new_live, jnp.exp(new_scores - row_top[..., None, None]), 0.0)
    denominator = jnp.sum(res_w, axis=-1) + jnp.sum(new_w, axis=(-2, -1))
    weighted = jnp.einsum(
        "rkgt,rtkd->rkgd", res_w.astype(jnp.bfloat16), res_vals, preferred_element_type=jnp.float32
    )
    weighted = weighted + jnp.einsum(
        "rkgsm,smkd->rkgd", new_w.astype(jnp.bfloat16), got_vals, preferred_element_type=jnp.float32
    )
    return (weighted / denominator[..., None]).reshape(rows_dev, QH * HD).astype(jnp.bfloat16)


def solution(mesh):
    placed = (
        P(("replica", "section"), None),
        P("section", None),
        P(("replica", "section")),
        P(("replica", "section")),
        P(("replica", "section"), None),
        P(("replica", "section"), None, None),
        P(("replica", "section")),
    )
    return jax.shard_map(
        per_device,
        mesh=mesh,
        in_specs=placed,
        out_specs=P(("replica", "section"), None),
        check_vma=False,
    )
```

profile of v0, /device:TPU:13, one launch (start us, length us, event | category | flops | bytes accessed | tf_op | source)
XLA Modules:
  0.0 225.4 jit_solution(8202701356475807618)
XLA Ops:
  6.5 0.0 all-gather.2.cloned.1.call-start
  6.5 0.7 all-gather.2.cloned.1.call-update
  7.3 0.7 fusion.29
  8.0 0.8 select_reduce_fusion
  8.8 0.7 copy.77
  9.4 6.6 %all-to-all-start = ((s32[16,1,1]{2,1,0:T(1,128)}), s32[16,1,1]{2,1,0:T(1,128)S(1)}, u32[]{:S(2)}, u32[]{:S(2)}) async-start(s32[16,1,1]{2,1,0:T(1,128)} %copy.77), calls=%async_computation | async-start | bytes 16384 | tf_op jit(solution)/shard_map/all_to_all | solution.py:67
  16.0 5.5 %fusion = f32[512]{0:T(512)S(1)} fusion(bf16[512,8192]{1,0:T(8,128)(2,1)} %param.7), kind=kLoop, calls=%fused_computation.3 | loop fusion | flops 12582400 | bytes 8390656 | tf_op jit(solution)/shard_map/reduce_sum | solution.py:19
  21.5 113.6 %all-gather.2.cloned.1.call-done = bf16[8192,1024]{1,0:T(8,128)(2,1)} async-done(((bf16[512,1024]{1,0:T(8,128)(2,1)}), bf16[8192,1024]{1,0:T(8,128)(2,1)}) %all-gather.2.cloned.1.call-update) | async-done | bytes 16777232 | tf_op jit(solution)/shard_map/all_gather | solution.py:34
  135.1 14.9 %fusion.6 = bf16[512,1024]{1,0:T(8,128)(2,1)S(1)} fusion(bf16[8192,1024]{1,0:T(8,128)(2,1)} %all-gather.2.cloned.1.call-done, bf16[512,8192]{1,0:T(8,128)(2,1)} %param.7, f32[512]{0:T(512)S(1)} %add_rsqrt_fusion), kind=kOutput, calls=%fused_computation.10 | convolution fusion | flops 8603041792 | bytes 26216448 | tf_op jit(solution)/shard_map/dot_general | solution.py:32
  150.0 0.0 copy-start.3
  150.0 0.5 reshape_reshape.3
  150.5 0.2 copy-done.3
  150.7 0.8 convolution_convert_fusion
  151.5 2.4 %copy.99 = bf16[2,8,64,1024]{3,2,1,0:T(8,128)(2,1)} copy(bf16[2,8,64,1024]{3,1,2,0:T(8,128)(2,1)S(1)} %bitcast.53) | data formatting | bytes 4194304
  153.9 0.0 all-to-all-done
  153.9 7.5 %all-to-all-start.1 = ((bf16[16,64,1024]{2,1,0:T(8,128)(2,1)}), bf16[16,64,1024]{2,1,0:T(8,128)(2,1)}, u32[]{:S(2)}, u32[]{:S(2)}) async-start(bf16[16,64,1024]{2,1,0:T(8,128)(2,1)} %bitcast.16), calls=%async_computation.1 | async-start | bytes 4194304 | tf_op jit(solution)/shard_map/all_to_all | solution.py:60
  161.4 3.9 %fusion.32 = (bf16[8,256,512]{2,1,0:T(8,128)(2,1)S(1)}, bf16[8,256,512]{2,1,0:T(8,128)(2,1)}) fusion(bf16[8,256,1024]{2,1,0:T(8,128)(2,1)} %param.12), kind=kLoop, calls=%fused_computation.47 | loop fusion | bytes 8388608 | tf_op jit(solution)/shard_map/slice | solution.py:39
  165.3 2.4 %copy.96 = bf16[8,256,512]{1,2,0:T(8,128)(2,1)} copy(bf16[8,256,512]{2,1,0:T(8,128)(2,1)S(1)} %get-tuple-element.5) | data formatting | bytes 4194304
  167.7 0.0 copy-start.2
  167.7 0.0 copy-start.1
  167.7 2.9 %copy.97 = bf16[8,256,512]{1,2,0:T(8,128)(2,1)S(1)} copy(bf16[8,256,512]{2,1,0:T(8,128)(2,1)} %get-tuple-element.6) | data formatting | bytes 4194304
  170.6 0.0 copy-done.2
  170.6 0.1 iota_compare_fusion.1
  170.7 0.0 copy-done.1
  170.7 2.1 fusion.33
  172.8 0.4 reduce
  173.1 0.1 iota_compare_fusion
  173.2 35.7 %all-to-all-done.1 = bf16[16,64,1024]{2,1,0:T(8,128)(2,1)} async-done(((bf16[16,64,1024]{2,1,0:T(8,128)(2,1)}), bf16[16,64,1024]{2,1,0:T(8,128)(2,1)}, u32[]{:S(2)}, u32[]{:S(2)}) %all-to-all-start.1) | async-done | bytes 2097184 | tf_op jit(solution)/shard_map/all_to_all | solution.py:60
  208.9 2.8 %slice_bitcast_fusion = (bf16[16,8,4,8,128]{4,3,2,1,0:T(8,128)(2,1)}, bf16[16,64,512]{2,1,0:T(8,128)(2,1)S(1)}) fusion(bf16[16,64,1024]{2,1,0:T(8,128)(2,1)} %all-to-all-done.1), kind=kLoop, calls=%fused_computation.22 | loop fusion | bytes 4194304
  211.8 1.1 reshape.105
  212.9 2.4 %fusion.5 = (f32[8,4,8]{2,0,1:T(8,128)S(1)}, f32[4,16,64,8,8]{2,4,3,1,0:T(8,128)S(1)}) fusion(pred[8,16]{0,1:T(8,128)(4,1)S(1)} %iota_compare_fusion, bf16[8,4,8,128,1]{3,0,2,1,4:T(8,128)(2,1)S(1)} %bitcast.56, bf16[16,64,4,128,1]{3,2,1,0,4:T(4,128)(2,1)} %bitcast.54), kind=kOutput, calls=%fused_computation.9 | convolution fusion | flops 67895040 | bytes 2163840 | tf_op jit(solution)/shard_map/rkgd,smkd->rkgsm/dot_general | solution.py:74
  215.4 0.9 fusion.9
  216.2 0.0 copy-start
  216.2 0.2 fusion.20
  216.5 0.7 fusion.22
  217.2 0.3 copy-done
  217.5 0.4 fusion.15
  217.9 0.7 copy.122
  (5 shorter events, 0.0 us)
Async XLA Ops:
  6.5 128.6 %all-gather.2.cloned.1.call-start = ((), (), s32[]{:S(2)}) async-start(), calls=%async_computation.2 | async-start | bytes 17825792 | tf_op jit(solution)/shard_map/all_gather | solution.py:34
  9.4 144.5 %all-to-all-start = ((s32[16,1,1]{2,1,0:T(1,128)}), s32[16,1,1]{2,1,0:T(1,128)S(1)}, u32[]{:S(2)}, u32[]{:S(2)}) async-start(s32[16,1,1]{2,1,0:T(1,128)} %copy.77), calls=%async_computation | async-start | bytes 16384 | tf_op jit(solution)/shard_map/all_to_all | solution.py:67
  150.0 0.7 copy-start.3
  153.9 55.0 %all-to-all-start.1 = ((bf16[16,64,1024]{2,1,0:T(8,128)(2,1)}), bf16[16,64,1024]{2,1,0:T(8,128)(2,1)}, u32[]{:S(2)}, u32[]{:S(2)}) async-start(bf16[16,64,1024]{2,1,0:T(8,128)(2,1)} %bitcast.16), calls=%async_computation.1 | async-start | bytes 4194304 | tf_op jit(solution)/shard_map/all_to_all | solution.py:60
  167.7 2.9 %copy-start.2 = (s32[8]{0:T(128)S(1)}, s32[8]{0:T(128)}, u32[]{:S(2)}) copy-start(s32[8]{0:T(128)} %param.13) | copy-start | bytes 100
  167.7 3.0 %copy-start.1 = (bf16[8,4096]{1,0:T(8,128)(2,1)S(1)}, bf16[8,4096]{1,0:T(8,128)(2,1)}, u32[]{:S(2)}) copy-start(bf16[8,4096]{1,0:T(8,128)(2,1)} %param.11) | copy-start | bytes 196612
  216.2 1.2 copy-start
Sparse Core Ops, SparseCore 0:
  9.5 125.5 all-gather.1
where the time goes:
time: 226 us; the launch traced here: 225 us
  waiting for transfers between devices  150 us (66%)
  matrix products  21.3 us (9%)
  local copies, waits for them, and re-layouts  17.9 us (8%)
  starting transfers between devices  14 us (6%)
  between operations  13.5 us (6%)
  other arithmetic  8.63 us (4%)
    all_gather x1, waiting for transfers between devices, per_device(): lax.all_gather(kv_weight, 'section', axis=0, tiled=True)  114 us
    all_to_all x1, waiting for transfers between devices, per_device(): lax.all_to_all(kv_slots.reshape(peer_count, IMG_TOK, kv_width), 'section'...  35.7 us
    dot_general x1, matrix products, per_device(): jnp.dot(normed, lax.all_gather(kv_weight, 'section', axis=0, tiled=True),...  14.9 us
    unnamed x13, local copies, waits for them, and re-layouts  11.7 us
    all_to_all x1, starting transfers between devices, per_device(): lax.all_to_all(kv_slots.reshape(peer_count, IMG_TOK, kv_width), 'section'...  7.45 us
    all_to_all x1, starting transfers between devices, per_device(): lax.all_to_all(row_slots.reshape(peer_count, 1), 'section', split_axis=0,...  6.59 us
    reduce_sum x1, other arithmetic, normalize_rows(): jnp.mean(values * values, axis=-1, keepdims=True) + 1e-05  5.49 us
  transfers between devices with their start and end apart: 3, of which 2 were waited for; matrix products, arithmetic and copies ran while one was open for 17% of the time, Pallas kernels for 0%

commit v1 on v0

v1 whole, which is shorter than its diff:
```python
import functools
import math

import jax
import jax.numpy as jnp
from jax import lax
from jax.experimental import pallas as pl
from jax.experimental.pallas import tpu as pltpu
from jax.sharding import PartitionSpec as P

HD = 128
KVH = 4
QH = 32
IMG_TOK = 64
GROUP = QH // KVH
HALF_KVH = KVH // 2
HALF_QH = QH // 2
SCALE = 1.0 / math.sqrt(HD)

masked_score = -1e30


def normalize_rows(states):
    values = states.astype(jnp.float32)
    return values * lax.rsqrt(jnp.mean(values * values, axis=-1, keepdims=True) + 1e-05)


def swap_core(x, n):
    return lax.ppermute(x, "section", [(i, i ^ 1) for i in range(n)])


def swap_replica(x):
    count = lax.axis_size("replica")
    return lax.ppermute(x, "replica", [(i, i ^ 1) for i in range(count)])


def same_core_groups(n):
    return [list(range(core, n, 2)) for core in range(2)]


def gather_plain(chunk, n):
    chip_rows = chunk.shape[0]
    whole = lax.all_gather(chunk, "section", axis=0, tiled=True, axis_index_groups=same_core_groups(n))
    return [(whole, chip * chip_rows, chip_rows, chip, 0) for chip in range(n // 2)]


def gather_grid(chunk, span, z, y, rep):
    rows = chunk.shape[0]
    rest = rows - span
    order = [0, 1, 3, 2]
    ring = [
        (order[p] * 4 + low, order[(p + 1) % 4] * 4 + low) for p in range(4) for low in range(4)
    ]
    swap_y = [(i, i ^ 2) for i in range(16)]
    places = jnp.array([0, 1, 3, 2], jnp.int32)
    place = places[z]
    mine = lax.dynamic_slice_in_dim(chunk, rep * rest, span, 0)
    along_z = [mine]
    along_y = []
    for step in range(4):
        if step < 3:
            along_z.append(lax.ppermute(along_z[-1], "section", ring))
        along_y.append(lax.ppermute(along_z[step], "section", swap_y))
    pieces = [(chunk, 0, rows, z * 2 + y, 0)]
    for step in range(4):
        from_z = places[(place - step) % 4]
        for piece, chip in ((along_z[step], from_z * 2 + y), (along_y[step], from_z * 2 + 1 - y)):
            if piece is mine:
                continue
            if rest == span:
                extra = swap_replica(piece)
            else:
                extra = swap_replica(lax.dynamic_slice_in_dim(piece, rep * (span - rest), rest, 0))
            pieces.append((piece, 0, span, chip, rep * rest))
            pieces.append((extra, 0, rest, chip, (1 - rep) * span))
    return pieces


def granules(pieces, rows_dev, core, size):
    arrays, layout, offsets = [], [], []
    for array, start, rows, chip, first in pieces:
        at = [i for i, known in enumerate(arrays) if known is array]
        if not at:
            arrays.append(array)
            at = [len(arrays) - 1]
        for part in range(rows // size):
            row = first + part * size
            half = row // rows_dev
            place = (half + core) % 2 * rows_dev + row % rows_dev
            layout.append((at[0], start + part * size))
            offsets.append(jnp.asarray(chip * 2 * rows_dev + place, jnp.int32))
    return arrays, layout, jnp.stack(offsets)


def project(layout, size, offsets_ref, own_ref, other_ref, piece_refs, weight, total, sems):
    step = pl.program_id(0)
    tokens, depth = own_ref.shape

    @pl.when(step == 0)
    def _():
        copies = [
            pltpu.make_async_copy(
                piece_refs[which].at[pl.ds(start, size)],
                weight.at[pl.ds(pl.multiple_of(offsets_ref[i], size), size)],
                sems.at[i],
            )
            for i, (which, start) in enumerate(layout)
        ]
        for copy in copies:
            copy.start()
        total[...] = jnp.zeros_like(total)
        for copy in copies:
            copy.wait()

    block = weight[pl.ds(pl.multiple_of(step * depth, depth), depth), :]
    total[:tokens, :] += jnp.dot(own_ref[...], block, preferred_element_type=jnp.float32)
    total[tokens:, :] += jnp.dot(other_ref[...], block, preferred_element_type=jnp.float32)


def key_kernel(layout, size, n_pieces, offsets_ref, own_ref, other_ref, query_ref, *refs):
    piece_refs = refs[:n_pieces]
    weights_ref, max_ref, sum_ref, weight, total, sems = refs[n_pieces:]
    project(layout, size, offsets_ref, own_ref, other_ref, piece_refs, weight, total, sems)

    @pl.when(pl.program_id(0) == pl.num_programs(0) - 1)
    def _():
        tokens = total.shape[0]
        queries = query_ref.shape[1]
        image_of_query = lax.broadcasted_iota(jnp.int32, (queries, tokens), 0) // GROUP
        image_of_token = lax.broadcasted_iota(jnp.int32, (queries, tokens), 1) // IMG_TOK
        live = image_of_query == image_of_token
        for head in range(HALF_KVH):
            keys = total[:, head * HD : (head + 1) * HD].astype(jnp.bfloat16)
            scores = (
                lax.dot_general(
                    query_ref[head], keys, (((1,), (1,)), ((), ())), preferred_element_type=jnp.float32
                )
                * SCALE
            )
            scores = jnp.where(live, scores, masked_score)
            top = jnp.max(scores, axis=1, keepdims=True)
            weights = jnp.where(live, jnp.exp(scores - top), 0.0)
            weights_ref[head] = weights.astype(jnp.bfloat16)
            max_ref[head] = jnp.broadcast_to(top, (queries, HD))
            sum_ref[head] = jnp.broadcast_to(jnp.sum(weights, axis=1, keepdims=True), (queries, HD))


def value_kernel(layout, size, n_pieces, offsets_ref, slot_ref, own_ref, other_ref, weights_ref, *refs):
    piece_refs = refs[:n_pieces]
    slots_ref, weight, total, summed, sems = refs[n_pieces:]
    project(layout, size, offsets_ref, own_ref, other_ref, piece_refs, weight, total, sems)

    @pl.when(pl.program_id(0) == pl.num_programs(0) - 1)
    def _():
        slots_ref[...] = jnp.zeros_like(slots_ref)
        images = weights_ref.shape[1] // GROUP
        for head in range(HALF_KVH):
            values = total[:, head * HD : (head + 1) * HD].astype(jnp.bfloat16)
            out = jnp.dot(weights_ref[head], values, preferred_element_type=jnp.float32)
            summed[:, head * GROUP : (head + 1) * GROUP, :] = out.reshape(images, GROUP, HD)
        for image in range(images):
            slots_ref[slot_ref[image]] = summed[image].astype(jnp.bfloat16)


def combine_kernel(row_ref, got_ref, factor_ref, base_ref, out_ref, acc):
    acc[...] = base_ref[...]
    images = factor_ref.shape[0]

    def add(image, carry):
        row = row_ref[image]
        chip, which = image // 2, image % 2
        for core in range(2):
            part = pl.ds(core * HALF_QH, HALF_QH)
            acc[row, part, :] += factor_ref[image, part, :] * got_ref[
                (chip * 2 + core) * 2 + which
            ].astype(jnp.float32)
        return carry

    lax.fori_loop(0, images, add, 0, unroll=4)
    for head in range(QH):
        out_ref[:, head * HD : (head + 1) * HD] = acc[:, head, :].astype(jnp.bfloat16)


def resident(queries, cache, context_length):
    rows, context = cache.shape[:2]
    local_queries = queries.reshape(rows, KVH, GROUP, HD)
    keys = cache[:, :, : KVH * HD].reshape(rows, context, KVH, HD)
    vals = cache[:, :, KVH * HD :].reshape(rows, context, KVH, HD)
    scores = jnp.einsum("rkgd,rtkd->rkgt", local_queries, keys, preferred_element_type=jnp.float32) * SCALE
    live = (jnp.arange(context)[None, :] < context_length[:, None])[:, None, None, :]
    scores = jnp.where(live, scores, masked_score)
    top = jnp.max(scores, axis=-1)
    weights = jnp.where(live, jnp.exp(scores - top[..., None]), 0.0)
    total = jnp.einsum("rkgt,rtkd->rkgd", weights.astype(jnp.bfloat16), vals, preferred_element_type=jnp.float32)
    return (
        top.reshape(rows, QH),
        jnp.sum(weights, axis=-1).reshape(rows, QH),
        total.reshape(rows, QH, HD),
    )


def per_device(prompt_states, kv_weight, image_owner, image_row, queries, cache, context_length):
    n = lax.axis_size("section")
    section = lax.axis_index("section")
    rep = lax.axis_index("replica")
    core = section % 2
    tokens, width = prompt_states.shape
    rows_dev, kv_width = kv_weight.shape
    half = kv_width // 4
    images = image_owner.shape[0]
    decode_rows = queries.shape[0]
    grid_form = n == 16 and lax.axis_size("replica") == 2

    columns = kv_weight.reshape(rows_dev, 2, 2, half)
    keep = jnp.where(core == 0, columns[:, :, 0], columns[:, :, 1])
    give = jnp.where(core == 0, columns[:, :, 1], columns[:, :, 0])
    phases = []
    for kind in range(2):
        got = swap_core(give[:, kind], n)
        chunk = jnp.concatenate([keep[:, kind], got], axis=0)
        if grid_form:
            span = chunk.shape[0] * (2 + kind) // 4
            phases.append(gather_grid(chunk, span, section // 4, section // 2 % 2, rep))
        else:
            phases.append(gather_plain(chunk, n))

    normed = normalize_rows(prompt_states).astype(jnp.bfloat16)
    other = swap_core(normed, n)

    target = image_owner * decode_rows + image_row
    all_target = lax.all_gather(target, "section", axis=0, tiled=False)
    chip_target = jnp.concatenate([target, jnp.take(all_target, section ^ 1, axis=0)])
    query_halves = queries.reshape(decode_rows, 2, HALF_QH * HD)
    keep_q = jnp.where(core == 0, query_halves[:, 0], query_halves[:, 1])
    give_q = jnp.where(core == 0, query_halves[:, 1], query_halves[:, 0])
    chip_q = jnp.concatenate([keep_q, swap_core(give_q, n)], axis=0)
    all_q = lax.all_gather(chip_q, "section", axis=0, tiled=True, axis_index_groups=same_core_groups(n))
    place = jnp.where(core == 0, chip_target, chip_target ^ decode_rows)
    pick = (place[:, None] == jnp.arange(n * decode_rows)[None, :]).astype(jnp.bfloat16)
    image_q = jnp.dot(pick, all_q, preferred_element_type=jnp.float32).astype(jnp.bfloat16)
    image_q = image_q.reshape(2 * images, HALF_KVH, GROUP, HD).transpose(1, 0, 2, 3)
    image_q = image_q.reshape(HALF_KVH, 2 * images * GROUP, HD)

    res_top, res_sum, res_out = resident(queries, cache, context_length)

    size = min(rows_dev, 256)
    depth = 1024
    steps = width // depth
    n_queries = 2 * images * GROUP
    token_spec = pl.BlockSpec((tokens, depth), lambda i, *_: (0, i))
    flops = 2 * 2 * tokens * width * 2 * HD

    arrays, layout, offsets = granules(phases[0], rows_dev, core, size)
    weights, maxes, sums = pl.pallas_call(
        functools.partial(key_kernel, layout, size, len(arrays)),
        grid_spec=pltpu.PrefetchScalarGridSpec(
            num_scalar_prefetch=1,
            grid=(steps,),
            in_specs=[token_spec, token_spec, pl.BlockSpec((HALF_KVH, n_queries, HD), lambda i, *_: (0, 0, 0))]
            + [pl.BlockSpec(memory_space=pl.ANY)] * len(arrays),
            out_specs=[
                pl.BlockSpec((HALF_KVH, n_queries, 2 * tokens), lambda i, *_: (0, 0, 0)),
                pl.BlockSpec((HALF_KVH, n_queries, HD), lambda i, *_: (0, 0, 0)),
                pl.BlockSpec((HALF_KVH, n_queries, HD), lambda i, *_: (0, 0, 0)),
            ],
            scratch_shapes=[
                pltpu.VMEM((width, 2 * HD), jnp.bfloat16),
                pltpu.VMEM((2 * tokens, 2 * HD), jnp.float32),
                pltpu.SemaphoreType.DMA((len(layout),)),
            ],
        ),
        out_shape=[
            jax.ShapeDtypeStruct((HALF_KVH, n_queries, 2 * tokens), jnp.bfloat16),
            jax.ShapeDtypeStruct((HALF_KVH, n_queries, HD), jnp.float32),
            jax.ShapeDtypeStruct((HALF_KVH, n_queries, HD), jnp.float32),
        ],
        compiler_params=pltpu.CompilerParams(vmem_limit_bytes=32 * 2**20),
        cost_estimate=pl.CostEstimate(flops=flops, bytes_accessed=22 * 2**20, transcendentals=0),
        name="keys",
    )(offsets, normed, other, image_q, *arrays)

    stats = jnp.stack([maxes[:, :, 0], sums[:, :, 0]]).reshape(2, HALF_KVH, 2, images, GROUP)
    all_stats = lax.all_gather(stats, "section", axis=0, tiled=False)
    all_stats = all_stats.reshape(n // 2, 2, 2, HALF_KVH, 2, images, GROUP)
    flipped = jnp.stack([all_stats[:, 0], all_stats[:, 1, :, :, ::-1]], axis=1)
    by_image = flipped.transpose(0, 4, 5, 2, 1, 3, 6).reshape(n, images, 2, QH)
    mine = (all_target // decode_rows) == section
    slot_stats = jnp.sum(jnp.where(mine[:, :, None, None], by_image, 0.0), axis=1)
    slot_has = jnp.any(mine, axis=1)
    slot_row = jnp.sum(jnp.where(mine, all_target % decode_rows, 0), axis=1)
    joins = slot_has[None, :] & (slot_row[None, :] == jnp.arange(decode_rows)[:, None])
    slot_max = jnp.where(joins[:, :, None], slot_stats[None, :, 0], masked_score)
    row_top = jnp.maximum(res_top, jnp.max(slot_max, axis=1))
    res_factor = jnp.exp(res_top - row_top)
    slot_factor = jnp.where(joins[:, :, None], jnp.exp(slot_max - row_top[:, None]), 0.0)
    denominator = res_sum * res_factor + jnp.sum(slot_factor * slot_stats[None, :, 1], axis=1)
    slot_factor = jnp.sum(slot_factor / denominator[:, None], axis=0)
    base = res_out * (res_factor / denominator)[..., None]
    factor = jnp.broadcast_to(slot_factor[..., None], (n, QH, HD))

    arrays, layout, offsets = granules(phases[1], rows_dev, core, size)
    slot = jnp.concatenate([image_owner * 2 + core, chip_target[images:] // decode_rows * 2 + 1 - core])
    slots = pl.pallas_call(
        functools.partial(value_kernel, layout, size, len(arrays)),
        grid_spec=pltpu.PrefetchScalarGridSpec(
            num_scalar_prefetch=2,
            grid=(steps,),
            in_specs=[
                token_spec,
                token_spec,
                pl.BlockSpec((HALF_KVH, n_queries, 2 * tokens), lambda i, *_: (0, 0, 0)),
            ]
            + [pl.BlockSpec(memory_space=pl.ANY)] * len(arrays),
            out_specs=pl.BlockSpec((2 * n, HALF_QH, HD), lambda i, *_: (0, 0, 0)),
            scratch_shapes=[
                pltpu.VMEM((width, 2 * HD), jnp.bfloat16),
                pltpu.VMEM((2 * tokens, 2 * HD), jnp.float32),
                pltpu.VMEM((2 * images, HALF_QH, HD), jnp.float32),
                pltpu.SemaphoreType.DMA((len(layout),)),
            ],
        ),
        out_shape=jax.ShapeDtypeStruct((2 * n, HALF_QH, HD), jnp.bfloat16),
        compiler_params=pltpu.CompilerParams(vmem_limit_bytes=32 * 2**20),
        cost_estimate=pl.CostEstimate(flops=flops, bytes_accessed=22 * 2**20, transcendentals=0),
        name="values",
    )(offsets, slot, normed, other, weights, *arrays)
    got = lax.all_to_all(
        slots.reshape(n, 2, HALF_QH, HD), "section", split_axis=0, concat_axis=0, tiled=True
    ).reshape(2 * n, HALF_QH, HD)

    return pl.pallas_call(
        combine_kernel,
        grid_spec=pltpu.PrefetchScalarGridSpec(
            num_scalar_prefetch=1,
            grid=(1,),
            in_specs=[
                pl.BlockSpec((2 * n, HALF_QH, HD), lambda i, *_: (0, 0, 0)),
                pl.BlockSpec((n, QH, HD), lambda i, *_: (0, 0, 0)),
                pl.BlockSpec((decode_rows, QH, HD), lambda i, *_: (0, 0, 0)),
            ],
            out_specs=pl.BlockSpec((decode_rows, QH * HD), lambda i, *_: (0, 0)),
            scratch_shapes=[pltpu.VMEM((decode_rows, QH, HD), jnp.float32)],
        ),
        out_shape=jax.ShapeDtypeStruct((decode_rows, QH * HD), jnp.bfloat16),
        compiler_params=pltpu.CompilerParams(vmem_limit_bytes=32 * 2**20),
        name="combine",
    )(slot_row, got, factor, base)


def solution(mesh):
    placed = (
        P(("replica", "section"), None),
        P("section", None),
        P(("replica", "section")),
        P(("replica", "section")),
        P(("replica", "section"), None),
        P(("replica", "section"), None, None),
        P(("replica", "section")),
    )
    return jax.shard_map(
        per_device,
        mesh=mesh,
        in_specs=placed,
        out_specs=P(("replica", "section"), None),
        check_vma=False,
    )
```

time: 226 us -> 249 us (1.10)
  the two profiles are of different devices: /device:TPU:13 before, /device:TPU:0 now
where the time goes in v1:
time: 249 us; the launch traced here: 248 us
  blocking collectives  76 us (31%)
  starting transfers between devices  41.3 us (17%)
  waiting for transfers between devices  38.2 us (15%)
  Pallas kernels  35.7 us (14%)
  local copies, waits for them, and re-layouts  23 us (9%)
  other arithmetic  22.7 us (9%)
  between operations  7.91 us (3%)
  matrix products  2.97 us (1%)
    all_gather x1, blocking collectives, per_device(): lax.all_gather(chip_q, 'section', axis=0, tiled=True, axis_index_groups=s...  32.7 us
    ppermute x14, starting transfers between devices, swap_replica(): return lax.ppermute(x, 'replica', [(i, i ^ 1) for i in range(count)])  23.6 us
    all_gather x1, blocking collectives, per_device(): all_stats = lax.all_gather(stats, 'section', axis=0, tiled=False)  23.2 us
    unnamed x1, blocking collectives  20.2 us
    ppermute x8, waiting for transfers between devices, gather_grid(): along_y.append(lax.ppermute(along_z[step], 'section', swap_y))  17.9 us
    pallas_call x1, Pallas kernels, per_device(): pl.pallas_call(functools.partial(value_kernel, layout, size, len(arrays))...  17.3 us
    pallas_call x1, Pallas kernels, per_device(): pl.pallas_call(functools.partial(key_kernel, layout, size, len(arrays)),...  16.9 us
    ppermute x14, waiting for transfers between devices, swap_replica(): return lax.ppermute(x, 'replica', [(i, i ^ 1) for i in range(count)])  12.8 us
  transfers between devices with their start and end apart: 33, of which 11 were waited for; matrix products, arithmetic and copies ran while one was open for 12% of the time, Pallas kernels for 7%

profile of v1, /device:TPU:0, one launch (start us, length us, event | category | flops | bytes accessed | tf_op | source)
XLA Modules:
  0.0 247.8 jit_solution(16279944885420483784)
XLA Ops:
  0.0 5.1 %fusion = f32[512]{0:T(512)S(1)} fusion(bf16[512,8192]{1,0:T(8,128)(2,1)} %param.9), kind=kLoop, calls=%fused_computation.2 | loop fusion | flops 12582400 | bytes 8390656 | tf_op jit(solution)/shard_map/reduce_sum | solution.py:25
  5.1 9.7 %fusion.1.own_ref = bf16[512,8192]{1,0:T(8,128)(2,1)} fusion(bf16[512,8192]{1,0:T(8,128)(2,1)} %param.9, f32[512]{0:T(512)S(1)} %add_rsqrt_fusion), kind=kLoop, calls=%fused_computation.3 | loop fusion | flops 12582912 | bytes 16779264 | tf_op jit(solution)/shard_map/convert_element_type | solution.py:227
  14.8 0.5 collective-permute-start
  15.2 0.5 copy.41
  16.4 0.9 slice_bitcast_fusion
  17.3 0.5 collective-permute-start.17
  17.8 0.6 dynamic-slice.4
  19.0 0.6 fusion.34
  19.7 20.2 %all-reduce = s32[128]{0:T(128)S(1)} all-reduce(s32[128]{0:T(128)S(1)} %get-tuple-element.28), channel_id=2, replica_groups=mesh['replica'=2,'section'=16] {'section'}, use_global_device_ids=true, to_apply=%add | all-reduce | flops 128 | bytes 1024
  40.0 4.5 %fusion.35 = (bf16[8,256,512]{2,1,0:T(8,128)(2,1)}, bf16[8,256,512]{2,1,0:T(8,128)(2,1)}) fusion(bf16[8,256,1024]{2,1,0:T(8,128)(2,1)} %param.14), kind=kLoop, calls=%fused_computation.92 | loop fusion | bytes 8388608 | tf_op jit(solution)/shard_map/slice | solution.py:188
  44.5 2.9 %copy.54 = bf16[8,256,512]{1,2,0:T(8,128)(2,1)S(1)} copy(bf16[8,256,512]{2,1,0:T(8,128)(2,1)} %get-tuple-element.31) | data formatting | bytes 4194304
  47.5 0.5 fusion.39
  48.3 0.4 fusion.7
  48.7 0.6 collective-permute-start.3
  49.3 0.4 collective-permute-start.5
  49.7 1.4 fusion.6
  51.1 0.6 fusion.27
  51.7 1.8 collective-permute-start.18
  53.6 0.9 fusion.9
  54.4 3.5 %collective-permute-done.3.refs_1_ = bf16[512,256]{1,0:T(8,128)(2,1)S(1)} collective-permute-done((bf16[512,256]{1,0:T(8,128)(2,1)S(1)}, bf16[512,256]{1,0:T(8,128)(2,1)S(1)}, u32[]{:S(2)}, u32[]{:S(2)}) %collective-permute-start.3) | collective-permute-done | bytes 262176 | tf_op jit(solution)/shard_map/ppermute | solution.py:63
  58.0 2.4 collective-permute-start.4
  60.4 1.4 collective-permute-start.6
  61.8 0.7 pad_add_fusion.slot_ref
  62.5 1.6 collective-permute-done.20.refs_3_
  64.2 1.3 broadcast_select_fusion.1
  65.4 1.2 dynamic_slice.57
  70.8 1.4 fusion.38
  74.9 0.7 reshape.216
  75.5 0.6 broadcast_in_dim.99
  76.1 0.7 reshape.217
  76.8 3.9 %copy.55 = bf16[8,256,512]{1,2,0:T(8,128)(2,1)} copy(bf16[8,256,512]{2,1,0:T(8,128)(2,1)} %get-tuple-element.30) | data formatting | bytes 4194304
  81.1 1.2 collective-permute-done.1
  82.2 1.5 collective-permute-start.7
  83.7 0.6 collective-permute-start.9
  84.4 2.4 collective-permute-start.19
  86.8 1.7 collective-permute-start.28
  88.5 2.1 collective-permute-done.7.refs_5_
  90.6 2.4 collective-permute-start.21
  93.0 0.8 collective-permute-done.9.refs_7_
  93.8 0.8 collective-permute-start.22
  94.5 2.2 collective-permute-start.8
  96.7 32.7 %all_gather.14 = bf16[128,2048]{1,0:T(8,128)(2,1)S(1)} all-gather(bf16[16,2048]{1,0:T(8,128)(2,1)S(1)} %pad_maximum_fusion.2), channel_id=1, replica_groups={{0,2,4,6,8,10,12,14},{1,3,5,7,9,11,13,15},{16,18,20,22,24,26,28,30},{17..., dimensions={0}, use_global_device_ids=true | all-gather | bytes 589824 | tf_op jit(solution)/shard_map/all_gather | solution.py:237
  129.9 2.0 collective-permute-start.30
  131.9 1.0 pad_maximum_fusion.refs_0_
  132.9 3.9 %collective-permute-done.13.refs_11_ = bf16[512,256]{1,0:T(8,128)(2,1)S(1)} collective-permute-done((bf16[512,256]{1,0:T(8,128)(2,1)S(1)}, bf16[512,256]{1,0:T(8,128)(2,1)S(1)}, u32[]{:S(2)}, u32[]{:S(2)}) %collective-permute-start.13) | collective-permute-done | bytes 262176 | tf_op jit(solution)/shard_map/ppermute | solution.py:62
  136.8 2.0 collective-permute-start.15
  138.9 11.7 %collective-permute-done.11.refs_9_ = bf16[512,256]{1,0:T(8,128)(2,1)S(1)} collective-permute-done((bf16[512,256]{1,0:T(8,128)(2,1)S(1)}, bf16[512,256]{1,0:T(8,128)(2,1)S(1)}, u32[]{:S(2)}, u32[]{:S(2)}) %collective-permute-start.11) | collective-permute-done | bytes 262176 | tf_op jit(solution)/shard_map/ppermute | solution.py:63
  150.6 2.3 collective-permute-start.10
  152.9 0.5 collective-permute-done.15.refs_13_
  153.4 2.3 collective-permute-start.14
  155.7 2.0 collective-permute-start.16
  157.8 2.3 collective-permute-done.10.refs_8_
  160.1 2.0 collective-permute-start.23
  162.1 9.2 %collective-permute-done.12.refs_10_ = bf16[512,256]{1,0:T(8,128)(2,1)S(1)} collective-permute-done((bf16[512,256]{1,0:T(8,128)(2,1)S(1)}, bf16[512,256]{1,0:T(8,128)(2,1)S(1)}, u32[]{:S(2)}, u32[]{:S(2)}) %collective-permute-start.12) | collective-permute-done | bytes 262176 | tf_op jit(solution)/shard_map/ppermute | solution.py:34
  171.3 2.0 collective-permute-start.25
  173.4 1.3 collective-permute-done.16.refs_14_
  174.7 1.7 collective-permute-start.29
  176.7 3.4 %copy-done = bf16[512,8192]{1,0:T(8,128)(2,1)S(1)} copy-done((bf16[512,8192]{1,0:T(8,128)(2,1)S(1)}, bf16[512,8192]{1,0:T(8,128)(2,1)}, u32[]{:S(2)}) %copy-start) | copy-done | bytes 8388632
  180.1 16.9 %keys.1 = (bf16[2,128,1024]{2,1,0:T(8,128)(2,1)S(1)}, f32[2,128,128]{2,1,0:T(8,128)S(1)}, f32[2,128,128]{2,1,0:T(8,128)S(1)}) custom-call(s32[32]{0:T(128)S(1)} %stack.261.offsets_ref, bf16[512,8192]{1,0:T(8,128)(2,1)S(1)} %copy-done, bf16[512,8192]{1,0:T(8,128)(2,1)} %collective-permute-done.other_ref, bf16[2,128,128]{2,1,0:T(8,128)(2,1)S(1)} %bitcast.117, ...), custom_call_target="tpu_custom_call" | custom-call | flops 4294967296 | bytes 23068672 | tf_op jit(solution)/shard_map/keys/pallas_call | solution.py:254
  197.1 17.3 %values.1 = bf16[32,16,128]{2,1,0:T(8,128)(2,1)} custom-call(s32[32]{0:T(128)S(1)} %stack.232.offsets_ref, s32[16]{0:T(128)S(1)} %pad_add_fusion.slot_ref, bf16[512,8192]{1,0:T(8,128)(2,1)S(1)} %copy-done, bf16[512,8192]{1,0:T(8,128)(2,1)} %collective-permute-done.other_ref, bf16[2,128,1024]{2,1,0:T(8,128)(2,1)S(1)} %get-tuple-element.8.weights_ref, ...), custom_call_target="tpu_custom_call" | custom-call | flops 4294967296 | bytes 23068672 | tf_op jit(solution)/shard_map/values/pallas_call | solution.py:303
  214.4 5.1 %all-to-all-start = ((bf16[16,2,16,128]{3,2,1,0:T(8,128)(2,1)}), bf16[16,2,16,128]{3,2,1,0:T(8,128)(2,1)S(1)}, u32[]{:S(2)}, u32[]{:S(2)}) async-start(bf16[16,2,16,128]{3,2,1,0:T(8,128)(2,1)} %bitcast.79), calls=%async_computation | async-start | bytes 262144 | tf_op jit(solution)/shard_map/all_to_all | solution.py:327
  219.9 23.2 %all_gather.15 = f32[16,2,2,2,8,8]{5,4,3,2,1,0:T(8,128)S(1)} all-gather(f32[1,2,2,2,8,8]{5,4,3,2,1,0:T(8,128)S(1)} %pad_maximum_fusion.3), channel_id=1, replica_groups=mesh['replica'=2,'section'=16] {'section'}, dimensions={0}, use_global_device_ids=true | all-gather | bytes 34816 | tf_op jit(solution)/shard_map/all_gather | solution.py:283
  244.0 2.3 fusion.3.base_ref
  246.4 1.5 combine.1
  (102 shorter events, 3.7 us)
Async XLA Ops:
  5.1 10.1 %copy-start.1 = (bf16[512,1024]{1,0:T(8,128)(2,1)S(1)}, bf16[512,1024]{1,0:T(8,128)(2,1)}, u32[]{:S(2)}) copy-start(bf16[512,1024]{1,0:T(8,128)(2,1)} %param.10) | copy-start | bytes 3145732
  14.8 161.6 %collective-permute-start = (bf16[512,8192]{1,0:T(8,128)(2,1)}, bf16[512,8192]{1,0:T(8,128)(2,1)}, u32[]{:S(2)}, u32[]{:S(2)}) collective-permute-start(bf16[512,8192]{1,0:T(8,128)(2,1)} %fusion.1.own_ref), channel_id=1, source_target_pairs={{0,1},{1,0},{2,3},{3,2},{4,5},{5,4},{6,7},{7,6},{8,9},{9,8},{10,11... | collective-permute-start | bytes 25165832 | tf_op jit(solution)/shard_map/ppermute | solution.py:29
  15.8 2.0 copy-start.13
  15.8 3.2 %copy-start.10 = (s32[8]{0:T(128)S(1)}, s32[8]{0:T(128)}, u32[]{:S(2)}) copy-start(s32[8]{0:T(128)} %param.12) | copy-start | bytes 100
  15.8 3.2 %copy-start.11 = (s32[8]{0:T(128)S(1)}, s32[8]{0:T(128)}, u32[]{:S(2)}) copy-start(s32[8]{0:T(128)} %param.11) | copy-start | bytes 100
  17.3 31.0 %collective-permute-start.2 = (bf16[512,256]{1,0:T(8,128)(2,1)}, bf16[512,256]{1,0:T(8,128)(2,1)}, u32[]{:S(2)}, u32[]{:S(2)}) collective-permute-start(bf16[512,256]{1,0:T(8,128)(2,1)} %get-tuple-element.41), channel_id=1, source_target_pairs={{0,1},{1,0},{2,3},{3,2},{4,5},{5,4},{6,7},{7,6},{8,9},{9,8},{10,11... | collective-permute-start | bytes 786440 | tf_op jit(solution)/shard_map/ppermute | solution.py:29
  17.3 32.4 %collective-permute-start.17 = (bf16[512,256]{1,0:T(8,128)(2,1)}, bf16[512,256]{1,0:T(8,128)(2,1)S(1)}, u32[]{:S(2)}, u32[]{:S(2)}) collective-permute-start(bf16[512,256]{1,0:T(8,128)(2,1)} %get-tuple-element.40), channel_id=1, source_target_pairs={{0,1},{1,0},{2,3},{3,2},{4,5},{5,4},{6,7},{7,6},{8,9},{9,8},{10,11... | collective-permute-start | bytes 786440 | tf_op jit(solution)/shard_map/ppermute | solution.py:29
  44.5 2.9 %copy-start.12 = (s32[8]{0:T(128)S(1)}, s32[8]{0:T(128)}, u32[]{:S(2)}) copy-start(s32[8]{0:T(128)} %param.15) | copy-start | bytes 100
  44.5 3.0 %copy-start.2 = (bf16[8,4096]{1,0:T(8,128)(2,1)S(1)}, bf16[8,4096]{1,0:T(8,128)(2,1)}, u32[]{:S(2)}) copy-start(bf16[8,4096]{1,0:T(8,128)(2,1)} %param.13) | copy-start | bytes 196612
  47.5 0.8 copy-start.4
  48.7 9.3 %collective-permute-start.3 = (bf16[512,256]{1,0:T(8,128)(2,1)S(1)}, bf16[512,256]{1,0:T(8,128)(2,1)S(1)}, u32[]{:S(2)}, u32[]{:S(2)}) collective-permute-start(bf16[512,256]{1,0:T(8,128)(2,1)S(1)} %fusion.7), channel_id=1, source_target_pairs={{0,2},{1,3},{2,0},{3,1},{4,6},{5,7},{6,4},{7,5},{8,10},{9,11},{10,... | collective-permute-start | bytes 786440 | tf_op jit(solution)/shard_map/ppermute | solution.py:63
  49.3 11.2 %collective-permute-start.5 = (bf16[512,256]{1,0:T(8,128)(2,1)S(1)}, bf16[512,256]{1,0:T(8,128)(2,1)S(1)}, u32[]{:S(2)}, u32[]{:S(2)}) collective-permute-start(bf16[512,256]{1,0:T(8,128)(2,1)S(1)} %fusion.7), channel_id=1, source_target_pairs={{0,4},{1,5},{2,6},{3,7},{4,12},{5,13},{6,14},{7,15},{12,8},{13,9},... | collective-permute-start | bytes 786440 | tf_op jit(solution)/shard_map/ppermute | solution.py:62
  51.1 13.1 %collective-permute-start.20 = (bf16[768,256]{1,0:T(8,128)(2,1)}, bf16[768,256]{1,0:T(8,128)(2,1)S(1)}, u32[]{:S(2)}, u32[]{:S(2)}) collective-permute-start(bf16[768,256]{1,0:T(8,128)(2,1)} %fusion.6), channel_id=1, source_target_pairs={{0,4},{1,5},{2,6},{3,7},{4,12},{5,13},{6,14},{7,15},{12,8},{13,9},... | collective-permute-start | bytes 1179656 | tf_op jit(solution)/shard_map/ppermute | solution.py:62
  51.7 29.2 %collective-permute-start.18 = (bf16[768,256]{1,0:T(8,128)(2,1)}, bf16[768,256]{1,0:T(8,128)(2,1)S(1)}, u32[]{:S(2)}, u32[]{:S(2)}) collective-permute-start(bf16[768,256]{1,0:T(8,128)(2,1)} %fusion.6), channel_id=1, source_target_pairs={{0,2},{1,3},{2,0},{3,1},{4,6},{5,7},{6,4},{7,5},{8,10},{9,11},{10,... | collective-permute-start | bytes 1179656 | tf_op jit(solution)/shard_map/ppermute | solution.py:63
  58.0 25.8 %collective-permute-start.4 = (bf16[512,256]{1,0:T(8,128)(2,1)S(1)}, bf16[512,256]{1,0:T(8,128)(2,1)S(1)}, u32[]{:S(2)}, u32[]{:S(2)}) collective-permute-start(bf16[512,256]{1,0:T(8,128)(2,1)S(1)} %collective-permute-done.3.refs_1_), channel_id=1, source_target_pairs={{0,16},{16,0},{1,17},{17,1},{2,18},{18,2},{3,19},{19,3},{4,20},{20... | collective-permute-start | bytes 786440 | tf_op jit(solution)/shard_map/ppermute | solution.py:34
  60.4 23.9 %collective-permute-start.6 = (bf16[512,256]{1,0:T(8,128)(2,1)S(1)}, bf16[512,256]{1,0:T(8,128)(2,1)S(1)}, u32[]{:S(2)}, u32[]{:S(2)}) collective-permute-start(bf16[512,256]{1,0:T(8,128)(2,1)S(1)} %collective-permute-done.5.refs_3_), channel_id=1, source_target_pairs={{0,16},{16,0},{1,17},{17,1},{2,18},{18,2},{3,19},{19,3},{4,20},{20... | collective-permute-start | bytes 786440 | tf_op jit(solution)/shard_map/ppermute | solution.py:34
  64.2 22.6 %collective-permute-start.24 = (bf16[768,256]{1,0:T(8,128)(2,1)S(1)}, bf16[768,256]{1,0:T(8,128)(2,1)S(1)}, u32[]{:S(2)}, u32[]{:S(2)}) collective-permute-start(bf16[768,256]{1,0:T(8,128)(2,1)S(1)} %collective-permute-done.20.refs_3_), channel_id=1, source_target_pairs={{0,4},{1,5},{2,6},{3,7},{4,12},{5,13},{6,14},{7,15},{12,8},{13,9},... | collective-permute-start | bytes 1179656 | tf_op jit(solution)/shard_map/ppermute | solution.py:62
  76.8 52.7 %copy-start.9 = (s32[16]{0:T(128)S(1)}, s32[16]{0:T(128)}, u32[]{:S(2)}) copy-start(s32[16]{0:T(128)} %broadcast_select_fusion.1) | copy-start | bytes 196
  80.9 1.3 collective-permute-start.1
  82.2 8.4 %collective-permute-start.7 = (bf16[512,256]{1,0:T(8,128)(2,1)S(1)}, bf16[512,256]{1,0:T(8,128)(2,1)S(1)}, u32[]{:S(2)}, u32[]{:S(2)}) collective-permute-start(bf16[512,256]{1,0:T(8,128)(2,1)S(1)} %collective-permute-done.5.refs_3_), channel_id=1, source_target_pairs={{0,2},{1,3},{2,0},{3,1},{4,6},{5,7},{6,4},{7,5},{8,10},{9,11},{10,... | collective-permute-start | bytes 786440 | tf_op jit(solution)/shard_map/ppermute | solution.py:63
  83.7 10.1 %collective-permute-start.9 = (bf16[512,256]{1,0:T(8,128)(2,1)S(1)}, bf16[512,256]{1,0:T(8,128)(2,1)S(1)}, u32[]{:S(2)}, u32[]{:S(2)}) collective-permute-start(bf16[512,256]{1,0:T(8,128)(2,1)S(1)} %collective-permute-done.5.refs_3_), channel_id=1, source_target_pairs={{0,4},{1,5},{2,6},{3,7},{4,12},{5,13},{6,14},{7,15},{12,8},{13,9},... | collective-permute-start | bytes 786440 | tf_op jit(solution)/shard_map/ppermute | solution.py:62
  84.4 10.2 %collective-permute-start.19 = (bf16[256,256]{1,0:T(8,128)(2,1)S(1)}, bf16[256,256]{1,0:T(8,128)(2,1)S(1)}, u32[]{:S(2)}, u32[]{:S(2)}) collective-permute-start(bf16[256,256]{1,0:T(8,128)(2,1)S(1)} %constant_dynamic-slice_fusion.1), channel_id=1, source_target_pairs={{0,16},{16,0},{1,17},{17,1},{2,18},{18,2},{3,19},{19,3},{4,20},{20... | collective-permute-start | bytes 393224 | tf_op jit(solution)/shard_map/ppermute | solution.py:34
  86.8 43.1 %collective-permute-start.28 = (bf16[768,256]{1,0:T(8,128)(2,1)S(1)}, bf16[768,256]{1,0:T(8,128)(2,1)S(1)}, u32[]{:S(2)}, u32[]{:S(2)}) collective-permute-start(bf16[768,256]{1,0:T(8,128)(2,1)S(1)} %collective-permute-done.24.refs_7_), channel_id=1, source_target_pairs={{0,4},{1,5},{2,6},{3,7},{4,12},{5,13},{6,14},{7,15},{12,8},{13,9},... | collective-permute-start | bytes 1179656 | tf_op jit(solution)/shard_map/ppermute | solution.py:62
  90.6 38.8 %collective-permute-start.21 = (bf16[256,256]{1,0:T(8,128)(2,1)S(1)}, bf16[256,256]{1,0:T(8,128)(2,1)S(1)}, u32[]{:S(2)}, u32[]{:S(2)}) collective-permute-start(bf16[256,256]{1,0:T(8,128)(2,1)S(1)} %constant_dynamic-slice_fusion.2), channel_id=1, source_target_pairs={{0,16},{16,0},{1,17},{17,1},{2,18},{18,2},{3,19},{19,3},{4,20},{20... | collective-permute-start | bytes 393224 | tf_op jit(solution)/shard_map/ppermute | solution.py:34
  93.8 43.0 %collective-permute-start.22 = (bf16[768,256]{1,0:T(8,128)(2,1)S(1)}, bf16[768,256]{1,0:T(8,128)(2,1)S(1)}, u32[]{:S(2)}, u32[]{:S(2)}) collective-permute-start(bf16[768,256]{1,0:T(8,128)(2,1)S(1)} %collective-permute-done.20.refs_3_), channel_id=1, source_target_pairs={{0,2},{1,3},{2,0},{3,1},{4,6},{5,7},{6,4},{7,5},{8,10},{9,11},{10,... | collective-permute-start | bytes 1179656 | tf_op jit(solution)/shard_map/ppermute | solution.py:63
  94.5 35.2 %collective-permute-start.8 = (bf16[512,256]{1,0:T(8,128)(2,1)S(1)}, bf16[512,256]{1,0:T(8,128)(2,1)S(1)}, u32[]{:S(2)}, u32[]{:S(2)}) collective-permute-start(bf16[512,256]{1,0:T(8,128)(2,1)S(1)} %collective-permute-done.7.refs_5_), channel_id=1, source_target_pairs={{0,16},{16,0},{1,17},{17,1},{2,18},{18,2},{3,19},{19,3},{4,20},{20... | collective-permute-start | bytes 786440 | tf_op jit(solution)/shard_map/ppermute | solution.py:34
  129.4 7.3 %collective-permute-start.13 = (bf16[512,256]{1,0:T(8,128)(2,1)S(1)}, bf16[512,256]{1,0:T(8,128)(2,1)S(1)}, u32[]{:S(2)}, u32[]{:S(2)}) collective-permute-start(bf16[512,256]{1,0:T(8,128)(2,1)S(1)} %collective-permute-done.9.refs_7_), channel_id=1, source_target_pairs={{0,4},{1,5},{2,6},{3,7},{4,12},{5,13},{6,14},{7,15},{12,8},{13,9},... | collective-permute-start | bytes 786440 | tf_op jit(solution)/shard_map/ppermute | solution.py:62
  129.8 25.9 %collective-permute-start.26 = (bf16[768,256]{1,0:T(8,128)(2,1)S(1)}, bf16[768,256]{1,0:T(8,128)(2,1)S(1)}, u32[]{:S(2)}, u32[]{:S(2)}) collective-permute-start(bf16[768,256]{1,0:T(8,128)(2,1)S(1)} %collective-permute-done.24.refs_7_), channel_id=1, source_target_pairs={{0,2},{1,3},{2,0},{3,1},{4,6},{5,7},{6,4},{7,5},{8,10},{9,11},{10,... | collective-permute-start | bytes 1179656 | tf_op jit(solution)/shard_map/ppermute | solution.py:63
  129.9 25.8 %collective-permute-start.30 = (bf16[768,256]{1,0:T(8,128)(2,1)S(1)}, bf16[768,256]{1,0:T(8,128)(2,1)S(1)}, u32[]{:S(2)}, u32[]{:S(2)}) collective-permute-start(bf16[768,256]{1,0:T(8,128)(2,1)S(1)} %collective-permute-done.28.refs_11_), channel_id=1, source_target_pairs={{0,2},{1,3},{2,0},{3,1},{4,6},{5,7},{6,4},{7,5},{8,10},{9,11},{10,... | collective-permute-start | bytes 1179656 | tf_op jit(solution)/shard_map/ppermute | solution.py:63
  136.7 13.9 %collective-permute-start.11 = (bf16[512,256]{1,0:T(8,128)(2,1)S(1)}, bf16[512,256]{1,0:T(8,128)(2,1)S(1)}, u32[]{:S(2)}, u32[]{:S(2)}) collective-permute-start(bf16[512,256]{1,0:T(8,128)(2,1)S(1)} %collective-permute-done.9.refs_7_), channel_id=1, source_target_pairs={{0,2},{1,3},{2,0},{3,1},{4,6},{5,7},{6,4},{7,5},{8,10},{9,11},{10,... | collective-permute-start | bytes 786440 | tf_op jit(solution)/shard_map/ppermute | solution.py:63
  136.8 16.6 %collective-permute-start.15 = (bf16[512,256]{1,0:T(8,128)(2,1)S(1)}, bf16[512,256]{1,0:T(8,128)(2,1)S(1)}, u32[]{:S(2)}, u32[]{:S(2)}) collective-permute-start(bf16[512,256]{1,0:T(8,128)(2,1)S(1)} %collective-permute-done.13.refs_11_), channel_id=1, source_target_pairs={{0,2},{1,3},{2,0},{3,1},{4,6},{5,7},{6,4},{7,5},{8,10},{9,11},{10,... | collective-permute-start | bytes 786440 | tf_op jit(solution)/shard_map/ppermute | solution.py:63
  150.6 9.5 %collective-permute-start.10 = (bf16[512,256]{1,0:T(8,128)(2,1)S(1)}, bf16[512,256]{1,0:T(8,128)(2,1)S(1)}, u32[]{:S(2)}, u32[]{:S(2)}) collective-permute-start(bf16[512,256]{1,0:T(8,128)(2,1)S(1)} %collective-permute-done.9.refs_7_), channel_id=1, source_target_pairs={{0,16},{16,0},{1,17},{17,1},{2,18},{18,2},{3,19},{19,3},{4,20},{20... | collective-permute-start | bytes 786440 | tf_op jit(solution)/shard_map/ppermute | solution.py:34
  153.4 19.9 %collective-permute-start.14 = (bf16[512,256]{1,0:T(8,128)(2,1)S(1)}, bf16[512,256]{1,0:T(8,128)(2,1)S(1)}, u32[]{:S(2)}, u32[]{:S(2)}) collective-permute-start(bf16[512,256]{1,0:T(8,128)(2,1)S(1)} %collective-permute-done.13.refs_11_), channel_id=1, source_target_pairs={{0,16},{16,0},{1,17},{17,1},{2,18},{18,2},{3,19},{19,3},{4,20},{20... | collective-permute-start | bytes 786440 | tf_op jit(solution)/shard_map/ppermute | solution.py:34
  155.7 15.6 %collective-permute-start.12 = (bf16[512,256]{1,0:T(8,128)(2,1)S(1)}, bf16[512,256]{1,0:T(8,128)(2,1)S(1)}, u32[]{:S(2)}, u32[]{:S(2)}) collective-permute-start(bf16[512,256]{1,0:T(8,128)(2,1)S(1)} %collective-permute-done.11.refs_9_), channel_id=1, source_target_pairs={{0,16},{16,0},{1,17},{17,1},{2,18},{18,2},{3,19},{19,3},{4,20},{20... | collective-permute-start | bytes 786440 | tf_op jit(solution)/shard_map/ppermute | solution.py:34
  155.7 18.9 %collective-permute-start.16 = (bf16[512,256]{1,0:T(8,128)(2,1)S(1)}, bf16[512,256]{1,0:T(8,128)(2,1)S(1)}, u32[]{:S(2)}, u32[]{:S(2)}) collective-permute-start(bf16[512,256]{1,0:T(8,128)(2,1)S(1)} %collective-permute-done.15.refs_13_), channel_id=1, source_target_pairs={{0,16},{16,0},{1,17},{17,1},{2,18},{18,2},{3,19},{19,3},{4,20},{20... | collective-permute-start | bytes 786440 | tf_op jit(solution)/shard_map/ppermute | solution.py:34
  160.1 36.9 %collective-permute-start.23 = (bf16[256,256]{1,0:T(8,128)(2,1)S(1)}, bf16[256,256]{1,0:T(8,128)(2,1)S(1)}, u32[]{:S(2)}, u32[]{:S(2)}) collective-permute-start(bf16[256,256]{1,0:T(8,128)(2,1)S(1)} %constant_dynamic-slice_fusion.3), channel_id=1, source_target_pairs={{0,16},{16,0},{1,17},{17,1},{2,18},{18,2},{3,19},{19,3},{4,20},{20... | collective-permute-start | bytes 393224 | tf_op jit(solution)/shard_map/ppermute | solution.py:34
  171.3 25.7 %collective-permute-start.25 = (bf16[256,256]{1,0:T(8,128)(2,1)S(1)}, bf16[256,256]{1,0:T(8,128)(2,1)S(1)}, u32[]{:S(2)}, u32[]{:S(2)}) collective-permute-start(bf16[256,256]{1,0:T(8,128)(2,1)S(1)} %constant_dynamic-slice_fusion.4), channel_id=1, source_target_pairs={{0,16},{16,0},{1,17},{17,1},{2,18},{18,2},{3,19},{19,3},{4,20},{20... | collective-permute-start | bytes 393224 | tf_op jit(solution)/shard_map/ppermute | solution.py:34
  173.4 23.6 %collective-permute-start.27 = (bf16[256,256]{1,0:T(8,128)(2,1)S(1)}, bf16[256,256]{1,0:T(8,128)(2,1)S(1)}, u32[]{:S(2)}, u32[]{:S(2)}) collective-permute-start(bf16[256,256]{1,0:T(8,128)(2,1)S(1)} %constant_dynamic-slice_fusion.5), channel_id=1, source_target_pairs={{0,16},{16,0},{1,17},{17,1},{2,18},{18,2},{3,19},{19,3},{4,20},{20... | collective-permute-start | bytes 393224 | tf_op jit(solution)/shard_map/ppermute | solution.py:34
  174.7 22.3 %collective-permute-start.29 = (bf16[256,256]{1,0:T(8,128)(2,1)S(1)}, bf16[256,256]{1,0:T(8,128)(2,1)S(1)}, u32[]{:S(2)}, u32[]{:S(2)}) collective-permute-start(bf16[256,256]{1,0:T(8,128)(2,1)S(1)} %constant_dynamic-slice_fusion.6), channel_id=1, source_target_pairs={{0,16},{16,0},{1,17},{17,1},{2,18},{18,2},{3,19},{19,3},{4,20},{20... | collective-permute-start | bytes 393224 | tf_op jit(solution)/shard_map/ppermute | solution.py:34
  176.4 20.6 %collective-permute-start.31 = (bf16[256,256]{1,0:T(8,128)(2,1)S(1)}, bf16[256,256]{1,0:T(8,128)(2,1)S(1)}, u32[]{:S(2)}, u32[]{:S(2)}) collective-permute-start(bf16[256,256]{1,0:T(8,128)(2,1)S(1)} %constant_dynamic-slice_fusion.7), channel_id=1, source_target_pairs={{0,16},{16,0},{1,17},{17,1},{2,18},{18,2},{3,19},{19,3},{4,20},{20... | collective-permute-start | bytes 393224 | tf_op jit(solution)/shard_map/ppermute | solution.py:34
  176.7 3.4 %copy-start = (bf16[512,8192]{1,0:T(8,128)(2,1)S(1)}, bf16[512,8192]{1,0:T(8,128)(2,1)}, u32[]{:S(2)}) copy-start(bf16[512,8192]{1,0:T(8,128)(2,1)} %fusion.1.own_ref) | copy-start | bytes 25165828
  197.0 46.1 %copy-start.6 = (pred[8,2,8]{2,1,0:T(4,128)(4,1)S(1)}, pred[8,2,8]{2,1,0:T(4,128)(4,1)}, u32[]{:S(2)}) copy-start(pred[8,2,8]{2,1,0:T(4,128)(4,1)} %broadcast_in_dim.99) | copy-start | bytes 388
  197.0 46.5 %copy-start.8 = (pred[8,16]{1,0:T(8,128)(4,1)S(1)}, pred[8,16]{1,0:T(8,128)(4,1)}, u32[]{:S(2)}) copy-start(pred[8,16]{1,0:T(8,128)(4,1)} %fusion.27) | copy-start | bytes 388
  197.1 46.6 %copy-start.3 = (f32[8,32]{1,0:T(8,128)S(1)}, f32[8,32]{1,0:T(8,128)}, u32[]{:S(2)}) copy-start(f32[8,32]{1,0:T(8,128)} %reshape.216) | copy-start | bytes 3076
  197.1 46.8 %copy-start.7 = (f32[8,32]{1,0:T(8,128)S(1)}, f32[8,32]{1,0:T(8,128)}, u32[]{:S(2)}) copy-start(f32[8,32]{1,0:T(8,128)} %reshape.217) | copy-start | bytes 3076
  197.1 46.9 %copy-start.5 = (pred[8,256]{1,0:T(8,128)(4,1)S(1)}, pred[8,256]{1,0:T(8,128)(4,1)}, u32[]{:S(2)}) copy-start(pred[8,256]{1,0:T(8,128)(4,1)} %copy-done.4) | copy-start | bytes 6148
  214.4 31.8 %all-to-all-start = ((bf16[16,2,16,128]{3,2,1,0:T(8,128)(2,1)}), bf16[16,2,16,128]{3,2,1,0:T(8,128)(2,1)S(1)}, u32[]{:S(2)}, u32[]{:S(2)}) async-start(bf16[16,2,16,128]{3,2,1,0:T(8,128)(2,1)} %bitcast.79), calls=%async_computation | async-start | bytes 262144 | tf_op jit(solution)/shard_map/all_to_all | solution.py:327

commit v2 on v0

--- a/solution.py
+++ b/solution.py
@@ -28,10 +28,14 @@
     key_width = kv_width // 2
     group_size = QH // KVH
     score_scale = 1.0 / math.sqrt(HD)
+    copies = lax.axis_size("replica")
+    part = kv_weight.shape[0] // copies
+    share = lax.dynamic_slice_in_dim(kv_weight, lax.axis_index("replica") * part, part, 0)
     normed = normalize_rows(prompt_states).astype(jnp.bfloat16)
+    normed = normed.reshape(-1, peer_count, copies, part).transpose(0, 2, 1, 3).reshape(normed.shape)
     new_kv = jnp.dot(
         normed,
-        lax.all_gather(kv_weight, "section", axis=0, tiled=True),
+        lax.all_gather(share, ("replica", "section"), axis=0, tiled=True),
         preferred_element_type=jnp.float32,
     ).astype(jnp.bfloat16)
     image_kv = new_kv.reshape(image_count, IMG_TOK, kv_width)

time: 226 us -> 215 us (0.951)
  waiting for transfers between devices: 150 us -> 109 us
  local copies, waits for them, and re-layouts: 17.9 us -> 41.6 us
  other arithmetic: 8.63 us -> 16.7 us
    all_gather x1, waiting for transfers between devices: 114 us -> 75.3 us  [per_device(): lax.all_gather(share, ('replica', 'section'), axis=0, tiled=True)]
    unnamed x13 -> x18, local copies, waits for them, and re-layouts: 11.7 us -> 26.5 us
    convert_element_type x0 -> x1, other arithmetic: none -> 8.29 us  [per_device(): normed = normalize_rows(prompt_states).astype(jnp.bfloat16)]
    transpose x0 -> x1, local copies, waits for them, and re-layouts: none -> 7.48 us  [per_device(): normed.reshape(-1, peer_count, copies, part).transpose(0, 2, 1, 3)]
  transfers between devices with their start and end apart: 3 -> 3, of which waited for: 2 -> 2; matrix products, arithmetic and copies ran while one was open for 17% -> 32% of each run, Pallas kernels for 0% -> 0%
where the time goes in v2:
time: 215 us; the launch traced here: 214 us
  waiting for transfers between devices  109 us (51%)
  local copies, waits for them, and re-layouts  41.6 us (19%)
  matrix products  21.2 us (10%)
  other arithmetic  16.7 us (8%)
  between operations  13.5 us (6%)
  starting transfers between devices  12.2 us (6%)
    all_gather x1, waiting for transfers between devices, per_device(): lax.all_gather(share, ('replica', 'section'), axis=0, tiled=True)  75.3 us
    all_to_all x1, waiting for transfers between devices, per_device(): lax.all_to_all(kv_slots.reshape(peer_count, IMG_TOK, kv_width), 'section'...  33.5 us
    unnamed x18, local copies, waits for them, and re-layouts  26.5 us
    dot_general x1, matrix products, per_device(): jnp.dot(normed, lax.all_gather(share, ('replica', 'section'), axis=0, til...  14.9 us
    convert_element_type x1, other arithmetic, per_device(): normed = normalize_rows(prompt_states).astype(jnp.bfloat16)  8.29 us
    transpose x1, local copies, waits for them, and re-layouts, per_device(): normed.reshape(-1, peer_count, copies, part).transpose(0, 2, 1, 3)  7.48 us
    all_to_all x1, starting transfers between devices, per_device(): lax.all_to_all(row_slots.reshape(peer_count, 1), 'section', split_axis=0,...  6.55 us
    all_to_all x1, starting transfers between devices, per_device(): lax.all_to_all(kv_slots.reshape(peer_count, IMG_TOK, kv_width), 'section'...  5.69 us
  transfers between devices with their start and end apart: 3, of which 2 were waited for; matrix products, arithmetic and copies ran while one was open for 32% of the time, Pallas kernels for 0%

profile of v2, /device:TPU:13, one launch (start us, length us, event | category | flops | bytes accessed | tf_op | source)
XLA Modules:
  0.0 214.2 jit_solution(18030569765483432063)
XLA Ops:
  6.5 0.0 copy-start
  6.5 0.0 all-gather.2.cloned.1.call-start
  6.5 1.2 copy-done
  7.8 0.8 constant_dynamic-slice_fusion
  8.6 0.0 all-gather.2.cloned.1.call-update
  8.6 0.7 fusion.23
  9.4 0.8 select_reduce_fusion
  10.1 0.7 copy.97
  10.8 6.6 %all-to-all-start = ((s32[16,1,1]{2,1,0:T(1,128)}), s32[16,1,1]{2,1,0:T(1,128)S(1)}, u32[]{:S(2)}, u32[]{:S(2)}) async-start(s32[16,1,1]{2,1,0:T(1,128)} %copy.97), calls=%async_computation | async-start | bytes 16384 | tf_op jit(solution)/shard_map/all_to_all | solution.py:71
  17.4 11.9 %copy.98 = bf16[512,8192]{0,1:T(8,128)(2,1)} copy(bf16[512,8192]{1,0:T(8,128)(2,1)} %param.7) | data formatting | bytes 16777216 | tf_op args[0]
  29.3 5.2 %fusion = f32[512]{0:T(512)S(1)} fusion(bf16[512,8192]{0,1:T(8,128)(2,1)} %copy.98), kind=kLoop, calls=%fused_computation.3 | loop fusion | flops 12582400 | bytes 8390656 | tf_op jit(solution)/shard_map/reduce_sum | solution.py:19
  34.5 8.3 %fusion.1 = bf16[512,8192]{0,1:T(8,128)(2,1)} fusion(bf16[512,8192]{0,1:T(8,128)(2,1)} %copy.98, f32[512]{0:T(512)S(1)} %add_rsqrt_fusion), kind=kLoop, calls=%fused_computation.4 | loop fusion | flops 12582912 | bytes 16779264 | tf_op jit(solution)/shard_map/convert_element_type | solution.py:34
  42.8 7.5 %copy.99 = bf16[512,2,16,256]{0,3,2,1:T(8,128)(2,1)} copy(bf16[512,2,16,256]{0,3,1,2:T(8,128)(2,1)} %bitcast.56) | data formatting | bytes 16777216 | tf_op jit(solution)/shard_map/transpose | solution.py:35
  50.3 75.3 %all-gather.2.cloned.1.call-done = bf16[8192,1024]{1,0:T(8,128)(2,1)} async-done(((bf16[256,1024]{1,0:T(8,128)(2,1)}), bf16[8192,1024]{1,0:T(8,128)(2,1)}) %all-gather.2.cloned.1.call-update) | async-done | bytes 16777232 | tf_op jit(solution)/shard_map/all_gather | solution.py:38
  125.6 14.9 %convolution_convert_fusion.1 = bf16[512,1024]{1,0:T(8,128)(2,1)S(1)} fusion(bf16[512,8192]{0,1:T(8,128)(2,1)} %bitcast.57, bf16[8192,1024]{1,0:T(8,128)(2,1)} %all-gather.2.cloned.1.call-done), kind=kOutput, calls=%fused_computation.8 | convolution fusion | flops 8590458880 | bytes 26214400 | tf_op jit(solution)/shard_map/dot_general | solution.py:36
  140.5 0.0 copy-start.5
  140.5 0.5 reshape_reshape.3
  141.0 0.2 copy-done.5
  141.1 0.8 convolution_convert_fusion
  142.0 2.4 %copy.121 = bf16[2,8,64,1024]{3,2,1,0:T(8,128)(2,1)} copy(bf16[2,8,64,1024]{3,1,2,0:T(8,128)(2,1)S(1)} %bitcast.60) | data formatting | bytes 4194304
  144.4 0.0 all-to-all-done
  144.4 5.7 %all-to-all-start.1 = ((bf16[16,64,1024]{2,1,0:T(8,128)(2,1)}), bf16[16,64,1024]{2,1,0:T(8,128)(2,1)}, u32[]{:S(2)}, u32[]{:S(2)}) async-start(bf16[16,64,1024]{2,1,0:T(8,128)(2,1)} %bitcast.20), calls=%async_computation.1 | async-start | bytes 4194304 | tf_op jit(solution)/shard_map/all_to_all | solution.py:64
  150.1 4.6 %fusion.26 = (bf16[8,256,512]{2,1,0:T(8,128)(2,1)}, bf16[8,256,512]{2,1,0:T(8,128)(2,1)}) fusion(bf16[8,256,1024]{2,1,0:T(8,128)(2,1)} %param.12), kind=kLoop, calls=%fused_computation.46 | loop fusion | bytes 8388608 | tf_op jit(solution)/shard_map/slice | solution.py:43
  154.7 2.8 %copy.119 = bf16[8,256,512]{1,2,0:T(8,128)(2,1)S(1)} copy(bf16[8,256,512]{2,1,0:T(8,128)(2,1)} %get-tuple-element.6) | data formatting | bytes 4194304
  157.5 0.0 copy-start.4
  157.5 0.0 copy-start.3
  157.5 4.0 %copy.118 = bf16[8,256,512]{1,2,0:T(8,128)(2,1)} copy(bf16[8,256,512]{2,1,0:T(8,128)(2,1)} %get-tuple-element.5) | data formatting | bytes 4194304
  161.5 0.0 copy-done.4
  161.5 0.1 iota_compare_fusion.1
  161.6 0.0 copy-done.3
  161.6 2.1 fusion.27
  163.6 0.4 reduce
  164.0 0.1 iota_compare_fusion
  164.1 33.5 %all-to-all-done.1 = bf16[16,64,1024]{2,1,0:T(8,128)(2,1)} async-done(((bf16[16,64,1024]{2,1,0:T(8,128)(2,1)}), bf16[16,64,1024]{2,1,0:T(8,128)(2,1)}, u32[]{:S(2)}, u32[]{:S(2)}) %all-to-all-start.1) | async-done | bytes 2097184 | tf_op jit(solution)/shard_map/all_to_all | solution.py:64
  197.6 2.9 %slice_bitcast_fusion = (bf16[16,8,4,8,128]{4,3,2,1,0:T(8,128)(2,1)}, bf16[16,64,512]{2,1,0:T(8,128)(2,1)S(1)}) fusion(bf16[16,64,1024]{2,1,0:T(8,128)(2,1)} %all-to-all-done.1), kind=kLoop, calls=%fused_computation.20 | loop fusion | bytes 4194304
  200.5 1.1 reshape.113
  201.6 2.4 %fusion.2 = (f32[8,4,8]{2,0,1:T(8,128)S(1)}, f32[4,16,64,8,8]{2,4,3,1,0:T(8,128)S(1)}) fusion(pred[8,16]{0,1:T(8,128)(4,1)S(1)} %iota_compare_fusion, bf16[8,4,8,128,1]{3,0,2,1,4:T(8,128)(2,1)S(1)} %bitcast.63, bf16[16,64,4,128,1]{3,2,1,0,4:T(4,128)(2,1)} %bitcast.61), kind=kOutput, calls=%fused_computation.7 | convolution fusion | flops 67895040 | bytes 2163840 | tf_op jit(solution)/shard_map/rkgd,smkd->rkgsm/dot_general | solution.py:78
  204.1 0.2 fusion.14
  204.3 0.7 fusion.16
  205.0 0.0 copy-start.2
  205.0 0.0 copy-start.1
  205.0 0.9 fusion.3
  205.9 0.3 copy-done.2
  206.3 0.4 fusion.9
  206.6 0.7 copy.144
  207.3 0.0 copy-done.1
  (5 shorter events, 0.0 us)
Async XLA Ops:
  6.5 1.2 copy-start
  6.5 119.1 %all-gather.2.cloned.1.call-start = ((), (), s32[]{:S(2)}) async-start(), calls=%async_computation.2 | async-start | bytes 17301504 | tf_op jit(solution)/shard_map/all_gather | solution.py:38
  10.8 133.6 %all-to-all-start = ((s32[16,1,1]{2,1,0:T(1,128)}), s32[16,1,1]{2,1,0:T(1,128)S(1)}, u32[]{:S(2)}, u32[]{:S(2)}) async-start(s32[16,1,1]{2,1,0:T(1,128)} %copy.97), calls=%async_computation | async-start | bytes 16384 | tf_op jit(solution)/shard_map/all_to_all | solution.py:71
  140.5 0.7 copy-start.5
  144.4 53.2 %all-to-all-start.1 = ((bf16[16,64,1024]{2,1,0:T(8,128)(2,1)}), bf16[16,64,1024]{2,1,0:T(8,128)(2,1)}, u32[]{:S(2)}, u32[]{:S(2)}) async-start(bf16[16,64,1024]{2,1,0:T(8,128)(2,1)} %bitcast.20), calls=%async_computation.1 | async-start | bytes 4194304 | tf_op jit(solution)/shard_map/all_to_all | solution.py:64
  157.5 4.0 %copy-start.4 = (s32[8]{0:T(128)S(1)}, s32[8]{0:T(128)}, u32[]{:S(2)}) copy-start(s32[8]{0:T(128)} %param.13) | copy-start | bytes 100
  157.5 4.1 %copy-start.3 = (bf16[8,4096]{1,0:T(8,128)(2,1)S(1)}, bf16[8,4096]{1,0:T(8,128)(2,1)}, u32[]{:S(2)}) copy-start(bf16[8,4096]{1,0:T(8,128)(2,1)} %param.11) | copy-start | bytes 196612
  205.0 1.2 copy-start.2
  205.0 2.3 %copy-start.1 = (bf16[512,1024]{1,0:T(8,128)(2,1)S(1)}, bf16[512,1024]{1,0:T(8,128)(2,1)}, u32[]{:S(2)}) copy-start(bf16[512,1024]{1,0:T(8,128)(2,1)} %param.8) | copy-start | bytes 3145732
Sparse Core Ops, SparseCore 0:
  10.2 115.3 all-gather.1

commit v3 on v0

v3 whole, which is shorter than its diff:
```python
import functools
import math

import jax
import jax.numpy as jnp
from jax import lax
from jax.experimental import pallas as pl
from jax.experimental.pallas import tpu as pltpu
from jax.sharding import PartitionSpec as P

HD = 128
KVH = 4
QH = 32
IMG_TOK = 64
GROUP = QH // KVH
HALF_KVH = KVH // 2
HALF_QH = QH // 2
SCALE = 1.0 / math.sqrt(HD)
EPS = 1e-05

LANES = 64
N_KINDS = 7

masked_score = -1e30


def swap_core(x):
    n = lax.axis_size("section")
    return lax.ppermute(x, "section", [(i, i ^ 1) for i in range(n)])


def gather_plain(chunk):
    n = lax.axis_size("section")
    rows = chunk.shape[0]
    groups = [list(range(core, n, 2)) for core in range(2)]
    whole = lax.all_gather(chunk, "section", axis=0, tiled=True, axis_index_groups=groups)
    return [(chip, [(whole, chip * rows, rows, 0)]) for chip in range(n // 2)]


def gather_grid(chunk, span):
    section = lax.axis_index("section")
    rep = lax.axis_index("replica")
    z, y = section // 4, section // 2 % 2
    rows = chunk.shape[0]
    rest = rows - span
    order = [0, 1, 3, 2]
    ring = [(order[p] * 4 + low, order[(p + 1) % 4] * 4 + low) for p in range(4) for low in range(4)]
    swap_y = [(i, i ^ 2) for i in range(16)]
    places = jnp.array([0, 1, 3, 2], jnp.int32)
    place = places[z]
    along_z = [lax.dynamic_slice_in_dim(chunk, rep * rest, span, 0)]
    along_y = []
    for step in range(4):
        if step < 3:
            along_z.append(lax.ppermute(along_z[-1], "section", ring))
        along_y.append(lax.ppermute(along_z[step], "section", swap_y))
    groups = [(z * 2 + y, [(chunk, 0, rows, 0)])]
    for step in range(4):
        from_z = places[(place - step) % 4]
        for piece, chip in ((along_z[step], from_z * 2 + y), (along_y[step], from_z * 2 + 1 - y)):
            if piece is along_z[0]:
                continue
            part = piece if rest == span else lax.dynamic_slice_in_dim(piece, rep * (span - rest), rest, 0)
            extra = lax.ppermute(part, "replica", [(0, 1), (1, 0)])
            groups.append((chip, [(piece, 0, span, rep * rest), (extra, 0, rest, (1 - rep) * span)]))
    return groups


def flatten(groups):
    arrays, layout, numbers = [], [], []
    for index, (chip, parts) in enumerate(groups):
        for array, start, rows, place in parts:
            at = [i for i, known in enumerate(arrays) if known is array]
            if not at:
                arrays.append(array)
                at = [len(arrays) - 1]
            layout.append((at[0], start, rows, index))
            numbers.append(jnp.asarray(place, jnp.int32))
    chips = [jnp.asarray(chip, jnp.int32) for chip, _ in groups]
    return arrays, layout, jnp.stack(chips), jnp.stack(numbers)


def split_kernel(core_ref, keep_in, give_in, keep_ref, give_ref):
    keep_ref[...] = keep_in[...]
    give_ref[...] = give_in[...]


def accumulate(layout, place_ref, own_ref, other_ref, piece_refs, weight, total, squares, sems):
    step = pl.program_id(0)
    tokens, depth = own_ref.shape
    copies = [
        pltpu.make_async_copy(
            piece_refs[which].at[pl.ds(start, rows)],
            weight.at[group, pl.ds(pl.multiple_of(place_ref[i], 32), rows)],
            sems.at[i],
        )
        for i, (which, start, rows, group) in enumerate(layout)
    ]

    @pl.when(step == 0)
    def _():
        for copy in copies:
            copy.start()

    for group in range(weight.shape[0]):

        @pl.when(step == group)
        def _():
            for copy, (_, _, _, owner) in zip(copies, layout):
                if owner == group:
                    copy.wait()

    states = jnp.concatenate([own_ref[...], other_ref[...]], axis=0)
    total[...] += jnp.dot(states, weight[step], preferred_element_type=jnp.float32)
    values = states.astype(jnp.float32)
    values = values * values
    squares[...] += sum(values[:, i : i + HD] for i in range(0, depth, HD))


def first_kernel(layout, n_pieces, block_ref, place_ref, own_ref, other_ref, *refs):
    piece_refs = refs[:n_pieces]
    total, squares, weight, sems = refs[n_pieces:]

    @pl.when(pl.program_id(0) == 0)
    def _():
        total[...] = jnp.zeros_like(total)
        squares[...] = jnp.zeros_like(squares)

    accumulate(layout, place_ref, own_ref, other_ref, piece_refs, weight, total, squares, sems)


def parts_of(values, count):
    out = []
    for _ in range(count):
        part = values.astype(jnp.bfloat16).astype(jnp.float32)
        out.append(part)
        values = values - part
    return out


def last_kernel(
    layout, n_pieces, width, block_ref, place_ref, slot_ref, own_ref, other_ref, query_ref, row_lane_ref, in_total, in_squares, *refs
):
    piece_refs = refs[:n_pieces]
    slots_ref, weight, total, squares, summed, stats, sems = refs[n_pieces:]
    images = query_ref.shape[1] // GROUP

    @pl.when(pl.program_id(0) == 0)
    def _():
        total[...] = in_total[...]
        squares[...] = in_squares[...]
        slots_ref[...] = jnp.zeros_like(slots_ref)

    accumulate(layout, place_ref, own_ref, other_ref, piece_refs, weight, total, squares, sems)

    @pl.when(pl.program_id(0) == pl.num_programs(0) - 1)
    def _():
        tokens = total.shape[0]
        queries = query_ref.shape[1]
        factor = lax.rsqrt(jnp.sum(squares[...], axis=1, keepdims=True) / width + EPS)
        image_of_query = lax.broadcasted_iota(jnp.int32, (queries, tokens), 0) // GROUP
        image_of_token = lax.broadcasted_iota(jnp.int32, (queries, tokens), 1) // IMG_TOK
        live = image_of_query == image_of_token
        lane = lax.broadcasted_iota(jnp.int32, (queries, HD), 1)
        first_lane = row_lane_ref[:, :1]
        for head in range(HALF_KVH):
            part = slice(head * GROUP, (head + 1) * GROUP)
            keys = (total[:, head * HD : (head + 1) * HD] * factor).astype(jnp.bfloat16)
            at = (HALF_KVH + head) * HD
            values = (total[:, at : at + HD] * factor).astype(jnp.bfloat16)
            scores = (
                lax.dot_general(
                    query_ref[head], keys, (((1,), (1,)), ((), ())), preferred_element_type=jnp.float32
                )
                * SCALE
            )
            scores = jnp.where(live, scores, masked_score)
            top = jnp.max(scores, axis=1, keepdims=True)
            weights = jnp.where(live, jnp.exp(scores - top), 0.0)
            total_weight = jnp.sum(weights, axis=1, keepdims=True)
            out = jnp.dot(weights.astype(jnp.bfloat16), values, preferred_element_type=jnp.float32)
            summed[:, part, :] = out.reshape(images, GROUP, HD)
            kinds = parts_of(top, 3) + parts_of(total_weight, 3) + [jnp.ones_like(top)]
            tile = jnp.zeros((queries, HD), jnp.float32)
            for kind, column in enumerate(kinds):
                tile = jnp.where(lane == first_lane + kind * 8, column, tile)
            stats[:, part, :] = tile.reshape(images, GROUP, HD)
        for image in range(images):
            owner, which = slot_ref[0, image], slot_ref[1, image]
            slots_ref[owner, which] = summed[image].astype(jnp.bfloat16)
            slots_ref[owner, 2] = slots_ref[owner, 2] + stats[image].astype(jnp.bfloat16)


def resident_kernel(length_ref, query_ref, cache_ref, out_ref, top_ref, sum_ref):
    row = pl.program_id(0)
    context = cache_ref.shape[1]
    live = lax.broadcasted_iota(jnp.int32, (GROUP, context), 1) < length_ref[row]
    lane = lax.broadcasted_iota(jnp.int32, (GROUP, HD), 1)

    @pl.when(row == 0)
    def _():
        top_ref[...] = jnp.zeros_like(top_ref)
        sum_ref[...] = jnp.zeros_like(sum_ref)

    for head in range(KVH):
        part = slice(head * GROUP, (head + 1) * GROUP)
        keys = cache_ref[0, :, head * HD : (head + 1) * HD]
        values = cache_ref[0, :, (KVH + head) * HD : (KVH + head + 1) * HD]
        scores = (
            lax.dot_general(
                query_ref[0, part, :], keys, (((1,), (1,)), ((), ())), preferred_element_type=jnp.float32
            )
            * SCALE
        )
        scores = jnp.where(live, scores, masked_score)
        top = jnp.max(scores, axis=1, keepdims=True)
        weights = jnp.where(live, jnp.exp(scores - top), 0.0)
        out_ref[0, part, :] = jnp.dot(weights.astype(jnp.bfloat16), values, preferred_element_type=jnp.float32)
        top_ref[part, :] = jnp.where(lane == row, top, top_ref[part, :])
        sum_ref[part, :] = jnp.where(lane == row, jnp.sum(weights, axis=1, keepdims=True), sum_ref[part, :])


def combine_kernel(got_ref, res_out_ref, res_top_ref, res_sum_ref, out_ref, acc, shares):
    chips = got_ref.shape[0] // 2
    rows = res_out_ref.shape[0]
    lane = lax.broadcasted_iota(jnp.int32, (HALF_QH, HD), 1)
    head_lane = (lane % LANES) < 8

    def moved(tile, by):
        return pltpu.roll(tile, HD - by, 1)

    for core in range(2):
        part = slice(core * HALF_QH, (core + 1) * HALF_QH)
        tops, sums, here = [], [], []
        for chip in range(chips):
            tile = got_ref[chip * 2 + core, 2].astype(jnp.float32)
            present = (moved(tile, 48) > 0.5) & head_lane
            tops.append(jnp.where(present, tile + moved(tile, 8) + moved(tile, 16), masked_score))
            sums.append(moved(tile, 24) + moved(tile, 32) + moved(tile, 40))
            here.append(present)
        row_top = functools.reduce(jnp.maximum, tops)
        row_top = jnp.maximum(row_top, pltpu.roll(row_top, LANES, 1))
        res_top = jnp.where(lane < 8, res_top_ref[part, :], masked_score)
        res_top = jnp.maximum(res_top, pltpu.roll(res_top, LANES, 1))
        row_top = jnp.maximum(row_top, res_top)
        weights = [jnp.where(a, jnp.exp(t - row_top), 0.0) for a, t in zip(here, tops)]
        joined = sum(w * s for w, s in zip(weights, sums))
        res_weight = jnp.exp(res_top - row_top)
        denominator = joined + pltpu.roll(joined, LANES, 1) + res_weight * res_sum_ref[part, :]
        scale = jnp.where(lane < 8, 1.0 / denominator, 0.0)
        scale = scale + pltpu.roll(scale, LANES, 1)
        res_share = res_weight * scale
        weights = [w * scale for w in weights]
        for row in range(rows):
            value = res_out_ref[row, part, :] * res_share[:, row : row + 1]
            for chip in range(chips):
                for which in range(2):
                    at = which * LANES + row
                    value += weights[chip][:, at : at + 1] * got_ref[chip * 2 + core, which].astype(jnp.float32)
            acc[row, part, :] = value
    for head in range(QH):
        out_ref[:, head * HD : (head + 1) * HD] = acc[:, head, :].astype(jnp.bfloat16)


def whole(shape):
    return pl.BlockSpec(shape, lambda i, *_: (0,) * len(shape))


def per_device(prompt_states, kv_weight, image_owner, image_row, queries, cache, context_length):
    n = lax.axis_size("section")
    section = lax.axis_index("section")
    core = section % 2
    tokens, width = prompt_states.shape
    rows_dev, kv_width = kv_weight.shape
    columns_dev = kv_width // 2
    images = image_owner.shape[0]
    decode_rows = queries.shape[0]
    context = cache.shape[1]
    grid_form = n == 16 and lax.axis_size("replica") == 2

    cut = columns_dev // 2
    keep, give = pl.pallas_call(
        split_kernel,
        grid_spec=pltpu.PrefetchScalarGridSpec(
            num_scalar_prefetch=1,
            grid=(2,),
            in_specs=[
                pl.BlockSpec((rows_dev, cut), lambda i, core_ref: (0, 2 * i + core_ref[0])),
                pl.BlockSpec((rows_dev, cut), lambda i, core_ref: (0, 2 * i + 1 - core_ref[0])),
            ],
            out_specs=[pl.BlockSpec((rows_dev, cut), lambda i, core_ref: (0, i))] * 2,
        ),
        out_shape=[jax.ShapeDtypeStruct((rows_dev, columns_dev), jnp.bfloat16)] * 2,
        cost_estimate=pl.CostEstimate(flops=0, bytes_accessed=2 * 2**20, transcendentals=0),
        name="split",
    )(core.reshape(1), kv_weight, kv_weight)
    taken = swap_core(give)
    if grid_form:
        phases = [gather_grid(keep, rows_dev // 2), gather_grid(taken, rows_dev * 13 // 16)]
    else:
        phases = [gather_plain(keep), gather_plain(taken)]

    states, taken = lax.optimization_barrier((prompt_states, taken))
    other = swap_core(states)

    owner_and_row = jnp.stack([image_owner, image_row])
    chip_images = jnp.concatenate([owner_and_row, swap_core(owner_and_row)], axis=1)
    send_q = queries.reshape(decode_rows, 2, HALF_QH * HD).transpose(1, 0, 2)
    send_q = jnp.broadcast_to(send_q[None], (n // 2, 2, decode_rows, HALF_QH * HD)).reshape(
        n, decode_rows, HALF_QH * HD
    )
    all_q = lax.all_to_all(send_q, "section", split_axis=0, concat_axis=0, tiled=True)
    all_q = all_q.reshape(n * decode_rows, HALF_QH * HD)
    target = chip_images[0] * decode_rows + chip_images[1]
    pick = (target[:, None] == jnp.arange(n * decode_rows)[None, :]).astype(jnp.bfloat16)
    image_q = jnp.dot(pick, all_q, preferred_element_type=jnp.float32).astype(jnp.bfloat16)
    image_q = image_q.reshape(2 * images, HALF_KVH, GROUP, HD).transpose(1, 0, 2, 3)
    image_q = image_q.reshape(HALF_KVH, 2 * images * GROUP, HD)
    n_queries = 2 * images * GROUP

    which = jnp.concatenate([jnp.full((images,), core), jnp.full((images,), 1 - core)]).astype(jnp.int32)
    slot = jnp.stack([chip_images[0], which])
    row_lane = jnp.broadcast_to(jnp.repeat(which * LANES + chip_images[1], GROUP)[:, None], (n_queries, HD))

    res_out, res_top, res_sum = pl.pallas_call(
        resident_kernel,
        grid_spec=pltpu.PrefetchScalarGridSpec(
            num_scalar_prefetch=1,
            grid=(decode_rows,),
            in_specs=[
                pl.BlockSpec((1, QH, HD), lambda i, *_: (i, 0, 0)),
                pl.BlockSpec((1, context, kv_width), lambda i, *_: (i, 0, 0)),
            ],
            out_specs=[pl.BlockSpec((1, QH, HD), lambda i, *_: (i, 0, 0)), whole((QH, HD)), whole((QH, HD))],
        ),
        out_shape=[
            jax.ShapeDtypeStruct((decode_rows, QH, HD), jnp.float32),
            jax.ShapeDtypeStruct((QH, HD), jnp.float32),
            jax.ShapeDtypeStruct((QH, HD), jnp.float32),
        ],
        compiler_params=pltpu.CompilerParams(vmem_limit_bytes=16 * 2**20),
        cost_estimate=pl.CostEstimate(flops=2**28, bytes_accessed=4 * 2**20, transcendentals=0),
        name="resident",
    )(context_length, queries.reshape(decode_rows, QH, HD), cache)

    flops = 2 * 2 * tokens * width // 2 * columns_dev
    cost = pl.CostEstimate(flops=flops, bytes_accessed=16 * 2**20, transcendentals=0)
    params = pltpu.CompilerParams(vmem_limit_bytes=56 * 2**20)
    token_spec = pl.BlockSpec((tokens, rows_dev), lambda i, block_ref, *_: (0, block_ref[i]))
    anywhere = pl.BlockSpec(memory_space=pl.ANY)

    arrays, layout, chips, places = flatten(phases[0])
    total, squares = pl.pallas_call(
        functools.partial(first_kernel, layout, len(arrays)),
        grid_spec=pltpu.PrefetchScalarGridSpec(
            num_scalar_prefetch=2,
            grid=(n // 2,),
            in_specs=[token_spec, token_spec] + [anywhere] * len(arrays),
            out_specs=[whole((2 * tokens, columns_dev)), whole((2 * tokens, HD))],
            scratch_shapes=[
                pltpu.VMEM((n // 2, rows_dev, columns_dev), jnp.bfloat16),
                pltpu.SemaphoreType.DMA((len(layout),)),
            ],
        ),
        out_shape=[
            jax.ShapeDtypeStruct((2 * tokens, columns_dev), jnp.float32),
            jax.ShapeDtypeStruct((2 * tokens, HD), jnp.float32),
        ],
        compiler_params=params,
        cost_estimate=cost,
        name="first_rows",
    )(chips * 2 + core, places, prompt_states, other, *arrays)

    arrays, layout, chips, places = flatten(phases[1])
    slots = pl.pallas_call(
        functools.partial(last_kernel, layout, len(arrays), width),
        grid_spec=pltpu.PrefetchScalarGridSpec(
            num_scalar_prefetch=3,
            grid=(n // 2,),
            in_specs=[
                token_spec,
                token_spec,
                whole((HALF_KVH, n_queries, HD)),
                whole((n_queries, HD)),
                whole((2 * tokens, columns_dev)),
                whole((2 * tokens, HD)),
            ]
            + [anywhere] * len(arrays),
            out_specs=whole((n, 3, HALF_QH, HD)),
            scratch_shapes=[
                pltpu.VMEM((n // 2, rows_dev, columns_dev), jnp.bfloat16),
                pltpu.VMEM((2 * tokens, columns_dev), jnp.float32),
                pltpu.VMEM((2 * tokens, HD), jnp.float32),
                pltpu.VMEM((2 * images, HALF_QH, HD), jnp.float32),
                pltpu.VMEM((2 * images, HALF_QH, HD), jnp.float32),
                pltpu.SemaphoreType.DMA((len(layout),)),
            ],
        ),
        out_shape=jax.ShapeDtypeStruct((n, 3, HALF_QH, HD), jnp.bfloat16),
        compiler_params=params,
        cost_estimate=cost,
        name="last_rows",
    )(chips * 2 + 1 - core, places, slot, prompt_states, other, image_q, row_lane, total, squares, *arrays)
    got = lax.all_to_all(slots, "section", split_axis=0, concat_axis=0, tiled=True)

    return pl.pallas_call(
        combine_kernel,
        grid=(1,),
        in_specs=[
            whole((n, 3, HALF_QH, HD)),
            whole((decode_rows, QH, HD)),
            whole((QH, HD)),
            whole((QH, HD)),
        ],
        out_specs=whole((decode_rows, QH * HD)),
        scratch_shapes=[
            pltpu.VMEM((decode_rows, QH, HD), jnp.float32),
            pltpu.VMEM((HALF_QH, HD), jnp.float32),
        ],
        out_shape=jax.ShapeDtypeStruct((decode_rows, QH * HD), jnp.bfloat16),
        compiler_params=pltpu.CompilerParams(vmem_limit_bytes=32 * 2**20),
        name="combine",
    )(got, res_out, res_top, res_sum)


def solution(mesh):
    placed = (
        P(("replica", "section"), None),
        P("section", None),
        P(("replica", "section")),
        P(("replica", "section")),
        P(("replica", "section"), None),
        P(("replica", "section"), None, None),
        P(("replica", "section")),
    )
    return jax.shard_map(
        per_device,
        mesh=mesh,
        in_specs=placed,
        out_specs=P(("replica", "section"), None),
        check_vma=False,
    )
```

time: 226 us -> 156 us (0.69)
  the two profiles are of different devices: /device:TPU:13 before, /device:TPU:0 now
where the time goes in v3:
time: 156 us; the launch traced here: 155 us
  starting transfers between devices  52.2 us (33%)
  waiting for transfers between devices  40.4 us (26%)
  Pallas kernels  39.7 us (25%)
  local copies, waits for them, and re-layouts  12.9 us (8%)
  between operations  6.9 us (4%)
  other arithmetic  2.61 us (2%)
    ppermute x8, waiting for transfers between devices, gather_grid(): along_y.append(lax.ppermute(along_z[step], 'section', swap_y))  23 us
    ppermute x14, starting transfers between devices, gather_grid(): extra = lax.ppermute(part, 'replica', [(0, 1), (1, 0)])  18.3 us
    pallas_call x1, Pallas kernels, per_device(): pl.pallas_call(functools.partial(last_kernel, layout, len(arrays), width)...  13.8 us
    pallas_call x1, Pallas kernels, per_device(): pl.pallas_call(functools.partial(first_kernel, layout, len(arrays)), grid...  12.5 us
    ppermute x6, starting transfers between devices, gather_grid(): along_z.append(lax.ppermute(along_z[-1], 'section', ring))  11.7 us
    ppermute x8, starting transfers between devices, gather_grid(): along_y.append(lax.ppermute(along_z[step], 'section', swap_y))  11.5 us
    pallas_call x1, Pallas kernels, per_device(): pl.pallas_call(resident_kernel, grid_spec=pltpu.PrefetchScalarGridSpec(nu...  9.01 us
    ppermute x6, waiting for transfers between devices, gather_grid(): along_z.append(lax.ppermute(along_z[-1], 'section', ring))  8.56 us
  transfers between devices with their start and end apart: 33, of which 13 were waited for; matrix products, arithmetic and copies ran while one was open for 8% of the time, Pallas kernels for 14%

profile of v3, /device:TPU:0, one launch (start us, length us, event | category | flops | bytes accessed | tf_op | source)
XLA Modules:
  0.0 155.0 jit_solution(7129103952385879554)
XLA Ops:
  0.0 2.1 %split.1 = (bf16[512,512]{1,0:T(8,128)(2,1)}, bf16[512,512]{1,0:T(8,128)(2,1)}) custom-call(s32[1]{0:T(128)} %bitcast.18.core_ref, bf16[512,1024]{1,0:T(8,128)(2,1)} %give_in.1, bf16[512,1024]{1,0:T(8,128)(2,1)} %give_in.1), custom_call_target="tpu_custom_call" | custom-call | bytes 2097152 | tf_op jit(solution)/shard_map/split/pallas_call | solution.py:282
  2.1 0.5 collective-permute-start.1
  2.6 1.7 %collective-permute-done.1.refs_0_ = bf16[512,512]{1,0:T(8,128)(2,1)S(1)} collective-permute-done((bf16[512,512]{1,0:T(8,128)(2,1)}, bf16[512,512]{1,0:T(8,128)(2,1)S(1)}, u32[]{:S(2)}, u32[]{:S(2)}) %collective-permute-start.1) | collective-permute-done | bytes 524320 | tf_op jit(solution)/shard_map/ppermute | solution.py:29
  4.7 1.0 constant_dynamic-slice_fusion
  5.6 2.8 %collective-permute-start.5 = (bf16[256,512]{1,0:T(8,128)(2,1)S(1)}, bf16[256,512]{1,0:T(8,128)(2,1)S(1)}, u32[]{:S(2)}, u32[]{:S(2)}) collective-permute-start(bf16[256,512]{1,0:T(8,128)(2,1)S(1)} %constant_dynamic-slice_fusion), channel_id=1, source_target_pairs={{0,4},{1,5},{2,6},{3,7},{4,12},{5,13},{6,14},{7,15},{12,8},{13,9},... | collective-permute-start | bytes 786440 | tf_op jit(solution)/shard_map/ppermute | solution.py:55
  8.5 0.8 constant_dynamic-slice_fusion.1
  9.3 2.6 %collective-permute-start.19 = (bf16[416,512]{1,0:T(8,128)(2,1)}, bf16[416,512]{1,0:T(8,128)(2,1)S(1)}, u32[]{:S(2)}, u32[]{:S(2)}) collective-permute-start(bf16[416,512]{1,0:T(8,128)(2,1)} %constant_dynamic-slice_fusion.1), channel_id=1, source_target_pairs={{0,4},{1,5},{2,6},{3,7},{4,12},{5,13},{6,14},{7,15},{12,8},{13,9},... | collective-permute-start | bytes 1277960 | tf_op jit(solution)/shard_map/ppermute | solution.py:55
  11.9 1.5 collective-permute-start.3
  13.4 0.7 pad_add_fusion
  14.1 2.5 %collective-permute-done.5.refs_3_ = bf16[256,512]{1,0:T(8,128)(2,1)S(1)} collective-permute-done((bf16[256,512]{1,0:T(8,128)(2,1)S(1)}, bf16[256,512]{1,0:T(8,128)(2,1)S(1)}, u32[]{:S(2)}, u32[]{:S(2)}) %collective-permute-start.5) | collective-permute-done | bytes 262176 | tf_op jit(solution)/shard_map/ppermute | solution.py:55
  16.6 1.2 collective-permute-start.9
  17.7 2.6 %collective-permute-start.7 = (bf16[256,512]{1,0:T(8,128)(2,1)S(1)}, bf16[256,512]{1,0:T(8,128)(2,1)}, u32[]{:S(2)}, u32[]{:S(2)}) collective-permute-start(bf16[256,512]{1,0:T(8,128)(2,1)S(1)} %collective-permute-done.5.refs_3_), channel_id=1, source_target_pairs={{0,2},{1,3},{2,0},{3,1},{4,6},{5,7},{6,4},{7,5},{8,10},{9,11},{10,... | collective-permute-start | bytes 786440 | tf_op jit(solution)/shard_map/ppermute | solution.py:56
  20.3 1.7 %broadcast_in_dim.8 = bf16[8,2,8,2048]{3,2,1,0:T(8,128)(2,1)} broadcast(bf16[2,8,2048]{2,1,0:T(8,128)(2,1)} %bitcast.49), dimensions={1,2,3} | broadcast | bytes 589824 | tf_op jit(solution)/shard_map/broadcast_in_dim | solution.py:309
  22.0 5.0 %all-to-all-start = ((bf16[16,8,2048]{2,1,0:T(8,128)(2,1)}), bf16[16,8,2048]{2,1,0:T(8,128)(2,1)S(1)}, u32[]{:S(2)}, u32[]{:S(2)}) async-start(bf16[16,8,2048]{2,1,0:T(8,128)(2,1)} %bitcast.23), calls=%async_computation | async-start | bytes 1048576 | tf_op jit(solution)/shard_map/all_to_all | solution.py:312
  27.0 1.6 %collective-permute-start.6 = (bf16[256,512]{1,0:T(8,128)(2,1)S(1)}, bf16[256,512]{1,0:T(8,128)(2,1)S(1)}, u32[]{:S(2)}, u32[]{:S(2)}) collective-permute-start(bf16[256,512]{1,0:T(8,128)(2,1)S(1)} %collective-permute-done.5.refs_3_), channel_id=1, source_target_pairs={{0,16},{16,0},{1,17},{17,1},{2,18},{18,2},{3,19},{19,3},{4,20},{20... | collective-permute-start | bytes 786440 | tf_op jit(solution)/shard_map/ppermute | solution.py:64
  28.6 1.2 dynamic_slice.57
  33.8 1.5 fusion.3
  37.9 0.6 collective-permute-start.4
  38.5 1.9 %collective-permute-start.13 = (bf16[256,512]{1,0:T(8,128)(2,1)S(1)}, bf16[256,512]{1,0:T(8,128)(2,1)}, u32[]{:S(2)}, u32[]{:S(2)}) collective-permute-start(bf16[256,512]{1,0:T(8,128)(2,1)S(1)} %collective-permute-done.9.refs_7_), channel_id=1, source_target_pairs={{0,4},{1,5},{2,6},{3,7},{4,12},{5,13},{6,14},{7,15},{12,8},{13,9},... | collective-permute-start | bytes 786440 | tf_op jit(solution)/shard_map/ppermute | solution.py:55
  40.4 2.4 %collective-permute-start.23 = (bf16[416,512]{1,0:T(8,128)(2,1)S(1)}, bf16[416,512]{1,0:T(8,128)(2,1)S(1)}, u32[]{:S(2)}, u32[]{:S(2)}) collective-permute-start(bf16[416,512]{1,0:T(8,128)(2,1)S(1)} %collective-permute-done.19.refs_3_), channel_id=1, source_target_pairs={{0,4},{1,5},{2,6},{3,7},{4,12},{5,13},{6,14},{7,15},{12,8},{13,9},... | collective-permute-start | bytes 1277960 | tf_op jit(solution)/shard_map/ppermute | solution.py:55
  42.8 0.6 multiply_add_fusion
  43.4 0.6 stack.136.place_ref
  44.0 0.6 stack.120.place_ref
  44.6 1.5 collective-permute-start.11
  46.1 0.7 pad_add_fusion.1
  46.9 1.1 collective-permute-start.17
  48.0 0.7 collective-permute-done.13.refs_11_
  48.7 1.5 collective-permute-start.10
  50.3 3.7 %collective-permute-done.11.refs_9_ = bf16[256,512]{1,0:T(8,128)(2,1)} collective-permute-done((bf16[256,512]{1,0:T(8,128)(2,1)S(1)}, bf16[256,512]{1,0:T(8,128)(2,1)}, u32[]{:S(2)}, u32[]{:S(2)}) %collective-permute-start.11) | collective-permute-done | bytes 262176 | tf_op jit(solution)/shard_map/ppermute | solution.py:56
  54.0 1.5 collective-permute-start.8
  55.5 1.5 collective-permute-done.23.refs_7_
  57.0 0.8 collective-permute-start.27
  57.8 0.6 pad_add_fusion.2.slot_ref
  58.6 1.6 %collective-permute-start.21 = (bf16[416,512]{1,0:T(8,128)(2,1)S(1)}, bf16[416,512]{1,0:T(8,128)(2,1)S(1)}, u32[]{:S(2)}, u32[]{:S(2)}) collective-permute-start(bf16[416,512]{1,0:T(8,128)(2,1)S(1)} %collective-permute-done.19.refs_3_), channel_id=1, source_target_pairs={{0,2},{1,3},{2,0},{3,1},{4,6},{5,7},{6,4},{7,5},{8,10},{9,11},{10,... | collective-permute-start | bytes 1277960 | tf_op jit(solution)/shard_map/ppermute | solution.py:56
  60.2 1.5 collective-permute-done.17.refs_1_
  61.7 1.4 collective-permute-start.25
  63.1 0.6 constant_dynamic-slice_fusion.2
  63.7 0.6 collective-permute-start.15
  64.6 0.6 copy.17
  65.3 3.8 %collective-permute-done.27.refs_11_ = bf16[416,512]{1,0:T(8,128)(2,1)S(1)} collective-permute-done((bf16[416,512]{1,0:T(8,128)(2,1)S(1)}, bf16[416,512]{1,0:T(8,128)(2,1)S(1)}, u32[]{:S(2)}, u32[]{:S(2)}) %collective-permute-start.27) | collective-permute-done | bytes 426016 | tf_op jit(solution)/shard_map/ppermute | solution.py:55
  69.1 1.2 collective-permute-start.29
  70.3 1.2 collective-permute-done.21.refs_5_
  71.4 1.5 collective-permute-start.14
  72.9 13.3 %collective-permute-done.15.refs_13_ = bf16[256,512]{1,0:T(8,128)(2,1)} collective-permute-done((bf16[256,512]{1,0:T(8,128)(2,1)}, bf16[256,512]{1,0:T(8,128)(2,1)}, u32[]{:S(2)}, u32[]{:S(2)}) %collective-permute-start.15) | collective-permute-done | bytes 262176 | tf_op jit(solution)/shard_map/ppermute | solution.py:56
  86.3 1.5 collective-permute-start.12
  87.8 0.5 collective-permute-start.16
  88.3 0.9 constant_dynamic-slice_fusion.6
  89.2 1.6 %collective-permute-start.20 = (bf16[96,512]{1,0:T(8,128)(2,1)S(1)}, bf16[96,512]{1,0:T(8,128)(2,1)S(1)}, u32[]{:S(2)}, u32[]{:S(2)}) collective-permute-start(bf16[96,512]{1,0:T(8,128)(2,1)S(1)} %constant_dynamic-slice_fusion.3), channel_id=1, source_target_pairs={{0,16},{16,0},{1,17},{17,1},{2,18},{18,2},{3,19},{19,3},{4,20},{20... | collective-permute-start | bytes 294920 | tf_op jit(solution)/shard_map/ppermute | solution.py:64
  90.8 3.2 %collective-permute-done.29.refs_13_ = bf16[416,512]{1,0:T(8,128)(2,1)S(1)} collective-permute-done((bf16[416,512]{1,0:T(8,128)(2,1)S(1)}, bf16[416,512]{1,0:T(8,128)(2,1)S(1)}, u32[]{:S(2)}, u32[]{:S(2)}) %collective-permute-start.29) | collective-permute-done | bytes 426016 | tf_op jit(solution)/shard_map/ppermute | solution.py:56
  94.0 1.5 collective-permute-start.18
  95.7 1.5 collective-permute-start.24
  97.2 6.2 %collective-permute-done.20.refs_4_ = bf16[96,512]{1,0:T(8,128)(2,1)S(1)} collective-permute-done((bf16[96,512]{1,0:T(8,128)(2,1)S(1)}, bf16[96,512]{1,0:T(8,128)(2,1)S(1)}, u32[]{:S(2)}, u32[]{:S(2)}) %collective-permute-start.20) | collective-permute-done | bytes 98336 | tf_op jit(solution)/shard_map/ppermute | solution.py:64
  103.5 1.5 collective-permute-start.22
  104.9 0.6 collective-permute-done.18.refs_2_
  105.6 1.5 collective-permute-start.28
  107.1 0.5 collective-permute-start.26
  107.6 1.5 collective-permute-start.30
  109.1 12.5 %first_rows.1 = (f32[1024,512]{1,0:T(8,128)}, f32[1024,128]{1,0:T(8,128)}) custom-call(s32[8]{0:T(128)} %get-tuple-element.23.block_ref, s32[15]{0:T(128)} %stack.136.place_ref, bf16[512,8192]{1,0:T(8,128)(2,1)} %own_ref.3, bf16[512,8192]{1,0:T(8,128)(2,1)} %collective-permute-done.2.other_ref, bf16[512,512]{1,0:T(8,128)(2,1)} %get-tuple-element.15.refs_0_, ...), custom_call_target="tpu_custom_call" | custom-call | flops 4294967296 | bytes 16777216 | tf_op jit(solution)/shard_map/first_rows/pallas_call | solution.py:353
  121.8 0.7 broadcast_in_dim.11.row_lane_ref
  122.6 13.8 %last_rows.1 = bf16[16,3,16,128]{3,2,1,0:T(8,128)(2,1)} custom-call(s32[8]{0:T(128)} %get-tuple-element.24.block_ref, s32[15]{0:T(128)} %stack.120.place_ref, s32[2,16]{1,0:T(2,128)} %pad_add_fusion.2.slot_ref, bf16[512,8192]{1,0:T(8,128)(2,1)} %own_ref.3, bf16[512,8192]{1,0:T(8,128)(2,1)} %collective-permute-done.2.other_ref, ...), custom_call_target="tpu_custom_call" | custom-call | flops 4294967296 | bytes 16777216 | tf_op jit(solution)/shard_map/last_rows/pallas_call | solution.py:375
  136.4 5.0 %all-to-all-start.1 = ((bf16[16,3,16,128]{3,2,1,0:T(8,128)(2,1)}), bf16[16,3,16,128]{3,2,1,0:T(8,128)(2,1)S(1)}, u32[]{:S(2)}, u32[]{:S(2)}) async-start(bf16[16,3,16,128]{3,2,1,0:T(8,128)(2,1)} %last_rows.1), calls=%async_computation.1 | async-start | bytes 393216 | tf_op jit(solution)/shard_map/all_to_all | solution.py:404
  141.5 2.2 %copy-done = bf16[8,256,1024]{2,1,0:T(8,128)(2,1)S(1)} copy-done((bf16[8,256,1024]{2,1,0:T(8,128)(2,1)S(1)}, bf16[8,256,1024]{2,1,0:T(8,128)(2,1)}, u32[]{:S(2)}) %copy-start) | copy-done | bytes 4194328
  143.7 9.0 %resident.1 = (f32[8,32,128]{2,1,0:T(8,128)S(1)}, f32[32,128]{1,0:T(8,128)S(1)}, f32[32,128]{1,0:T(8,128)S(1)}) custom-call(s32[8]{0:T(128)S(1)} %copy-done.1, bf16[8,32,128]{2,1,0:T(8,128)(2,1)S(1)} %bitcast.47, bf16[8,256,1024]{2,1,0:T(8,128)(2,1)S(1)} %copy-done), custom_call_target="tpu_custom_call" | custom-call | flops 268435456 | bytes 4194304 | tf_op jit(solution)/shard_map/resident/pallas_call | solution.py:325
  152.7 2.3 %combine.1 = bf16[8,4096]{1,0:T(8,128)(2,1)} custom-call(bf16[16,3,16,128]{3,2,1,0:T(8,128)(2,1)S(1)} %all-to-all-done.1.got_ref, f32[8,32,128]{2,1,0:T(8,128)S(1)} %get-tuple-element.18.res_out_ref, f32[32,128]{1,0:T(8,128)S(1)} %get-tuple-element.19.res_top_ref, f32[32,128]{1,0:T(8,128)S(1)} %get-tuple-element.20.res_sum_ref), custom_call_target="tpu_custom_call" | custom-call | tf_op jit(solution)/shard_map/combine/pallas_call | solution.py:406
  (86 shorter events, 1.3 us)
Async XLA Ops:
  2.1 2.2 %collective-permute-start.1 = (bf16[512,512]{1,0:T(8,128)(2,1)}, bf16[512,512]{1,0:T(8,128)(2,1)S(1)}, u32[]{:S(2)}, u32[]{:S(2)}) collective-permute-start(bf16[512,512]{1,0:T(8,128)(2,1)} %get-tuple-element.13), channel_id=1, source_target_pairs={{0,1},{1,0},{2,3},{3,2},{4,5},{5,4},{6,7},{7,6},{8,9},{9,8},{10,11... | collective-permute-start | bytes 1572872 | tf_op jit(solution)/shard_map/ppermute | solution.py:29
  4.3 117.3 %copy-start.2 = (bf16[512,512]{1,0:T(8,128)(2,1)}, bf16[512,512]{1,0:T(8,128)(2,1)S(1)}, u32[]{:S(2)}) copy-start(bf16[512,512]{1,0:T(8,128)(2,1)S(1)} %collective-permute-done.1.refs_0_) | copy-start | bytes 1572868
  4.3 103.3 %collective-permute-start.2 = (bf16[512,8192]{1,0:T(8,128)(2,1)}, bf16[512,8192]{1,0:T(8,128)(2,1)}, u32[]{:S(2)}, u32[]{:S(2)}) collective-permute-start(bf16[512,8192]{1,0:T(8,128)(2,1)} %own_ref.3), channel_id=1, source_target_pairs={{0,1},{1,0},{2,3},{3,2},{4,5},{5,4},{6,7},{7,6},{8,9},{9,8},{10,11... | collective-permute-start | bytes 25165832 | tf_op jit(solution)/shard_map/ppermute | solution.py:29
  5.6 10.9 %collective-permute-start.5 = (bf16[256,512]{1,0:T(8,128)(2,1)S(1)}, bf16[256,512]{1,0:T(8,128)(2,1)S(1)}, u32[]{:S(2)}, u32[]{:S(2)}) collective-permute-start(bf16[256,512]{1,0:T(8,128)(2,1)S(1)} %constant_dynamic-slice_fusion), channel_id=1, source_target_pairs={{0,4},{1,5},{2,6},{3,7},{4,12},{5,13},{6,14},{7,15},{12,8},{13,9},... | collective-permute-start | bytes 786440 | tf_op jit(solution)/shard_map/ppermute | solution.py:55
  9.3 31.2 %collective-permute-start.19 = (bf16[416,512]{1,0:T(8,128)(2,1)}, bf16[416,512]{1,0:T(8,128)(2,1)S(1)}, u32[]{:S(2)}, u32[]{:S(2)}) collective-permute-start(bf16[416,512]{1,0:T(8,128)(2,1)} %constant_dynamic-slice_fusion.1), channel_id=1, source_target_pairs={{0,4},{1,5},{2,6},{3,7},{4,12},{5,13},{6,14},{7,15},{12,8},{13,9},... | collective-permute-start | bytes 1277960 | tf_op jit(solution)/shard_map/ppermute | solution.py:55
  11.9 15.1 %collective-permute-start.3 = (bf16[256,512]{1,0:T(8,128)(2,1)S(1)}, bf16[256,512]{1,0:T(8,128)(2,1)S(1)}, u32[]{:S(2)}, u32[]{:S(2)}) collective-permute-start(bf16[256,512]{1,0:T(8,128)(2,1)S(1)} %constant_dynamic-slice_fusion), channel_id=1, source_target_pairs={{0,2},{1,3},{2,0},{3,1},{4,6},{5,7},{6,4},{7,5},{8,10},{9,11},{10,... | collective-permute-start | bytes 786440 | tf_op jit(solution)/shard_map/ppermute | solution.py:56
  14.1 3.6 %collective-permute-start = (s32[2,8]{1,0:T(2,128)S(1)}, s32[2,8]{1,0:T(2,128)S(1)}, u32[]{:S(2)}, u32[]{:S(2)}) collective-permute-start(s32[2,8]{1,0:T(2,128)S(1)} %pad_add_fusion), channel_id=1, source_target_pairs={{0,1},{1,0},{2,3},{3,2},{4,5},{5,4},{6,7},{7,6},{8,9},{9,8},{10,11... | collective-permute-start | bytes 200 | tf_op jit(solution)/shard_map/ppermute | solution.py:29
  16.6 92.5 %copy-start.9 = (bf16[256,512]{1,0:T(8,128)(2,1)}, bf16[256,512]{1,0:T(8,128)(2,1)S(1)}, u32[]{:S(2)}) copy-start(bf16[256,512]{1,0:T(8,128)(2,1)S(1)} %collective-permute-done.5.refs_3_) | copy-start | bytes 786436
  16.6 21.3 %collective-permute-start.9 = (bf16[256,512]{1,0:T(8,128)(2,1)S(1)}, bf16[256,512]{1,0:T(8,128)(2,1)S(1)}, u32[]{:S(2)}, u32[]{:S(2)}) collective-permute-start(bf16[256,512]{1,0:T(8,128)(2,1)S(1)} %collective-permute-done.5.refs_3_), channel_id=1, source_target_pairs={{0,4},{1,5},{2,6},{3,7},{4,12},{5,13},{6,14},{7,15},{12,8},{13,9},... | collective-permute-start | bytes 786440 | tf_op jit(solution)/shard_map/ppermute | solution.py:55
  17.7 20.8 %collective-permute-start.7 = (bf16[256,512]{1,0:T(8,128)(2,1)S(1)}, bf16[256,512]{1,0:T(8,128)(2,1)}, u32[]{:S(2)}, u32[]{:S(2)}) collective-permute-start(bf16[256,512]{1,0:T(8,128)(2,1)S(1)} %collective-permute-done.5.refs_3_), channel_id=1, source_target_pairs={{0,2},{1,3},{2,0},{3,1},{4,6},{5,7},{6,4},{7,5},{8,10},{9,11},{10,... | collective-permute-start | bytes 786440 | tf_op jit(solution)/shard_map/ppermute | solution.py:56
  22.0 42.4 %all-to-all-start = ((bf16[16,8,2048]{2,1,0:T(8,128)(2,1)}), bf16[16,8,2048]{2,1,0:T(8,128)(2,1)S(1)}, u32[]{:S(2)}, u32[]{:S(2)}) async-start(bf16[16,8,2048]{2,1,0:T(8,128)(2,1)} %bitcast.23), calls=%async_computation | async-start | bytes 1048576 | tf_op jit(solution)/shard_map/all_to_all | solution.py:312
  27.0 19.8 %copy-start.10 = (bf16[256,512]{1,0:T(8,128)(2,1)}, bf16[256,512]{1,0:T(8,128)(2,1)S(1)}, u32[]{:S(2)}) copy-start(bf16[256,512]{1,0:T(8,128)(2,1)S(1)} %collective-permute-done.3.refs_1_) | copy-start | bytes 786436
  27.0 17.6 %collective-permute-start.6 = (bf16[256,512]{1,0:T(8,128)(2,1)S(1)}, bf16[256,512]{1,0:T(8,128)(2,1)S(1)}, u32[]{:S(2)}, u32[]{:S(2)}) collective-permute-start(bf16[256,512]{1,0:T(8,128)(2,1)S(1)} %collective-permute-done.5.refs_3_), channel_id=1, source_target_pairs={{0,16},{16,0},{1,17},{17,1},{2,18},{18,2},{3,19},{19,3},{4,20},{20... | collective-permute-start | bytes 786440 | tf_op jit(solution)/shard_map/ppermute | solution.py:64
  37.9 20.7 %copy-start.11 = (bf16[256,512]{1,0:T(8,128)(2,1)}, bf16[256,512]{1,0:T(8,128)(2,1)S(1)}, u32[]{:S(2)}) copy-start(bf16[256,512]{1,0:T(8,128)(2,1)S(1)} %collective-permute-done.9.refs_7_) | copy-start | bytes 786436
  37.9 9.0 %collective-permute-start.4 = (bf16[256,512]{1,0:T(8,128)(2,1)S(1)}, bf16[256,512]{1,0:T(8,128)(2,1)S(1)}, u32[]{:S(2)}, u32[]{:S(2)}) collective-permute-start(bf16[256,512]{1,0:T(8,128)(2,1)S(1)} %collective-permute-done.3.refs_1_), channel_id=1, source_target_pairs={{0,16},{16,0},{1,17},{17,1},{2,18},{18,2},{3,19},{19,3},{4,20},{20... | collective-permute-start | bytes 786440 | tf_op jit(solution)/shard_map/ppermute | solution.py:64
  38.5 10.2 %collective-permute-start.13 = (bf16[256,512]{1,0:T(8,128)(2,1)S(1)}, bf16[256,512]{1,0:T(8,128)(2,1)}, u32[]{:S(2)}, u32[]{:S(2)}) collective-permute-start(bf16[256,512]{1,0:T(8,128)(2,1)S(1)} %collective-permute-done.9.refs_7_), channel_id=1, source_target_pairs={{0,4},{1,5},{2,6},{3,7},{4,12},{5,13},{6,14},{7,15},{12,8},{13,9},... | collective-permute-start | bytes 786440 | tf_op jit(solution)/shard_map/ppermute | solution.py:55
  40.4 81.2 %copy-start.3 = (bf16[416,512]{1,0:T(8,128)(2,1)}, bf16[416,512]{1,0:T(8,128)(2,1)S(1)}, u32[]{:S(2)}) copy-start(bf16[416,512]{1,0:T(8,128)(2,1)S(1)} %collective-permute-done.19.refs_3_) | copy-start | bytes 1277956
  40.4 16.6 %collective-permute-start.23 = (bf16[416,512]{1,0:T(8,128)(2,1)S(1)}, bf16[416,512]{1,0:T(8,128)(2,1)S(1)}, u32[]{:S(2)}, u32[]{:S(2)}) collective-permute-start(bf16[416,512]{1,0:T(8,128)(2,1)S(1)} %collective-permute-done.19.refs_3_), channel_id=1, source_target_pairs={{0,4},{1,5},{2,6},{3,7},{4,12},{5,13},{6,14},{7,15},{12,8},{13,9},... | collective-permute-start | bytes 1277960 | tf_op jit(solution)/shard_map/ppermute | solution.py:55
  44.6 2.2 %copy-start.12 = (bf16[256,512]{1,0:T(8,128)(2,1)}, bf16[256,512]{1,0:T(8,128)(2,1)S(1)}, u32[]{:S(2)}) copy-start(bf16[256,512]{1,0:T(8,128)(2,1)S(1)} %collective-permute-done.6.refs_4_) | copy-start | bytes 786436
  44.6 9.3 %collective-permute-start.11 = (bf16[256,512]{1,0:T(8,128)(2,1)S(1)}, bf16[256,512]{1,0:T(8,128)(2,1)}, u32[]{:S(2)}, u32[]{:S(2)}) collective-permute-start(bf16[256,512]{1,0:T(8,128)(2,1)S(1)} %collective-permute-done.9.refs_7_), channel_id=1, source_target_pairs={{0,2},{1,3},{2,0},{3,1},{4,6},{5,7},{6,4},{7,5},{8,10},{9,11},{10,... | collective-permute-start | bytes 786440 | tf_op jit(solution)/shard_map/ppermute | solution.py:56
  46.9 8.6 %copy-start.13 = (bf16[256,512]{1,0:T(8,128)(2,1)}, bf16[256,512]{1,0:T(8,128)(2,1)S(1)}, u32[]{:S(2)}) copy-start(bf16[256,512]{1,0:T(8,128)(2,1)S(1)} %collective-permute-done.4.refs_2_) | copy-start | bytes 786436
  46.9 14.8 %collective-permute-start.17 = (bf16[416,512]{1,0:T(8,128)(2,1)}, bf16[416,512]{1,0:T(8,128)(2,1)S(1)}, u32[]{:S(2)}, u32[]{:S(2)}) collective-permute-start(bf16[416,512]{1,0:T(8,128)(2,1)} %constant_dynamic-slice_fusion.1), channel_id=1, source_target_pairs={{0,2},{1,3},{2,0},{3,1},{4,6},{5,7},{6,4},{7,5},{8,10},{9,11},{10,... | collective-permute-start | bytes 1277960 | tf_op jit(solution)/shard_map/ppermute | solution.py:56
  48.7 9.9 %collective-permute-start.10 = (bf16[256,512]{1,0:T(8,128)(2,1)S(1)}, bf16[256,512]{1,0:T(8,128)(2,1)}, u32[]{:S(2)}, u32[]{:S(2)}) collective-permute-start(bf16[256,512]{1,0:T(8,128)(2,1)S(1)} %collective-permute-done.9.refs_7_), channel_id=1, source_target_pairs={{0,16},{16,0},{1,17},{17,1},{2,18},{18,2},{3,19},{19,3},{4,20},{20... | collective-permute-start | bytes 786440 | tf_op jit(solution)/shard_map/ppermute | solution.py:64
  54.0 9.7 %collective-permute-start.8 = (bf16[256,512]{1,0:T(8,128)(2,1)}, bf16[256,512]{1,0:T(8,128)(2,1)}, u32[]{:S(2)}, u32[]{:S(2)}) collective-permute-start(bf16[256,512]{1,0:T(8,128)(2,1)} %collective-permute-done.7.refs_5_), channel_id=1, source_target_pairs={{0,16},{16,0},{1,17},{17,1},{2,18},{18,2},{3,19},{19,3},{4,20},{20... | collective-permute-start | bytes 786440 | tf_op jit(solution)/shard_map/ppermute | solution.py:64
  57.0 64.6 %copy-start.4 = (bf16[416,512]{1,0:T(8,128)(2,1)}, bf16[416,512]{1,0:T(8,128)(2,1)S(1)}, u32[]{:S(2)}) copy-start(bf16[416,512]{1,0:T(8,128)(2,1)S(1)} %collective-permute-done.23.refs_7_) | copy-start | bytes 1277956
  57.0 12.0 %collective-permute-start.27 = (bf16[416,512]{1,0:T(8,128)(2,1)S(1)}, bf16[416,512]{1,0:T(8,128)(2,1)S(1)}, u32[]{:S(2)}, u32[]{:S(2)}) collective-permute-start(bf16[416,512]{1,0:T(8,128)(2,1)S(1)} %collective-permute-done.23.refs_7_), channel_id=1, source_target_pairs={{0,4},{1,5},{2,6},{3,7},{4,12},{5,13},{6,14},{7,15},{12,8},{13,9},... | collective-permute-start | bytes 1277960 | tf_op jit(solution)/shard_map/ppermute | solution.py:55
  58.6 12.8 %collective-permute-start.21 = (bf16[416,512]{1,0:T(8,128)(2,1)S(1)}, bf16[416,512]{1,0:T(8,128)(2,1)S(1)}, u32[]{:S(2)}, u32[]{:S(2)}) collective-permute-start(bf16[416,512]{1,0:T(8,128)(2,1)S(1)} %collective-permute-done.19.refs_3_), channel_id=1, source_target_pairs={{0,2},{1,3},{2,0},{3,1},{4,6},{5,7},{6,4},{7,5},{8,10},{9,11},{10,... | collective-permute-start | bytes 1277960 | tf_op jit(solution)/shard_map/ppermute | solution.py:56
  61.7 59.9 %copy-start.5 = (bf16[416,512]{1,0:T(8,128)(2,1)}, bf16[416,512]{1,0:T(8,128)(2,1)S(1)}, u32[]{:S(2)}) copy-start(bf16[416,512]{1,0:T(8,128)(2,1)S(1)} %collective-permute-done.17.refs_1_) | copy-start | bytes 1277956
  61.7 26.1 %collective-permute-start.25 = (bf16[416,512]{1,0:T(8,128)(2,1)S(1)}, bf16[416,512]{1,0:T(8,128)(2,1)}, u32[]{:S(2)}, u32[]{:S(2)}) collective-permute-start(bf16[416,512]{1,0:T(8,128)(2,1)S(1)} %collective-permute-done.23.refs_7_), channel_id=1, source_target_pairs={{0,2},{1,3},{2,0},{3,1},{4,6},{5,7},{6,4},{7,5},{8,10},{9,11},{10,... | collective-permute-start | bytes 1277960 | tf_op jit(solution)/shard_map/ppermute | solution.py:56
  63.7 22.5 %collective-permute-start.15 = (bf16[256,512]{1,0:T(8,128)(2,1)}, bf16[256,512]{1,0:T(8,128)(2,1)}, u32[]{:S(2)}, u32[]{:S(2)}) collective-permute-start(bf16[256,512]{1,0:T(8,128)(2,1)} %collective-permute-done.13.refs_11_), channel_id=1, source_target_pairs={{0,2},{1,3},{2,0},{3,1},{4,6},{5,7},{6,4},{7,5},{8,10},{9,11},{10,... | collective-permute-start | bytes 786440 | tf_op jit(solution)/shard_map/ppermute | solution.py:56
  69.1 52.6 %copy-start.6 = (bf16[416,512]{1,0:T(8,128)(2,1)}, bf16[416,512]{1,0:T(8,128)(2,1)S(1)}, u32[]{:S(2)}) copy-start(bf16[416,512]{1,0:T(8,128)(2,1)S(1)} %collective-permute-done.27.refs_11_) | copy-start | bytes 1277956
  69.1 24.9 %collective-permute-start.29 = (bf16[416,512]{1,0:T(8,128)(2,1)S(1)}, bf16[416,512]{1,0:T(8,128)(2,1)S(1)}, u32[]{:S(2)}, u32[]{:S(2)}) collective-permute-start(bf16[416,512]{1,0:T(8,128)(2,1)S(1)} %collective-permute-done.27.refs_11_), channel_id=1, source_target_pairs={{0,2},{1,3},{2,0},{3,1},{4,6},{5,7},{6,4},{7,5},{8,10},{9,11},{10,... | collective-permute-start | bytes 1277960 | tf_op jit(solution)/shard_map/ppermute | solution.py:56
  71.4 50.2 %copy-start.7 = (bf16[416,512]{1,0:T(8,128)(2,1)}, bf16[416,512]{1,0:T(8,128)(2,1)S(1)}, u32[]{:S(2)}) copy-start(bf16[416,512]{1,0:T(8,128)(2,1)S(1)} %collective-permute-done.21.refs_5_) | copy-start | bytes 1277956
  71.4 17.8 %collective-permute-start.14 = (bf16[256,512]{1,0:T(8,128)(2,1)}, bf16[256,512]{1,0:T(8,128)(2,1)S(1)}, u32[]{:S(2)}, u32[]{:S(2)}) collective-permute-start(bf16[256,512]{1,0:T(8,128)(2,1)} %collective-permute-done.13.refs_11_), channel_id=1, source_target_pairs={{0,16},{16,0},{1,17},{17,1},{2,18},{18,2},{3,19},{19,3},{4,20},{20... | collective-permute-start | bytes 786440 | tf_op jit(solution)/shard_map/ppermute | solution.py:64
  86.3 9.5 %collective-permute-start.12 = (bf16[256,512]{1,0:T(8,128)(2,1)}, bf16[256,512]{1,0:T(8,128)(2,1)S(1)}, u32[]{:S(2)}, u32[]{:S(2)}) collective-permute-start(bf16[256,512]{1,0:T(8,128)(2,1)} %collective-permute-done.11.refs_9_), channel_id=1, source_target_pairs={{0,16},{16,0},{1,17},{17,1},{2,18},{18,2},{3,19},{19,3},{4,20},{20... | collective-permute-start | bytes 786440 | tf_op jit(solution)/shard_map/ppermute | solution.py:64
  87.8 19.3 %collective-permute-start.16 = (bf16[256,512]{1,0:T(8,128)(2,1)}, bf16[256,512]{1,0:T(8,128)(2,1)S(1)}, u32[]{:S(2)}, u32[]{:S(2)}) collective-permute-start(bf16[256,512]{1,0:T(8,128)(2,1)} %collective-permute-done.15.refs_13_), channel_id=1, source_target_pairs={{0,16},{16,0},{1,17},{17,1},{2,18},{18,2},{3,19},{19,3},{4,20},{20... | collective-permute-start | bytes 786440 | tf_op jit(solution)/shard_map/ppermute | solution.py:64
  89.2 19.9 %copy-start.14 = (bf16[256,512]{1,0:T(8,128)(2,1)}, bf16[256,512]{1,0:T(8,128)(2,1)S(1)}, u32[]{:S(2)}) copy-start(bf16[256,512]{1,0:T(8,128)(2,1)S(1)} %collective-permute-done.14.refs_12_) | copy-start | bytes 786436
  89.2 14.2 %collective-permute-start.20 = (bf16[96,512]{1,0:T(8,128)(2,1)S(1)}, bf16[96,512]{1,0:T(8,128)(2,1)S(1)}, u32[]{:S(2)}, u32[]{:S(2)}) collective-permute-start(bf16[96,512]{1,0:T(8,128)(2,1)S(1)} %constant_dynamic-slice_fusion.3), channel_id=1, source_target_pairs={{0,16},{16,0},{1,17},{17,1},{2,18},{18,2},{3,19},{19,3},{4,20},{20... | collective-permute-start | bytes 294920 | tf_op jit(solution)/shard_map/ppermute | solution.py:64
  94.0 27.6 %copy-start.8 = (bf16[416,512]{1,0:T(8,128)(2,1)}, bf16[416,512]{1,0:T(8,128)(2,1)S(1)}, u32[]{:S(2)}) copy-start(bf16[416,512]{1,0:T(8,128)(2,1)S(1)} %collective-permute-done.29.refs_13_) | copy-start | bytes 1277956
  94.0 11.5 %collective-permute-start.18 = (bf16[96,512]{1,0:T(8,128)(2,1)}, bf16[96,512]{1,0:T(8,128)(2,1)S(1)}, u32[]{:S(2)}, u32[]{:S(2)}) collective-permute-start(bf16[96,512]{1,0:T(8,128)(2,1)} %constant_dynamic-slice_fusion.2), channel_id=1, source_target_pairs={{0,16},{16,0},{1,17},{17,1},{2,18},{18,2},{3,19},{19,3},{4,20},{20... | collective-permute-start | bytes 294920 | tf_op jit(solution)/shard_map/ppermute | solution.py:64
  95.7 13.4 %copy-start.15 = (bf16[256,512]{1,0:T(8,128)(2,1)}, bf16[256,512]{1,0:T(8,128)(2,1)S(1)}, u32[]{:S(2)}) copy-start(bf16[256,512]{1,0:T(8,128)(2,1)S(1)} %collective-permute-done.12.refs_10_) | copy-start | bytes 786436
  95.7 25.9 %collective-permute-start.24 = (bf16[96,512]{1,0:T(8,128)(2,1)S(1)}, bf16[96,512]{1,0:T(8,128)(2,1)S(1)}, u32[]{:S(2)}, u32[]{:S(2)}) collective-permute-start(bf16[96,512]{1,0:T(8,128)(2,1)S(1)} %constant_dynamic-slice_fusion.5), channel_id=1, source_target_pairs={{0,16},{16,0},{1,17},{17,1},{2,18},{18,2},{3,19},{19,3},{4,20},{20... | collective-permute-start | bytes 294920 | tf_op jit(solution)/shard_map/ppermute | solution.py:64
  103.5 19.0 %copy-start.18 = (bf16[96,512]{1,0:T(8,128)(2,1)}, bf16[96,512]{1,0:T(8,128)(2,1)S(1)}, u32[]{:S(2)}) copy-start(bf16[96,512]{1,0:T(8,128)(2,1)S(1)} %collective-permute-done.20.refs_4_) | copy-start | bytes 294916
  103.5 18.2 %collective-permute-start.22 = (bf16[96,512]{1,0:T(8,128)(2,1)S(1)}, bf16[96,512]{1,0:T(8,128)(2,1)S(1)}, u32[]{:S(2)}, u32[]{:S(2)}) collective-permute-start(bf16[96,512]{1,0:T(8,128)(2,1)S(1)} %constant_dynamic-slice_fusion.4), channel_id=1, source_target_pairs={{0,16},{16,0},{1,17},{17,1},{2,18},{18,2},{3,19},{19,3},{4,20},{20... | collective-permute-start | bytes 294920 | tf_op jit(solution)/shard_map/ppermute | solution.py:64
  105.6 16.9 %copy-start.19 = (bf16[96,512]{1,0:T(8,128)(2,1)}, bf16[96,512]{1,0:T(8,128)(2,1)S(1)}, u32[]{:S(2)}) copy-start(bf16[96,512]{1,0:T(8,128)(2,1)S(1)} %collective-permute-done.18.refs_2_) | copy-start | bytes 294916
  105.6 16.1 %collective-permute-start.28 = (bf16[96,512]{1,0:T(8,128)(2,1)S(1)}, bf16[96,512]{1,0:T(8,128)(2,1)S(1)}, u32[]{:S(2)}, u32[]{:S(2)}) collective-permute-start(bf16[96,512]{1,0:T(8,128)(2,1)S(1)} %constant_dynamic-slice_fusion.7), channel_id=1, source_target_pairs={{0,16},{16,0},{1,17},{17,1},{2,18},{18,2},{3,19},{19,3},{4,20},{20... | collective-permute-start | bytes 294920 | tf_op jit(solution)/shard_map/ppermute | solution.py:64
  107.1 2.0 %copy-start.16 = (bf16[256,512]{1,0:T(8,128)(2,1)}, bf16[256,512]{1,0:T(8,128)(2,1)S(1)}, u32[]{:S(2)}) copy-start(bf16[256,512]{1,0:T(8,128)(2,1)S(1)} %collective-permute-done.16.refs_14_) | copy-start | bytes 786436
  107.1 14.7 %collective-permute-start.26 = (bf16[96,512]{1,0:T(8,128)(2,1)S(1)}, bf16[96,512]{1,0:T(8,128)(2,1)S(1)}, u32[]{:S(2)}, u32[]{:S(2)}) collective-permute-start(bf16[96,512]{1,0:T(8,128)(2,1)S(1)} %constant_dynamic-slice_fusion.6), channel_id=1, source_target_pairs={{0,16},{16,0},{1,17},{17,1},{2,18},{18,2},{3,19},{19,3},{4,20},{20... | collective-permute-start | bytes 294920 | tf_op jit(solution)/shard_map/ppermute | solution.py:64
  107.6 14.1 %collective-permute-start.30 = (bf16[96,512]{1,0:T(8,128)(2,1)S(1)}, bf16[96,512]{1,0:T(8,128)(2,1)S(1)}, u32[]{:S(2)}, u32[]{:S(2)}) collective-permute-start(bf16[96,512]{1,0:T(8,128)(2,1)S(1)} %constant_dynamic-slice_fusion.8), channel_id=1, source_target_pairs={{0,16},{16,0},{1,17},{17,1},{2,18},{18,2},{3,19},{19,3},{4,20},{20... | collective-permute-start | bytes 294920 | tf_op jit(solution)/shard_map/ppermute | solution.py:64
  121.7 0.8 copy-start.20
  121.7 0.8 copy-start.21
  121.7 0.8 copy-start.22
  121.7 0.8 copy-start.23
  121.7 0.8 copy-start.24
  122.5 18.9 %copy-start.17 = (bf16[8,4096]{1,0:T(8,128)(2,1)S(1)}, bf16[8,4096]{1,0:T(8,128)(2,1)}, u32[]{:S(2)}) copy-start(bf16[8,4096]{1,0:T(8,128)(2,1)} %param.13) | copy-start | bytes 196612
  122.5 18.9 %copy-start.1 = (s32[8]{0:T(128)S(1)}, s32[8]{0:T(128)}, u32[]{:S(2)}) copy-start(s32[8]{0:T(128)} %length_ref.1) | copy-start | bytes 100
  136.4 16.3 %all-to-all-start.1 = ((bf16[16,3,16,128]{3,2,1,0:T(8,128)(2,1)}), bf16[16,3,16,128]{3,2,1,0:T(8,128)(2,1)S(1)}, u32[]{:S(2)}, u32[]{:S(2)}) async-start(bf16[16,3,16,128]{3,2,1,0:T(8,128)(2,1)} %last_rows.1), calls=%async_computation.1 | async-start | bytes 393216 | tf_op jit(solution)/shard_map/all_to_all | solution.py:404
  141.5 2.2 %copy-start = (bf16[8,256,1024]{2,1,0:T(8,128)(2,1)S(1)}, bf16[8,256,1024]{2,1,0:T(8,128)(2,1)}, u32[]{:S(2)}) copy-start(bf16[8,256,1024]{2,1,0:T(8,128)(2,1)} %cache_ref.1) | copy-start | bytes 12582916

commit v4 on v3

--- a/solution.py
+++ b/solution.py
@@ -34,50 +34,42 @@
     rows = chunk.shape[0]
     groups = [list(range(core, n, 2)) for core in range(2)]
     whole = lax.all_gather(chunk, "section", axis=0, tiled=True, axis_index_groups=groups)
-    return [(chip, [(whole, chip * rows, rows, 0)]) for chip in range(n // 2)]
-
-
-def gather_grid(chunk, span):
+    return [(chip, whole, chip * rows) for chip in range(n // 2)]
+
+
+RING = [0, 1, 3, 2]
+
+
+def along_ring(x):
+    perm = []
+    for rep, way in ((0, 1), (1, -1)):
+        for p in range(4):
+            for low in range(4):
+                perm.append((rep * 16 + RING[p] * 4 + low, rep * 16 + RING[(p + way) % 4] * 4 + low))
+    return lax.ppermute(x, ("replica", "section"), perm)
+
+
+def across_y(x):
+    return lax.ppermute(x, "section", [(i, i ^ 2) for i in range(16)])
+
+
+def across_replica(x):
+    return lax.ppermute(x, "replica", [(0, 1), (1, 0)])
+
+
+def ring_chips():
     section = lax.axis_index("section")
     rep = lax.axis_index("replica")
     z, y = section // 4, section // 2 % 2
-    rows = chunk.shape[0]
-    rest = rows - span
-    order = [0, 1, 3, 2]
-    ring = [(order[p] * 4 + low, order[(p + 1) % 4] * 4 + low) for p in range(4) for low in range(4)]
-    swap_y = [(i, i ^ 2) for i in range(16)]
-    places = jnp.array([0, 1, 3, 2], jnp.int32)
-    place = places[z]
-    along_z = [lax.dynamic_slice_in_dim(chunk, rep * rest, span, 0)]
-    along_y = []
-    for step in range(4):
-        if step < 3:
-            along_z.append(lax.ppermute(along_z[-1], "section", ring))
-        along_y.append(lax.ppermute(along_z[step], "section", swap_y))
-    groups = [(z * 2 + y, [(chunk, 0, rows, 0)])]
-    for step in range(4):
-        from_z = places[(place - step) % 4]
-        for piece, chip in ((along_z[step], from_z * 2 + y), (along_y[step], from_z * 2 + 1 - y)):
-            if piece is along_z[0]:
-                continue
-            part = piece if rest == span else lax.dynamic_slice_in_dim(piece, rep * (span - rest), rest, 0)
-            extra = lax.ppermute(part, "replica", [(0, 1), (1, 0)])
-            groups.append((chip, [(piece, 0, span, rep * rest), (extra, 0, rest, (1 - rep) * span)]))
-    return groups
-
-
-def flatten(groups):
-    arrays, layout, numbers = [], [], []
-    for index, (chip, parts) in enumerate(groups):
-        for array, start, rows, place in parts:
-            at = [i for i, known in enumerate(arrays) if known is array]
-            if not at:
-                arrays.append(array)
-                at = [len(arrays) - 1]
-            layout.append((at[0], start, rows, index))
-            numbers.append(jnp.asarray(place, jnp.int32))
-    chips = [jnp.asarray(chip, jnp.int32) for chip, _ in groups]
-    return arrays, layout, jnp.stack(chips), jnp.stack(numbers)
+    ring = jnp.array(RING, jnp.int32)
+    way = 1 - 2 * rep
+    place = ring[z]
+    chips = {}
+    for name, at in (("own", place), ("behind", place - way), ("ahead", place + way), ("opposite", place + 2)):
+        there = ring[at % 4] * 2
+        chips[name] = there + y
+        chips[name + "_y"] = there + 1 - y
+    return chips
 
 
 def split_kernel(core_ref, keep_in, give_in, keep_ref, give_ref):
@@ -85,16 +77,12 @@
     give_ref[...] = give_in[...]
 
 
-def accumulate(layout, place_ref, own_ref, other_ref, piece_refs, weight, total, squares, sems):
+def accumulate(layout, own_ref, other_ref, piece_refs, weight, total, squares, sems):
     step = pl.program_id(0)
     tokens, depth = own_ref.shape
     copies = [
-        pltpu.make_async_copy(
-            piece_refs[which].at[pl.ds(start, rows)],
-            weight.at[group, pl.ds(pl.multiple_of(place_ref[i], 32), rows)],
-            sems.at[i],
-        )
-        for i, (which, start, rows, group) in enumerate(layout)
+        pltpu.make_async_copy(piece_refs[which].at[pl.ds(start, depth)], weight.at[i], sems.at[i])
+        for i, (which, start) in enumerate(layout)
     ]
 
     @pl.when(step == 0)
@@ -102,13 +90,11 @@
         for copy in copies:
             copy.start()
 
-    for group in range(weight.shape[0]):
-
-        @pl.when(step == group)
+    for i, copy in enumerate(copies):
+
+        @pl.when(step == i)
         def _():
-            for copy, (_, _, _, owner) in zip(copies, layout):
-                if owner == group:
-                    copy.wait()
+            copy.wait()
 
     states = jnp.concatenate([own_ref[...], other_ref[...]], axis=0)
     total[...] += jnp.dot(states, weight[step], preferred_element_type=jnp.float32)
@@ -117,7 +103,7 @@
     squares[...] += sum(values[:, i : i + HD] for i in range(0, depth, HD))
 
 
-def first_kernel(layout, n_pieces, block_ref, place_ref, own_ref, other_ref, *refs):
+def first_kernel(layout, n_pieces, block_ref, own_ref, other_ref, *refs):
     piece_refs = refs[:n_pieces]
     total, squares, weight, sems = refs[n_pieces:]
 
@@ -126,7 +112,19 @@
         total[...] = jnp.zeros_like(total)
         squares[...] = jnp.zeros_like(squares)
 
-    accumulate(layout, place_ref, own_ref, other_ref, piece_refs, weight, total, squares, sems)
+    accumulate(layout, own_ref, other_ref, piece_refs, weight, total, squares, sems)
+
+
+def next_kernel(layout, n_pieces, block_ref, own_ref, other_ref, in_total, in_squares, *refs):
+    piece_refs = refs[:n_pieces]
+    total, squares, weight, sems = refs[n_pieces:]
+
+    @pl.when(pl.program_id(0) == 0)
+    def _():
+        total[...] = in_total[...]
+        squares[...] = in_squares[...]
+
+    accumulate(layout, own_ref, other_ref, piece_refs, weight, total, squares, sems)
 
 
 def parts_of(values, count):
@@ -139,7 +137,7 @@
 
 
 def last_kernel(
-    layout, n_pieces, width, block_ref, place_ref, slot_ref, own_ref, other_ref, query_ref, row_lane_ref, in_total, in_squares, *refs
+    layout, n_pieces, width, block_ref, slot_ref, own_ref, other_ref, in_total, in_squares, query_ref, row_lane_ref, *refs
 ):
     piece_refs = refs[:n_pieces]
     slots_ref, weight, total, squares, summed, stats, sems = refs[n_pieces:]
@@ -151,7 +149,7 @@
         squares[...] = in_squares[...]
         slots_ref[...] = jnp.zeros_like(slots_ref)
 
-    accumulate(layout, place_ref, own_ref, other_ref, piece_refs, weight, total, squares, sems)
+    accumulate(layout, own_ref, other_ref, piece_refs, weight, total, squares, sems)
 
     @pl.when(pl.program_id(0) == pl.num_programs(0) - 1)
     def _():
@@ -220,7 +218,7 @@
         sum_ref[part, :] = jnp.where(lane == row, jnp.sum(weights, axis=1, keepdims=True), sum_ref[part, :])
 
 
-def combine_kernel(got_ref, res_out_ref, res_top_ref, res_sum_ref, out_ref, acc, shares):
+def combine_kernel(got_ref, res_out_ref, res_top_ref, res_sum_ref, out_ref, acc):
     chips = got_ref.shape[0] // 2
     rows = res_out_ref.shape[0]
     lane = lax.broadcasted_iota(jnp.int32, (HALF_QH, HD), 1)
@@ -276,7 +274,7 @@
     images = image_owner.shape[0]
     decode_rows = queries.shape[0]
     context = cache.shape[1]
-    grid_form = n == 16 and lax.axis_size("replica") == 2
+    n_queries = 2 * images * GROUP
 
     cut = columns_dev // 2
     keep, give = pl.pallas_call(
@@ -295,13 +293,7 @@
         name="split",
     )(core.reshape(1), kv_weight, kv_weight)
     taken = swap_core(give)
-    if grid_form:
-        phases = [gather_grid(keep, rows_dev // 2), gather_grid(taken, rows_dev * 13 // 16)]
-    else:
-        phases = [gather_plain(keep), gather_plain(taken)]
-
-    states, taken = lax.optimization_barrier((prompt_states, taken))
-    other = swap_core(states)
+    other = swap_core(prompt_states)
 
     owner_and_row = jnp.stack([image_owner, image_row])
     chip_images = jnp.concatenate([owner_and_row, swap_core(owner_and_row)], axis=1)
@@ -315,8 +307,7 @@
     pick = (target[:, None] == jnp.arange(n * decode_rows)[None, :]).astype(jnp.bfloat16)
     image_q = jnp.dot(pick, all_q, preferred_element_type=jnp.float32).astype(jnp.bfloat16)
     image_q = image_q.reshape(2 * images, HALF_KVH, GROUP, HD).transpose(1, 0, 2, 3)
-    image_q = image_q.reshape(HALF_KVH, 2 * images * GROUP, HD)
-    n_queries = 2 * images * GROUP
+    image_q = image_q.reshape(HALF_KVH, n_queries, HD)
 
     which = jnp.concatenate([jnp.full((images,), core), jnp.full((images,), 1 - core)]).astype(jnp.int32)
     slot = jnp.stack([chip_images[0], which])
@@ -339,68 +330,98 @@
             jax.ShapeDtypeStruct((QH, HD), jnp.float32),
         ],
         compiler_params=pltpu.CompilerParams(vmem_limit_bytes=16 * 2**20),
-        cost_estimate=pl.CostEstimate(flops=2**28, bytes_accessed=4 * 2**20, transcendentals=0),
+        cost_estimate=pl.CostEstimate(flops=2**28, bytes_accessed=24 * 2**20, transcendentals=0),
         name="resident",
     )(context_length, queries.reshape(decode_rows, QH, HD), cache)
 
-    flops = 2 * 2 * tokens * width // 2 * columns_dev
-    cost = pl.CostEstimate(flops=flops, bytes_accessed=16 * 2**20, transcendentals=0)
-    params = pltpu.CompilerParams(vmem_limit_bytes=56 * 2**20)
-    token_spec = pl.BlockSpec((tokens, rows_dev), lambda i, block_ref, *_: (0, block_ref[i]))
-    anywhere = pl.BlockSpec(memory_space=pl.ANY)
-
-    arrays, layout, chips, places = flatten(phases[0])
-    total, squares = pl.pallas_call(
-        functools.partial(first_kernel, layout, len(arrays)),
-        grid_spec=pltpu.PrefetchScalarGridSpec(
-            num_scalar_prefetch=2,
-            grid=(n // 2,),
-            in_specs=[token_spec, token_spec] + [anywhere] * len(arrays),
-            out_specs=[whole((2 * tokens, columns_dev)), whole((2 * tokens, HD))],
-            scratch_shapes=[
-                pltpu.VMEM((n // 2, rows_dev, columns_dev), jnp.bfloat16),
-                pltpu.SemaphoreType.DMA((len(layout),)),
-            ],
-        ),
-        out_shape=[
+    def product(groups, carry, name, last=False):
+        arrays, layout, blocks = [], [], []
+        for block, array, start in groups:
+            at = [i for i, known in enumerate(arrays) if known is array]
+            if not at:
+                arrays.append(array)
+                at = [len(arrays) - 1]
+            layout.append((at[0], start))
+            blocks.append(jnp.asarray(block, jnp.int32))
+        steps = len(groups)
+        token_spec = pl.BlockSpec((tokens, rows_dev), lambda i, block_ref, *_: (0, block_ref[i]))
+        sums = [whole((2 * tokens, columns_dev)), whole((2 * tokens, HD))]
+        sum_shapes = [
             jax.ShapeDtypeStruct((2 * tokens, columns_dev), jnp.float32),
             jax.ShapeDtypeStruct((2 * tokens, HD), jnp.float32),
-        ],
-        compiler_params=params,
-        cost_estimate=cost,
-        name="first_rows",
-    )(chips * 2 + core, places, prompt_states, other, *arrays)
-
-    arrays, layout, chips, places = flatten(phases[1])
-    slots = pl.pallas_call(
-        functools.partial(last_kernel, layout, len(arrays), width),
-        grid_spec=pltpu.PrefetchScalarGridSpec(
-            num_scalar_prefetch=3,
-            grid=(n // 2,),
-            in_specs=[
-                token_spec,
-                token_spec,
-                whole((HALF_KVH, n_queries, HD)),
-                whole((n_queries, HD)),
-                whole((2 * tokens, columns_dev)),
-                whole((2 * tokens, HD)),
-            ]
-            + [anywhere] * len(arrays),
-            out_specs=whole((n, 3, HALF_QH, HD)),
-            scratch_shapes=[
-                pltpu.VMEM((n // 2, rows_dev, columns_dev), jnp.bfloat16),
+        ]
+        scratch = [pltpu.VMEM((steps, rows_dev, columns_dev), jnp.bfloat16)]
+        in_specs = [token_spec, token_spec]
+        scalars = [jnp.stack(blocks)]
+        inputs = [prompt_states, other]
+        kernel = first_kernel
+        if carry is not None:
+            kernel = next_kernel
+            in_specs = in_specs + sums
+            inputs = inputs + list(carry)
+        out_specs, out_shape = sums, sum_shapes
+        body = functools.partial(kernel, layout, len(arrays))
+        if last:
+            body = functools.partial(last_kernel, layout, len(arrays), width)
+            scalars = scalars + [slot]
+            in_specs = in_specs + [whole((HALF_KVH, n_queries, HD)), whole((n_queries, HD))]
+            inputs = inputs + [image_q, row_lane]
+            out_specs = whole((n, 3, HALF_QH, HD))
+            out_shape = jax.ShapeDtypeStruct((n, 3, HALF_QH, HD), jnp.bfloat16)
+            scratch = scratch + [
                 pltpu.VMEM((2 * tokens, columns_dev), jnp.float32),
                 pltpu.VMEM((2 * tokens, HD), jnp.float32),
                 pltpu.VMEM((2 * images, HALF_QH, HD), jnp.float32),
                 pltpu.VMEM((2 * images, HALF_QH, HD), jnp.float32),
-                pltpu.SemaphoreType.DMA((len(layout),)),
-            ],
-        ),
-        out_shape=jax.ShapeDtypeStruct((n, 3, HALF_QH, HD), jnp.bfloat16),
-        compiler_params=params,
-        cost_estimate=cost,
-        name="last_rows",
-    )(chips * 2 + 1 - core, places, slot, prompt_states, other, image_q, row_lane, total, squares, *arrays)
+            ]
+        return pl.pallas_call(
+            body,
+            grid_spec=pltpu.PrefetchScalarGridSpec(
+                num_scalar_prefetch=len(scalars),
+                grid=(steps,),
+                in_specs=in_specs + [pl.BlockSpec(memory_space=pl.ANY)] * len(arrays),
+                out_specs=out_specs,
+                scratch_shapes=scratch + [pltpu.SemaphoreType.DMA((steps,))],
+            ),
+            out_shape=out_shape,
+            compiler_params=pltpu.CompilerParams(vmem_limit_bytes=56 * 2**20),
+            cost_estimate=pl.CostEstimate(
+                flops=2 * 2 * tokens * rows_dev * columns_dev * steps,
+                bytes_accessed=5 * steps * 2**20,
+                transcendentals=0,
+            ),
+            name=name,
+        )(*scalars, *inputs, *arrays)
+
+    if n == 16 and lax.axis_size("replica") == 2:
+        chips = ring_chips()
+        at_a = {name: chip * 2 + core for name, chip in chips.items()}
+        at_b = {name: chip * 2 + 1 - core for name, chip in chips.items()}
+
+        def rows(at, names, arrays):
+            return [(at[name], array, 0) for name, array in zip(names, arrays)]
+
+        step1 = ("own", "behind", "own_y")
+        step2 = ("ahead", "opposite", "behind_y")
+        step3 = ("ahead_y", "opposite_y")
+        a1 = (keep, along_ring(keep), across_y(keep))
+        b1 = (taken, along_ring(taken), across_y(taken))
+        a2 = (across_replica(a1[1]), along_ring(a1[1]), across_y(a1[1]))
+        b_behind, res_out = lax.optimization_barrier((b1[1], res_out))
+        b2 = (across_replica(b_behind), along_ring(b_behind), across_y(b_behind))
+        carry = product(rows(at_a, step1, a1) + rows(at_b, step1, b1), None, "rows_1")
+        a_behind_y, a_opposite, carry = lax.optimization_barrier((a2[2], a2[1], carry))
+        a3 = (across_replica(a_behind_y), across_y(a_opposite))
+        carry = product(rows(at_a, step2, a2), carry, "rows_2a")
+        b_behind_y, carry = lax.optimization_barrier((b2[2], carry))
+        b3 = (across_replica(b_behind_y), along_ring(b_behind_y))
+        carry = product(rows(at_b, step2, b2), carry, "rows_2b")
+        carry = product(rows(at_a, step3, a3), carry, "rows_3a")
+        slots = product(rows(at_b, step3, b3), carry, "rows_3b", last=True)
+    else:
+        a = [(chip * 2 + core, array, start) for chip, array, start in gather_plain(keep)]
+        b = [(chip * 2 + 1 - core, array, start) for chip, array, start in gather_plain(taken)]
+        slots = product(b, product(a, None, "rows_a"), "rows_b", last=True)
     got = lax.all_to_all(slots, "section", split_axis=0, concat_axis=0, tiled=True)
 
     return pl.pallas_call(
@@ -413,10 +434,7 @@
             whole((QH, HD)),
         ],
         out_specs=whole((decode_rows, QH * HD)),
-        scratch_shapes=[
-            pltpu.VMEM((decode_rows, QH, HD), jnp.float32),
-            pltpu.VMEM((HALF_QH, HD), jnp.float32),
-        ],
+        scratch_shapes=[pltpu.VMEM((decode_rows, QH, HD), jnp.float32)],
         out_shape=jax.ShapeDtypeStruct((decode_rows, QH * HD), jnp.bfloat16),
         compiler_params=pltpu.CompilerParams(vmem_limit_bytes=32 * 2**20),
         name="combine",

time: 156 us -> 131 us (0.84)
  starting transfers between devices: 52.2 us -> 27.1 us
  waiting for transfers between devices: 40.4 us -> 15.7 us
  Pallas kernels: 39.7 us -> 53.8 us
  blocking collectives: 0 us -> 12.9 us
  local copies, waits for them, and re-layouts: 12.9 us -> 10.9 us
    ppermute x28 -> x14, waiting for transfers between devices: 38.6 us -> 7.5 us  [the longest x4 7.47 us: across_replica(): return lax.ppermute(x, 'replica', [(0, 1), (1, 0)])]
    ppermute x28 -> x14, starting transfers between devices: 41.4 us -> 22.5 us  [the longest x5 9.35 us: along_ring(): return lax.ppermute(x, ('replica', 'section'), perm)]
    pallas_call x2 -> x5, Pallas kernels: 26.3 us -> 40.4 us  [product(): pl.pallas_call(body, grid_spec=pltpu.PrefetchScalarGridSpec(num_scalar_pr...]
    all_to_all x0 -> x1, blocking collectives: none -> 12.9 us  [per_device(): lax.all_to_all(slots, 'section', split_axis=0, concat_axis=0, tiled=True)]
    ppermute x3, waiting for transfers between devices: 1.75 us -> 8.19 us  [swap_core(): return lax.ppermute(x, 'section', [(i, i ^ 1) for i in range(n)])]
    all_to_all x1 -> x0, starting transfers between devices: 5.03 us -> none  [per_device(): lax.all_to_all(slots, 'section', split_axis=0, concat_axis=0, tiled=True)]
    dynamic_slice x11 -> x2, local copies, waits for them, and re-layouts: 6.06 us -> 1.26 us  [the longest x1 0.68 us: ring_chips(): there = ring[at % 4] * 2]
    unnamed x52 -> x42, local copies, waits for them, and re-layouts: 2.31 us -> 6.45 us
  transfers between devices with their start and end apart: 33 -> 18, of which waited for: 13 -> 3; matrix products, arithmetic and copies ran while one was open for 8% -> 5% of each run, Pallas kernels for 14% -> 34%
where the time goes in v4:
time: 131 us; the launch traced here: 130 us
  Pallas kernels  53.8 us (41%)
  starting transfers between devices  27.1 us (21%)
  waiting for transfers between devices  15.7 us (12%)
  blocking collectives  12.9 us (10%)
  local copies, waits for them, and re-layouts  10.9 us (8%)
  between operations  6.76 us (5%)
  other arithmetic  3.15 us (2%)
    pallas_call x5, Pallas kernels, product(): pl.pallas_call(body, grid_spec=pltpu.PrefetchScalarGridSpec(num_scalar_pr...  40.4 us
    all_to_all x1, blocking collectives, per_device(): lax.all_to_all(slots, 'section', split_axis=0, concat_axis=0, tiled=True)  12.9 us
    ppermute x5, starting transfers between devices, along_ring(): return lax.ppermute(x, ('replica', 'section'), perm)  9.35 us
    pallas_call x1, Pallas kernels, per_device(): pl.pallas_call(resident_kernel, grid_spec=pltpu.PrefetchScalarGridSpec(nu...  9.01 us
    ppermute x3, waiting for transfers between devices, swap_core(): return lax.ppermute(x, 'section', [(i, i ^ 1) for i in range(n)])  8.19 us
    ppermute x4, waiting for transfers between devices, across_replica(): return lax.ppermute(x, 'replica', [(0, 1), (1, 0)])  7.47 us
    ppermute x5, starting transfers between devices, across_y(): return lax.ppermute(x, 'section', [(i, i ^ 2) for i in range(16)])  6.91 us
    unnamed x42, local copies, waits for them, and re-layouts  6.45 us
  transfers between devices with their start and end apart: 18, of which 3 were waited for; matrix products, arithmetic and copies ran while one was open for 5% of the time, Pallas kernels for 34%

profile of v4, /device:TPU:0, one launch (start us, length us, event | category | flops | bytes accessed | tf_op | source)
XLA Modules:
  0.0 130.5 jit_solution(11064269952882769299)
XLA Ops:
  0.0 0.5 collective-permute-start.1
  0.5 2.1 %split.1 = (bf16[512,512]{1,0:T(8,128)(2,1)}, bf16[512,512]{1,0:T(8,128)(2,1)}) custom-call(s32[1]{0:T(128)} %bitcast.14.core_ref, bf16[512,1024]{1,0:T(8,128)(2,1)} %give_in.1, bf16[512,1024]{1,0:T(8,128)(2,1)} %give_in.1), custom_call_target="tpu_custom_call" | custom-call | bytes 2097152 | tf_op jit(solution)/shard_map/split/pallas_call | solution.py:280
  2.6 0.1 collective-permute-start.2
  2.7 3.0 %collective-permute-start.5 = (bf16[512,512]{1,0:T(8,128)(2,1)}, bf16[512,512]{1,0:T(8,128)(2,1)S(1)}, u32[]{:S(2)}, u32[]{:S(2)}) collective-permute-start(bf16[512,512]{1,0:T(8,128)(2,1)} %get-tuple-element.30.refs_0_), channel_id=1, source_target_pairs={{0,4},{1,5},{2,6},{3,7},{4,12},{5,13},{6,14},{7,15},{12,8},{13,9},... | collective-permute-start | bytes 1572872 | tf_op jit(solution)/shard_map/ppermute | solution.py:49
  5.7 1.5 %collective-permute-start.8 = (bf16[512,512]{1,0:T(8,128)(2,1)}, bf16[512,512]{1,0:T(8,128)(2,1)S(1)}, u32[]{:S(2)}, u32[]{:S(2)}) collective-permute-start(bf16[512,512]{1,0:T(8,128)(2,1)} %get-tuple-element.30.refs_0_), channel_id=1, source_target_pairs={{0,2},{1,3},{2,0},{3,1},{4,6},{5,7},{6,4},{7,5},{8,10},{9,11},{10,... | collective-permute-start | bytes 1572872 | tf_op jit(solution)/shard_map/ppermute | solution.py:53
  7.2 7.1 %collective-permute-done.2.refs_3_ = bf16[512,512]{1,0:T(8,128)(2,1)S(1)} collective-permute-done((bf16[512,512]{1,0:T(8,128)(2,1)}, bf16[512,512]{1,0:T(8,128)(2,1)S(1)}, u32[]{:S(2)}, u32[]{:S(2)}) %collective-permute-start.2) | collective-permute-done | bytes 524320 | tf_op jit(solution)/shard_map/ppermute | solution.py:29
  14.3 2.9 %collective-permute-start.3 = (bf16[512,512]{1,0:T(8,128)(2,1)S(1)}, bf16[512,512]{1,0:T(8,128)(2,1)S(1)}, u32[]{:S(2)}, u32[]{:S(2)}) collective-permute-start(bf16[512,512]{1,0:T(8,128)(2,1)S(1)} %collective-permute-done.2.refs_3_), channel_id=1, source_target_pairs={{0,4},{1,5},{2,6},{3,7},{4,12},{5,13},{6,14},{7,15},{12,8},{13,9},... | collective-permute-start | bytes 1572872 | tf_op jit(solution)/shard_map/ppermute | solution.py:49
  17.2 0.1 collective-permute-start
  17.3 1.1 collective-permute-done
  18.5 1.5 %collective-permute-start.9 = (bf16[512,512]{1,0:T(8,128)(2,1)S(1)}, bf16[512,512]{1,0:T(8,128)(2,1)S(1)}, u32[]{:S(2)}, u32[]{:S(2)}) collective-permute-start(bf16[512,512]{1,0:T(8,128)(2,1)S(1)} %collective-permute-done.2.refs_3_), channel_id=1, source_target_pairs={{0,2},{1,3},{2,0},{3,1},{4,6},{5,7},{6,4},{7,5},{8,10},{9,11},{10,... | collective-permute-start | bytes 1572872 | tf_op jit(solution)/shard_map/ppermute | solution.py:53
  20.0 0.9 broadcast_in_dim.11
  20.8 4.0 %all-to-all-start = ((bf16[16,8,2048]{2,1,0:T(8,128)(2,1)}), bf16[16,8,2048]{2,1,0:T(8,128)(2,1)S(1)}, u32[]{:S(2)}, u32[]{:S(2)}) async-start(bf16[16,8,2048]{2,1,0:T(8,128)(2,1)} %bitcast.29), calls=%async_computation | async-start | bytes 1048576 | tf_op jit(solution)/shard_map/all_to_all | solution.py:304
  24.9 0.6 dynamic_slice.15
  29.4 0.7 fusion.3
  32.7 0.7 stack.103.block_ref
  33.4 2.2 %copy-done = bf16[8,256,1024]{2,1,0:T(8,128)(2,1)S(1)} copy-done((bf16[8,256,1024]{2,1,0:T(8,128)(2,1)S(1)}, bf16[8,256,1024]{2,1,0:T(8,128)(2,1)}, u32[]{:S(2)}) %copy-start) | copy-done | bytes 4194328
  35.5 9.0 %resident.1 = (f32[8,32,128]{2,1,0:T(8,128)S(1)}, f32[32,128]{1,0:T(8,128)S(1)}, f32[32,128]{1,0:T(8,128)S(1)}) custom-call(s32[8]{0:T(128)S(1)} %copy-done.1, bf16[8,32,128]{2,1,0:T(8,128)(2,1)S(1)} %bitcast.51, bf16[8,256,1024]{2,1,0:T(8,128)(2,1)S(1)} %copy-done), custom_call_target="tpu_custom_call" | custom-call | flops 268435456 | bytes 25165824 | tf_op jit(solution)/shard_map/resident/pallas_call | solution.py:316
  44.6 0.7 pad_add_fusion.4.block_ref
  45.2 0.6 pad_add_fusion.3.block_ref
  45.8 0.6 pad_add_fusion.6.block_ref
  46.4 0.0 collective-permute-done.5.refs_1_
  46.4 1.9 %collective-permute-start.6 = (bf16[512,512]{1,0:T(8,128)(2,1)S(1)}, bf16[512,512]{1,0:T(8,128)(2,1)S(1)}, u32[]{:S(2)}, u32[]{:S(2)}) collective-permute-start(bf16[512,512]{1,0:T(8,128)(2,1)S(1)} %collective-permute-done.5.refs_1_), channel_id=1, source_target_pairs={{0,2},{1,3},{2,0},{3,1},{4,6},{5,7},{6,4},{7,5},{8,10},{9,11},{10,... | collective-permute-start | bytes 1572872 | tf_op jit(solution)/shard_map/ppermute | solution.py:53
  48.3 0.0 collective-permute-done.8.refs_2_
  48.3 1.5 %collective-permute-start.7 = (bf16[512,512]{1,0:T(8,128)(2,1)S(1)}, bf16[512,512]{1,0:T(8,128)(2,1)S(1)}, u32[]{:S(2)}, u32[]{:S(2)}) collective-permute-start(bf16[512,512]{1,0:T(8,128)(2,1)S(1)} %collective-permute-done.5.refs_1_), channel_id=1, source_target_pairs={{0,4},{1,5},{2,6},{3,7},{4,12},{5,13},{6,14},{7,15},{12,8},{13,9},... | collective-permute-start | bytes 1572872 | tf_op jit(solution)/shard_map/ppermute | solution.py:49
  49.7 0.0 collective-permute-done.3.refs_4_
  49.7 2.9 %collective-permute-start.10 = (bf16[512,512]{1,0:T(8,128)(2,1)S(1)}, bf16[512,512]{1,0:T(8,128)(2,1)S(1)}, u32[]{:S(2)}, u32[]{:S(2)}) collective-permute-start(bf16[512,512]{1,0:T(8,128)(2,1)S(1)} %collective-permute-done.5.refs_1_), channel_id=1, source_target_pairs={{0,16},{16,0},{1,17},{17,1},{2,18},{18,2},{3,19},{19,3},{4,20},{20... | collective-permute-start | bytes 1572872 | tf_op jit(solution)/shard_map/ppermute | solution.py:57
  52.7 0.7 pad_add_fusion.5.block_ref
  53.3 0.0 collective-permute-done.9.refs_5_
  53.3 0.6 collective-permute-start.4
  53.9 0.0 collective-permute-done.1.other_ref
  53.9 0.1 collective-permute-start.11
  54.0 0.1 pad_add_fusion.1
  54.1 0.0 copy-done.6
  54.1 10.2 %rows_1.1 = (f32[1024,512]{1,0:T(8,128)}, f32[1024,128]{1,0:T(8,128)}) custom-call(s32[6]{0:T(128)} %stack.103.block_ref, bf16[512,8192]{1,0:T(8,128)(2,1)} %own_ref.9, bf16[512,8192]{1,0:T(8,128)(2,1)} %collective-permute-done.1.other_ref, bf16[512,512]{1,0:T(8,128)(2,1)} %get-tuple-element.30.refs_0_, bf16[512,512]{1,0:T(8,128)(2,1)} %copy-done.3, ...), custom_call_target="tpu_custom_call" | custom-call | flops 3221225472 | bytes 31457280 | tf_op jit(solution)/shard_map/rows_1/pallas_call | solution.py:377
  64.3 0.0 collective-permute-done.6.refs_2_
  64.3 1.4 %collective-permute-start.12 = (bf16[512,512]{1,0:T(8,128)(2,1)}, bf16[512,512]{1,0:T(8,128)(2,1)S(1)}, u32[]{:S(2)}, u32[]{:S(2)}) collective-permute-start(bf16[512,512]{1,0:T(8,128)(2,1)} %copy-done.2), channel_id=1, source_target_pairs={{0,4},{1,5},{2,6},{3,7},{4,12},{5,13},{6,14},{7,15},{12,8},{13,9},... | collective-permute-start | bytes 1572872 | tf_op jit(solution)/shard_map/ppermute | solution.py:49
  65.7 0.0 collective-permute-done.7.refs_1_
  65.7 0.8 copy-done.8
  66.5 0.8 copy-done.15
  67.3 8.0 %rows_2a.1 = (f32[1024,512]{1,0:T(8,128)}, f32[1024,128]{1,0:T(8,128)}) custom-call(s32[3]{0:T(128)} %pad_add_fusion.6.block_ref, bf16[512,8192]{1,0:T(8,128)(2,1)} %own_ref.9, bf16[512,8192]{1,0:T(8,128)(2,1)} %collective-permute-done.1.other_ref, f32[1024,512]{1,0:T(8,128)} %get-tuple-element.33.in_total, f32[1024,128]{1,0:T(8,128)} %get-tuple-element.34.in_squares, ...), custom_call_target="tpu_custom_call" | custom-call | flops 1610612736 | bytes 15728640 | tf_op jit(solution)/shard_map/rows_2a/pallas_call | solution.py:377
  75.4 0.0 collective-permute-done.4.refs_2_
  75.4 2.1 %collective-permute-start.15 = (bf16[512,512]{1,0:T(8,128)(2,1)S(1)}, bf16[512,512]{1,0:T(8,128)(2,1)S(1)}, u32[]{:S(2)}, u32[]{:S(2)}) collective-permute-start(bf16[512,512]{1,0:T(8,128)(2,1)S(1)} %collective-permute-done.4.refs_2_), channel_id=1, source_target_pairs={{0,16},{16,0},{1,17},{17,1},{2,18},{18,2},{3,19},{19,3},{4,20},{20... | collective-permute-start | bytes 1572872 | tf_op jit(solution)/shard_map/ppermute | solution.py:57
  77.5 0.5 collective-permute-start.16
  78.0 1.0 collective-permute-start.13
  79.1 0.0 collective-permute-done.11.refs_0_
  79.1 0.8 copy-done.10
  79.9 1.4 %collective-permute-start.14 = (bf16[512,512]{1,0:T(8,128)(2,1)}, bf16[512,512]{1,0:T(8,128)(2,1)S(1)}, u32[]{:S(2)}, u32[]{:S(2)}) collective-permute-start(bf16[512,512]{1,0:T(8,128)(2,1)} %copy-done.8), channel_id=1, source_target_pairs={{0,2},{1,3},{2,0},{3,1},{4,6},{5,7},{6,4},{7,5},{8,10},{9,11},{10,... | collective-permute-start | bytes 1572872 | tf_op jit(solution)/shard_map/ppermute | solution.py:53
  81.3 0.1 broadcast_in_dim.24
  81.4 0.1 broadcast_in_dim.25
  81.5 0.6 pad_add_fusion.2.slot_ref
  82.1 0.2 fusion
  82.3 0.6 copy.16
  83.0 0.8 copy-done.13
  83.8 8.1 %rows_2b.1 = (f32[1024,512]{1,0:T(8,128)}, f32[1024,128]{1,0:T(8,128)}) custom-call(s32[3]{0:T(128)} %pad_add_fusion.5.block_ref, bf16[512,8192]{1,0:T(8,128)(2,1)} %own_ref.9, bf16[512,8192]{1,0:T(8,128)(2,1)} %collective-permute-done.1.other_ref, f32[1024,512]{1,0:T(8,128)} %get-tuple-element.37.in_total, f32[1024,128]{1,0:T(8,128)} %get-tuple-element.38.in_squares, ...), custom_call_target="tpu_custom_call" | custom-call | flops 1610612736 | bytes 15728640 | tf_op jit(solution)/shard_map/rows_2b/pallas_call | solution.py:377
  91.9 7.5 %collective-permute-done.13.refs_0_ = bf16[512,512]{1,0:T(8,128)(2,1)} collective-permute-done((bf16[512,512]{1,0:T(8,128)(2,1)}, bf16[512,512]{1,0:T(8,128)(2,1)}, u32[]{:S(2)}, u32[]{:S(2)}) %collective-permute-start.13) | collective-permute-done | bytes 524320 | tf_op jit(solution)/shard_map/ppermute | solution.py:57
  99.4 0.0 collective-permute-done.14.refs_1_
  99.4 0.8 copy-done.14
  100.2 6.8 %rows_3a.1 = (f32[1024,512]{1,0:T(8,128)}, f32[1024,128]{1,0:T(8,128)}) custom-call(s32[2]{0:T(128)} %pad_add_fusion.4.block_ref, bf16[512,8192]{1,0:T(8,128)(2,1)} %own_ref.9, bf16[512,8192]{1,0:T(8,128)(2,1)} %collective-permute-done.1.other_ref, f32[1024,512]{1,0:T(8,128)} %get-tuple-element.39.in_total, f32[1024,128]{1,0:T(8,128)} %get-tuple-element.40.in_squares, ...), custom_call_target="tpu_custom_call" | custom-call | flops 1073741824 | bytes 10485760 | tf_op jit(solution)/shard_map/rows_3a/pallas_call | solution.py:377
  107.0 0.0 collective-permute-done.15.refs_0_
  107.1 0.8 broadcast_in_dim.26.row_lane_ref
  107.9 0.2 copy-done.12
  108.0 7.3 %rows_3b.1 = bf16[16,3,16,128]{3,2,1,0:T(8,128)(2,1)} custom-call(s32[2]{0:T(128)} %pad_add_fusion.3.block_ref, s32[2,16]{1,0:T(2,128)} %pad_add_fusion.2.slot_ref, bf16[512,8192]{1,0:T(8,128)(2,1)} %own_ref.9, bf16[512,8192]{1,0:T(8,128)(2,1)} %collective-permute-done.1.other_ref, f32[1024,512]{1,0:T(8,128)} %get-tuple-element.43.in_total, ...), custom_call_target="tpu_custom_call" | custom-call | flops 1073741824 | bytes 10485760 | tf_op jit(solution)/shard_map/rows_3b/pallas_call | solution.py:377
  115.3 12.9 %all_to_all.10.got_ref = bf16[16,3,16,128]{3,2,1,0:T(8,128)(2,1)S(1)} all-to-all(bf16[16,3,16,128]{3,2,1,0:T(8,128)(2,1)} %rows_3b.1), channel_id=1, replica_groups=mesh['replica'=2,'section'=16] {'section'}, dimensions={0} | all-to-all | bytes 393216 | tf_op jit(solution)/shard_map/all_to_all | solution.py:425
  128.2 2.3 %combine.1 = bf16[8,4096]{1,0:T(8,128)(2,1)} custom-call(bf16[16,3,16,128]{3,2,1,0:T(8,128)(2,1)S(1)} %all_to_all.10.got_ref, f32[8,32,128]{2,1,0:T(8,128)S(1)} %get-tuple-element.46.res_out_ref, f32[32,128]{1,0:T(8,128)S(1)} %get-tuple-element.47.res_top_ref, f32[32,128]{1,0:T(8,128)S(1)} %get-tuple-element.48.res_sum_ref), custom_call_target="tpu_custom_call" | custom-call | tf_op jit(solution)/shard_map/combine/pallas_call | solution.py:427
  (42 shorter events, 0.1 us)
Async XLA Ops:
  0.0 24.9 %copy-start.17 = (s32[4]{0:T(128)S(1)}, s32[4]{0:T(128)}, u32[]{:S(2)}) copy-start(s32[4]{0:T(128)} %constant.80.clone) | copy-start | bytes 52
  0.0 17.2 %copy-start.19 = (s32[8]{0:T(128)S(1)}, s32[8]{0:T(128)}, u32[]{:S(2)}) copy-start(s32[8]{0:T(128)} %param.10) | copy-start | bytes 100
  0.0 17.2 %copy-start.18 = (s32[8]{0:T(128)S(1)}, s32[8]{0:T(128)}, u32[]{:S(2)}) copy-start(s32[8]{0:T(128)} %param.11) | copy-start | bytes 100
  0.0 20.0 %copy-start.16 = (bf16[8,4096]{1,0:T(8,128)(2,1)S(1)}, bf16[8,4096]{1,0:T(8,128)(2,1)}, u32[]{:S(2)}) copy-start(bf16[8,4096]{1,0:T(8,128)(2,1)} %param.12) | copy-start | bytes 196612
  0.0 53.9 %collective-permute-start.1 = (bf16[512,8192]{1,0:T(8,128)(2,1)}, bf16[512,8192]{1,0:T(8,128)(2,1)}, u32[]{:S(2)}, u32[]{:S(2)}) collective-permute-start(bf16[512,8192]{1,0:T(8,128)(2,1)} %own_ref.9), channel_id=1, source_target_pairs={{0,1},{1,0},{2,3},{3,2},{4,5},{5,4},{6,7},{7,6},{8,9},{9,8},{10,11... | collective-permute-start | bytes 25165832 | tf_op jit(solution)/shard_map/ppermute | solution.py:29
  0.5 32.8 %copy-start.1 = (s32[8]{0:T(128)S(1)}, s32[8]{0:T(128)}, u32[]{:S(2)}) copy-start(s32[8]{0:T(128)} %length_ref.1) | copy-start | bytes 100
  2.6 11.7 %collective-permute-start.2 = (bf16[512,512]{1,0:T(8,128)(2,1)}, bf16[512,512]{1,0:T(8,128)(2,1)S(1)}, u32[]{:S(2)}, u32[]{:S(2)}) collective-permute-start(bf16[512,512]{1,0:T(8,128)(2,1)} %get-tuple-element.27), channel_id=1, source_target_pairs={{0,1},{1,0},{2,3},{3,2},{4,5},{5,4},{6,7},{7,6},{8,9},{9,8},{10,11... | collective-permute-start | bytes 1572872 | tf_op jit(solution)/shard_map/ppermute | solution.py:29
  2.7 43.7 %collective-permute-start.5 = (bf16[512,512]{1,0:T(8,128)(2,1)}, bf16[512,512]{1,0:T(8,128)(2,1)S(1)}, u32[]{:S(2)}, u32[]{:S(2)}) collective-permute-start(bf16[512,512]{1,0:T(8,128)(2,1)} %get-tuple-element.30.refs_0_), channel_id=1, source_target_pairs={{0,4},{1,5},{2,6},{3,7},{4,12},{5,13},{6,14},{7,15},{12,8},{13,9},... | collective-permute-start | bytes 1572872 | tf_op jit(solution)/shard_map/ppermute | solution.py:49
  5.7 42.6 %collective-permute-start.8 = (bf16[512,512]{1,0:T(8,128)(2,1)}, bf16[512,512]{1,0:T(8,128)(2,1)S(1)}, u32[]{:S(2)}, u32[]{:S(2)}) collective-permute-start(bf16[512,512]{1,0:T(8,128)(2,1)} %get-tuple-element.30.refs_0_), channel_id=1, source_target_pairs={{0,2},{1,3},{2,0},{3,1},{4,6},{5,7},{6,4},{7,5},{8,10},{9,11},{10,... | collective-permute-start | bytes 1572872 | tf_op jit(solution)/shard_map/ppermute | solution.py:53
  14.3 30.3 %copy-start.4 = (bf16[512,512]{1,0:T(8,128)(2,1)}, bf16[512,512]{1,0:T(8,128)(2,1)S(1)}, u32[]{:S(2)}) copy-start(bf16[512,512]{1,0:T(8,128)(2,1)S(1)} %collective-permute-done.2.refs_3_) | copy-start | bytes 1572868
  14.3 35.5 %collective-permute-start.3 = (bf16[512,512]{1,0:T(8,128)(2,1)S(1)}, bf16[512,512]{1,0:T(8,128)(2,1)S(1)}, u32[]{:S(2)}, u32[]{:S(2)}) collective-permute-start(bf16[512,512]{1,0:T(8,128)(2,1)S(1)} %collective-permute-done.2.refs_3_), channel_id=1, source_target_pairs={{0,4},{1,5},{2,6},{3,7},{4,12},{5,13},{6,14},{7,15},{12,8},{13,9},... | collective-permute-start | bytes 1572872 | tf_op jit(solution)/shard_map/ppermute | solution.py:49
  17.2 1.2 collective-permute-start
  18.5 34.9 %collective-permute-start.9 = (bf16[512,512]{1,0:T(8,128)(2,1)S(1)}, bf16[512,512]{1,0:T(8,128)(2,1)S(1)}, u32[]{:S(2)}, u32[]{:S(2)}) collective-permute-start(bf16[512,512]{1,0:T(8,128)(2,1)S(1)} %collective-permute-done.2.refs_3_), channel_id=1, source_target_pairs={{0,2},{1,3},{2,0},{3,1},{4,6},{5,7},{6,4},{7,5},{8,10},{9,11},{10,... | collective-permute-start | bytes 1572872 | tf_op jit(solution)/shard_map/ppermute | solution.py:53
  20.8 61.2 %all-to-all-start = ((bf16[16,8,2048]{2,1,0:T(8,128)(2,1)}), bf16[16,8,2048]{2,1,0:T(8,128)(2,1)S(1)}, u32[]{:S(2)}, u32[]{:S(2)}) async-start(bf16[16,8,2048]{2,1,0:T(8,128)(2,1)} %bitcast.29), calls=%async_computation | async-start | bytes 1048576 | tf_op jit(solution)/shard_map/all_to_all | solution.py:304
  33.4 2.2 %copy-start = (bf16[8,256,1024]{2,1,0:T(8,128)(2,1)S(1)}, bf16[8,256,1024]{2,1,0:T(8,128)(2,1)}, u32[]{:S(2)}) copy-start(bf16[8,256,1024]{2,1,0:T(8,128)(2,1)} %cache_ref.1) | copy-start | bytes 12582916
  46.4 7.7 %copy-start.3 = (bf16[512,512]{1,0:T(8,128)(2,1)}, bf16[512,512]{1,0:T(8,128)(2,1)S(1)}, u32[]{:S(2)}) copy-start(bf16[512,512]{1,0:T(8,128)(2,1)S(1)} %collective-permute-done.5.refs_1_) | copy-start | bytes 1572868
  46.4 17.9 %collective-permute-start.6 = (bf16[512,512]{1,0:T(8,128)(2,1)S(1)}, bf16[512,512]{1,0:T(8,128)(2,1)S(1)}, u32[]{:S(2)}, u32[]{:S(2)}) collective-permute-start(bf16[512,512]{1,0:T(8,128)(2,1)S(1)} %collective-permute-done.5.refs_1_), channel_id=1, source_target_pairs={{0,2},{1,3},{2,0},{3,1},{4,6},{5,7},{6,4},{7,5},{8,10},{9,11},{10,... | collective-permute-start | bytes 1572872 | tf_op jit(solution)/shard_map/ppermute | solution.py:53
  48.3 5.8 %copy-start.5 = (bf16[512,512]{1,0:T(8,128)(2,1)}, bf16[512,512]{1,0:T(8,128)(2,1)S(1)}, u32[]{:S(2)}) copy-start(bf16[512,512]{1,0:T(8,128)(2,1)S(1)} %collective-permute-done.8.refs_2_) | copy-start | bytes 1572868
  48.3 17.4 %collective-permute-start.7 = (bf16[512,512]{1,0:T(8,128)(2,1)S(1)}, bf16[512,512]{1,0:T(8,128)(2,1)S(1)}, u32[]{:S(2)}, u32[]{:S(2)}) collective-permute-start(bf16[512,512]{1,0:T(8,128)(2,1)S(1)} %collective-permute-done.5.refs_1_), channel_id=1, source_target_pairs={{0,4},{1,5},{2,6},{3,7},{4,12},{5,13},{6,14},{7,15},{12,8},{13,9},... | collective-permute-start | bytes 1572872 | tf_op jit(solution)/shard_map/ppermute | solution.py:49
  49.7 4.4 %copy-start.2 = (bf16[512,512]{1,0:T(8,128)(2,1)}, bf16[512,512]{1,0:T(8,128)(2,1)S(1)}, u32[]{:S(2)}) copy-start(bf16[512,512]{1,0:T(8,128)(2,1)S(1)} %collective-permute-done.3.refs_4_) | copy-start | bytes 1572868
  49.7 16.0 %collective-permute-start.10 = (bf16[512,512]{1,0:T(8,128)(2,1)S(1)}, bf16[512,512]{1,0:T(8,128)(2,1)S(1)}, u32[]{:S(2)}, u32[]{:S(2)}) collective-permute-start(bf16[512,512]{1,0:T(8,128)(2,1)S(1)} %collective-permute-done.5.refs_1_), channel_id=1, source_target_pairs={{0,16},{16,0},{1,17},{17,1},{2,18},{18,2},{3,19},{19,3},{4,20},{20... | collective-permute-start | bytes 1572872 | tf_op jit(solution)/shard_map/ppermute | solution.py:57
  53.3 0.8 copy-start.6
  53.3 22.0 %collective-permute-start.4 = (bf16[512,512]{1,0:T(8,128)(2,1)S(1)}, bf16[512,512]{1,0:T(8,128)(2,1)S(1)}, u32[]{:S(2)}, u32[]{:S(2)}) collective-permute-start(bf16[512,512]{1,0:T(8,128)(2,1)S(1)} %collective-permute-done.3.refs_4_), channel_id=1, source_target_pairs={{0,2},{1,3},{2,0},{3,1},{4,6},{5,7},{6,4},{7,5},{8,10},{9,11},{10,... | collective-permute-start | bytes 1572872 | tf_op jit(solution)/shard_map/ppermute | solution.py:53
  53.9 25.2 %collective-permute-start.11 = (bf16[512,512]{1,0:T(8,128)(2,1)S(1)}, bf16[512,512]{1,0:T(8,128)(2,1)S(1)}, u32[]{:S(2)}, u32[]{:S(2)}) collective-permute-start(bf16[512,512]{1,0:T(8,128)(2,1)S(1)} %collective-permute-done.3.refs_4_), channel_id=1, source_target_pairs={{0,16},{16,0},{1,17},{17,1},{2,18},{18,2},{3,19},{19,3},{4,20},{20... | collective-permute-start | bytes 1572872 | tf_op jit(solution)/shard_map/ppermute | solution.py:57
  64.3 1.4 %copy-start.7 = (bf16[512,512]{1,0:T(8,128)(2,1)}, bf16[512,512]{1,0:T(8,128)(2,1)S(1)}, u32[]{:S(2)}) copy-start(bf16[512,512]{1,0:T(8,128)(2,1)S(1)} %collective-permute-done.6.refs_2_) | copy-start | bytes 1572868
  64.3 18.6 %collective-permute-start.12 = (bf16[512,512]{1,0:T(8,128)(2,1)}, bf16[512,512]{1,0:T(8,128)(2,1)S(1)}, u32[]{:S(2)}, u32[]{:S(2)}) collective-permute-start(bf16[512,512]{1,0:T(8,128)(2,1)} %copy-done.2), channel_id=1, source_target_pairs={{0,4},{1,5},{2,6},{3,7},{4,12},{5,13},{6,14},{7,15},{12,8},{13,9},... | collective-permute-start | bytes 1572872 | tf_op jit(solution)/shard_map/ppermute | solution.py:49
  65.7 0.8 copy-start.8
  66.5 0.8 copy-start.15
  75.4 7.6 %copy-start.9 = (bf16[512,512]{1,0:T(8,128)(2,1)}, bf16[512,512]{1,0:T(8,128)(2,1)S(1)}, u32[]{:S(2)}) copy-start(bf16[512,512]{1,0:T(8,128)(2,1)S(1)} %collective-permute-done.4.refs_2_) | copy-start | bytes 1572868
  75.4 31.6 %collective-permute-start.15 = (bf16[512,512]{1,0:T(8,128)(2,1)S(1)}, bf16[512,512]{1,0:T(8,128)(2,1)S(1)}, u32[]{:S(2)}, u32[]{:S(2)}) collective-permute-start(bf16[512,512]{1,0:T(8,128)(2,1)S(1)} %collective-permute-done.4.refs_2_), channel_id=1, source_target_pairs={{0,16},{16,0},{1,17},{17,1},{2,18},{18,2},{3,19},{19,3},{4,20},{20... | collective-permute-start | bytes 1572872 | tf_op jit(solution)/shard_map/ppermute | solution.py:57
  77.5 29.5 %collective-permute-start.16 = (bf16[512,512]{1,0:T(8,128)(2,1)S(1)}, bf16[512,512]{1,0:T(8,128)(2,1)S(1)}, u32[]{:S(2)}, u32[]{:S(2)}) collective-permute-start(bf16[512,512]{1,0:T(8,128)(2,1)S(1)} %collective-permute-done.4.refs_2_), channel_id=1, source_target_pairs={{0,4},{1,5},{2,6},{3,7},{4,12},{5,13},{6,14},{7,15},{12,8},{13,9},... | collective-permute-start | bytes 1572872 | tf_op jit(solution)/shard_map/ppermute | solution.py:49
  78.0 21.4 %collective-permute-start.13 = (bf16[512,512]{1,0:T(8,128)(2,1)}, bf16[512,512]{1,0:T(8,128)(2,1)}, u32[]{:S(2)}, u32[]{:S(2)}) collective-permute-start(bf16[512,512]{1,0:T(8,128)(2,1)} %copy-done.7), channel_id=1, source_target_pairs={{0,16},{16,0},{1,17},{17,1},{2,18},{18,2},{3,19},{19,3},{4,20},{20... | collective-permute-start | bytes 1572872 | tf_op jit(solution)/shard_map/ppermute | solution.py:57
  79.1 0.8 copy-start.10
  79.9 19.5 %collective-permute-start.14 = (bf16[512,512]{1,0:T(8,128)(2,1)}, bf16[512,512]{1,0:T(8,128)(2,1)S(1)}, u32[]{:S(2)}, u32[]{:S(2)}) collective-permute-start(bf16[512,512]{1,0:T(8,128)(2,1)} %copy-done.8), channel_id=1, source_target_pairs={{0,2},{1,3},{2,0},{3,1},{4,6},{5,7},{6,4},{7,5},{8,10},{9,11},{10,... | collective-permute-start | bytes 1572872 | tf_op jit(solution)/shard_map/ppermute | solution.py:53
  83.0 0.8 copy-start.13
  99.4 0.8 copy-start.14
  107.0 0.9 copy-start.11
  107.0 1.0 copy-start.12

commit v5 on v4

v5 whole, which is shorter than its diff:
```python
import functools
import math

import jax
import jax.numpy as jnp
import numpy as np
from jax import lax
from jax.experimental import pallas as pl
from jax.experimental.pallas import tpu as pltpu
from jax.sharding import PartitionSpec as P

HD = 128
KVH = 4
QH = 32
IMG_TOK = 64
GROUP = QH // KVH
HALF_KVH = KVH // 2
HALF_QH = QH // 2
SCALE = 1.0 / math.sqrt(HD)
EPS = 1e-05

LANES = 64
N_KINDS = 7

masked_score = -1e30


def swap_core(x):
    n = lax.axis_size("section")
    return lax.ppermute(x, "section", [(i, i ^ 1) for i in range(n)])


def gather_plain(chunk):
    n = lax.axis_size("section")
    rows = chunk.shape[0]
    groups = [list(range(core, n, 2)) for core in range(2)]
    whole = lax.all_gather(chunk, "section", axis=0, tiled=True, axis_index_groups=groups)
    return [(chip, whole, chip * rows) for chip in range(n // 2)]


RING = [0, 1, 3, 2]


def along_ring(x):
    perm = []
    for rep, way in ((0, 1), (1, -1)):
        for p in range(4):
            for low in range(4):
                perm.append((rep * 16 + RING[p] * 4 + low, rep * 16 + RING[(p + way) % 4] * 4 + low))
    return lax.ppermute(x, ("replica", "section"), perm)


def across_y(x):
    return lax.ppermute(x, "section", [(i, i ^ 2) for i in range(16)])


def across_replica(x):
    return lax.ppermute(x, "replica", [(0, 1), (1, 0)])


STEPS = (("own", "behind", "own_y"), ("ahead", "opposite", "behind_y"), ("ahead_y", "opposite_y"))


def block_table():
    table = []
    for rep in range(2):
        for section in range(16):
            z, y, core = section // 4, section // 2 % 2, section % 2
            way = 1 - 2 * rep
            place = RING.index(z)
            ring = {"own": place, "behind": place - way, "ahead": place + way, "opposite": place + 2}

            def blocks(step, other):
                out = []
                for name in STEPS[step]:
                    chip = RING[ring[name.removesuffix("_y")] % 4] * 2 + (1 - y if name.endswith("_y") else y)
                    out.append(chip * 2 + (core ^ other))
                return out

            table.append(blocks(0, 0) + blocks(0, 1) + blocks(1, 0) + blocks(1, 1) + blocks(2, 0) + blocks(2, 1))
    return np.array(table, np.int32)


def square_kernel(states_ref, out_ref):
    total = None
    for i in range(0, states_ref.shape[1], HD):
        values = states_ref[:, i : i + HD].astype(jnp.float32)
        values = values * values
        total = values if total is None else total + values
    out_ref[...] = total


def split_kernel(core_ref, keep_in, give_in, keep_ref, give_ref):
    keep_ref[...] = keep_in[...]
    give_ref[...] = give_in[...]


def accumulate(layout, token_refs, piece_refs, weight, total, sems, carry_ref=None, carry=None):
    step = pl.program_id(0)
    depth = token_refs[0].shape[1]
    copies = [
        pltpu.make_async_copy(
            piece_refs[which].at[pl.ds(start, depth)], weight.at[pl.ds(i * depth, depth)], sems.at[i]
        )
        for i, (which, start) in enumerate(layout)
    ]
    carried = []
    if carry_ref is not None:
        carried = [pltpu.make_async_copy(carry_ref, carry, sems.at[len(layout)])]

    @pl.when(step == 0)
    def _():
        for copy in copies + carried:
            copy.start()

    for i in range(0, len(copies), 2):

        @pl.when(step == i // 2)
        def _():
            copies[i].wait()
            copies[i + 1].wait()

    states = jnp.concatenate(
        [
            jnp.concatenate([token_refs[0][...], token_refs[1][...]], axis=1),
            jnp.concatenate([token_refs[2][...], token_refs[3][...]], axis=1),
        ],
        axis=0,
    )
    block = weight[pl.ds(pl.multiple_of(step * 2 * depth, 2 * depth), 2 * depth), :]
    product = jnp.dot(states, block, preferred_element_type=jnp.float32)

    @pl.when(step == 0)
    def _():
        total[...] = product

    @pl.when(step > 0)
    def _():
        total[...] += product

    if carry_ref is not None:

        @pl.when(step == pl.num_programs(0) - 1)
        def _():
            carried[0].wait()
            total[...] += carry[...]


def first_kernel(layout, block_ref, *refs):
    total, weight, sems = refs[-3:]
    accumulate(layout, refs[:4], refs[4:-3], weight, total, sems)


def next_kernel(layout, block_ref, *refs):
    total, weight, carry, sems = refs[-4:]
    accumulate(layout, refs[:4], refs[5:-4], weight, total, sems, refs[4], carry)


def parts_of(values, count):
    out = []
    for _ in range(count):
        part = values.astype(jnp.bfloat16).astype(jnp.float32)
        out.append(part)
        values = values - part
    return out


def last_kernel(layout, width, block_ref, slot_ref, *refs):
    query_ref, row_lane_ref, own_squares, other_squares = refs[5:9]
    slots_ref, weight, carry, total, summed, stats, sems = refs[-7:]
    images = query_ref.shape[1] // GROUP

    @pl.when(pl.program_id(0) == 0)
    def _():
        slots_ref[...] = jnp.zeros_like(slots_ref)

    accumulate(layout, refs[:4], refs[9:-7], weight, total, sems, refs[4], carry)

    @pl.when(pl.program_id(0) == pl.num_programs(0) - 1)
    def _():
        tokens = total.shape[0]
        queries = query_ref.shape[1]
        squares = jnp.concatenate([own_squares[...], other_squares[...]], axis=0)
        factor = lax.rsqrt(jnp.sum(squares, axis=1, keepdims=True) / width + EPS)
        image_of_query = lax.broadcasted_iota(jnp.int32, (queries, tokens), 0) // GROUP
        image_of_token = lax.broadcasted_iota(jnp.int32, (queries, tokens), 1) // IMG_TOK
        live = image_of_query == image_of_token
        lane = lax.broadcasted_iota(jnp.int32, (queries, HD), 1)
        first_lane = row_lane_ref[:, :1]
        for head in range(HALF_KVH):
            part = slice(head * GROUP, (head + 1) * GROUP)
            keys = (total[:, head * HD : (head + 1) * HD] * factor).astype(jnp.bfloat16)
            at = (HALF_KVH + head) * HD
            values = (total[:, at : at + HD] * factor).astype(jnp.bfloat16)
            scores = (
                lax.dot_general(
                    query_ref[head], keys, (((1,), (1,)), ((), ())), preferred_element_type=jnp.float32
                )
                * SCALE
            )
            scores = jnp.where(live, scores, masked_score)
            top = jnp.max(scores, axis=1, keepdims=True)
            weights = jnp.where(live, jnp.exp(scores - top), 0.0)
            total_weight = jnp.sum(weights, axis=1, keepdims=True)
            out = jnp.dot(weights.astype(jnp.bfloat16), values, preferred_element_type=jnp.float32)
            summed[:, part, :] = out.reshape(images, GROUP, HD)
            kinds = parts_of(top, 3) + parts_of(total_weight, 3) + [jnp.ones_like(top)]
            tile = jnp.zeros((queries, HD), jnp.float32)
            for kind, column in enumerate(kinds):
                tile = jnp.where(lane == first_lane + kind * 8, column, tile)
            stats[:, part, :] = tile.reshape(images, GROUP, HD)
        for image in range(images):
            owner, which = slot_ref[0, image], slot_ref[1, image]
            slots_ref[owner, which] = summed[image].astype(jnp.bfloat16)
            slots_ref[owner, 2] = slots_ref[owner, 2] + stats[image].astype(jnp.bfloat16)


def resident_kernel(length_ref, query_ref, cache_ref, out_ref, top_ref, sum_ref):
    step = pl.program_id(0)
    rows, context = cache_ref.shape[:2]
    place = lax.broadcasted_iota(jnp.int32, (QH, context), 1)
    lane = lax.broadcasted_iota(jnp.int32, (QH, HD), 1)

    @pl.when(step == 0)
    def _():
        top_ref[...] = jnp.zeros_like(top_ref)
        sum_ref[...] = jnp.zeros_like(sum_ref)

    parts = [slice(head * GROUP, (head + 1) * GROUP) for head in range(KVH)]
    scores = [
        jnp.concatenate(
            [
                lax.dot_general(
                    query_ref[row, part, :],
                    cache_ref[row, :, head * HD : (head + 1) * HD],
                    (((1,), (1,)), ((), ())),
                    preferred_element_type=jnp.float32,
                )
                for head, part in enumerate(parts)
            ],
            axis=0,
        )
        for row in range(rows)
    ]
    for row in range(rows):
        live = place < length_ref[step * rows + row]
        score = jnp.where(live, scores[row] * SCALE, masked_score)
        top = jnp.max(score, axis=1, keepdims=True)
        weights = jnp.where(live, jnp.exp(score - top), 0.0)
        mine = lane == step * rows + row
        top_ref[...] = jnp.where(mine, top, top_ref[...])
        sum_ref[...] = jnp.where(mine, jnp.sum(weights, axis=1, keepdims=True), sum_ref[...])
        weights = weights.astype(jnp.bfloat16)
        for head, part in enumerate(parts):
            at = (KVH + head) * HD
            out_ref[row, part, :] = jnp.dot(
                weights[part], cache_ref[row, :, at : at + HD], preferred_element_type=jnp.float32
            )


def combine_kernel(got_ref, res_out_ref, res_top_ref, res_sum_ref, out_ref, acc):
    chips = got_ref.shape[0] // 2
    rows = res_out_ref.shape[0]
    lane = lax.broadcasted_iota(jnp.int32, (HALF_QH, HD), 1)
    head_lane = (lane % LANES) < 8

    def moved(tile, by):
        return pltpu.roll(tile, HD - by, 1)

    for core in range(2):
        part = slice(core * HALF_QH, (core + 1) * HALF_QH)
        tops, sums, here = [], [], []
        for chip in range(chips):
            tile = got_ref[chip * 2 + core, 2].astype(jnp.float32)
            present = (moved(tile, 48) > 0.5) & head_lane
            tops.append(jnp.where(present, tile + moved(tile, 8) + moved(tile, 16), masked_score))
            sums.append(moved(tile, 24) + moved(tile, 32) + moved(tile, 40))
            here.append(present)
        row_top = functools.reduce(jnp.maximum, tops)
        row_top = jnp.maximum(row_top, pltpu.roll(row_top, LANES, 1))
        res_top = jnp.where(lane < 8, res_top_ref[part, :], masked_score)
        res_top = jnp.maximum(res_top, pltpu.roll(res_top, LANES, 1))
        row_top = jnp.maximum(row_top, res_top)
        weights = [jnp.where(a, jnp.exp(t - row_top), 0.0) for a, t in zip(here, tops)]
        joined = sum(w * s for w, s in zip(weights, sums))
        res_weight = jnp.exp(res_top - row_top)
        denominator = joined + pltpu.roll(joined, LANES, 1) + res_weight * res_sum_ref[part, :]
        scale = jnp.where(lane < 8, 1.0 / denominator, 0.0)
        scale = scale + pltpu.roll(scale, LANES, 1)
        res_share = res_weight * scale
        weights = [w * scale for w in weights]
        for row in range(rows):
            value = res_out_ref[row, part, :] * res_share[:, row : row + 1]
            for chip in range(chips):
                for which in range(2):
                    at = which * LANES + row
                    value += weights[chip][:, at : at + 1] * got_ref[chip * 2 + core, which].astype(jnp.float32)
            acc[row, part, :] = value
    for head in range(QH):
        out_ref[:, head * HD : (head + 1) * HD] = acc[:, head, :].astype(jnp.bfloat16)


def whole(shape):
    return pl.BlockSpec(shape, lambda i, *_: (0,) * len(shape))


def per_device(prompt_states, kv_weight, image_owner, image_row, queries, cache, context_length):
    n = lax.axis_size("section")
    section = lax.axis_index("section")
    core = section % 2
    tokens, width = prompt_states.shape
    rows_dev, kv_width = kv_weight.shape
    columns_dev = kv_width // 2
    images = image_owner.shape[0]
    decode_rows = queries.shape[0]
    context = cache.shape[1]
    n_queries = 2 * images * GROUP

    cut = columns_dev // 2
    keep, give = pl.pallas_call(
        split_kernel,
        grid_spec=pltpu.PrefetchScalarGridSpec(
            num_scalar_prefetch=1,
            grid=(2,),
            in_specs=[
                pl.BlockSpec((rows_dev, cut), lambda i, core_ref: (0, 2 * i + core_ref[0])),
                pl.BlockSpec((rows_dev, cut), lambda i, core_ref: (0, 2 * i + 1 - core_ref[0])),
            ],
            out_specs=[pl.BlockSpec((rows_dev, cut), lambda i, core_ref: (0, i))] * 2,
        ),
        out_shape=[jax.ShapeDtypeStruct((rows_dev, columns_dev), jnp.bfloat16)] * 2,
        cost_estimate=pl.CostEstimate(flops=0, bytes_accessed=2 * 2**20, transcendentals=0),
        name="split",
    )(core.reshape(1), kv_weight, kv_weight)
    taken = swap_core(give)
    squares = pl.pallas_call(
        square_kernel,
        grid=(8,),
        in_specs=[pl.BlockSpec((tokens // 8, width), lambda i: (i, 0))],
        out_specs=pl.BlockSpec((tokens // 8, HD), lambda i: (i, 0)),
        out_shape=jax.ShapeDtypeStruct((tokens, HD), jnp.float32),
        cost_estimate=pl.CostEstimate(flops=2 * tokens * width, bytes_accessed=16 * 2**20, transcendentals=0),
        compiler_params=pltpu.CompilerParams(vmem_limit_bytes=56 * 2**20),
        name="squares",
    )(prompt_states)
    swapped_states, tied = lax.optimization_barrier((prompt_states, taken))
    other = swap_core(swapped_states)
    other_squares = swap_core(squares)

    owner_and_row = jnp.stack([image_owner, image_row])
    chip_images = jnp.concatenate([owner_and_row, swap_core(owner_and_row)], axis=1)
    send_q = queries.reshape(decode_rows, 2, HALF_QH * HD).transpose(1, 0, 2)
    send_q = jnp.broadcast_to(send_q[None], (n // 2, 2, decode_rows, HALF_QH * HD)).reshape(
        n, decode_rows, HALF_QH * HD
    )
    all_q = lax.all_to_all(send_q, "section", split_axis=0, concat_axis=0, tiled=True)
    all_q = all_q.reshape(n * decode_rows, HALF_QH * HD)
    target = chip_images[0] * decode_rows + chip_images[1]
    pick = (target[:, None] == jnp.arange(n * decode_rows)[None, :]).astype(jnp.bfloat16)
    image_q = jnp.dot(pick, all_q, preferred_element_type=jnp.float32).astype(jnp.bfloat16)
    image_q = image_q.reshape(2 * images, HALF_KVH, GROUP, HD).transpose(1, 0, 2, 3)
    image_q = image_q.reshape(HALF_KVH, n_queries, HD)

    which = jnp.concatenate([jnp.full((images,), core), jnp.full((images,), 1 - core)]).astype(jnp.int32)
    slot = jnp.stack([chip_images[0], which])
    row_lane = jnp.broadcast_to(jnp.repeat(which * LANES + chip_images[1], GROUP)[:, None], (n_queries, HD))

    def resident(length):
        step_rows = 2
        return pl.pallas_call(
            resident_kernel,
            grid_spec=pltpu.PrefetchScalarGridSpec(
                num_scalar_prefetch=1,
                grid=(decode_rows // step_rows,),
                in_specs=[
                    pl.BlockSpec((step_rows, QH, HD), lambda i, *_: (i, 0, 0)),
                    pl.BlockSpec((step_rows, context, kv_width), lambda i, *_: (i, 0, 0)),
                ],
                out_specs=[
                    pl.BlockSpec((step_rows, QH, HD), lambda i, *_: (i, 0, 0)),
                    whole((QH, HD)),
                    whole((QH, HD)),
                ],
            ),
            out_shape=[
                jax.ShapeDtypeStruct((decode_rows, QH, HD), jnp.float32),
                jax.ShapeDtypeStruct((QH, HD), jnp.float32),
                jax.ShapeDtypeStruct((QH, HD), jnp.float32),
            ],
            compiler_params=pltpu.CompilerParams(vmem_limit_bytes=56 * 2**20),
            cost_estimate=pl.CostEstimate(flops=2**28, bytes_accessed=20 * 2**20, transcendentals=0),
            name="resident",
        )(length, queries.reshape(decode_rows, QH, HD), cache)

    def product(blocks, pieces, carry, name, last=False):
        arrays, layout = [], []
        for array, start in pieces:
            at = [i for i, known in enumerate(arrays) if known is array]
            if not at:
                arrays.append(array)
                at = [len(arrays) - 1]
            layout.append((at[0], start))
        steps = len(pieces) // 2
        first = pl.BlockSpec((tokens, rows_dev), lambda i, block_ref, *_: (0, block_ref[2 * i]))
        second = pl.BlockSpec((tokens, rows_dev), lambda i, block_ref, *_: (0, block_ref[2 * i + 1]))
        in_hbm = pl.BlockSpec(memory_space=pltpu.HBM)
        in_specs = [first, second, first, second]
        inputs = [prompt_states, prompt_states, other, other]
        scalars = [blocks]
        scratch = [pltpu.VMEM((len(pieces) * rows_dev, columns_dev), jnp.bfloat16)]
        total = (2 * tokens, columns_dev)
        body = functools.partial(first_kernel, layout)
        if carry is not None:
            body = functools.partial(next_kernel, layout)
            in_specs = in_specs + [pl.BlockSpec(memory_space=pl.ANY)]
            inputs = inputs + [carry]
            scratch = scratch + [pltpu.VMEM(total, jnp.float32)]
        out_specs, out_shape = whole(total), jax.ShapeDtypeStruct(total, jnp.float32)
        if last:
            body = functools.partial(last_kernel, layout, width)
            scalars = scalars + [slot]
            in_specs = in_specs + [
                whole((HALF_KVH, n_queries, HD)),
                whole((n_queries, HD)),
                whole((tokens, HD)),
                whole((tokens, HD)),
            ]
            inputs = inputs + [image_q, row_lane, squares, other_squares]
            out_specs = whole((n, 3, HALF_QH, HD))
            out_shape = jax.ShapeDtypeStruct((n, 3, HALF_QH, HD), jnp.bfloat16)
            scratch = scratch + [
                pltpu.VMEM(total, jnp.float32),
                pltpu.VMEM((2 * images, HALF_QH, HD), jnp.float32),
                pltpu.VMEM((2 * images, HALF_QH, HD), jnp.float32),
            ]
        return pl.pallas_call(
            body,
            grid_spec=pltpu.PrefetchScalarGridSpec(
                num_scalar_prefetch=len(scalars),
                grid=(steps,),
                in_specs=in_specs + [in_hbm] * len(arrays),
                out_specs=out_specs,
                scratch_shapes=scratch + [pltpu.SemaphoreType.DMA((len(pieces) + 1,))],
            ),
            out_shape=out_shape,
            compiler_params=pltpu.CompilerParams(vmem_limit_bytes=56 * 2**20),
            cost_estimate=pl.CostEstimate(
                flops=2 * 2 * tokens * 2 * rows_dev * columns_dev * steps,
                bytes_accessed=10 * steps * 2**20,
                transcendentals=0,
            ),
            name=name,
        )(*scalars, *inputs, *arrays)

    if n == 16 and lax.axis_size("replica") == 2:
        blocks = jnp.array(block_table())[lax.axis_index("replica") * 16 + section]

        def starts(*arrays):
            return [(array, 0) for array in arrays]

        a1 = (keep, along_ring(keep), across_y(keep))
        b1 = (taken, along_ring(taken), across_y(taken))
        a2 = (across_replica(a1[1]), along_ring(a1[1]), across_y(a1[1]))
        length, tied = lax.optimization_barrier((context_length, a1[1]))
        res_out, res_top, res_sum = resident(length)
        b2 = (across_replica(b1[1]), along_ring(b1[1]), across_y(b1[1]))
        total = product(blocks[:6], starts(*a1, *b1), None, "rows_1")
        a_behind_y, a_opposite, total = lax.optimization_barrier((a2[2], a2[1], total))
        a3 = (across_replica(a_behind_y), across_y(a_opposite))
        b_behind_y, res_out = lax.optimization_barrier((b2[2], res_out))
        b3 = (across_replica(b_behind_y), along_ring(b_behind_y))
        total = product(blocks[6:12], starts(*a2, *b2), total, "rows_2")
        total = product(blocks[12:14], starts(*a3), total, "rows_3a")
        slots = product(blocks[14:], starts(*b3), total, "rows_3b", last=True)
    else:
        res_out, res_top, res_sum = resident(context_length)
        a = gather_plain(keep)
        b = gather_plain(taken)
        chips = jnp.array([chip for chip, _, _ in a], jnp.int32)
        total = product(chips * 2 + core, [piece[1:] for piece in a], None, "rows_a")
        slots = product(chips * 2 + 1 - core, [piece[1:] for piece in b], total, "rows_b", last=True)
    got = lax.all_to_all(slots, "section", split_axis=0, concat_axis=0, tiled=True)

    return pl.pallas_call(
        combine_kernel,
        grid=(1,),
        in_specs=[
            whole((n, 3, HALF_QH, HD)),
            whole((decode_rows, QH, HD)),
            whole((QH, HD)),
            whole((QH, HD)),
        ],
        out_specs=whole((decode_rows, QH * HD)),
        scratch_shapes=[pltpu.VMEM((decode_rows, QH, HD), jnp.float32)],
        out_shape=jax.ShapeDtypeStruct((decode_rows, QH * HD), jnp.bfloat16),
        compiler_params=pltpu.CompilerParams(vmem_limit_bytes=32 * 2**20),
        name="combine",
    )(got, res_out, res_top, res_sum)


def solution(mesh):
    placed = (
        P(("replica", "section"), None),
        P("section", None),
        P(("replica", "section")),
        P(("replica", "section")),
        P(("replica", "section"), None),
        P(("replica", "section"), None, None),
        P(("replica", "section")),
    )
    return jax.shard_map(
        per_device,
        mesh=mesh,
        in_specs=placed,
        out_specs=P(("replica", "section"), None),
        check_vma=False,
    )
```

time: 131 us -> 119 us (0.908)
  between operations: 6.76 us -> 0.23 us
  waiting for transfers between devices: 15.7 us -> 20.5 us
  Pallas kernels: 53.8 us -> 49.2 us
  local copies, waits for them, and re-layouts: 10.9 us -> 7.61 us
  starting transfers between devices: 27.1 us -> 25.2 us
  other arithmetic: 3.15 us -> 1.33 us
    ppermute x5, waiting for transfers between devices: 0.01 us -> 11.3 us  [along_ring(): return lax.ppermute(x, ('replica', 'section'), perm)]
    pallas_call x5 -> x4, Pallas kernels: 40.4 us -> 32.1 us  [product(): pl.pallas_call(body, grid_spec=pltpu.PrefetchScalarGridSpec(num_scalar_pr...]
    ppermute x4, waiting for transfers between devices: 7.47 us -> 0.01 us  [across_replica(): return lax.ppermute(x, 'replica', [(0, 1), (1, 0)])]
    ppermute x5, waiting for transfers between devices: 0.01 us -> 7.34 us  [across_y(): return lax.ppermute(x, 'section', [(i, i ^ 2) for i in range(16)])]
    ppermute x3 -> x4, waiting for transfers between devices: 8.19 us -> 1.76 us  [swap_core(): return lax.ppermute(x, 'section', [(i, i ^ 1) for i in range(n)])]
    unnamed x42 -> x34, local copies, waits for them, and re-layouts: 6.45 us -> 2.31 us
    pallas_call x1 -> x2, Pallas kernels: 9.01 us -> 12.7 us  [the longest x1 7.34 us: per_device(): pl.pallas_call(square_kernel, grid=(8,), in_specs=[pl.BlockSpec((tokens /...]
    another operation x4 -> x0, other arithmetic: 2.47 us -> none  [product(): scalars = [jnp.stack(blocks)]]
  transfers between devices with their start and end apart: 18 -> 19, of which waited for: 3 -> 3; matrix products, arithmetic and copies ran while one was open for 5% -> 6% of each run, Pallas kernels for 34% -> 32%
where the time goes in v5:
time: 119 us; the launch traced here: 118 us
  Pallas kernels  49.2 us (41%)
  starting transfers between devices  25.2 us (21%)
  waiting for transfers between devices  20.5 us (17%)
  blocking collectives  13.5 us (11%)
  local copies, waits for them, and re-layouts  7.61 us (6%)
  other arithmetic  1.33 us (1%)
    pallas_call x4, Pallas kernels, product(): pl.pallas_call(body, grid_spec=pltpu.PrefetchScalarGridSpec(num_scalar_pr...  32.1 us
    all_to_all x1, blocking collectives, per_device(): lax.all_to_all(slots, 'section', split_axis=0, concat_axis=0, tiled=True)  13.5 us
    ppermute x5, waiting for transfers between devices, along_ring(): return lax.ppermute(x, ('replica', 'section'), perm)  11.3 us
    ppermute x5, starting transfers between devices, along_ring(): return lax.ppermute(x, ('replica', 'section'), perm)  11 us
    pallas_call x1, Pallas kernels, per_device(): pl.pallas_call(square_kernel, grid=(8,), in_specs=[pl.BlockSpec((tokens /...  7.34 us
    ppermute x5, waiting for transfers between devices, across_y(): return lax.ppermute(x, 'section', [(i, i ^ 2) for i in range(16)])  7.34 us
    pallas_call x1, Pallas kernels, resident(): pl.pallas_call(resident_kernel, grid_spec=pltpu.PrefetchScalarGridSpec(nu...  5.37 us
    ppermute x5, starting transfers between devices, across_y(): return lax.ppermute(x, 'section', [(i, i ^ 2) for i in range(16)])  5.3 us
  transfers between devices with their start and end apart: 19, of which 3 were waited for; matrix products, arithmetic and copies ran while one was open for 6% of the time, Pallas kernels for 32%

profile of v5, /device:TPU:0, one launch (start us, length us, event | category | flops | bytes accessed | tf_op | source)
XLA Modules:
  0.0 117.8 jit_solution(10809535988407448356)
XLA Ops:
  0.0 2.1 %split.1 = (bf16[512,512]{1,0:T(8,128)(2,1)}, bf16[512,512]{1,0:T(8,128)(2,1)}) custom-call(s32[1]{0:T(128)} %bitcast.4.core_ref, bf16[512,1024]{1,0:T(8,128)(2,1)} %give_in.1, bf16[512,1024]{1,0:T(8,128)(2,1)} %give_in.1), custom_call_target="tpu_custom_call" | custom-call | bytes 2097152 | tf_op jit(solution)/shard_map/split/pallas_call | solution.py:320
  2.1 0.5 collective-permute-start.1
  2.5 1.7 %collective-permute-done.1.refs_7_ = bf16[512,512]{1,0:T(8,128)(2,1)S(1)} collective-permute-done((bf16[512,512]{1,0:T(8,128)(2,1)}, bf16[512,512]{1,0:T(8,128)(2,1)S(1)}, u32[]{:S(2)}, u32[]{:S(2)}) %collective-permute-start.1) | collective-permute-done | bytes 524320 | tf_op jit(solution)/shard_map/ppermute | solution.py:30
  4.3 0.4 collective-permute-start.2
  4.6 2.7 %collective-permute-start.3 = (bf16[512,512]{1,0:T(8,128)(2,1)}, bf16[512,512]{1,0:T(8,128)(2,1)S(1)}, u32[]{:S(2)}, u32[]{:S(2)}) collective-permute-start(bf16[512,512]{1,0:T(8,128)(2,1)} %get-tuple-element.19.refs_4_), channel_id=1, source_target_pairs={{0,4},{1,5},{2,6},{3,7},{4,12},{5,13},{6,14},{7,15},{12,8},{13,9},... | collective-permute-start | bytes 1572872 | tf_op jit(solution)/shard_map/ppermute | solution.py:50
  7.4 1.5 %collective-permute-start.6 = (bf16[512,512]{1,0:T(8,128)(2,1)}, bf16[512,512]{1,0:T(8,128)(2,1)S(1)}, u32[]{:S(2)}, u32[]{:S(2)}) collective-permute-start(bf16[512,512]{1,0:T(8,128)(2,1)} %get-tuple-element.19.refs_4_), channel_id=1, source_target_pairs={{0,2},{1,3},{2,0},{3,1},{4,6},{5,7},{6,4},{7,5},{8,10},{9,11},{10,... | collective-permute-start | bytes 1572872 | tf_op jit(solution)/shard_map/ppermute | solution.py:54
  8.9 0.7 pad_add_fusion
  9.6 0.0 collective-permute-start
  9.6 1.7 %broadcast_in_dim.11 = bf16[8,2,8,2048]{3,2,1,0:T(8,128)(2,1)} broadcast(bf16[2,8,2048]{2,1,0:T(8,128)(2,1)} %bitcast.40), dimensions={1,2,3} | broadcast | bytes 589824 | tf_op jit(solution)/shard_map/broadcast_in_dim | solution.py:353
  11.2 4.1 %all-to-all-start = ((bf16[16,8,2048]{2,1,0:T(8,128)(2,1)}), bf16[16,8,2048]{2,1,0:T(8,128)(2,1)S(1)}, u32[]{:S(2)}, u32[]{:S(2)}) async-start(bf16[16,8,2048]{2,1,0:T(8,128)(2,1)} %bitcast.12), calls=%async_computation | async-start | bytes 1048576 | tf_op jit(solution)/shard_map/all_to_all | solution.py:356
  15.3 1.5 %copy.15 = bf16[1,8,32,128]{3,2,1,0:T(8,128)(2,1)} copy(bf16[1,8,32,128]{3,1,2,0:T(8,128)(2,1)} %bitcast.41) | data formatting | bytes 131072
  16.8 7.3 %squares.1.refs_7_ = f32[512,128]{1,0:T(8,128)} custom-call(bf16[512,8192]{1,0:T(8,128)(2,1)} %refs_1_.7), custom_call_target="tpu_custom_call" | custom-call | flops 8388608 | bytes 16777216 | tf_op jit(solution)/shard_map/squares/pallas_call | solution.py:336
  24.2 0.7 constant_dynamic-slice_fusion
  24.9 2.0 %collective-permute-start.7 = (bf16[512,512]{1,0:T(8,128)(2,1)S(1)}, bf16[512,512]{1,0:T(8,128)(2,1)S(1)}, u32[]{:S(2)}, u32[]{:S(2)}) collective-permute-start(bf16[512,512]{1,0:T(8,128)(2,1)S(1)} %collective-permute-done.1.refs_7_), channel_id=1, source_target_pairs={{0,4},{1,5},{2,6},{3,7},{4,12},{5,13},{6,14},{7,15},{12,8},{13,9},... | collective-permute-start | bytes 1572872 | tf_op jit(solution)/shard_map/ppermute | solution.py:50
  26.8 0.0 collective-permute-done
  26.8 0.0 copy-done.5
  26.8 1.4 %collective-permute-start.8 = (bf16[512,512]{1,0:T(8,128)(2,1)S(1)}, bf16[512,512]{1,0:T(8,128)(2,1)S(1)}, u32[]{:S(2)}, u32[]{:S(2)}) collective-permute-start(bf16[512,512]{1,0:T(8,128)(2,1)S(1)} %collective-permute-done.1.refs_7_), channel_id=1, source_target_pairs={{0,2},{1,3},{2,0},{3,1},{4,6},{5,7},{6,4},{7,5},{8,10},{9,11},{10,... | collective-permute-start | bytes 1572872 | tf_op jit(solution)/shard_map/ppermute | solution.py:54
  28.2 0.0 collective-permute-done.3.refs_5_
  28.2 0.6 collective-permute-start.4
  28.9 0.6 slice_bitcast_fusion
  29.5 0.7 slice_bitcast_fusion.2
  30.1 0.0 copy-done.15
  30.1 0.1 pad_add_fusion.1
  30.2 0.0 collective-permute-done.6.refs_6_
  30.2 2.3 %collective-permute-start.5 = (bf16[512,512]{1,0:T(8,128)(2,1)S(1)}, bf16[512,512]{1,0:T(8,128)(2,1)}, u32[]{:S(2)}, u32[]{:S(2)}) collective-permute-start(bf16[512,512]{1,0:T(8,128)(2,1)S(1)} %collective-permute-done.3.refs_5_), channel_id=1, source_target_pairs={{0,4},{1,5},{2,6},{3,7},{4,12},{5,13},{6,14},{7,15},{12,8},{13,9},... | collective-permute-start | bytes 1572872 | tf_op jit(solution)/shard_map/ppermute | solution.py:50
  32.5 11.3 %collective-permute-done.7.refs_8_ = bf16[512,512]{1,0:T(8,128)(2,1)S(1)} collective-permute-done((bf16[512,512]{1,0:T(8,128)(2,1)S(1)}, bf16[512,512]{1,0:T(8,128)(2,1)S(1)}, u32[]{:S(2)}, u32[]{:S(2)}) %collective-permute-start.7) | collective-permute-done | bytes 524320 | tf_op jit(solution)/shard_map/ppermute | solution.py:50
  43.9 0.0 collective-permute-start.9
  43.9 0.0 collective-permute-done.8.refs_9_
  43.9 2.0 %collective-permute-start.10 = (bf16[512,512]{1,0:T(8,128)(2,1)S(1)}, bf16[512,512]{1,0:T(8,128)(2,1)}, u32[]{:S(2)}, u32[]{:S(2)}) collective-permute-start(bf16[512,512]{1,0:T(8,128)(2,1)S(1)} %collective-permute-done.7.refs_8_), channel_id=1, source_target_pairs={{0,16},{16,0},{1,17},{17,1},{2,18},{18,2},{3,19},{19,3},{4,20},{20... | collective-permute-start | bytes 1572872 | tf_op jit(solution)/shard_map/ppermute | solution.py:58
  45.9 7.3 %collective-permute-done.4.refs_7_ = bf16[512,512]{1,0:T(8,128)(2,1)S(1)} collective-permute-done((bf16[512,512]{1,0:T(8,128)(2,1)S(1)}, bf16[512,512]{1,0:T(8,128)(2,1)S(1)}, u32[]{:S(2)}, u32[]{:S(2)}) %collective-permute-start.4) | collective-permute-done | bytes 524320 | tf_op jit(solution)/shard_map/ppermute | solution.py:54
  53.2 0.7 collective-permute-start.12
  53.9 0.1 broadcast_in_dim.24
  54.0 0.1 broadcast_in_dim.25
  54.1 0.0 collective-permute-done.2.refs_2_.refs_3_
  54.1 2.4 %collective-permute-start.11 = (bf16[512,512]{1,0:T(8,128)(2,1)S(1)}, bf16[512,512]{1,0:T(8,128)(2,1)}, u32[]{:S(2)}, u32[]{:S(2)}) collective-permute-start(bf16[512,512]{1,0:T(8,128)(2,1)S(1)} %collective-permute-done.7.refs_8_), channel_id=1, source_target_pairs={{0,4},{1,5},{2,6},{3,7},{4,12},{5,13},{6,14},{7,15},{12,8},{13,9},... | collective-permute-start | bytes 1572872 | tf_op jit(solution)/shard_map/ppermute | solution.py:50
  56.5 9.4 %rows_1.1.refs_4_ = f32[1024,512]{1,0:T(8,128)} custom-call(s32[6]{0:T(128)} %get-tuple-element.32.block_ref, bf16[512,8192]{1,0:T(8,128)(2,1)} %refs_1_.7, bf16[512,8192]{1,0:T(8,128)(2,1)} %refs_1_.7, bf16[512,8192]{1,0:T(8,128)(2,1)} %collective-permute-done.2.refs_2_.refs_3_, bf16[512,8192]{1,0:T(8,128)(2,1)} %collective-permute-done.2.refs_2_.refs_3_, ...), custom_call_target="tpu_custom_call" | custom-call | flops 3221225472 | bytes 31457280 | tf_op jit(solution)/shard_map/rows_1/pallas_call | solution.py:436
  65.9 0.0 collective-permute-done.5.refs_6_
  65.9 0.0 copy-done.7
  65.9 1.3 %collective-permute-start.13 = (bf16[512,512]{1,0:T(8,128)(2,1)S(1)}, bf16[512,512]{1,0:T(8,128)(2,1)S(1)}, u32[]{:S(2)}, u32[]{:S(2)}) collective-permute-start(bf16[512,512]{1,0:T(8,128)(2,1)S(1)} %collective-permute-done.4.refs_7_), channel_id=1, source_target_pairs={{0,16},{16,0},{1,17},{17,1},{2,18},{18,2},{3,19},{19,3},{4,20},{20... | collective-permute-start | bytes 1572872 | tf_op jit(solution)/shard_map/ppermute | solution.py:58
  67.2 0.0 collective-permute-done.12.refs_10_
  67.2 1.1 collective-permute-start.14
  68.3 0.6 pad_add_fusion.2.slot_ref
  68.9 5.4 %resident.1 = (f32[8,32,128]{2,1,0:T(8,128)}, f32[32,128]{1,0:T(8,128)}, f32[32,128]{1,0:T(8,128)}) custom-call(s32[8]{0:T(128)} %length_ref, bf16[8,32,128]{2,1,0:T(8,128)(2,1)} %bitcast.38, bf16[8,256,1024]{2,1,0:T(8,128)(2,1)} %cache_ref.1), custom_call_target="tpu_custom_call" | custom-call | flops 268435456 | bytes 20971520 | tf_op jit(solution)/shard_map/resident/pallas_call | solution.py:370
  74.3 0.0 collective-permute-done.9.refs_5_
  74.3 0.7 collective-permute-start.16
  74.9 0.0 collective-permute-done.10.refs_8_
  74.9 1.6 %collective-permute-start.17 = (bf16[512,512]{1,0:T(8,128)(2,1)S(1)}, bf16[512,512]{1,0:T(8,128)(2,1)}, u32[]{:S(2)}, u32[]{:S(2)}) collective-permute-start(bf16[512,512]{1,0:T(8,128)(2,1)S(1)} %collective-permute-done.12.refs_10_), channel_id=1, source_target_pairs={{0,4},{1,5},{2,6},{3,7},{4,12},{5,13},{6,14},{7,15},{12,8},{13,9},... | collective-permute-start | bytes 1572872 | tf_op jit(solution)/shard_map/ppermute | solution.py:50
  76.5 0.0 all-to-all-done
  76.6 0.2 fusion
  76.8 0.6 copy.16
  77.4 0.0 collective-permute-done.11.refs_9_
  77.4 0.0 collective-permute-start.15
  77.5 9.6 %rows_2.1.refs_4_ = f32[1024,512]{1,0:T(8,128)} custom-call(s32[6]{0:T(128)} %get-tuple-element.33.block_ref, bf16[512,8192]{1,0:T(8,128)(2,1)} %refs_1_.7, bf16[512,8192]{1,0:T(8,128)(2,1)} %refs_1_.7, bf16[512,8192]{1,0:T(8,128)(2,1)} %collective-permute-done.2.refs_2_.refs_3_, bf16[512,8192]{1,0:T(8,128)(2,1)} %collective-permute-done.2.refs_2_.refs_3_, ...), custom_call_target="tpu_custom_call" | custom-call | flops 3221225472 | bytes 31457280 | tf_op jit(solution)/shard_map/rows_2/pallas_call | solution.py:436
  87.1 0.0 collective-permute-done.13.refs_5_
  87.1 0.0 collective-permute-done.14.refs_6_
  87.1 0.8 copy-done.11
  87.9 6.2 %rows_3a.1.refs_4_ = f32[1024,512]{1,0:T(8,128)} custom-call(s32[2]{0:T(128)} %get-tuple-element.34.block_ref, bf16[512,8192]{1,0:T(8,128)(2,1)} %refs_1_.7, bf16[512,8192]{1,0:T(8,128)(2,1)} %refs_1_.7, bf16[512,8192]{1,0:T(8,128)(2,1)} %collective-permute-done.2.refs_2_.refs_3_, bf16[512,8192]{1,0:T(8,128)(2,1)} %collective-permute-done.2.refs_2_.refs_3_, ...), custom_call_target="tpu_custom_call" | custom-call | flops 1073741824 | bytes 10485760 | tf_op jit(solution)/shard_map/rows_3a/pallas_call | solution.py:436
  94.1 0.0 collective-permute-done.15.refs_8_
  94.1 0.0 collective-permute-done.16.refs_9_
  94.2 0.0 collective-permute-done.17.refs_10_
  94.2 0.9 broadcast_in_dim.26.refs_6_
  95.1 6.9 %rows_3b.1 = bf16[16,3,16,128]{3,2,1,0:T(8,128)(2,1)} custom-call(s32[2]{0:T(128)} %get-tuple-element.35.block_ref, s32[2,16]{1,0:T(2,128)} %pad_add_fusion.2.slot_ref, bf16[512,8192]{1,0:T(8,128)(2,1)} %refs_1_.7, bf16[512,8192]{1,0:T(8,128)(2,1)} %refs_1_.7, bf16[512,8192]{1,0:T(8,128)(2,1)} %collective-permute-done.2.refs_2_.refs_3_, ...), custom_call_target="tpu_custom_call" | custom-call | flops 1073741824 | bytes 10485760 | tf_op jit(solution)/shard_map/rows_3b/pallas_call | solution.py:436
  102.0 13.5 %all_to_all.10.got_ref = bf16[16,3,16,128]{3,2,1,0:T(8,128)(2,1)S(1)} all-to-all(bf16[16,3,16,128]{3,2,1,0:T(8,128)(2,1)} %rows_3b.1), channel_id=1, replica_groups=mesh['replica'=2,'section'=16] {'section'}, dimensions={0} | all-to-all | bytes 393216 | tf_op jit(solution)/shard_map/all_to_all | solution.py:482
  115.5 2.3 %combine.1 = bf16[8,4096]{1,0:T(8,128)(2,1)} custom-call(bf16[16,3,16,128]{3,2,1,0:T(8,128)(2,1)S(1)} %all_to_all.10.got_ref, f32[8,32,128]{2,1,0:T(8,128)S(1)} %copy-done, f32[32,128]{1,0:T(8,128)S(1)} %copy-done.1, f32[32,128]{1,0:T(8,128)S(1)} %copy-done.2), custom_call_target="tpu_custom_call" | custom-call | tf_op jit(solution)/shard_map/combine/pallas_call | solution.py:484
  (32 shorter events, 0.1 us)
Async XLA Ops:
  2.1 2.2 %collective-permute-start.1 = (bf16[512,512]{1,0:T(8,128)(2,1)}, bf16[512,512]{1,0:T(8,128)(2,1)S(1)}, u32[]{:S(2)}, u32[]{:S(2)}) collective-permute-start(bf16[512,512]{1,0:T(8,128)(2,1)} %get-tuple-element.17), channel_id=1, source_target_pairs={{0,1},{1,0},{2,3},{3,2},{4,5},{5,4},{6,7},{7,6},{8,9},{9,8},{10,11... | collective-permute-start | bytes 1572872 | tf_op jit(solution)/shard_map/ppermute | solution.py:30
  4.3 22.6 %copy-start.5 = (bf16[512,512]{1,0:T(8,128)(2,1)}, bf16[512,512]{1,0:T(8,128)(2,1)S(1)}, u32[]{:S(2)}) copy-start(bf16[512,512]{1,0:T(8,128)(2,1)S(1)} %collective-permute-done.1.refs_7_) | copy-start | bytes 1572868
  4.3 49.8 %collective-permute-start.2 = (bf16[512,8192]{1,0:T(8,128)(2,1)}, bf16[512,8192]{1,0:T(8,128)(2,1)}, u32[]{:S(2)}, u32[]{:S(2)}) collective-permute-start(bf16[512,8192]{1,0:T(8,128)(2,1)} %refs_1_.7), channel_id=1, source_target_pairs={{0,1},{1,0},{2,3},{3,2},{4,5},{5,4},{6,7},{7,6},{8,9},{9,8},{10,11... | collective-permute-start | bytes 25165832 | tf_op jit(solution)/shard_map/ppermute | solution.py:30
  4.6 23.6 %collective-permute-start.3 = (bf16[512,512]{1,0:T(8,128)(2,1)}, bf16[512,512]{1,0:T(8,128)(2,1)S(1)}, u32[]{:S(2)}, u32[]{:S(2)}) collective-permute-start(bf16[512,512]{1,0:T(8,128)(2,1)} %get-tuple-element.19.refs_4_), channel_id=1, source_target_pairs={{0,4},{1,5},{2,6},{3,7},{4,12},{5,13},{6,14},{7,15},{12,8},{13,9},... | collective-permute-start | bytes 1572872 | tf_op jit(solution)/shard_map/ppermute | solution.py:50
  7.4 22.8 %collective-permute-start.6 = (bf16[512,512]{1,0:T(8,128)(2,1)}, bf16[512,512]{1,0:T(8,128)(2,1)S(1)}, u32[]{:S(2)}, u32[]{:S(2)}) collective-permute-start(bf16[512,512]{1,0:T(8,128)(2,1)} %get-tuple-element.19.refs_4_), channel_id=1, source_target_pairs={{0,2},{1,3},{2,0},{3,1},{4,6},{5,7},{6,4},{7,5},{8,10},{9,11},{10,... | collective-permute-start | bytes 1572872 | tf_op jit(solution)/shard_map/ppermute | solution.py:54
  9.6 17.3 %collective-permute-start = (s32[2,8]{1,0:T(2,128)S(1)}, s32[2,8]{1,0:T(2,128)S(1)}, u32[]{:S(2)}, u32[]{:S(2)}) collective-permute-start(s32[2,8]{1,0:T(2,128)S(1)} %pad_add_fusion), channel_id=1, source_target_pairs={{0,1},{1,0},{2,3},{3,2},{4,5},{5,4},{6,7},{7,6},{8,9},{9,8},{10,11... | collective-permute-start | bytes 200 | tf_op jit(solution)/shard_map/ppermute | solution.py:30
  11.2 65.3 %all-to-all-start = ((bf16[16,8,2048]{2,1,0:T(8,128)(2,1)}), bf16[16,8,2048]{2,1,0:T(8,128)(2,1)S(1)}, u32[]{:S(2)}, u32[]{:S(2)}) async-start(bf16[16,8,2048]{2,1,0:T(8,128)(2,1)} %bitcast.12), calls=%async_computation | async-start | bytes 1048576 | tf_op jit(solution)/shard_map/all_to_all | solution.py:356
  16.8 13.3 %copy-start.14 = (s32[8]{0:T(128)S(1)}, s32[8]{0:T(128)}, u32[]{:S(2)}) copy-start(s32[8]{0:T(128)} %param.11) | copy-start | bytes 100
  16.8 13.3 %copy-start.15 = (s32[8]{0:T(128)S(1)}, s32[8]{0:T(128)}, u32[]{:S(2)}) copy-start(s32[8]{0:T(128)} %param.10) | copy-start | bytes 100
  24.9 19.0 %collective-permute-start.7 = (bf16[512,512]{1,0:T(8,128)(2,1)S(1)}, bf16[512,512]{1,0:T(8,128)(2,1)S(1)}, u32[]{:S(2)}, u32[]{:S(2)}) collective-permute-start(bf16[512,512]{1,0:T(8,128)(2,1)S(1)} %collective-permute-done.1.refs_7_), channel_id=1, source_target_pairs={{0,4},{1,5},{2,6},{3,7},{4,12},{5,13},{6,14},{7,15},{12,8},{13,9},... | collective-permute-start | bytes 1572872 | tf_op jit(solution)/shard_map/ppermute | solution.py:50
  26.8 17.0 %collective-permute-start.8 = (bf16[512,512]{1,0:T(8,128)(2,1)S(1)}, bf16[512,512]{1,0:T(8,128)(2,1)S(1)}, u32[]{:S(2)}, u32[]{:S(2)}) collective-permute-start(bf16[512,512]{1,0:T(8,128)(2,1)S(1)} %collective-permute-done.1.refs_7_), channel_id=1, source_target_pairs={{0,2},{1,3},{2,0},{3,1},{4,6},{5,7},{6,4},{7,5},{8,10},{9,11},{10,... | collective-permute-start | bytes 1572872 | tf_op jit(solution)/shard_map/ppermute | solution.py:54
  28.2 28.2 %copy-start.4 = (bf16[512,512]{1,0:T(8,128)(2,1)}, bf16[512,512]{1,0:T(8,128)(2,1)S(1)}, u32[]{:S(2)}) copy-start(bf16[512,512]{1,0:T(8,128)(2,1)S(1)} %collective-permute-done.3.refs_5_) | copy-start | bytes 1572868
  28.2 25.0 %collective-permute-start.4 = (bf16[512,512]{1,0:T(8,128)(2,1)S(1)}, bf16[512,512]{1,0:T(8,128)(2,1)S(1)}, u32[]{:S(2)}, u32[]{:S(2)}) collective-permute-start(bf16[512,512]{1,0:T(8,128)(2,1)S(1)} %collective-permute-done.3.refs_5_), channel_id=1, source_target_pairs={{0,2},{1,3},{2,0},{3,1},{4,6},{5,7},{6,4},{7,5},{8,10},{9,11},{10,... | collective-permute-start | bytes 1572872 | tf_op jit(solution)/shard_map/ppermute | solution.py:54
  30.2 26.3 %copy-start.8 = (bf16[512,512]{1,0:T(8,128)(2,1)}, bf16[512,512]{1,0:T(8,128)(2,1)S(1)}, u32[]{:S(2)}) copy-start(bf16[512,512]{1,0:T(8,128)(2,1)S(1)} %collective-permute-done.6.refs_6_) | copy-start | bytes 1572868
  30.2 35.7 %collective-permute-start.5 = (bf16[512,512]{1,0:T(8,128)(2,1)S(1)}, bf16[512,512]{1,0:T(8,128)(2,1)}, u32[]{:S(2)}, u32[]{:S(2)}) collective-permute-start(bf16[512,512]{1,0:T(8,128)(2,1)S(1)} %collective-permute-done.3.refs_5_), channel_id=1, source_target_pairs={{0,4},{1,5},{2,6},{3,7},{4,12},{5,13},{6,14},{7,15},{12,8},{13,9},... | collective-permute-start | bytes 1572872 | tf_op jit(solution)/shard_map/ppermute | solution.py:50
  43.9 12.6 %copy-start.6 = (bf16[512,512]{1,0:T(8,128)(2,1)}, bf16[512,512]{1,0:T(8,128)(2,1)S(1)}, u32[]{:S(2)}) copy-start(bf16[512,512]{1,0:T(8,128)(2,1)S(1)} %collective-permute-done.7.refs_8_) | copy-start | bytes 1572868
  43.9 30.4 %collective-permute-start.9 = (bf16[512,512]{1,0:T(8,128)(2,1)S(1)}, bf16[512,512]{1,0:T(8,128)(2,1)}, u32[]{:S(2)}, u32[]{:S(2)}) collective-permute-start(bf16[512,512]{1,0:T(8,128)(2,1)S(1)} %collective-permute-done.3.refs_5_), channel_id=1, source_target_pairs={{0,16},{16,0},{1,17},{17,1},{2,18},{18,2},{3,19},{19,3},{4,20},{20... | collective-permute-start | bytes 1572872 | tf_op jit(solution)/shard_map/ppermute | solution.py:58
  43.9 9.4 %copy-start.10 = (bf16[512,512]{1,0:T(8,128)(2,1)}, bf16[512,512]{1,0:T(8,128)(2,1)S(1)}, u32[]{:S(2)}) copy-start(bf16[512,512]{1,0:T(8,128)(2,1)S(1)} %collective-permute-done.8.refs_9_) | copy-start | bytes 1572868
  43.9 31.1 %collective-permute-start.10 = (bf16[512,512]{1,0:T(8,128)(2,1)S(1)}, bf16[512,512]{1,0:T(8,128)(2,1)}, u32[]{:S(2)}, u32[]{:S(2)}) collective-permute-start(bf16[512,512]{1,0:T(8,128)(2,1)S(1)} %collective-permute-done.7.refs_8_), channel_id=1, source_target_pairs={{0,16},{16,0},{1,17},{17,1},{2,18},{18,2},{3,19},{19,3},{4,20},{20... | collective-permute-start | bytes 1572872 | tf_op jit(solution)/shard_map/ppermute | solution.py:58
  53.2 12.7 %copy-start.7 = (bf16[512,512]{1,0:T(8,128)(2,1)}, bf16[512,512]{1,0:T(8,128)(2,1)S(1)}, u32[]{:S(2)}) copy-start(bf16[512,512]{1,0:T(8,128)(2,1)S(1)} %collective-permute-done.4.refs_7_) | copy-start | bytes 1572868
  53.2 14.0 %collective-permute-start.12 = (bf16[512,512]{1,0:T(8,128)(2,1)S(1)}, bf16[512,512]{1,0:T(8,128)(2,1)S(1)}, u32[]{:S(2)}, u32[]{:S(2)}) collective-permute-start(bf16[512,512]{1,0:T(8,128)(2,1)S(1)} %collective-permute-done.7.refs_8_), channel_id=1, source_target_pairs={{0,2},{1,3},{2,0},{3,1},{4,6},{5,7},{6,4},{7,5},{8,10},{9,11},{10,... | collective-permute-start | bytes 1572872 | tf_op jit(solution)/shard_map/ppermute | solution.py:54
  54.1 23.4 %collective-permute-start.11 = (bf16[512,512]{1,0:T(8,128)(2,1)S(1)}, bf16[512,512]{1,0:T(8,128)(2,1)}, u32[]{:S(2)}, u32[]{:S(2)}) collective-permute-start(bf16[512,512]{1,0:T(8,128)(2,1)S(1)} %collective-permute-done.7.refs_8_), channel_id=1, source_target_pairs={{0,4},{1,5},{2,6},{3,7},{4,12},{5,13},{6,14},{7,15},{12,8},{13,9},... | collective-permute-start | bytes 1572872 | tf_op jit(solution)/shard_map/ppermute | solution.py:50
  65.9 11.6 %copy-start.3 = (f32[512,128]{1,0:T(8,128)S(1)}, f32[512,128]{1,0:T(8,128)}, u32[]{:S(2)}) copy-start(f32[512,128]{1,0:T(8,128)} %squares.1.refs_7_) | copy-start | bytes 786436
  65.9 21.2 %collective-permute-start.13 = (bf16[512,512]{1,0:T(8,128)(2,1)S(1)}, bf16[512,512]{1,0:T(8,128)(2,1)S(1)}, u32[]{:S(2)}, u32[]{:S(2)}) collective-permute-start(bf16[512,512]{1,0:T(8,128)(2,1)S(1)} %collective-permute-done.4.refs_7_), channel_id=1, source_target_pairs={{0,16},{16,0},{1,17},{17,1},{2,18},{18,2},{3,19},{19,3},{4,20},{20... | collective-permute-start | bytes 1572872 | tf_op jit(solution)/shard_map/ppermute | solution.py:58
  67.2 10.2 %copy-start.9 = (bf16[512,512]{1,0:T(8,128)(2,1)}, bf16[512,512]{1,0:T(8,128)(2,1)S(1)}, u32[]{:S(2)}) copy-start(bf16[512,512]{1,0:T(8,128)(2,1)S(1)} %collective-permute-done.12.refs_10_) | copy-start | bytes 1572868
  67.2 19.9 %collective-permute-start.14 = (bf16[512,512]{1,0:T(8,128)(2,1)}, bf16[512,512]{1,0:T(8,128)(2,1)}, u32[]{:S(2)}, u32[]{:S(2)}) collective-permute-start(bf16[512,512]{1,0:T(8,128)(2,1)} %collective-permute-done.5.refs_6_), channel_id=1, source_target_pairs={{0,2},{1,3},{2,0},{3,1},{4,6},{5,7},{6,4},{7,5},{8,10},{9,11},{10,... | collective-permute-start | bytes 1572872 | tf_op jit(solution)/shard_map/ppermute | solution.py:54
  74.3 19.9 %collective-permute-start.16 = (bf16[512,512]{1,0:T(8,128)(2,1)S(1)}, bf16[512,512]{1,0:T(8,128)(2,1)S(1)}, u32[]{:S(2)}, u32[]{:S(2)}) collective-permute-start(bf16[512,512]{1,0:T(8,128)(2,1)S(1)} %collective-permute-done.12.refs_10_), channel_id=1, source_target_pairs={{0,16},{16,0},{1,17},{17,1},{2,18},{18,2},{3,19},{19,3},{4,20},{20... | collective-permute-start | bytes 1572872 | tf_op jit(solution)/shard_map/ppermute | solution.py:58
  74.9 19.2 %collective-permute-start.17 = (bf16[512,512]{1,0:T(8,128)(2,1)S(1)}, bf16[512,512]{1,0:T(8,128)(2,1)}, u32[]{:S(2)}, u32[]{:S(2)}) collective-permute-start(bf16[512,512]{1,0:T(8,128)(2,1)S(1)} %collective-permute-done.12.refs_10_), channel_id=1, source_target_pairs={{0,4},{1,5},{2,6},{3,7},{4,12},{5,13},{6,14},{7,15},{12,8},{13,9},... | collective-permute-start | bytes 1572872 | tf_op jit(solution)/shard_map/ppermute | solution.py:50
  77.4 16.7 %collective-permute-start.15 = (f32[512,128]{1,0:T(8,128)S(1)}, f32[512,128]{1,0:T(8,128)S(1)}, u32[]{:S(2)}, u32[]{:S(2)}) collective-permute-start(f32[512,128]{1,0:T(8,128)S(1)} %copy-done.3), channel_id=1, source_target_pairs={{0,1},{1,0},{2,3},{3,2},{4,5},{5,4},{6,7},{7,6},{8,9},{9,8},{10,11... | collective-permute-start | bytes 786440 | tf_op jit(solution)/shard_map/ppermute | solution.py:30
  87.1 0.8 copy-start.11
  94.1 0.9 copy-start.13
  94.1 0.9 copy-start.12
  95.1 20.4 %copy-start = (f32[8,32,128]{2,1,0:T(8,128)S(1)}, f32[8,32,128]{2,1,0:T(8,128)}, u32[]{:S(2)}) copy-start(f32[8,32,128]{2,1,0:T(8,128)} %get-tuple-element.26.res_out_ref) | copy-start | bytes 393220
  95.1 20.4 %copy-start.1 = (f32[32,128]{1,0:T(8,128)S(1)}, f32[32,128]{1,0:T(8,128)}, u32[]{:S(2)}) copy-start(f32[32,128]{1,0:T(8,128)} %get-tuple-element.27.res_top_ref) | copy-start | bytes 49156
  95.1 20.4 %copy-start.2 = (f32[32,128]{1,0:T(8,128)S(1)}, f32[32,128]{1,0:T(8,128)}, u32[]{:S(2)}) copy-start(f32[32,128]{1,0:T(8,128)} %get-tuple-element.28.res_sum_ref) | copy-start | bytes 49156

commit v6 on v5

--- a/solution.py
+++ b/solution.py
@@ -77,7 +77,9 @@
                     out.append(chip * 2 + (core ^ other))
                 return out
 
-            table.append(blocks(0, 0) + blocks(0, 1) + blocks(1, 0) + blocks(1, 1) + blocks(2, 0) + blocks(2, 1))
+            (own_a, *one_a), (own_b, *one_b) = blocks(0, 0), blocks(0, 1)
+            two_a, two_b = blocks(1, 0), blocks(1, 1)
+            table.append(one_a + one_b + [own_a] + two_a + [own_b] + two_b + blocks(2, 0) + blocks(2, 1))
     return np.array(table, np.int32)
 
 
@@ -87,7 +89,7 @@
         values = states_ref[:, i : i + HD].astype(jnp.float32)
         values = values * values
         total = values if total is None else total + values
-    out_ref[...] = total
+    out_ref[...] = jnp.sum(total, axis=1, keepdims=True)
 
 
 def split_kernel(core_ref, keep_in, give_in, keep_ref, give_ref):
@@ -96,8 +98,8 @@
 
 
 def accumulate(layout, token_refs, piece_refs, weight, total, sems, carry_ref=None, carry=None):
-    step = pl.program_id(0)
-    depth = token_refs[0].shape[1]
+    pair, half = pl.program_id(0), pl.program_id(1)
+    tokens, depth = token_refs[0].shape
     copies = [
         pltpu.make_async_copy(
             piece_refs[which].at[pl.ds(start, depth)], weight.at[pl.ds(i * depth, depth)], sems.at[i]
@@ -108,39 +110,38 @@
     if carry_ref is not None:
         carried = [pltpu.make_async_copy(carry_ref, carry, sems.at[len(layout)])]
 
-    @pl.when(step == 0)
+    @pl.when((pair == 0) & (half == 0))
     def _():
         for copy in copies + carried:
             copy.start()
 
     for i in range(0, len(copies), 2):
 
-        @pl.when(step == i // 2)
+        @pl.when((pair == i // 2) & (half == 0))
         def _():
             copies[i].wait()
             copies[i + 1].wait()
 
-    states = jnp.concatenate(
-        [
-            jnp.concatenate([token_refs[0][...], token_refs[1][...]], axis=1),
-            jnp.concatenate([token_refs[2][...], token_refs[3][...]], axis=1),
-        ],
-        axis=0,
-    )
-    block = weight[pl.ds(pl.multiple_of(step * 2 * depth, 2 * depth), 2 * depth), :]
-    product = jnp.dot(states, block, preferred_element_type=jnp.float32)
-
-    @pl.when(step == 0)
-    def _():
-        total[...] = product
-
-    @pl.when(step > 0)
-    def _():
-        total[...] += product
+    for side in range(2):
+
+        @pl.when(half == side)
+        def _():
+            states = jnp.concatenate([token_refs[2 * side][...], token_refs[2 * side + 1][...]], axis=1)
+            block = weight[pl.ds(pl.multiple_of(pair * 2 * depth, 2 * depth), 2 * depth), :]
+            product = jnp.dot(states, block, preferred_element_type=jnp.float32)
+            rows = pl.ds(side * tokens, tokens)
+
+            @pl.when(pair == 0)
+            def _():
+                total[rows, :] = product
+
+            @pl.when(pair > 0)
+            def _():
+                total[rows, :] += product
 
     if carry_ref is not None:
 
-        @pl.when(step == pl.num_programs(0) - 1)
+        @pl.when((pair == pl.num_programs(0) - 1) & (half == 1))
         def _():
             carried[0].wait()
             total[...] += carry[...]
@@ -166,27 +167,25 @@
 
 
 def last_kernel(layout, width, block_ref, slot_ref, *refs):
-    query_ref, row_lane_ref, own_squares, other_squares = refs[5:9]
+    query_ref, factor_ref = refs[5:7]
     slots_ref, weight, carry, total, summed, stats, sems = refs[-7:]
     images = query_ref.shape[1] // GROUP
 
-    @pl.when(pl.program_id(0) == 0)
+    @pl.when((pl.program_id(0) == 0) & (pl.program_id(1) == 0))
     def _():
         slots_ref[...] = jnp.zeros_like(slots_ref)
 
-    accumulate(layout, refs[:4], refs[9:-7], weight, total, sems, refs[4], carry)
-
-    @pl.when(pl.program_id(0) == pl.num_programs(0) - 1)
+    accumulate(layout, refs[:4], refs[7:-7], weight, total, sems, refs[4], carry)
+
+    @pl.when((pl.program_id(0) == pl.num_programs(0) - 1) & (pl.program_id(1) == 1))
     def _():
         tokens = total.shape[0]
         queries = query_ref.shape[1]
-        squares = jnp.concatenate([own_squares[...], other_squares[...]], axis=0)
-        factor = lax.rsqrt(jnp.sum(squares, axis=1, keepdims=True) / width + EPS)
+        factor = lax.rsqrt(factor_ref[...] / width + EPS)
         image_of_query = lax.broadcasted_iota(jnp.int32, (queries, tokens), 0) // GROUP
         image_of_token = lax.broadcasted_iota(jnp.int32, (queries, tokens), 1) // IMG_TOK
         live = image_of_query == image_of_token
         lane = lax.broadcasted_iota(jnp.int32, (queries, HD), 1)
-        first_lane = row_lane_ref[:, :1]
         for head in range(HALF_KVH):
             part = slice(head * GROUP, (head + 1) * GROUP)
             keys = (total[:, head * HD : (head + 1) * HD] * factor).astype(jnp.bfloat16)
@@ -207,12 +206,13 @@
             kinds = parts_of(top, 3) + parts_of(total_weight, 3) + [jnp.ones_like(top)]
             tile = jnp.zeros((queries, HD), jnp.float32)
             for kind, column in enumerate(kinds):
-                tile = jnp.where(lane == first_lane + kind * 8, column, tile)
+                tile = jnp.where(lane == kind * 8, column, tile)
             stats[:, part, :] = tile.reshape(images, GROUP, HD)
         for image in range(images):
             owner, which = slot_ref[0, image], slot_ref[1, image]
             slots_ref[owner, which] = summed[image].astype(jnp.bfloat16)
-            slots_ref[owner, 2] = slots_ref[owner, 2] + stats[image].astype(jnp.bfloat16)
+            tile = pltpu.roll(stats[image], which * LANES + slot_ref[2, image], 1)
+            slots_ref[owner, 2] = slots_ref[owner, 2] + tile.astype(jnp.bfloat16)
 
 
 def resident_kernel(length_ref, query_ref, cache_ref, out_ref, top_ref, sum_ref):
@@ -329,41 +329,52 @@
             out_specs=[pl.BlockSpec((rows_dev, cut), lambda i, core_ref: (0, i))] * 2,
         ),
         out_shape=[jax.ShapeDtypeStruct((rows_dev, columns_dev), jnp.bfloat16)] * 2,
-        cost_estimate=pl.CostEstimate(flops=0, bytes_accessed=2 * 2**20, transcendentals=0),
+        cost_estimate=pl.CostEstimate(flops=0, bytes_accessed=2**18, transcendentals=0),
         name="split",
     )(core.reshape(1), kv_weight, kv_weight)
     taken = swap_core(give)
+    states, _ = lax.optimization_barrier((prompt_states, taken))
     squares = pl.pallas_call(
         square_kernel,
         grid=(8,),
         in_specs=[pl.BlockSpec((tokens // 8, width), lambda i: (i, 0))],
-        out_specs=pl.BlockSpec((tokens // 8, HD), lambda i: (i, 0)),
-        out_shape=jax.ShapeDtypeStruct((tokens, HD), jnp.float32),
-        cost_estimate=pl.CostEstimate(flops=2 * tokens * width, bytes_accessed=16 * 2**20, transcendentals=0),
-        compiler_params=pltpu.CompilerParams(vmem_limit_bytes=56 * 2**20),
+        out_specs=pl.BlockSpec((tokens // 8, 1), lambda i: (i, 0)),
+        out_shape=jax.ShapeDtypeStruct((tokens, 1), jnp.float32),
+        cost_estimate=pl.CostEstimate(flops=0, bytes_accessed=2**18, transcendentals=0),
+        compiler_params=pltpu.CompilerParams(vmem_limit_bytes=32 * 2**20),
         name="squares",
-    )(prompt_states)
-    swapped_states, tied = lax.optimization_barrier((prompt_states, taken))
-    other = swap_core(swapped_states)
-    other_squares = swap_core(squares)
-
-    owner_and_row = jnp.stack([image_owner, image_row])
-    chip_images = jnp.concatenate([owner_and_row, swap_core(owner_and_row)], axis=1)
-    send_q = queries.reshape(decode_rows, 2, HALF_QH * HD).transpose(1, 0, 2)
-    send_q = jnp.broadcast_to(send_q[None], (n // 2, 2, decode_rows, HALF_QH * HD)).reshape(
-        n, decode_rows, HALF_QH * HD
-    )
-    all_q = lax.all_to_all(send_q, "section", split_axis=0, concat_axis=0, tiled=True)
-    all_q = all_q.reshape(n * decode_rows, HALF_QH * HD)
-    target = chip_images[0] * decode_rows + chip_images[1]
-    pick = (target[:, None] == jnp.arange(n * decode_rows)[None, :]).astype(jnp.bfloat16)
-    image_q = jnp.dot(pick, all_q, preferred_element_type=jnp.float32).astype(jnp.bfloat16)
-    image_q = image_q.reshape(2 * images, HALF_KVH, GROUP, HD).transpose(1, 0, 2, 3)
-    image_q = image_q.reshape(HALF_KVH, n_queries, HD)
-
-    which = jnp.concatenate([jnp.full((images,), core), jnp.full((images,), 1 - core)]).astype(jnp.int32)
-    slot = jnp.stack([chip_images[0], which])
-    row_lane = jnp.broadcast_to(jnp.repeat(which * LANES + chip_images[1], GROUP)[:, None], (n_queries, HD))
+    )(pltpu.with_memory_space_constraint(states, pltpu.HBM))[:, 0]
+    other = swap_core(states)
+
+    places = jnp.concatenate([image_owner, image_row]).astype(jnp.float32)
+    small = jnp.concatenate([squares, places])
+    small = jnp.pad(small, (0, -small.shape[0] % (8 * HD))).reshape(-1, HD)
+
+    def finish_small(tied):
+        mine, _ = lax.optimization_barrier((small, tied))
+        got = swap_core(mine).reshape(-1)
+        factor = jnp.concatenate([squares, got[:tokens]])[:, None]
+        at = tokens + images
+        owners = jnp.concatenate([image_owner, got[tokens:at].astype(jnp.int32)])
+        rows = jnp.concatenate([image_row, got[at : at + images].astype(jnp.int32)])
+        return factor, owners, rows
+
+    def gather_queries(tied):
+        mine, _ = lax.optimization_barrier((queries, tied))
+        send_q = mine.reshape(decode_rows, 2, HALF_QH * HD).transpose(1, 0, 2)
+        send_q = jnp.broadcast_to(send_q[None], (n // 2, 2, decode_rows, HALF_QH * HD)).reshape(
+            n, decode_rows, HALF_QH * HD
+        )
+        all_q = lax.all_to_all(send_q, "section", split_axis=0, concat_axis=0, tiled=True)
+        return all_q.reshape(n * decode_rows, HALF_QH * HD)
+
+    def place_images(all_q, owners, rows):
+        target = owners * decode_rows + rows
+        pick = (target[:, None] == jnp.arange(n * decode_rows)[None, :]).astype(jnp.bfloat16)
+        image_q = jnp.dot(pick, all_q, preferred_element_type=jnp.float32).astype(jnp.bfloat16)
+        image_q = image_q.reshape(2 * images, HALF_KVH, GROUP, HD).transpose(1, 0, 2, 3)
+        which = jnp.concatenate([jnp.full((images,), core), jnp.full((images,), 1 - core)]).astype(jnp.int32)
+        return image_q.reshape(HALF_KVH, n_queries, HD), jnp.stack([owners, which, rows])
 
     def resident(length):
         step_rows = 2
@@ -388,11 +399,11 @@
                 jax.ShapeDtypeStruct((QH, HD), jnp.float32),
             ],
             compiler_params=pltpu.CompilerParams(vmem_limit_bytes=56 * 2**20),
-            cost_estimate=pl.CostEstimate(flops=2**28, bytes_accessed=20 * 2**20, transcendentals=0),
+            cost_estimate=pl.CostEstimate(flops=0, bytes_accessed=2**18, transcendentals=0),
             name="resident",
         )(length, queries.reshape(decode_rows, QH, HD), cache)
 
-    def product(blocks, pieces, carry, name, last=False):
+    def product(blocks, base, pieces, carry, name, last=None):
         arrays, layout = [], []
         for array, start in pieces:
             at = [i for i, known in enumerate(arrays) if known is array]
@@ -401,31 +412,29 @@
                 at = [len(arrays) - 1]
             layout.append((at[0], start))
         steps = len(pieces) // 2
-        first = pl.BlockSpec((tokens, rows_dev), lambda i, block_ref, *_: (0, block_ref[2 * i]))
-        second = pl.BlockSpec((tokens, rows_dev), lambda i, block_ref, *_: (0, block_ref[2 * i + 1]))
-        in_hbm = pl.BlockSpec(memory_space=pltpu.HBM)
+        first = pl.BlockSpec((tokens, rows_dev), lambda i, half, block_ref, *_: (0, block_ref[base + 2 * i]))
+        second = pl.BlockSpec((tokens, rows_dev), lambda i, half, block_ref, *_: (0, block_ref[base + 2 * i + 1]))
+        anywhere = pl.BlockSpec(memory_space=pl.ANY)
         in_specs = [first, second, first, second]
-        inputs = [prompt_states, prompt_states, other, other]
+        own_tokens = pltpu.with_memory_space_constraint(prompt_states, pltpu.HBM)
+        other_tokens = pltpu.with_memory_space_constraint(other, pltpu.HBM)
+        inputs = [own_tokens, own_tokens, other_tokens, other_tokens]
         scalars = [blocks]
         scratch = [pltpu.VMEM((len(pieces) * rows_dev, columns_dev), jnp.bfloat16)]
         total = (2 * tokens, columns_dev)
         body = functools.partial(first_kernel, layout)
         if carry is not None:
             body = functools.partial(next_kernel, layout)
-            in_specs = in_specs + [pl.BlockSpec(memory_space=pl.ANY)]
+            in_specs = in_specs + [anywhere]
             inputs = inputs + [carry]
             scratch = scratch + [pltpu.VMEM(total, jnp.float32)]
         out_specs, out_shape = whole(total), jax.ShapeDtypeStruct(total, jnp.float32)
-        if last:
+        if last is not None:
+            image_q, slot, factor = last
             body = functools.partial(last_kernel, layout, width)
             scalars = scalars + [slot]
-            in_specs = in_specs + [
-                whole((HALF_KVH, n_queries, HD)),
-                whole((n_queries, HD)),
-                whole((tokens, HD)),
-                whole((tokens, HD)),
-            ]
-            inputs = inputs + [image_q, row_lane, squares, other_squares]
+            in_specs = in_specs + [whole((HALF_KVH, n_queries, HD)), whole((2 * tokens, 1))]
+            inputs = inputs + [image_q, factor]
             out_specs = whole((n, 3, HALF_QH, HD))
             out_shape = jax.ShapeDtypeStruct((n, 3, HALF_QH, HD), jnp.bfloat16)
             scratch = scratch + [
@@ -437,18 +446,14 @@
             body,
             grid_spec=pltpu.PrefetchScalarGridSpec(
                 num_scalar_prefetch=len(scalars),
-                grid=(steps,),
-                in_specs=in_specs + [in_hbm] * len(arrays),
+                grid=(steps, 2),
+                in_specs=in_specs + [anywhere] * len(arrays),
                 out_specs=out_specs,
                 scratch_shapes=scratch + [pltpu.SemaphoreType.DMA((len(pieces) + 1,))],
             ),
             out_shape=out_shape,
-            compiler_params=pltpu.CompilerParams(vmem_limit_bytes=56 * 2**20),
-            cost_estimate=pl.CostEstimate(
-                flops=2 * 2 * tokens * 2 * rows_dev * columns_dev * steps,
-                bytes_accessed=10 * steps * 2**20,
-                transcendentals=0,
-            ),
+            compiler_params=pltpu.CompilerParams(vmem_limit_bytes=32 * 2**20),
+            cost_estimate=pl.CostEstimate(flops=0, bytes_accessed=2**18, transcendentals=0),
             name=name,
         )(*scalars, *inputs, *arrays)
 
@@ -458,27 +463,34 @@
         def starts(*arrays):
             return [(array, 0) for array in arrays]
 
-        a1 = (keep, along_ring(keep), across_y(keep))
-        b1 = (taken, along_ring(taken), across_y(taken))
-        a2 = (across_replica(a1[1]), along_ring(a1[1]), across_y(a1[1]))
-        length, tied = lax.optimization_barrier((context_length, a1[1]))
+        a1 = (along_ring(keep), across_y(keep))
+        b1 = (along_ring(taken), across_y(taken))
+        a2 = (across_replica(a1[0]), along_ring(a1[0]), across_y(a1[0]))
+        all_q = gather_queries(a1[0])
+        length, _ = lax.optimization_barrier((context_length, squares))
         res_out, res_top, res_sum = resident(length)
-        b2 = (across_replica(b1[1]), along_ring(b1[1]), across_y(b1[1]))
-        total = product(blocks[:6], starts(*a1, *b1), None, "rows_1")
+        b_behind, res_out = lax.optimization_barrier((b1[0], res_out))
+        b2 = (across_replica(b_behind), along_ring(b_behind), across_y(b_behind))
+        factor, owners, rows = finish_small(b1[0])
+        total = product(blocks, 0, starts(*a1, *b1), None, "rows_1")
         a_behind_y, a_opposite, total = lax.optimization_barrier((a2[2], a2[1], total))
         a3 = (across_replica(a_behind_y), across_y(a_opposite))
-        b_behind_y, res_out = lax.optimization_barrier((b2[2], res_out))
-        b3 = (across_replica(b_behind_y), along_ring(b_behind_y))
-        total = product(blocks[6:12], starts(*a2, *b2), total, "rows_2")
-        total = product(blocks[12:14], starts(*a3), total, "rows_3a")
-        slots = product(blocks[14:], starts(*b3), total, "rows_3b", last=True)
+        image_q, slot = place_images(all_q, owners, rows)
+        b3 = (across_replica(b2[2]), along_ring(b2[2]))
+        total = product(blocks, 4, starts(keep, *a2), total, "rows_2a")
+        total = product(blocks, 8, starts(taken, *b2), total, "rows_2b")
+        slots = product(blocks, 12, starts(*a3, *b3), total, "rows_3", last=(image_q, slot, factor))
     else:
         res_out, res_top, res_sum = resident(context_length)
+        factor, owners, rows = finish_small(squares)
+        image_q, slot = place_images(gather_queries(squares), owners, rows)
         a = gather_plain(keep)
         b = gather_plain(taken)
         chips = jnp.array([chip for chip, _, _ in a], jnp.int32)
-        total = product(chips * 2 + core, [piece[1:] for piece in a], None, "rows_a")
-        slots = product(chips * 2 + 1 - core, [piece[1:] for piece in b], total, "rows_b", last=True)
+        total = product(chips * 2 + core, 0, [piece[1:] for piece in a], None, "rows_a")
+        slots = product(
+            chips * 2 + 1 - core, 0, [piece[1:] for piece in b], total, "rows_b", last=(image_q, slot, factor)
+        )
     got = lax.all_to_all(slots, "section", split_axis=0, concat_axis=0, tiled=True)
 
     return pl.pallas_call(

time: 119 us -> 123 us (1.034)
  starting transfers between devices: 25.2 us -> 28.3 us
  waiting for transfers between devices: 20.5 us -> 22.9 us
  Pallas kernels: 49.2 us -> 47.5 us
    unnamed x34 -> x24, local copies, waits for them, and re-layouts: 2.31 us -> 5.38 us
    all_to_all x1, starting transfers between devices: 4.07 us -> 6.04 us  [gather_queries(): lax.all_to_all(send_q, 'section', split_axis=0, concat_axis=0, tiled=True)]
    broadcast_in_dim x5 -> x3, local copies, waits for them, and re-layouts: 2.72 us -> 1.07 us  [the longest x1 0.84 us: gather_queries(): jnp.broadcast_to(send_q[None], (n // 2, 2, decode_rows, HALF_QH * HD))]
    ppermute x4, waiting for transfers between devices: 0.01 us -> 1.63 us  [across_replica(): return lax.ppermute(x, 'replica', [(0, 1), (1, 0)])]
    slice x3 -> x1, local copies, waits for them, and re-layouts: 1.25 us -> 0.01 us  [finish_small(): factor = jnp.concatenate([squares, got[:tokens]])[:, None]]
    another operation x2 -> x1, other arithmetic: 1.25 us -> 0.01 us  [place_images(): jnp.stack([owners, which, rows])]
  transfers between devices with their start and end apart: 19 -> 18, of which waited for: 3 -> 5; matrix products, arithmetic and copies ran while one was open for 6% -> 4% of each run, Pallas kernels for 32% -> 28%
where the time goes in v6:
time: 123 us; the launch traced here: 122 us
  Pallas kernels  47.5 us (39%)
  starting transfers between devices  28.3 us (23%)
  waiting for transfers between devices  22.9 us (19%)
  blocking collectives  13.8 us (11%)
  local copies, waits for them, and re-layouts  7.15 us (6%)
  matrix products  1.27 us (1%)
    pallas_call x4, Pallas kernels, product(): pl.pallas_call(body, grid_spec=pltpu.PrefetchScalarGridSpec(num_scalar_pr...  31 us
    all_to_all x1, blocking collectives, per_device(): lax.all_to_all(slots, 'section', split_axis=0, concat_axis=0, tiled=True)  13.8 us
    ppermute x5, waiting for transfers between devices, along_ring(): return lax.ppermute(x, ('replica', 'section'), perm)  11.9 us
    ppermute x5, starting transfers between devices, along_ring(): return lax.ppermute(x, ('replica', 'section'), perm)  11 us
    ppermute x5, waiting for transfers between devices, across_y(): return lax.ppermute(x, 'section', [(i, i ^ 2) for i in range(16)])  7.58 us
    pallas_call x1, Pallas kernels, per_device(): pl.pallas_call(square_kernel, grid=(8,), in_specs=[pl.BlockSpec((tokens /...  6.71 us
    all_to_all x1, starting transfers between devices, gather_queries(): lax.all_to_all(send_q, 'section', split_axis=0, concat_axis=0, tiled=True)  6.04 us
    ppermute x5, starting transfers between devices, across_y(): return lax.ppermute(x, 'section', [(i, i ^ 2) for i in range(16)])  5.61 us
  transfers between devices with their start and end apart: 18, of which 5 were waited for; matrix products, arithmetic and copies ran while one was open for 4% of the time, Pallas kernels for 28%

profile of v6, /device:TPU:0, one launch (start us, length us, event | category | flops | bytes accessed | tf_op | source)
XLA Modules:
  0.0 122.1 jit_solution(10169490421609966354)
XLA Ops:
  0.0 2.1 %split.1 = (bf16[512,512]{1,0:T(8,128)(2,1)}, bf16[512,512]{1,0:T(8,128)(2,1)}) custom-call(s32[1]{0:T(128)} %bitcast.1.core_ref, bf16[512,1024]{1,0:T(8,128)(2,1)} %give_in.1, bf16[512,1024]{1,0:T(8,128)(2,1)} %give_in.1), custom_call_target="tpu_custom_call" | custom-call | bytes 262144 | tf_op jit(solution)/shard_map/split/pallas_call | solution.py:320
  2.1 0.5 collective-permute-start
  2.5 1.7 %collective-permute-done.refs_5_ = bf16[512,512]{1,0:T(8,128)(2,1)S(1)} collective-permute-done((bf16[512,512]{1,0:T(8,128)(2,1)}, bf16[512,512]{1,0:T(8,128)(2,1)S(1)}, u32[]{:S(2)}, u32[]{:S(2)}) %collective-permute-start) | collective-permute-done | bytes 524320 | tf_op jit(solution)/shard_map/ppermute | solution.py:30
  4.3 0.4 collective-permute-start.3
  4.7 2.7 %collective-permute-start.1 = (bf16[512,512]{1,0:T(8,128)(2,1)S(1)}, bf16[512,512]{1,0:T(8,128)(2,1)}, u32[]{:S(2)}, u32[]{:S(2)}) collective-permute-start(bf16[512,512]{1,0:T(8,128)(2,1)S(1)} %collective-permute-done.refs_5_), channel_id=1, source_target_pairs={{0,4},{1,5},{2,6},{3,7},{4,12},{5,13},{6,14},{7,15},{12,8},{13,9},... | collective-permute-start | bytes 1572872 | tf_op jit(solution)/shard_map/ppermute | solution.py:50
  7.4 2.6 %collective-permute-start.4 = (bf16[512,512]{1,0:T(8,128)(2,1)}, bf16[512,512]{1,0:T(8,128)(2,1)}, u32[]{:S(2)}, u32[]{:S(2)}) collective-permute-start(bf16[512,512]{1,0:T(8,128)(2,1)} %get-tuple-element.22.refs_5_), channel_id=1, source_target_pairs={{0,4},{1,5},{2,6},{3,7},{4,12},{5,13},{6,14},{7,15},{12,8},{13,9},... | collective-permute-start | bytes 1572872 | tf_op jit(solution)/shard_map/ppermute | solution.py:50
  10.0 1.5 %collective-permute-start.7 = (bf16[512,512]{1,0:T(8,128)(2,1)}, bf16[512,512]{1,0:T(8,128)(2,1)S(1)}, u32[]{:S(2)}, u32[]{:S(2)}) collective-permute-start(bf16[512,512]{1,0:T(8,128)(2,1)} %get-tuple-element.22.refs_5_), channel_id=1, source_target_pairs={{0,2},{1,3},{2,0},{3,1},{4,6},{5,7},{6,4},{7,5},{8,10},{9,11},{10,... | collective-permute-start | bytes 1572872 | tf_op jit(solution)/shard_map/ppermute | solution.py:54
  11.5 0.5 collective-permute-start.8
  12.0 0.7 add_convert_fusion
  12.7 6.7 %squares.1 = f32[512,1]{1,0:T(8,128)S(1)} custom-call(bf16[512,8192]{1,0:T(8,128)(2,1)} %refs_1_.7), custom_call_target="tpu_custom_call" | custom-call | bytes 262144 | tf_op jit(solution)/shard_map/squares/pallas_call | solution.py:337
  19.5 0.1 reduce
  19.6 1.6 %collective-permute-done.1.refs_6_ = bf16[512,512]{1,0:T(8,128)(2,1)} collective-permute-done((bf16[512,512]{1,0:T(8,128)(2,1)S(1)}, bf16[512,512]{1,0:T(8,128)(2,1)}, u32[]{:S(2)}, u32[]{:S(2)}) %collective-permute-start.1) | collective-permute-done | bytes 524320 | tf_op jit(solution)/shard_map/ppermute | solution.py:50
  21.3 0.0 collective-permute-start.2
  21.3 0.0 copy-done.8
  21.3 0.6 copy.16
  21.9 10.3 %collective-permute-done.4.refs_4_ = bf16[512,512]{1,0:T(8,128)(2,1)} collective-permute-done((bf16[512,512]{1,0:T(8,128)(2,1)}, bf16[512,512]{1,0:T(8,128)(2,1)}, u32[]{:S(2)}, u32[]{:S(2)}) %collective-permute-start.4) | collective-permute-done | bytes 524320 | tf_op jit(solution)/shard_map/ppermute | solution.py:50
  32.2 0.8 broadcast_in_dim.7
  33.0 6.0 %all-to-all-start = ((bf16[16,8,2048]{2,1,0:T(8,128)(2,1)}), bf16[16,8,2048]{2,1,0:T(8,128)(2,1)}, u32[]{:S(2)}, u32[]{:S(2)}) async-start(bf16[16,8,2048]{2,1,0:T(8,128)(2,1)} %bitcast.9), calls=%async_computation | async-start | bytes 1048576 | tf_op jit(solution)/shard_map/all_to_all | solution.py:368
  39.1 5.4 %resident.1 = (f32[8,32,128]{2,1,0:T(8,128)}, f32[32,128]{1,0:T(8,128)}, f32[32,128]{1,0:T(8,128)}) custom-call(s32[8]{0:T(128)} %length_ref, bf16[8,32,128]{2,1,0:T(8,128)(2,1)} %bitcast.36, bf16[8,256,1024]{2,1,0:T(8,128)(2,1)} %cache_ref.1), custom_call_target="tpu_custom_call" | custom-call | bytes 262144 | tf_op jit(solution)/shard_map/resident/pallas_call | solution.py:381
  44.4 1.9 %collective-permute-start.5 = (bf16[512,512]{1,0:T(8,128)(2,1)}, bf16[512,512]{1,0:T(8,128)(2,1)}, u32[]{:S(2)}, u32[]{:S(2)}) collective-permute-start(bf16[512,512]{1,0:T(8,128)(2,1)} %collective-permute-done.4.refs_4_), channel_id=1, source_target_pairs={{0,2},{1,3},{2,0},{3,1},{4,6},{5,7},{6,4},{7,5},{8,10},{9,11},{10,... | collective-permute-start | bytes 1572872 | tf_op jit(solution)/shard_map/ppermute | solution.py:54
  46.3 0.0 collective-permute-done.7.refs_5_
  46.3 0.8 copy-done.1
  47.1 1.5 %collective-permute-start.6 = (bf16[512,512]{1,0:T(8,128)(2,1)}, bf16[512,512]{1,0:T(8,128)(2,1)}, u32[]{:S(2)}, u32[]{:S(2)}) collective-permute-start(bf16[512,512]{1,0:T(8,128)(2,1)} %collective-permute-done.4.refs_4_), channel_id=1, source_target_pairs={{0,4},{1,5},{2,6},{3,7},{4,12},{5,13},{6,14},{7,15},{12,8},{13,9},... | collective-permute-start | bytes 1572872 | tf_op jit(solution)/shard_map/ppermute | solution.py:50
  48.6 0.0 collective-permute-done.8.refs_7_
  48.6 0.8 copy-done.3
  49.4 1.5 %collective-permute-start.9 = (bf16[512,512]{1,0:T(8,128)(2,1)}, bf16[512,512]{1,0:T(8,128)(2,1)}, u32[]{:S(2)}, u32[]{:S(2)}) collective-permute-start(bf16[512,512]{1,0:T(8,128)(2,1)} %collective-permute-done.4.refs_4_), channel_id=1, source_target_pairs={{0,16},{16,0},{1,17},{17,1},{2,18},{18,2},{3,19},{19,3},{4,20},{20... | collective-permute-start | bytes 1572872 | tf_op jit(solution)/shard_map/ppermute | solution.py:58
  50.8 0.0 collective-permute-done.2
  50.9 0.5 collective-permute-start.10
  51.4 0.0 collective-permute-done.3.refs_2_.refs_3_
  51.4 0.6 collective-permute-start.12
  52.0 0.7 dynamic-slice_bitcast_fusion.block_ref
  52.7 0.2 copy.11.refs_6_
  52.9 0.0 copy-start.2
  52.9 1.0 copy-done.2
  54.0 1.0 copy-done.4
  55.0 7.3 %rows_1.1.refs_4_ = f32[1024,512]{1,0:T(8,128)S(1)} custom-call(s32[16]{0:T(128)S(1)} %dynamic-slice_bitcast_fusion.block_ref, bf16[512,8192]{1,0:T(8,128)(2,1)} %refs_1_.7, bf16[512,8192]{1,0:T(8,128)(2,1)} %refs_1_.7, bf16[512,8192]{1,0:T(8,128)(2,1)} %collective-permute-done.3.refs_2_.refs_3_, bf16[512,8192]{1,0:T(8,128)(2,1)} %collective-permute-done.3.refs_2_.refs_3_, ...), custom_call_target="tpu_custom_call" | custom-call | bytes 262144 | tf_op jit(solution)/shard_map/rows_1/pallas_call | solution.py:445
  62.3 0.0 collective-permute-done.5.refs_8_
  62.3 2.4 %collective-permute-start.11 = (bf16[512,512]{1,0:T(8,128)(2,1)}, bf16[512,512]{1,0:T(8,128)(2,1)}, u32[]{:S(2)}, u32[]{:S(2)}) collective-permute-start(bf16[512,512]{1,0:T(8,128)(2,1)} %collective-permute-done.1.refs_6_), channel_id=1, source_target_pairs={{0,4},{1,5},{2,6},{3,7},{4,12},{5,13},{6,14},{7,15},{12,8},{13,9},... | collective-permute-start | bytes 1572872 | tf_op jit(solution)/shard_map/ppermute | solution.py:50
  64.7 7.6 %collective-permute-done.12.refs_8_ = bf16[512,512]{1,0:T(8,128)(2,1)} collective-permute-done((bf16[512,512]{1,0:T(8,128)(2,1)}, bf16[512,512]{1,0:T(8,128)(2,1)}, u32[]{:S(2)}, u32[]{:S(2)}) %collective-permute-start.12) | collective-permute-done | bytes 524320 | tf_op jit(solution)/shard_map/ppermute | solution.py:54
  72.3 0.6 collective-permute-start.15
  72.9 0.0 collective-permute-done.6.refs_7_
  72.9 1.8 %collective-permute-start.16 = (bf16[512,512]{1,0:T(8,128)(2,1)}, bf16[512,512]{1,0:T(8,128)(2,1)}, u32[]{:S(2)}, u32[]{:S(2)}) collective-permute-start(bf16[512,512]{1,0:T(8,128)(2,1)} %collective-permute-done.12.refs_8_), channel_id=1, source_target_pairs={{0,4},{1,5},{2,6},{3,7},{4,12},{5,13},{6,14},{7,15},{12,8},{13,9},... | collective-permute-start | bytes 1572872 | tf_op jit(solution)/shard_map/ppermute | solution.py:50
  74.7 0.0 collective-permute-done.9.refs_6_
  74.7 2.2 %collective-permute-start.13 = (bf16[512,512]{1,0:T(8,128)(2,1)}, bf16[512,512]{1,0:T(8,128)(2,1)}, u32[]{:S(2)}, u32[]{:S(2)}) collective-permute-start(bf16[512,512]{1,0:T(8,128)(2,1)} %collective-permute-done.5.refs_8_), channel_id=1, source_target_pairs={{0,16},{16,0},{1,17},{17,1},{2,18},{18,2},{3,19},{19,3},{4,20},{20... | collective-permute-start | bytes 1572872 | tf_op jit(solution)/shard_map/ppermute | solution.py:58
  76.9 0.0 collective-permute-done.10.refs_6_
  76.9 1.1 collective-permute-start.14
  78.1 0.1 slice_convert_fusion.1
  78.1 0.0 copy-done.9
  78.1 0.0 copy-done.10
  78.1 0.1 multiply_add_fusion
  78.2 0.0 all-to-all-done
  78.2 1.3 %fusion = bf16[2,8,16,128]{3,1,2,0:T(8,128)(2,1)S(1)} fusion(bf16[16,8,2048]{2,1,0:T(8,128)(2,1)} %all-to-all-done, s32[16]{0:T(128)S(1)} %get-tuple-element.35), kind=kOutput, calls=%fused_computation.1 | convolution fusion | flops 8423424 | bytes 589888 | tf_op jit(solution)/shard_map/dot_general | solution.py:374
  79.5 0.0 copy-start
  79.6 1.0 copy-done
  80.6 7.5 %rows_2a.1.refs_4_ = f32[1024,512]{1,0:T(8,128)S(1)} custom-call(s32[16]{0:T(128)S(1)} %dynamic-slice_bitcast_fusion.block_ref, bf16[512,8192]{1,0:T(8,128)(2,1)} %refs_1_.7, bf16[512,8192]{1,0:T(8,128)(2,1)} %refs_1_.7, bf16[512,8192]{1,0:T(8,128)(2,1)} %collective-permute-done.3.refs_2_.refs_3_, bf16[512,8192]{1,0:T(8,128)(2,1)} %collective-permute-done.3.refs_2_.refs_3_, ...), custom_call_target="tpu_custom_call" | custom-call | bytes 262144 | tf_op jit(solution)/shard_map/rows_2a/pallas_call | solution.py:445
  88.1 0.0 collective-permute-done.11.refs_7_
  88.1 7.5 %rows_2b.1.refs_4_ = f32[1024,512]{1,0:T(8,128)S(1)} custom-call(s32[16]{0:T(128)S(1)} %dynamic-slice_bitcast_fusion.block_ref, bf16[512,8192]{1,0:T(8,128)(2,1)} %refs_1_.7, bf16[512,8192]{1,0:T(8,128)(2,1)} %refs_1_.7, bf16[512,8192]{1,0:T(8,128)(2,1)} %collective-permute-done.3.refs_2_.refs_3_, bf16[512,8192]{1,0:T(8,128)(2,1)} %collective-permute-done.3.refs_2_.refs_3_, ...), custom_call_target="tpu_custom_call" | custom-call | bytes 262144 | tf_op jit(solution)/shard_map/rows_2b/pallas_call | solution.py:445
  95.7 0.0 collective-permute-done.15.refs_9_
  95.7 0.0 collective-permute-done.16.refs_10_
  95.7 1.6 %collective-permute-done.13.refs_7_ = bf16[512,512]{1,0:T(8,128)(2,1)} collective-permute-done((bf16[512,512]{1,0:T(8,128)(2,1)}, bf16[512,512]{1,0:T(8,128)(2,1)}, u32[]{:S(2)}, u32[]{:S(2)}) %collective-permute-start.13) | collective-permute-done | bytes 524320 | tf_op jit(solution)/shard_map/ppermute | solution.py:58
  97.3 0.0 collective-permute-done.14.refs_8_
  97.3 8.7 %rows_3.1 = bf16[16,3,16,128]{3,2,1,0:T(8,128)(2,1)S(1)} custom-call(s32[16]{0:T(128)S(1)} %dynamic-slice_bitcast_fusion.block_ref, s32[3,16]{1,0:T(4,128)S(1)} %pad_add_fusion.slot_ref, bf16[512,8192]{1,0:T(8,128)(2,1)} %refs_1_.7, bf16[512,8192]{1,0:T(8,128)(2,1)} %refs_1_.7, bf16[512,8192]{1,0:T(8,128)(2,1)} %collective-permute-done.3.refs_2_.refs_3_, ...), custom_call_target="tpu_custom_call" | custom-call | bytes 262144 | tf_op jit(solution)/shard_map/rows_3/pallas_call | solution.py:445
  106.0 13.8 %all_to_all.10.got_ref = bf16[16,3,16,128]{3,2,1,0:T(8,128)(2,1)S(1)} all-to-all(bf16[16,3,16,128]{3,2,1,0:T(8,128)(2,1)S(1)} %rows_3.1), channel_id=1, replica_groups=mesh['replica'=2,'section'=16] {'section'}, dimensions={0} | all-to-all | bytes 393216 | tf_op jit(solution)/shard_map/all_to_all | solution.py:494
  119.8 2.3 %combine.1 = bf16[8,4096]{1,0:T(8,128)(2,1)} custom-call(bf16[16,3,16,128]{3,2,1,0:T(8,128)(2,1)S(1)} %all_to_all.10.got_ref, f32[8,32,128]{2,1,0:T(8,128)S(1)} %copy-done.5, f32[32,128]{1,0:T(8,128)S(1)} %copy-done.6, f32[32,128]{1,0:T(8,128)S(1)} %copy-done.7), custom_call_target="tpu_custom_call" | custom-call | tf_op jit(solution)/shard_map/combine/pallas_call | solution.py:496
  (20 shorter events, 0.1 us)
Async XLA Ops:
  2.1 2.2 %collective-permute-start = (bf16[512,512]{1,0:T(8,128)(2,1)}, bf16[512,512]{1,0:T(8,128)(2,1)S(1)}, u32[]{:S(2)}, u32[]{:S(2)}) collective-permute-start(bf16[512,512]{1,0:T(8,128)(2,1)} %get-tuple-element.19), channel_id=1, source_target_pairs={{0,1},{1,0},{2,3},{3,2},{4,5},{5,4},{6,7},{7,6},{8,9},{9,8},{10,11... | collective-permute-start | bytes 1572872 | tf_op jit(solution)/shard_map/ppermute | solution.py:30
  4.3 47.1 %collective-permute-start.3 = (bf16[512,8192]{1,0:T(8,128)(2,1)}, bf16[512,8192]{1,0:T(8,128)(2,1)}, u32[]{:S(2)}, u32[]{:S(2)}) collective-permute-start(bf16[512,8192]{1,0:T(8,128)(2,1)} %refs_1_.7), channel_id=1, source_target_pairs={{0,1},{1,0},{2,3},{3,2},{4,5},{5,4},{6,7},{7,6},{8,9},{9,8},{10,11... | collective-permute-start | bytes 25165832 | tf_op jit(solution)/shard_map/ppermute | solution.py:30
  4.7 16.6 %collective-permute-start.1 = (bf16[512,512]{1,0:T(8,128)(2,1)S(1)}, bf16[512,512]{1,0:T(8,128)(2,1)}, u32[]{:S(2)}, u32[]{:S(2)}) collective-permute-start(bf16[512,512]{1,0:T(8,128)(2,1)S(1)} %collective-permute-done.refs_5_), channel_id=1, source_target_pairs={{0,4},{1,5},{2,6},{3,7},{4,12},{5,13},{6,14},{7,15},{12,8},{13,9},... | collective-permute-start | bytes 1572872 | tf_op jit(solution)/shard_map/ppermute | solution.py:50
  7.4 24.8 %collective-permute-start.4 = (bf16[512,512]{1,0:T(8,128)(2,1)}, bf16[512,512]{1,0:T(8,128)(2,1)}, u32[]{:S(2)}, u32[]{:S(2)}) collective-permute-start(bf16[512,512]{1,0:T(8,128)(2,1)} %get-tuple-element.22.refs_5_), channel_id=1, source_target_pairs={{0,4},{1,5},{2,6},{3,7},{4,12},{5,13},{6,14},{7,15},{12,8},{13,9},... | collective-permute-start | bytes 1572872 | tf_op jit(solution)/shard_map/ppermute | solution.py:50
  10.0 36.3 %collective-permute-start.7 = (bf16[512,512]{1,0:T(8,128)(2,1)}, bf16[512,512]{1,0:T(8,128)(2,1)S(1)}, u32[]{:S(2)}, u32[]{:S(2)}) collective-permute-start(bf16[512,512]{1,0:T(8,128)(2,1)} %get-tuple-element.22.refs_5_), channel_id=1, source_target_pairs={{0,2},{1,3},{2,0},{3,1},{4,6},{5,7},{6,4},{7,5},{8,10},{9,11},{10,... | collective-permute-start | bytes 1572872 | tf_op jit(solution)/shard_map/ppermute | solution.py:54
  11.5 37.1 %collective-permute-start.8 = (bf16[512,512]{1,0:T(8,128)(2,1)S(1)}, bf16[512,512]{1,0:T(8,128)(2,1)S(1)}, u32[]{:S(2)}, u32[]{:S(2)}) collective-permute-start(bf16[512,512]{1,0:T(8,128)(2,1)S(1)} %collective-permute-done.refs_5_), channel_id=1, source_target_pairs={{0,2},{1,3},{2,0},{3,1},{4,6},{5,7},{6,4},{7,5},{8,10},{9,11},{10,... | collective-permute-start | bytes 1572872 | tf_op jit(solution)/shard_map/ppermute | solution.py:54
  12.7 8.5 %copy-start.8 = (bf16[8,4096]{1,0:T(8,128)(2,1)S(1)}, bf16[8,4096]{1,0:T(8,128)(2,1)}, u32[]{:S(2)}) copy-start(bf16[8,4096]{1,0:T(8,128)(2,1)} %param.12) | copy-start | bytes 196612
  21.3 29.6 %collective-permute-start.2 = (f32[8,128]{1,0:T(8,128)S(1)}, f32[8,128]{1,0:T(8,128)S(1)}, u32[]{:S(2)}, u32[]{:S(2)}) collective-permute-start(f32[8,128]{1,0:T(8,128)S(1)} %fusion.3), channel_id=1, source_target_pairs={{0,1},{1,0},{2,3},{3,2},{4,5},{5,4},{6,7},{7,6},{8,9},{9,8},{10,11... | collective-permute-start | bytes 12296 | tf_op jit(solution)/shard_map/ppermute | solution.py:30
  33.0 45.2 %all-to-all-start = ((bf16[16,8,2048]{2,1,0:T(8,128)(2,1)}), bf16[16,8,2048]{2,1,0:T(8,128)(2,1)}, u32[]{:S(2)}, u32[]{:S(2)}) async-start(bf16[16,8,2048]{2,1,0:T(8,128)(2,1)} %bitcast.9), calls=%async_computation | async-start | bytes 1048576 | tf_op jit(solution)/shard_map/all_to_all | solution.py:368
  44.4 17.8 %collective-permute-start.5 = (bf16[512,512]{1,0:T(8,128)(2,1)}, bf16[512,512]{1,0:T(8,128)(2,1)}, u32[]{:S(2)}, u32[]{:S(2)}) collective-permute-start(bf16[512,512]{1,0:T(8,128)(2,1)} %collective-permute-done.4.refs_4_), channel_id=1, source_target_pairs={{0,2},{1,3},{2,0},{3,1},{4,6},{5,7},{6,4},{7,5},{8,10},{9,11},{10,... | collective-permute-start | bytes 1572872 | tf_op jit(solution)/shard_map/ppermute | solution.py:54
  46.3 0.8 copy-start.1
  47.1 25.8 %collective-permute-start.6 = (bf16[512,512]{1,0:T(8,128)(2,1)}, bf16[512,512]{1,0:T(8,128)(2,1)}, u32[]{:S(2)}, u32[]{:S(2)}) collective-permute-start(bf16[512,512]{1,0:T(8,128)(2,1)} %collective-permute-done.4.refs_4_), channel_id=1, source_target_pairs={{0,4},{1,5},{2,6},{3,7},{4,12},{5,13},{6,14},{7,15},{12,8},{13,9},... | collective-permute-start | bytes 1572872 | tf_op jit(solution)/shard_map/ppermute | solution.py:50
  48.6 0.8 copy-start.3
  49.4 25.4 %collective-permute-start.9 = (bf16[512,512]{1,0:T(8,128)(2,1)}, bf16[512,512]{1,0:T(8,128)(2,1)}, u32[]{:S(2)}, u32[]{:S(2)}) collective-permute-start(bf16[512,512]{1,0:T(8,128)(2,1)} %collective-permute-done.4.refs_4_), channel_id=1, source_target_pairs={{0,16},{16,0},{1,17},{17,1},{2,18},{18,2},{3,19},{19,3},{4,20},{20... | collective-permute-start | bytes 1572872 | tf_op jit(solution)/shard_map/ppermute | solution.py:58
  50.9 26.1 %collective-permute-start.10 = (bf16[512,512]{1,0:T(8,128)(2,1)}, bf16[512,512]{1,0:T(8,128)(2,1)}, u32[]{:S(2)}, u32[]{:S(2)}) collective-permute-start(bf16[512,512]{1,0:T(8,128)(2,1)} %collective-permute-done.1.refs_6_), channel_id=1, source_target_pairs={{0,16},{16,0},{1,17},{17,1},{2,18},{18,2},{3,19},{19,3},{4,20},{20... | collective-permute-start | bytes 1572872 | tf_op jit(solution)/shard_map/ppermute | solution.py:58
  51.4 20.9 %collective-permute-start.12 = (bf16[512,512]{1,0:T(8,128)(2,1)}, bf16[512,512]{1,0:T(8,128)(2,1)}, u32[]{:S(2)}, u32[]{:S(2)}) collective-permute-start(bf16[512,512]{1,0:T(8,128)(2,1)} %collective-permute-done.1.refs_6_), channel_id=1, source_target_pairs={{0,2},{1,3},{2,0},{3,1},{4,6},{5,7},{6,4},{7,5},{8,10},{9,11},{10,... | collective-permute-start | bytes 1572872 | tf_op jit(solution)/shard_map/ppermute | solution.py:54
  52.9 1.0 copy-start.2
  54.0 1.0 copy-start.4
  55.0 23.1 %copy-start.9 = (s32[8]{0:T(128)S(1)}, s32[8]{0:T(128)}, u32[]{:S(2)}) copy-start(s32[8]{0:T(128)} %param.11) | copy-start | bytes 100
  55.0 23.1 %copy-start.10 = (s32[8]{0:T(128)S(1)}, s32[8]{0:T(128)}, u32[]{:S(2)}) copy-start(s32[8]{0:T(128)} %param.10) | copy-start | bytes 100
  62.3 25.9 %collective-permute-start.11 = (bf16[512,512]{1,0:T(8,128)(2,1)}, bf16[512,512]{1,0:T(8,128)(2,1)}, u32[]{:S(2)}, u32[]{:S(2)}) collective-permute-start(bf16[512,512]{1,0:T(8,128)(2,1)} %collective-permute-done.1.refs_6_), channel_id=1, source_target_pairs={{0,4},{1,5},{2,6},{3,7},{4,12},{5,13},{6,14},{7,15},{12,8},{13,9},... | collective-permute-start | bytes 1572872 | tf_op jit(solution)/shard_map/ppermute | solution.py:50
  72.3 23.4 %collective-permute-start.15 = (bf16[512,512]{1,0:T(8,128)(2,1)}, bf16[512,512]{1,0:T(8,128)(2,1)}, u32[]{:S(2)}, u32[]{:S(2)}) collective-permute-start(bf16[512,512]{1,0:T(8,128)(2,1)} %collective-permute-done.12.refs_8_), channel_id=1, source_target_pairs={{0,16},{16,0},{1,17},{17,1},{2,18},{18,2},{3,19},{19,3},{4,20},{20... | collective-permute-start | bytes 1572872 | tf_op jit(solution)/shard_map/ppermute | solution.py:58
  72.9 22.8 %collective-permute-start.16 = (bf16[512,512]{1,0:T(8,128)(2,1)}, bf16[512,512]{1,0:T(8,128)(2,1)}, u32[]{:S(2)}, u32[]{:S(2)}) collective-permute-start(bf16[512,512]{1,0:T(8,128)(2,1)} %collective-permute-done.12.refs_8_), channel_id=1, source_target_pairs={{0,4},{1,5},{2,6},{3,7},{4,12},{5,13},{6,14},{7,15},{12,8},{13,9},... | collective-permute-start | bytes 1572872 | tf_op jit(solution)/shard_map/ppermute | solution.py:50
  74.7 22.6 %collective-permute-start.13 = (bf16[512,512]{1,0:T(8,128)(2,1)}, bf16[512,512]{1,0:T(8,128)(2,1)}, u32[]{:S(2)}, u32[]{:S(2)}) collective-permute-start(bf16[512,512]{1,0:T(8,128)(2,1)} %collective-permute-done.5.refs_8_), channel_id=1, source_target_pairs={{0,16},{16,0},{1,17},{17,1},{2,18},{18,2},{3,19},{19,3},{4,20},{20... | collective-permute-start | bytes 1572872 | tf_op jit(solution)/shard_map/ppermute | solution.py:58
  76.9 20.4 %collective-permute-start.14 = (bf16[512,512]{1,0:T(8,128)(2,1)}, bf16[512,512]{1,0:T(8,128)(2,1)}, u32[]{:S(2)}, u32[]{:S(2)}) collective-permute-start(bf16[512,512]{1,0:T(8,128)(2,1)} %collective-permute-done.6.refs_7_), channel_id=1, source_target_pairs={{0,2},{1,3},{2,0},{3,1},{4,6},{5,7},{6,4},{7,5},{8,10},{9,11},{10,... | collective-permute-start | bytes 1572872 | tf_op jit(solution)/shard_map/ppermute | solution.py:54
  79.5 1.0 copy-start
  97.3 22.5 %copy-start.5 = (f32[8,32,128]{2,1,0:T(8,128)S(1)}, f32[8,32,128]{2,1,0:T(8,128)}, u32[]{:S(2)}) copy-start(f32[8,32,128]{2,1,0:T(8,128)} %get-tuple-element.30.res_out_ref) | copy-start | bytes 393220
  97.3 22.5 %copy-start.6 = (f32[32,128]{1,0:T(8,128)S(1)}, f32[32,128]{1,0:T(8,128)}, u32[]{:S(2)}) copy-start(f32[32,128]{1,0:T(8,128)} %get-tuple-element.31.res_top_ref) | copy-start | bytes 49156
  97.3 22.5 %copy-start.7 = (f32[32,128]{1,0:T(8,128)S(1)}, f32[32,128]{1,0:T(8,128)}, u32[]{:S(2)}) copy-start(f32[32,128]{1,0:T(8,128)} %get-tuple-element.32.res_sum_ref) | copy-start | bytes 49156

commit v7 on v6

--- a/solution.py
+++ b/solution.py
@@ -77,9 +77,8 @@
                     out.append(chip * 2 + (core ^ other))
                 return out
 
-            (own_a, *one_a), (own_b, *one_b) = blocks(0, 0), blocks(0, 1)
-            two_a, two_b = blocks(1, 0), blocks(1, 1)
-            table.append(one_a + one_b + [own_a] + two_a + [own_b] + two_b + blocks(2, 0) + blocks(2, 1))
+            one, two, three = (blocks(step, 0) + blocks(step, 1) for step in range(3))
+            table.append(one + two + three)
     return np.array(table, np.int32)
 
 
@@ -333,26 +332,27 @@
         name="split",
     )(core.reshape(1), kv_weight, kv_weight)
     taken = swap_core(give)
-    states, _ = lax.optimization_barrier((prompt_states, taken))
-    squares = pl.pallas_call(
-        square_kernel,
-        grid=(8,),
-        in_specs=[pl.BlockSpec((tokens // 8, width), lambda i: (i, 0))],
-        out_specs=pl.BlockSpec((tokens // 8, 1), lambda i: (i, 0)),
-        out_shape=jax.ShapeDtypeStruct((tokens, 1), jnp.float32),
-        cost_estimate=pl.CostEstimate(flops=0, bytes_accessed=2**18, transcendentals=0),
-        compiler_params=pltpu.CompilerParams(vmem_limit_bytes=32 * 2**20),
-        name="squares",
-    )(pltpu.with_memory_space_constraint(states, pltpu.HBM))[:, 0]
-    other = swap_core(states)
-
-    places = jnp.concatenate([image_owner, image_row]).astype(jnp.float32)
-    small = jnp.concatenate([squares, places])
-    small = jnp.pad(small, (0, -small.shape[0] % (8 * HD))).reshape(-1, HD)
-
-    def finish_small(tied):
-        mine, _ = lax.optimization_barrier((small, tied))
-        got = swap_core(mine).reshape(-1)
+    swapped_states, _ = lax.optimization_barrier((prompt_states, keep))
+    other = swap_core(swapped_states)
+
+    def square_sums(tied):
+        states, _ = lax.optimization_barrier((prompt_states, tied))
+        return pl.pallas_call(
+            square_kernel,
+            grid=(8,),
+            in_specs=[pl.BlockSpec((tokens // 8, width), lambda i: (i, 0))],
+            out_specs=pl.BlockSpec((tokens // 8, 1), lambda i: (i, 0)),
+            out_shape=jax.ShapeDtypeStruct((tokens, 1), jnp.float32),
+            cost_estimate=pl.CostEstimate(flops=0, bytes_accessed=2**18, transcendentals=0),
+            compiler_params=pltpu.CompilerParams(vmem_limit_bytes=32 * 2**20),
+            name="squares",
+        )(pltpu.with_memory_space_constraint(states, pltpu.HBM))[:, 0]
+
+    def swap_small(squares):
+        places = jnp.concatenate([image_owner, image_row]).astype(jnp.float32)
+        small = jnp.concatenate([squares, places])
+        small = jnp.pad(small, (0, -small.shape[0] % (8 * HD))).reshape(-1, HD)
+        got = swap_core(small).reshape(-1)
         factor = jnp.concatenate([squares, got[:tokens]])[:, None]
         at = tokens + images
         owners = jnp.concatenate([image_owner, got[tokens:at].astype(jnp.int32)])
@@ -463,26 +463,36 @@
         def starts(*arrays):
             return [(array, 0) for array in arrays]
 
-        a1 = (along_ring(keep), across_y(keep))
-        b1 = (along_ring(taken), across_y(taken))
-        a2 = (across_replica(a1[0]), along_ring(a1[0]), across_y(a1[0]))
-        all_q = gather_queries(a1[0])
-        length, _ = lax.optimization_barrier((context_length, squares))
+        tie = lax.optimization_barrier
+        a_behind, a_own_y = along_ring(keep), across_y(keep)
+
+        from_a, from_b, done = tie((a_behind, taken, a_own_y))
+        b_behind, b_own_y, a_ahead = along_ring(from_b), across_y(from_b), across_replica(from_a)
+        squares = square_sums(done)
+        all_q = gather_queries(squares)
+
+        from_a, from_b, squares, _ = tie((a_behind, b_behind, squares, (b_own_y, a_ahead, other)))
+        a_opposite, a_behind_y, b_ahead = along_ring(from_a), across_y(from_a), across_replica(from_b)
+        factor, owners, rows = swap_small(squares)
+        total = product(blocks, 0, starts(keep, a_behind, a_own_y, taken, b_behind, b_own_y), None, "rows_1")
+
+        from_a, from_b, total, done = tie((a_behind_y, b_behind, total, (a_opposite, b_ahead)))
+        b_opposite, b_behind_y, a_ahead_y = along_ring(from_b), across_y(from_b), across_replica(from_a)
+        all_q, owners, rows, _ = tie((all_q, owners, rows, done))
+        image_q, slot = place_images(all_q, owners, rows)
+
+        from_a, from_b, image_q, slot, _ = tie((a_opposite, b_behind_y, image_q, slot, (b_opposite, a_ahead_y)))
+        a_opposite_y, b_ahead_y, b_opposite_y = across_y(from_a), across_replica(from_b), along_ring(from_b)
+        twos = starts(a_ahead, a_opposite, a_behind_y, b_ahead, b_opposite, b_behind_y)
+        total = product(blocks, 6, twos, total, "rows_2")
+        threes = starts(a_ahead_y, a_opposite_y, b_ahead_y, b_opposite_y)
+        slots = product(blocks, 12, threes, total, "rows_3", last=(image_q, slot, factor))
+        length, slots = tie((context_length, slots))
         res_out, res_top, res_sum = resident(length)
-        b_behind, res_out = lax.optimization_barrier((b1[0], res_out))
-        b2 = (across_replica(b_behind), along_ring(b_behind), across_y(b_behind))
-        factor, owners, rows = finish_small(b1[0])
-        total = product(blocks, 0, starts(*a1, *b1), None, "rows_1")
-        a_behind_y, a_opposite, total = lax.optimization_barrier((a2[2], a2[1], total))
-        a3 = (across_replica(a_behind_y), across_y(a_opposite))
-        image_q, slot = place_images(all_q, owners, rows)
-        b3 = (across_replica(b2[2]), along_ring(b2[2]))
-        total = product(blocks, 4, starts(keep, *a2), total, "rows_2a")
-        total = product(blocks, 8, starts(taken, *b2), total, "rows_2b")
-        slots = product(blocks, 12, starts(*a3, *b3), total, "rows_3", last=(image_q, slot, factor))
     else:
         res_out, res_top, res_sum = resident(context_length)
-        factor, owners, rows = finish_small(squares)
+        squares = square_sums(taken)
+        factor, owners, rows = swap_small(squares)
         image_q, slot = place_images(gather_queries(squares), owners, rows)
         a = gather_plain(keep)
         b = gather_plain(taken)

time: 123 us -> 123 us (level)
  blocking collectives: 13.8 us -> 0 us
  waiting for transfers between devices: 22.9 us -> 34.8 us
  local copies, waits for them, and re-layouts: 7.15 us -> 13.5 us
  Pallas kernels: 47.5 us -> 44.6 us
  starting transfers between devices: 28.3 us -> 26.9 us
    all_to_all x1 -> x0, blocking collectives: 13.8 us -> none  [per_device(): lax.all_to_all(slots, 'section', split_axis=0, concat_axis=0, tiled=True)]
    ppermute x5, waiting for transfers between devices: 11.9 us -> 20.8 us  [along_ring(): return lax.ppermute(x, ('replica', 'section'), perm)]
    unnamed x24 -> x36, local copies, waits for them, and re-layouts: 5.38 us -> 11.7 us
    all_to_all x0 -> x1, starting transfers between devices: none -> 4.38 us  [per_device(): lax.all_to_all(slots, 'section', split_axis=0, concat_axis=0, tiled=True)]
    ppermute x5, waiting for transfers between devices: 7.58 us -> 11 us  [across_y(): return lax.ppermute(x, 'section', [(i, i ^ 2) for i in range(16)])]
    all_to_all x0 -> x1, waiting for transfers between devices: none -> 3 us  [per_device(): lax.all_to_all(slots, 'section', split_axis=0, concat_axis=0, tiled=True)]
    pallas_call x4 -> x3, Pallas kernels: 31 us -> 28.2 us  [product(): pl.pallas_call(body, grid_spec=pltpu.PrefetchScalarGridSpec(num_scalar_pr...]
    ppermute x5, starting transfers between devices: 11 us -> 8.23 us  [along_ring(): return lax.ppermute(x, ('replica', 'section'), perm)]
  transfers between devices with their start and end apart: 18 -> 19, of which waited for: 5 -> 7; matrix products, arithmetic and copies ran while one was open for 4% -> 3% of each run, Pallas kernels for 28% -> 25%
where the time goes in v7:
time: 123 us; the launch traced here: 122 us
  Pallas kernels  44.6 us (36%)
  waiting for transfers between devices  34.8 us (28%)
  starting transfers between devices  26.9 us (22%)
  local copies, waits for them, and re-layouts  13.5 us (11%)
  matrix products  1.27 us (1%)
    pallas_call x3, Pallas kernels, product(): pl.pallas_call(body, grid_spec=pltpu.PrefetchScalarGridSpec(num_scalar_pr...  28.2 us
    ppermute x5, waiting for transfers between devices, along_ring(): return lax.ppermute(x, ('replica', 'section'), perm)  20.8 us
    unnamed x36, local copies, waits for them, and re-layouts  11.7 us
    ppermute x5, waiting for transfers between devices, across_y(): return lax.ppermute(x, 'section', [(i, i ^ 2) for i in range(16)])  11 us
    ppermute x5, starting transfers between devices, along_ring(): return lax.ppermute(x, ('replica', 'section'), perm)  8.23 us
    pallas_call x1, Pallas kernels, square_sums(): pl.pallas_call(square_kernel, grid=(8,), in_specs=[pl.BlockSpec((tokens /...  6.68 us
    ppermute x5, starting transfers between devices, across_y(): return lax.ppermute(x, 'section', [(i, i ^ 2) for i in range(16)])  6.54 us
    pallas_call x1, Pallas kernels, resident(): pl.pallas_call(resident_kernel, grid_spec=pltpu.PrefetchScalarGridSpec(nu...  5.35 us
  transfers between devices with their start and end apart: 19, of which 7 were waited for; matrix products, arithmetic and copies ran while one was open for 3% of the time, Pallas kernels for 25%

profile of v7, /device:TPU:0, one launch (start us, length us, event | category | flops | bytes accessed | tf_op | source)
XLA Modules:
  0.0 121.7 jit_solution(4629398194755396022)
XLA Ops:
  0.0 2.1 %split.1 = (bf16[512,512]{1,0:T(8,128)(2,1)}, bf16[512,512]{1,0:T(8,128)(2,1)}) custom-call(s32[1]{0:T(128)} %bitcast.1.core_ref, bf16[512,1024]{1,0:T(8,128)(2,1)} %give_in.1, bf16[512,1024]{1,0:T(8,128)(2,1)} %give_in.1), custom_call_target="tpu_custom_call" | custom-call | bytes 262144 | tf_op jit(solution)/shard_map/split/pallas_call | solution.py:319
  2.1 0.5 collective-permute-start.6
  2.5 2.6 %collective-permute-start = (bf16[512,512]{1,0:T(8,128)(2,1)}, bf16[512,512]{1,0:T(8,128)(2,1)}, u32[]{:S(2)}, u32[]{:S(2)}) collective-permute-start(bf16[512,512]{1,0:T(8,128)(2,1)} %get-tuple-element.29.refs_4_), channel_id=1, source_target_pairs={{0,4},{1,5},{2,6},{3,7},{4,12},{5,13},{6,14},{7,15},{12,8},{13,9},... | collective-permute-start | bytes 1572872 | tf_op jit(solution)/shard_map/ppermute | solution.py:50
  5.1 1.5 %collective-permute-start.2 = (bf16[512,512]{1,0:T(8,128)(2,1)}, bf16[512,512]{1,0:T(8,128)(2,1)S(1)}, u32[]{:S(2)}, u32[]{:S(2)}) collective-permute-start(bf16[512,512]{1,0:T(8,128)(2,1)} %get-tuple-element.29.refs_4_), channel_id=1, source_target_pairs={{0,2},{1,3},{2,0},{3,1},{4,6},{5,7},{6,4},{7,5},{8,10},{9,11},{10,... | collective-permute-start | bytes 1572872 | tf_op jit(solution)/shard_map/ppermute | solution.py:54
  6.6 0.0 collective-permute-start.1
  6.6 12.4 %collective-permute-done.refs_5_ = bf16[512,512]{1,0:T(8,128)(2,1)} collective-permute-done((bf16[512,512]{1,0:T(8,128)(2,1)}, bf16[512,512]{1,0:T(8,128)(2,1)}, u32[]{:S(2)}, u32[]{:S(2)}) %collective-permute-start) | collective-permute-done | bytes 524320 | tf_op jit(solution)/shard_map/ppermute | solution.py:50
  19.0 0.3 collective-permute-done.2.refs_6_
  19.4 0.8 copy-done.5
  20.2 0.0 collective-permute-done.1.refs_7_
  20.2 2.6 %collective-permute-start.3 = (bf16[512,512]{1,0:T(8,128)(2,1)S(1)}, bf16[512,512]{1,0:T(8,128)(2,1)S(1)}, u32[]{:S(2)}, u32[]{:S(2)}) collective-permute-start(bf16[512,512]{1,0:T(8,128)(2,1)S(1)} %collective-permute-done.1.refs_7_), channel_id=1, source_target_pairs={{0,4},{1,5},{2,6},{3,7},{4,12},{5,13},{6,14},{7,15},{12,8},{13,9},... | collective-permute-start | bytes 1572872 | tf_op jit(solution)/shard_map/ppermute | solution.py:50
  22.8 1.5 %collective-permute-start.4 = (bf16[512,512]{1,0:T(8,128)(2,1)S(1)}, bf16[512,512]{1,0:T(8,128)(2,1)S(1)}, u32[]{:S(2)}, u32[]{:S(2)}) collective-permute-start(bf16[512,512]{1,0:T(8,128)(2,1)S(1)} %collective-permute-done.1.refs_7_), channel_id=1, source_target_pairs={{0,2},{1,3},{2,0},{3,1},{4,6},{5,7},{6,4},{7,5},{8,10},{9,11},{10,... | collective-permute-start | bytes 1572872 | tf_op jit(solution)/shard_map/ppermute | solution.py:54
  24.3 1.5 %collective-permute-start.5 = (bf16[512,512]{1,0:T(8,128)(2,1)}, bf16[512,512]{1,0:T(8,128)(2,1)S(1)}, u32[]{:S(2)}, u32[]{:S(2)}) collective-permute-start(bf16[512,512]{1,0:T(8,128)(2,1)} %collective-permute-done.refs_5_), channel_id=1, source_target_pairs={{0,16},{16,0},{1,17},{17,1},{2,18},{18,2},{3,19},{19,3},{4,20},{20... | collective-permute-start | bytes 1572872 | tf_op jit(solution)/shard_map/ppermute | solution.py:58
  25.8 6.7 %squares.1 = f32[512,1]{1,0:T(8,128)S(1)} custom-call(bf16[512,8192]{1,0:T(8,128)(2,1)} %refs_1_.5), custom_call_target="tpu_custom_call" | custom-call | bytes 262144 | tf_op jit(solution)/shard_map/squares/pallas_call | solution.py:340
  32.4 0.1 reduce
  32.6 0.9 broadcast_in_dim.6
  33.5 4.2 %all-to-all-start = ((bf16[16,8,2048]{2,1,0:T(8,128)(2,1)}), bf16[16,8,2048]{2,1,0:T(8,128)(2,1)}, u32[]{:S(2)}, u32[]{:S(2)}) async-start(bf16[16,8,2048]{2,1,0:T(8,128)(2,1)} %bitcast.4), calls=%async_computation | async-start | bytes 1048576 | tf_op jit(solution)/shard_map/all_to_all | solution.py:368
  37.7 0.1 add_convert_fusion
  37.8 0.0 collective-permute-done.3.refs_8_
  37.8 0.0 collective-permute-done.4.refs_9_
  37.8 0.8 copy-done.9
  38.7 0.0 collective-permute-done.5.refs_5_
  38.7 0.0 collective-permute-done.6.refs_2_.refs_3_
  38.7 1.8 %collective-permute-start.7 = (bf16[512,512]{1,0:T(8,128)(2,1)}, bf16[512,512]{1,0:T(8,128)(2,1)S(1)}, u32[]{:S(2)}, u32[]{:S(2)}) collective-permute-start(bf16[512,512]{1,0:T(8,128)(2,1)} %collective-permute-done.refs_5_), channel_id=1, source_target_pairs={{0,4},{1,5},{2,6},{3,7},{4,12},{5,13},{6,14},{7,15},{12,8},{13,9},... | collective-permute-start | bytes 1572872 | tf_op jit(solution)/shard_map/ppermute | solution.py:50
  40.4 1.5 %collective-permute-start.8 = (bf16[512,512]{1,0:T(8,128)(2,1)}, bf16[512,512]{1,0:T(8,128)(2,1)}, u32[]{:S(2)}, u32[]{:S(2)}) collective-permute-start(bf16[512,512]{1,0:T(8,128)(2,1)} %collective-permute-done.refs_5_), channel_id=1, source_target_pairs={{0,2},{1,3},{2,0},{3,1},{4,6},{5,7},{6,4},{7,5},{8,10},{9,11},{10,... | collective-permute-start | bytes 1572872 | tf_op jit(solution)/shard_map/ppermute | solution.py:54
  41.9 1.5 %collective-permute-start.9 = (bf16[512,512]{1,0:T(8,128)(2,1)S(1)}, bf16[512,512]{1,0:T(8,128)(2,1)S(1)}, u32[]{:S(2)}, u32[]{:S(2)}) collective-permute-start(bf16[512,512]{1,0:T(8,128)(2,1)S(1)} %collective-permute-done.3.refs_8_), channel_id=1, source_target_pairs={{0,16},{16,0},{1,17},{17,1},{2,18},{18,2},{3,19},{19,3},{4,20},{20... | collective-permute-start | bytes 1572872 | tf_op jit(solution)/shard_map/ppermute | solution.py:58
  43.4 0.7 dynamic-slice_bitcast_fusion.block_ref
  44.1 0.1 collective-permute-start.11
  44.2 1.0 copy-done.2
  45.2 1.0 copy-done.6
  46.2 1.0 copy-done.8
  47.3 1.0 copy-done.10
  48.3 9.7 %rows_1.1.refs_4_ = f32[1024,512]{1,0:T(8,128)S(1)} custom-call(s32[16]{0:T(128)S(1)} %dynamic-slice_bitcast_fusion.block_ref, bf16[512,8192]{1,0:T(8,128)(2,1)} %refs_1_.5, bf16[512,8192]{1,0:T(8,128)(2,1)} %refs_1_.5, bf16[512,8192]{1,0:T(8,128)(2,1)} %collective-permute-done.6.refs_2_.refs_3_, bf16[512,8192]{1,0:T(8,128)(2,1)} %collective-permute-done.6.refs_2_.refs_3_, ...), custom_call_target="tpu_custom_call" | custom-call | bytes 262144 | tf_op jit(solution)/shard_map/rows_1/pallas_call | solution.py:445
  58.0 0.0 collective-permute-done.11
  58.0 0.1 slice_convert_fusion
  58.1 6.0 %collective-permute-done.7.refs_6_ = bf16[512,512]{1,0:T(8,128)(2,1)S(1)} collective-permute-done((bf16[512,512]{1,0:T(8,128)(2,1)}, bf16[512,512]{1,0:T(8,128)(2,1)S(1)}, u32[]{:S(2)}, u32[]{:S(2)}) %collective-permute-start.7) | collective-permute-done | bytes 524320 | tf_op jit(solution)/shard_map/ppermute | solution.py:50
  64.1 0.0 collective-permute-done.8.refs_7_
  64.1 0.0 collective-permute-done.9.refs_8_
  64.1 0.8 copy-done.3
  65.0 1.5 %collective-permute-start.10 = (bf16[512,512]{1,0:T(8,128)(2,1)S(1)}, bf16[512,512]{1,0:T(8,128)(2,1)}, u32[]{:S(2)}, u32[]{:S(2)}) collective-permute-start(bf16[512,512]{1,0:T(8,128)(2,1)S(1)} %collective-permute-done.3.refs_8_), channel_id=1, source_target_pairs={{0,2},{1,3},{2,0},{3,1},{4,6},{5,7},{6,4},{7,5},{8,10},{9,11},{10,... | collective-permute-start | bytes 1572872 | tf_op jit(solution)/shard_map/ppermute | solution.py:54
  66.4 0.0 collective-permute-start.12
  66.5 0.1 pad_add_fusion.1
  66.5 0.0 all-to-all-done
  66.5 1.3 %fusion = bf16[2,8,16,128]{3,1,2,0:T(8,128)(2,1)S(1)} fusion(bf16[128,2048]{1,0:T(8,128)(2,1)} %bitcast.5, s32[16]{0:T(128)S(1)} %multiply_add_fusion), kind=kOutput, calls=%fused_computation.1 | convolution fusion | flops 8423424 | bytes 589888 | tf_op jit(solution)/shard_map/dot_general | solution.py:374
  67.9 10.7 %collective-permute-done.10.refs_10_ = bf16[512,512]{1,0:T(8,128)(2,1)} collective-permute-done((bf16[512,512]{1,0:T(8,128)(2,1)S(1)}, bf16[512,512]{1,0:T(8,128)(2,1)}, u32[]{:S(2)}, u32[]{:S(2)}) %collective-permute-start.10) | collective-permute-done | bytes 524320 | tf_op jit(solution)/shard_map/ppermute | solution.py:54
  78.5 2.1 %collective-permute-done.12.refs_9_ = bf16[512,512]{1,0:T(8,128)(2,1)} collective-permute-done((bf16[512,512]{1,0:T(8,128)(2,1)S(1)}, bf16[512,512]{1,0:T(8,128)(2,1)}, u32[]{:S(2)}, u32[]{:S(2)}) %collective-permute-start.12) | collective-permute-done | bytes 524320 | tf_op jit(solution)/shard_map/ppermute | solution.py:50
  80.6 0.0 collective-permute-done.13.refs_7_
  80.6 0.6 collective-permute-start.14
  81.2 0.0 collective-permute-start.15
  81.2 1.3 %collective-permute-start.16 = (bf16[512,512]{1,0:T(8,128)(2,1)}, bf16[512,512]{1,0:T(8,128)(2,1)}, u32[]{:S(2)}, u32[]{:S(2)}) collective-permute-start(bf16[512,512]{1,0:T(8,128)(2,1)} %collective-permute-done.10.refs_10_), channel_id=1, source_target_pairs={{0,4},{1,5},{2,6},{3,7},{4,12},{5,13},{6,14},{7,15},{12,8},{13,9},... | collective-permute-start | bytes 1572872 | tf_op jit(solution)/shard_map/ppermute | solution.py:50
  82.5 0.2 copy.11.refs_6_
  82.8 1.0 copy-done.1
  83.8 1.0 copy-done.4
  84.8 9.2 %rows_2.1.refs_4_ = f32[1024,512]{1,0:T(8,128)S(1)} custom-call(s32[16]{0:T(128)S(1)} %dynamic-slice_bitcast_fusion.block_ref, bf16[512,8192]{1,0:T(8,128)(2,1)} %refs_1_.5, bf16[512,8192]{1,0:T(8,128)(2,1)} %refs_1_.5, bf16[512,8192]{1,0:T(8,128)(2,1)} %collective-permute-done.6.refs_2_.refs_3_, bf16[512,8192]{1,0:T(8,128)(2,1)} %collective-permute-done.6.refs_2_.refs_3_, ...), custom_call_target="tpu_custom_call" | custom-call | bytes 262144 | tf_op jit(solution)/shard_map/rows_2/pallas_call | solution.py:445
  94.0 0.0 collective-permute-done.14.refs_8_
  94.1 0.3 collective-permute-done.16.refs_10_
  94.4 9.3 %rows_3.1 = bf16[16,3,16,128]{3,2,1,0:T(8,128)(2,1)} custom-call(s32[16]{0:T(128)S(1)} %dynamic-slice_bitcast_fusion.block_ref, s32[3,16]{1,0:T(4,128)S(1)} %pad_add_fusion.slot_ref, bf16[512,8192]{1,0:T(8,128)(2,1)} %refs_1_.5, bf16[512,8192]{1,0:T(8,128)(2,1)} %refs_1_.5, bf16[512,8192]{1,0:T(8,128)(2,1)} %collective-permute-done.6.refs_2_.refs_3_, ...), custom_call_target="tpu_custom_call" | custom-call | bytes 262144 | tf_op jit(solution)/shard_map/rows_3/pallas_call | solution.py:445
  103.7 4.4 %all-to-all-start.1 = ((bf16[16,3,16,128]{3,2,1,0:T(8,128)(2,1)}), bf16[16,3,16,128]{3,2,1,0:T(8,128)(2,1)S(1)}, u32[]{:S(2)}, u32[]{:S(2)}) async-start(bf16[16,3,16,128]{3,2,1,0:T(8,128)(2,1)} %rows_3.1), calls=%async_computation.1 | async-start | bytes 393216 | tf_op jit(solution)/shard_map/all_to_all | solution.py:504
  108.1 0.6 copy.16
  108.8 5.4 %resident.1 = (f32[8,32,128]{2,1,0:T(8,128)}, f32[32,128]{1,0:T(8,128)}, f32[32,128]{1,0:T(8,128)}) custom-call(s32[8]{0:T(128)} %length_ref, bf16[8,32,128]{2,1,0:T(8,128)(2,1)} %bitcast.33, bf16[8,256,1024]{2,1,0:T(8,128)(2,1)} %cache_ref.1), custom_call_target="tpu_custom_call" | custom-call | bytes 262144 | tf_op jit(solution)/shard_map/resident/pallas_call | solution.py:381
  114.1 3.0 %all-to-all-done.1.got_ref = bf16[16,3,16,128]{3,2,1,0:T(8,128)(2,1)S(1)} async-done(((bf16[16,3,16,128]{3,2,1,0:T(8,128)(2,1)}), bf16[16,3,16,128]{3,2,1,0:T(8,128)(2,1)S(1)}, u32[]{:S(2)}, u32[]{:S(2)}) %all-to-all-start.1) | async-done | bytes 196640 | tf_op jit(solution)/shard_map/all_to_all | solution.py:504
  117.1 0.9 copy-done.11
  118.0 0.7 copy-done.12
  118.7 0.7 copy-done.13
  119.5 2.3 %combine.1 = bf16[8,4096]{1,0:T(8,128)(2,1)} custom-call(bf16[16,3,16,128]{3,2,1,0:T(8,128)(2,1)S(1)} %all-to-all-done.1.got_ref, f32[8,32,128]{2,1,0:T(8,128)S(1)} %copy-done.11, f32[32,128]{1,0:T(8,128)S(1)} %copy-done.12, f32[32,128]{1,0:T(8,128)S(1)} %copy-done.13), custom_call_target="tpu_custom_call" | custom-call | tf_op jit(solution)/shard_map/combine/pallas_call | solution.py:506
  (33 shorter events, 0.1 us)
Async XLA Ops:
  2.1 36.6 %collective-permute-start.6 = (bf16[512,8192]{1,0:T(8,128)(2,1)}, bf16[512,8192]{1,0:T(8,128)(2,1)}, u32[]{:S(2)}, u32[]{:S(2)}) collective-permute-start(bf16[512,8192]{1,0:T(8,128)(2,1)} %refs_1_.5), channel_id=1, source_target_pairs={{0,1},{1,0},{2,3},{3,2},{4,5},{5,4},{6,7},{7,6},{8,9},{9,8},{10,11... | collective-permute-start | bytes 25165832 | tf_op jit(solution)/shard_map/ppermute | solution.py:30
  2.5 16.5 %collective-permute-start = (bf16[512,512]{1,0:T(8,128)(2,1)}, bf16[512,512]{1,0:T(8,128)(2,1)}, u32[]{:S(2)}, u32[]{:S(2)}) collective-permute-start(bf16[512,512]{1,0:T(8,128)(2,1)} %get-tuple-element.29.refs_4_), channel_id=1, source_target_pairs={{0,4},{1,5},{2,6},{3,7},{4,12},{5,13},{6,14},{7,15},{12,8},{13,9},... | collective-permute-start | bytes 1572872 | tf_op jit(solution)/shard_map/ppermute | solution.py:50
  5.1 14.3 %collective-permute-start.2 = (bf16[512,512]{1,0:T(8,128)(2,1)}, bf16[512,512]{1,0:T(8,128)(2,1)S(1)}, u32[]{:S(2)}, u32[]{:S(2)}) collective-permute-start(bf16[512,512]{1,0:T(8,128)(2,1)} %get-tuple-element.29.refs_4_), channel_id=1, source_target_pairs={{0,2},{1,3},{2,0},{3,1},{4,6},{5,7},{6,4},{7,5},{8,10},{9,11},{10,... | collective-permute-start | bytes 1572872 | tf_op jit(solution)/shard_map/ppermute | solution.py:54
  6.6 26.0 %copy-start.14 = (bf16[8,4096]{1,0:T(8,128)(2,1)S(1)}, bf16[8,4096]{1,0:T(8,128)(2,1)}, u32[]{:S(2)}) copy-start(bf16[8,4096]{1,0:T(8,128)(2,1)} %param.12) | copy-start | bytes 196612
  6.6 31.1 %copy-start.15 = (s32[8]{0:T(128)S(1)}, s32[8]{0:T(128)}, u32[]{:S(2)}) copy-start(s32[8]{0:T(128)} %param.11) | copy-start | bytes 100
  6.6 31.1 %copy-start.16 = (s32[8]{0:T(128)S(1)}, s32[8]{0:T(128)}, u32[]{:S(2)}) copy-start(s32[8]{0:T(128)} %param.10) | copy-start | bytes 100
  6.6 13.5 %collective-permute-start.1 = (bf16[512,512]{1,0:T(8,128)(2,1)}, bf16[512,512]{1,0:T(8,128)(2,1)S(1)}, u32[]{:S(2)}, u32[]{:S(2)}) collective-permute-start(bf16[512,512]{1,0:T(8,128)(2,1)} %get-tuple-element.30), channel_id=1, source_target_pairs={{0,1},{1,0},{2,3},{3,2},{4,5},{5,4},{6,7},{7,6},{8,9},{9,8},{10,11... | collective-permute-start | bytes 1572872 | tf_op jit(solution)/shard_map/ppermute | solution.py:30
  19.4 0.8 copy-start.5
  20.2 12.3 %copy-start.7 = (bf16[512,512]{1,0:T(8,128)(2,1)}, bf16[512,512]{1,0:T(8,128)(2,1)S(1)}, u32[]{:S(2)}) copy-start(bf16[512,512]{1,0:T(8,128)(2,1)S(1)} %collective-permute-done.1.refs_7_) | copy-start | bytes 1572868
  20.2 17.7 %collective-permute-start.3 = (bf16[512,512]{1,0:T(8,128)(2,1)S(1)}, bf16[512,512]{1,0:T(8,128)(2,1)S(1)}, u32[]{:S(2)}, u32[]{:S(2)}) collective-permute-start(bf16[512,512]{1,0:T(8,128)(2,1)S(1)} %collective-permute-done.1.refs_7_), channel_id=1, source_target_pairs={{0,4},{1,5},{2,6},{3,7},{4,12},{5,13},{6,14},{7,15},{12,8},{13,9},... | collective-permute-start | bytes 1572872 | tf_op jit(solution)/shard_map/ppermute | solution.py:50
  22.8 15.1 %collective-permute-start.4 = (bf16[512,512]{1,0:T(8,128)(2,1)S(1)}, bf16[512,512]{1,0:T(8,128)(2,1)S(1)}, u32[]{:S(2)}, u32[]{:S(2)}) collective-permute-start(bf16[512,512]{1,0:T(8,128)(2,1)S(1)} %collective-permute-done.1.refs_7_), channel_id=1, source_target_pairs={{0,2},{1,3},{2,0},{3,1},{4,6},{5,7},{6,4},{7,5},{8,10},{9,11},{10,... | collective-permute-start | bytes 1572872 | tf_op jit(solution)/shard_map/ppermute | solution.py:54
  24.3 14.4 %collective-permute-start.5 = (bf16[512,512]{1,0:T(8,128)(2,1)}, bf16[512,512]{1,0:T(8,128)(2,1)S(1)}, u32[]{:S(2)}, u32[]{:S(2)}) collective-permute-start(bf16[512,512]{1,0:T(8,128)(2,1)} %collective-permute-done.refs_5_), channel_id=1, source_target_pairs={{0,16},{16,0},{1,17},{17,1},{2,18},{18,2},{3,19},{19,3},{4,20},{20... | collective-permute-start | bytes 1572872 | tf_op jit(solution)/shard_map/ppermute | solution.py:58
  33.5 33.1 %all-to-all-start = ((bf16[16,8,2048]{2,1,0:T(8,128)(2,1)}), bf16[16,8,2048]{2,1,0:T(8,128)(2,1)}, u32[]{:S(2)}, u32[]{:S(2)}) async-start(bf16[16,8,2048]{2,1,0:T(8,128)(2,1)} %bitcast.4), calls=%async_computation | async-start | bytes 1048576 | tf_op jit(solution)/shard_map/all_to_all | solution.py:368
  37.8 0.8 copy-start.9
  38.7 25.4 %collective-permute-start.7 = (bf16[512,512]{1,0:T(8,128)(2,1)}, bf16[512,512]{1,0:T(8,128)(2,1)S(1)}, u32[]{:S(2)}, u32[]{:S(2)}) collective-permute-start(bf16[512,512]{1,0:T(8,128)(2,1)} %collective-permute-done.refs_5_), channel_id=1, source_target_pairs={{0,4},{1,5},{2,6},{3,7},{4,12},{5,13},{6,14},{7,15},{12,8},{13,9},... | collective-permute-start | bytes 1572872 | tf_op jit(solution)/shard_map/ppermute | solution.py:50
  40.4 23.7 %collective-permute-start.8 = (bf16[512,512]{1,0:T(8,128)(2,1)}, bf16[512,512]{1,0:T(8,128)(2,1)}, u32[]{:S(2)}, u32[]{:S(2)}) collective-permute-start(bf16[512,512]{1,0:T(8,128)(2,1)} %collective-permute-done.refs_5_), channel_id=1, source_target_pairs={{0,2},{1,3},{2,0},{3,1},{4,6},{5,7},{6,4},{7,5},{8,10},{9,11},{10,... | collective-permute-start | bytes 1572872 | tf_op jit(solution)/shard_map/ppermute | solution.py:54
  41.9 22.2 %collective-permute-start.9 = (bf16[512,512]{1,0:T(8,128)(2,1)S(1)}, bf16[512,512]{1,0:T(8,128)(2,1)S(1)}, u32[]{:S(2)}, u32[]{:S(2)}) collective-permute-start(bf16[512,512]{1,0:T(8,128)(2,1)S(1)} %collective-permute-done.3.refs_8_), channel_id=1, source_target_pairs={{0,16},{16,0},{1,17},{17,1},{2,18},{18,2},{3,19},{19,3},{4,20},{20... | collective-permute-start | bytes 1572872 | tf_op jit(solution)/shard_map/ppermute | solution.py:58
  44.1 14.0 %collective-permute-start.11 = (f32[8,128]{1,0:T(8,128)S(1)}, f32[8,128]{1,0:T(8,128)S(1)}, u32[]{:S(2)}, u32[]{:S(2)}) collective-permute-start(f32[8,128]{1,0:T(8,128)S(1)} %fusion.2), channel_id=1, source_target_pairs={{0,1},{1,0},{2,3},{3,2},{4,5},{5,4},{6,7},{7,6},{8,9},{9,8},{10,11... | collective-permute-start | bytes 12296 | tf_op jit(solution)/shard_map/ppermute | solution.py:30
  44.2 1.0 copy-start.2
  45.2 1.0 copy-start.6
  46.2 1.0 copy-start.8
  47.3 1.0 copy-start.10
  64.1 2.3 %copy-start = (bf16[512,512]{1,0:T(8,128)(2,1)}, bf16[512,512]{1,0:T(8,128)(2,1)S(1)}, u32[]{:S(2)}) copy-start(bf16[512,512]{1,0:T(8,128)(2,1)S(1)} %collective-permute-done.7.refs_6_) | copy-start | bytes 1572868
  64.1 0.9 copy-start.3
  65.0 13.6 %collective-permute-start.10 = (bf16[512,512]{1,0:T(8,128)(2,1)S(1)}, bf16[512,512]{1,0:T(8,128)(2,1)}, u32[]{:S(2)}, u32[]{:S(2)}) collective-permute-start(bf16[512,512]{1,0:T(8,128)(2,1)S(1)} %collective-permute-done.3.refs_8_), channel_id=1, source_target_pairs={{0,2},{1,3},{2,0},{3,1},{4,6},{5,7},{6,4},{7,5},{8,10},{9,11},{10,... | collective-permute-start | bytes 1572872 | tf_op jit(solution)/shard_map/ppermute | solution.py:54
  66.4 14.2 %collective-permute-start.12 = (bf16[512,512]{1,0:T(8,128)(2,1)S(1)}, bf16[512,512]{1,0:T(8,128)(2,1)}, u32[]{:S(2)}, u32[]{:S(2)}) collective-permute-start(bf16[512,512]{1,0:T(8,128)(2,1)S(1)} %collective-permute-done.3.refs_8_), channel_id=1, source_target_pairs={{0,4},{1,5},{2,6},{3,7},{4,12},{5,13},{6,14},{7,15},{12,8},{13,9},... | collective-permute-start | bytes 1572872 | tf_op jit(solution)/shard_map/ppermute | solution.py:50
  66.4 14.2 %collective-permute-start.13 = (bf16[512,512]{1,0:T(8,128)(2,1)}, bf16[512,512]{1,0:T(8,128)(2,1)}, u32[]{:S(2)}, u32[]{:S(2)}) collective-permute-start(bf16[512,512]{1,0:T(8,128)(2,1)} %collective-permute-done.8.refs_7_), channel_id=1, source_target_pairs={{0,16},{16,0},{1,17},{17,1},{2,18},{18,2},{3,19},{19,3},{4,20},{20... | collective-permute-start | bytes 1572872 | tf_op jit(solution)/shard_map/ppermute | solution.py:58
  80.6 13.4 %collective-permute-start.14 = (bf16[512,512]{1,0:T(8,128)(2,1)}, bf16[512,512]{1,0:T(8,128)(2,1)}, u32[]{:S(2)}, u32[]{:S(2)}) collective-permute-start(bf16[512,512]{1,0:T(8,128)(2,1)} %copy-done), channel_id=1, source_target_pairs={{0,2},{1,3},{2,0},{3,1},{4,6},{5,7},{6,4},{7,5},{8,10},{9,11},{10,... | collective-permute-start | bytes 1572872 | tf_op jit(solution)/shard_map/ppermute | solution.py:54
  81.2 12.9 %collective-permute-start.15 = (bf16[512,512]{1,0:T(8,128)(2,1)}, bf16[512,512]{1,0:T(8,128)(2,1)}, u32[]{:S(2)}, u32[]{:S(2)}) collective-permute-start(bf16[512,512]{1,0:T(8,128)(2,1)} %collective-permute-done.10.refs_10_), channel_id=1, source_target_pairs={{0,16},{16,0},{1,17},{17,1},{2,18},{18,2},{3,19},{19,3},{4,20},{20... | collective-permute-start | bytes 1572872 | tf_op jit(solution)/shard_map/ppermute | solution.py:58
  81.2 13.2 %collective-permute-start.16 = (bf16[512,512]{1,0:T(8,128)(2,1)}, bf16[512,512]{1,0:T(8,128)(2,1)}, u32[]{:S(2)}, u32[]{:S(2)}) collective-permute-start(bf16[512,512]{1,0:T(8,128)(2,1)} %collective-permute-done.10.refs_10_), channel_id=1, source_target_pairs={{0,4},{1,5},{2,6},{3,7},{4,12},{5,13},{6,14},{7,15},{12,8},{13,9},... | collective-permute-start | bytes 1572872 | tf_op jit(solution)/shard_map/ppermute | solution.py:50
  82.7 1.0 copy-start.1
  83.8 1.0 copy-start.4
  103.7 13.4 %all-to-all-start.1 = ((bf16[16,3,16,128]{3,2,1,0:T(8,128)(2,1)}), bf16[16,3,16,128]{3,2,1,0:T(8,128)(2,1)S(1)}, u32[]{:S(2)}, u32[]{:S(2)}) async-start(bf16[16,3,16,128]{3,2,1,0:T(8,128)(2,1)} %rows_3.1), calls=%async_computation.1 | async-start | bytes 393216 | tf_op jit(solution)/shard_map/all_to_all | solution.py:504
  117.1 0.9 copy-start.11
  118.0 0.7 copy-start.12
  118.7 0.7 copy-start.13

commit v8 on v7

--- a/solution.py
+++ b/solution.py
@@ -77,8 +77,9 @@
                     out.append(chip * 2 + (core ^ other))
                 return out
 
-            one, two, three = (blocks(step, 0) + blocks(step, 1) for step in range(3))
-            table.append(one + two + three)
+            one = blocks(0, 0) + blocks(0, 1)
+            two_a, two_b, three_a, three_b = blocks(1, 0), blocks(1, 1), blocks(2, 0), blocks(2, 1)
+            table.append(one + two_a + two_b + three_a + three_b)
     return np.array(table, np.int32)
 
 
@@ -97,63 +98,70 @@
 
 
 def accumulate(layout, token_refs, piece_refs, weight, total, sems, carry_ref=None, carry=None):
-    pair, half = pl.program_id(0), pl.program_id(1)
-    tokens, depth = token_refs[0].shape
+    step, half = pl.program_id(0), pl.program_id(1)
+    tokens, rows = token_refs[0].shape
+    count = len(token_refs) // 2
+    depth = count * rows
     copies = [
         pltpu.make_async_copy(
-            piece_refs[which].at[pl.ds(start, depth)], weight.at[pl.ds(i * depth, depth)], sems.at[i]
+            piece_refs[which].at[pl.ds(start, rows)], weight.at[pl.ds(i * rows, rows)], sems.at[i]
         )
         for i, (which, start) in enumerate(layout)
     ]
-    carried = []
+
+    @pl.when((step == 0) & (half == 0))
+    def _():
+        for copy in copies:
+            copy.start()
+
+    for i in range(0, len(copies), count):
+
+        @pl.when((step == i // count) & (half == 0))
+        def _():
+            for copy in copies[i : i + count]:
+                copy.wait()
+
     if carry_ref is not None:
-        carried = [pltpu.make_async_copy(carry_ref, carry, sems.at[len(layout)])]
-
-    @pl.when((pair == 0) & (half == 0))
-    def _():
-        for copy in copies + carried:
-            copy.start()
-
-    for i in range(0, len(copies), 2):
-
-        @pl.when((pair == i // 2) & (half == 0))
+        carried = pltpu.make_async_copy(carry_ref, carry, sems.at[len(layout)])
+
+        @pl.when((step == 0) & (half == 0))
         def _():
-            copies[i].wait()
-            copies[i + 1].wait()
+            carried.start()
 
     for side in range(2):
 
         @pl.when(half == side)
         def _():
-            states = jnp.concatenate([token_refs[2 * side][...], token_refs[2 * side + 1][...]], axis=1)
-            block = weight[pl.ds(pl.multiple_of(pair * 2 * depth, 2 * depth), 2 * depth), :]
+            states = jnp.concatenate([ref[...] for ref in token_refs[side * count : (side + 1) * count]], axis=1)
+            block = weight[pl.ds(pl.multiple_of(step * depth, depth), depth), :]
             product = jnp.dot(states, block, preferred_element_type=jnp.float32)
-            rows = pl.ds(side * tokens, tokens)
-
-            @pl.when(pair == 0)
+            rows_of_side = pl.ds(side * tokens, tokens)
+
+            @pl.when(step == 0)
             def _():
-                total[rows, :] = product
-
-            @pl.when(pair > 0)
+                total[rows_of_side, :] = product
+
+            @pl.when(step > 0)
             def _():
-                total[rows, :] += product
+                total[rows_of_side, :] += product
 
     if carry_ref is not None:
 
-        @pl.when((pair == pl.num_programs(0) - 1) & (half == 1))
+        @pl.when((step == pl.num_programs(0) - 1) & (half == 1))
         def _():
-            carried[0].wait()
+            carried.wait()
             total[...] += carry[...]
 
 
-def first_kernel(layout, block_ref, *refs):
+def first_kernel(layout, count, block_ref, *refs):
     total, weight, sems = refs[-3:]
-    accumulate(layout, refs[:4], refs[4:-3], weight, total, sems)
-
-
-def next_kernel(layout, block_ref, *refs):
+    accumulate(layout, refs[: 2 * count], refs[2 * count : -3], weight, total, sems)
+
+
+def next_kernel(layout, count, block_ref, *refs):
     total, weight, carry, sems = refs[-4:]
-    accumulate(layout, refs[:4], refs[5:-4], weight, total, sems, refs[4], carry)
+    token_refs, (carry_ref, *piece_refs) = refs[: 2 * count], refs[2 * count : -4]
+    accumulate(layout, token_refs, piece_refs, weight, total, sems, carry_ref, carry)
 
 
 def parts_of(values, count):
@@ -165,8 +173,8 @@
     return out
 
 
-def last_kernel(layout, width, block_ref, slot_ref, *refs):
-    query_ref, factor_ref = refs[5:7]
+def last_kernel(layout, count, width, block_ref, slot_ref, *refs):
+    token_refs, (carry_ref, query_ref, factor_ref, *piece_refs) = refs[: 2 * count], refs[2 * count : -7]
     slots_ref, weight, carry, total, summed, stats, sems = refs[-7:]
     images = query_ref.shape[1] // GROUP
 
@@ -174,7 +182,7 @@
     def _():
         slots_ref[...] = jnp.zeros_like(slots_ref)
 
-    accumulate(layout, refs[:4], refs[7:-7], weight, total, sems, refs[4], carry)
+    accumulate(layout, token_refs, piece_refs, weight, total, sems, carry_ref, carry)
 
     @pl.when((pl.program_id(0) == pl.num_programs(0) - 1) & (pl.program_id(1) == 1))
     def _():
@@ -344,7 +352,7 @@
             out_specs=pl.BlockSpec((tokens // 8, 1), lambda i: (i, 0)),
             out_shape=jax.ShapeDtypeStruct((tokens, 1), jnp.float32),
             cost_estimate=pl.CostEstimate(flops=0, bytes_accessed=2**18, transcendentals=0),
-            compiler_params=pltpu.CompilerParams(vmem_limit_bytes=32 * 2**20),
+            compiler_params=pltpu.CompilerParams(vmem_limit_bytes=60 * 2**20),
             name="squares",
         )(pltpu.with_memory_space_constraint(states, pltpu.HBM))[:, 0]
 
@@ -398,12 +406,12 @@
                 jax.ShapeDtypeStruct((QH, HD), jnp.float32),
                 jax.ShapeDtypeStruct((QH, HD), jnp.float32),
             ],
-            compiler_params=pltpu.CompilerParams(vmem_limit_bytes=56 * 2**20),
+            compiler_params=pltpu.CompilerParams(vmem_limit_bytes=60 * 2**20),
             cost_estimate=pl.CostEstimate(flops=0, bytes_accessed=2**18, transcendentals=0),
             name="resident",
         )(length, queries.reshape(decode_rows, QH, HD), cache)
 
-    def product(blocks, base, pieces, carry, name, last=None):
+    def product(blocks, base, count, pieces, carry, name, last=None):
         arrays, layout = [], []
         for array, start in pieces:
             at = [i for i, known in enumerate(arrays) if known is array]
@@ -411,27 +419,29 @@
                 arrays.append(array)
                 at = [len(arrays) - 1]
             layout.append((at[0], start))
-        steps = len(pieces) // 2
-        first = pl.BlockSpec((tokens, rows_dev), lambda i, half, block_ref, *_: (0, block_ref[base + 2 * i]))
-        second = pl.BlockSpec((tokens, rows_dev), lambda i, half, block_ref, *_: (0, block_ref[base + 2 * i + 1]))
+        steps = len(pieces) // count
+
+        def token_spec(k):
+            return pl.BlockSpec((tokens, rows_dev), lambda i, half, block_ref, *_: (0, block_ref[base + count * i + k]))
+
         anywhere = pl.BlockSpec(memory_space=pl.ANY)
-        in_specs = [first, second, first, second]
+        in_specs = [token_spec(k) for k in range(count)] * 2
         own_tokens = pltpu.with_memory_space_constraint(prompt_states, pltpu.HBM)
         other_tokens = pltpu.with_memory_space_constraint(other, pltpu.HBM)
-        inputs = [own_tokens, own_tokens, other_tokens, other_tokens]
+        inputs = [own_tokens] * count + [other_tokens] * count
         scalars = [blocks]
         scratch = [pltpu.VMEM((len(pieces) * rows_dev, columns_dev), jnp.bfloat16)]
         total = (2 * tokens, columns_dev)
-        body = functools.partial(first_kernel, layout)
+        body = functools.partial(first_kernel, layout, count)
         if carry is not None:
-            body = functools.partial(next_kernel, layout)
+            body = functools.partial(next_kernel, layout, count)
             in_specs = in_specs + [anywhere]
             inputs = inputs + [carry]
             scratch = scratch + [pltpu.VMEM(total, jnp.float32)]
         out_specs, out_shape = whole(total), jax.ShapeDtypeStruct(total, jnp.float32)
         if last is not None:
             image_q, slot, factor = last
-            body = functools.partial(last_kernel, layout, width)
+            body = functools.partial(last_kernel, layout, count, width)
             scalars = scalars + [slot]
             in_specs = in_specs + [whole((HALF_KVH, n_queries, HD)), whole((2 * tokens, 1))]
             inputs = inputs + [image_q, factor]
@@ -452,7 +462,7 @@
                 scratch_shapes=scratch + [pltpu.SemaphoreType.DMA((len(pieces) + 1,))],
             ),
             out_shape=out_shape,
-            compiler_params=pltpu.CompilerParams(vmem_limit_bytes=32 * 2**20),
+            compiler_params=pltpu.CompilerParams(vmem_limit_bytes=60 * 2**20),
             cost_estimate=pl.CostEstimate(flops=0, bytes_accessed=2**18, transcendentals=0),
             name=name,
         )(*scalars, *inputs, *arrays)
@@ -466,27 +476,34 @@
         tie = lax.optimization_barrier
         a_behind, a_own_y = along_ring(keep), across_y(keep)
 
-        from_a, from_b, done = tie((a_behind, taken, a_own_y))
-        b_behind, b_own_y, a_ahead = along_ring(from_b), across_y(from_b), across_replica(from_a)
-        squares = square_sums(done)
-        all_q = gather_queries(squares)
-
-        from_a, from_b, squares, _ = tie((a_behind, b_behind, squares, (b_own_y, a_ahead, other)))
-        a_opposite, a_behind_y, b_ahead = along_ring(from_a), across_y(from_a), across_replica(from_b)
-        factor, owners, rows = swap_small(squares)
-        total = product(blocks, 0, starts(keep, a_behind, a_own_y, taken, b_behind, b_own_y), None, "rows_1")
-
-        from_a, from_b, total, done = tie((a_behind_y, b_behind, total, (a_opposite, b_ahead)))
-        b_opposite, b_behind_y, a_ahead_y = along_ring(from_b), across_y(from_b), across_replica(from_a)
-        all_q, owners, rows, _ = tie((all_q, owners, rows, done))
+        squares = square_sums(keep)
+
+        b_behind = along_ring(tie((taken, a_behind, squares))[0])
+        b_own_y = across_y(tie((taken, a_own_y, squares))[0])
+        a_ahead = across_replica(a_behind)
+        all_q = gather_queries((squares, a_own_y))
+
+        a_opposite = along_ring(tie((a_behind, b_behind, other))[0])
+        a_behind_y = across_y(tie((a_behind, b_own_y, other))[0])
+        b_ahead = across_replica(tie((b_behind, a_ahead, other))[0])
+        factor, owners, rows = swap_small(tie((squares, a_ahead))[0])
+        ones = starts(keep, a_behind, a_own_y, taken, b_behind, b_own_y)
+        total = product(blocks, 0, 3, ones, None, "rows_1")
+
+        b_opposite = along_ring(tie((b_behind, a_opposite, total))[0])
+        b_behind_y = across_y(tie((b_behind, a_behind_y, total))[0])
+        a_ahead_y = across_replica(tie((a_behind_y, b_ahead, total))[0])
+        all_q, owners, rows, _ = tie((all_q, owners, rows, a_opposite))
         image_q, slot = place_images(all_q, owners, rows)
-
-        from_a, from_b, image_q, slot, _ = tie((a_opposite, b_behind_y, image_q, slot, (b_opposite, a_ahead_y)))
-        a_opposite_y, b_ahead_y, b_opposite_y = across_y(from_a), across_replica(from_b), along_ring(from_b)
-        twos = starts(a_ahead, a_opposite, a_behind_y, b_ahead, b_opposite, b_behind_y)
-        total = product(blocks, 6, twos, total, "rows_2")
-        threes = starts(a_ahead_y, a_opposite_y, b_ahead_y, b_opposite_y)
-        slots = product(blocks, 12, threes, total, "rows_3", last=(image_q, slot, factor))
+        twos = starts(a_ahead, a_opposite, a_behind_y, b_ahead)
+        total, image_q, slot = tie((product(blocks, 6, 2, twos, total, "rows_2"), image_q, slot))
+
+        a_opposite_y = across_y(tie((a_opposite, b_behind_y, total))[0])
+        b_opposite_y = along_ring(tie((b_behind_y, b_opposite, total))[0])
+        b_ahead_y = across_replica(tie((b_behind_y, a_ahead_y, total))[0])
+        total = product(blocks, 10, 3, starts(b_opposite, b_behind_y, a_ahead_y), total, "rows_3")
+        lasts = starts(a_opposite_y, b_ahead_y, b_opposite_y)
+        slots = product(blocks, 13, 3, lasts, total, "rows_4", last=(image_q, slot, factor))
         length, slots = tie((context_length, slots))
         res_out, res_top, res_sum = resident(length)
     else:
@@ -497,9 +514,9 @@
         a = gather_plain(keep)
         b = gather_plain(taken)
         chips = jnp.array([chip for chip, _, _ in a], jnp.int32)
-        total = product(chips * 2 + core, 0, [piece[1:] for piece in a], None, "rows_a")
+        total = product(chips * 2 + core, 0, 2, [piece[1:] for piece in a], None, "rows_a")
         slots = product(
-            chips * 2 + 1 - core, 0, [piece[1:] for piece in b], total, "rows_b", last=(image_q, slot, factor)
+            chips * 2 + 1 - core, 0, 2, [piece[1:] for piece in b], total, "rows_b", last=(image_q, slot, factor)
         )
     got = lax.all_to_all(slots, "section", split_axis=0, concat_axis=0, tiled=True)
 
@@ -515,7 +532,7 @@
         out_specs=whole((decode_rows, QH * HD)),
         scratch_shapes=[pltpu.VMEM((decode_rows, QH, HD), jnp.float32)],
         out_shape=jax.ShapeDtypeStruct((decode_rows, QH * HD), jnp.bfloat16),
-        compiler_params=pltpu.CompilerParams(vmem_limit_bytes=32 * 2**20),
+        compiler_params=pltpu.CompilerParams(vmem_limit_bytes=60 * 2**20),
         name="combine",
     )(got, res_out, res_top, res_sum)
 

time: 123 us -> 123 us (level)
  waiting for transfers between devices: 34.8 us -> 21.3 us
  starting transfers between devices: 26.9 us -> 38.4 us
  Pallas kernels: 44.6 us -> 53.8 us
  local copies, waits for them, and re-layouts: 13.5 us -> 6.73 us
  other arithmetic: 0.4 us -> 1.88 us
    ppermute x5, waiting for transfers between devices: 20.8 us -> 8.49 us  [along_ring(): return lax.ppermute(x, ('replica', 'section'), perm)]
    ppermute x4, starting transfers between devices: 2.96 us -> 13.4 us  [across_replica(): return lax.ppermute(x, 'replica', [(0, 1), (1, 0)])]
    unnamed x36, local copies, waits for them, and re-layouts: 11.7 us -> 2.99 us
    pallas_call x3 -> x4, Pallas kernels: 28.2 us -> 35.4 us  [product(): pl.pallas_call(body, grid_spec=pltpu.PrefetchScalarGridSpec(num_scalar_pr...]
    ppermute x5, waiting for transfers between devices: 11 us -> 5.43 us  [across_y(): return lax.ppermute(x, 'section', [(i, i ^ 2) for i in range(16)])]
    ppermute x4, waiting for transfers between devices: 0.01 us -> 3.25 us  [across_replica(): return lax.ppermute(x, 'replica', [(0, 1), (1, 0)])]
    ppermute x5, starting transfers between devices: 6.54 us -> 8.2 us  [across_y(): return lax.ppermute(x, 'section', [(i, i ^ 2) for i in range(16)])]
  transfers between devices with their start and end apart: 19 -> 19, of which waited for: 7 -> 10; matrix products, arithmetic and copies ran while one was open for 3% -> 5% of each run, Pallas kernels for 25% -> 33%
where the time goes in v8:
time: 123 us
  Pallas kernels  53.8 us (44%)
  starting transfers between devices  38.4 us (31%)
  waiting for transfers between devices  21.3 us (17%)
  local copies, waits for them, and re-layouts  6.73 us (5%)
  other arithmetic  1.88 us (2%)
    pallas_call x4, Pallas kernels, product(): pl.pallas_call(body, grid_spec=pltpu.PrefetchScalarGridSpec(num_scalar_pr...  35.4 us
    ppermute x4, starting transfers between devices, across_replica(): return lax.ppermute(x, 'replica', [(0, 1), (1, 0)])  13.4 us
    ppermute x5, starting transfers between devices, along_ring(): return lax.ppermute(x, ('replica', 'section'), perm)  8.8 us
    ppermute x5, waiting for transfers between devices, along_ring(): return lax.ppermute(x, ('replica', 'section'), perm)  8.49 us
    ppermute x5, starting transfers between devices, across_y(): return lax.ppermute(x, 'section', [(i, i ^ 2) for i in range(16)])  8.2 us
    pallas_call x1, Pallas kernels, square_sums(): pl.pallas_call(square_kernel, grid=(8,), in_specs=[pl.BlockSpec((tokens /...  7.6 us
    ppermute x5, waiting for transfers between devices, across_y(): return lax.ppermute(x, 'section', [(i, i ^ 2) for i in range(16)])  5.43 us
    pallas_call x1, Pallas kernels, resident(): pl.pallas_call(resident_kernel, grid_spec=pltpu.PrefetchScalarGridSpec(nu...  5.35 us
  transfers between devices with their start and end apart: 19, of which 10 were waited for; matrix products, arithmetic and copies ran while one was open for 5% of the time, Pallas kernels for 33%

profile of v8, /device:TPU:0, one launch (start us, length us, event | category | flops | bytes accessed | tf_op | source)
XLA Modules:
  0.0 122.5 jit_solution(15480737579760892145)
XLA Ops:
  0.0 2.1 %split.1 = (bf16[512,512]{1,0:T(8,128)(2,1)}, bf16[512,512]{1,0:T(8,128)(2,1)}) custom-call(s32[1]{0:T(128)} %bitcast.1.core_ref, bf16[512,1024]{1,0:T(8,128)(2,1)} %give_in.1, bf16[512,1024]{1,0:T(8,128)(2,1)} %give_in.1), custom_call_target="tpu_custom_call" | custom-call | bytes 262144 | tf_op jit(solution)/shard_map/split/pallas_call | solution.py:327
  2.1 0.5 collective-permute-start
  2.5 2.6 %collective-permute-start.2 = (bf16[512,512]{1,0:T(8,128)(2,1)}, bf16[512,512]{1,0:T(8,128)(2,1)S(1)}, u32[]{:S(2)}, u32[]{:S(2)}) collective-permute-start(bf16[512,512]{1,0:T(8,128)(2,1)} %get-tuple-element.32.refs_6_), channel_id=1, source_target_pairs={{0,2},{1,3},{2,0},{3,1},{4,6},{5,7},{6,4},{7,5},{8,10},{9,11},{10,... | collective-permute-start | bytes 1572872 | tf_op jit(solution)/shard_map/ppermute | solution.py:54
  5.1 0.2 collective-permute-start.3
  5.3 1.6 %collective-permute-start.1 = (bf16[512,512]{1,0:T(8,128)(2,1)}, bf16[512,512]{1,0:T(8,128)(2,1)S(1)}, u32[]{:S(2)}, u32[]{:S(2)}) collective-permute-start(bf16[512,512]{1,0:T(8,128)(2,1)} %get-tuple-element.32.refs_6_), channel_id=1, source_target_pairs={{0,4},{1,5},{2,6},{3,7},{4,12},{5,13},{6,14},{7,15},{12,8},{13,9},... | collective-permute-start | bytes 1572872 | tf_op jit(solution)/shard_map/ppermute | solution.py:50
  6.9 7.6 %squares.1 = f32[512,1]{1,0:T(8,128)} custom-call(bf16[512,8192]{1,0:T(8,128)(2,1)} %refs_2_.5), custom_call_target="tpu_custom_call" | custom-call | bytes 262144 | tf_op jit(solution)/shard_map/squares/pallas_call | solution.py:348
  14.5 1.1 reduce
  15.5 2.3 %collective-permute-done.2.refs_8_ = bf16[512,512]{1,0:T(8,128)(2,1)S(1)} collective-permute-done((bf16[512,512]{1,0:T(8,128)(2,1)}, bf16[512,512]{1,0:T(8,128)(2,1)S(1)}, u32[]{:S(2)}, u32[]{:S(2)}) %collective-permute-start.2) | collective-permute-done | bytes 524320 | tf_op jit(solution)/shard_map/ppermute | solution.py:54
  17.9 0.0 collective-permute-done.3.refs_9_
  17.9 1.8 %collective-permute-start.5 = (bf16[512,512]{1,0:T(8,128)(2,1)S(1)}, bf16[512,512]{1,0:T(8,128)(2,1)}, u32[]{:S(2)}, u32[]{:S(2)}) collective-permute-start(bf16[512,512]{1,0:T(8,128)(2,1)S(1)} %collective-permute-done.3.refs_9_), channel_id=1, source_target_pairs={{0,2},{1,3},{2,0},{3,1},{4,6},{5,7},{6,4},{7,5},{8,10},{9,11},{10,... | collective-permute-start | bytes 1572872 | tf_op jit(solution)/shard_map/ppermute | solution.py:54
  19.7 0.9 collective-permute-done.1.refs_7_
  20.5 0.9 collective-permute-start.4
  21.4 3.2 %collective-permute-start.6 = (bf16[512,512]{1,0:T(8,128)(2,1)S(1)}, bf16[512,512]{1,0:T(8,128)(2,1)S(1)}, u32[]{:S(2)}, u32[]{:S(2)}) collective-permute-start(bf16[512,512]{1,0:T(8,128)(2,1)S(1)} %collective-permute-done.1.refs_7_), channel_id=1, source_target_pairs={{0,16},{16,0},{1,17},{17,1},{2,18},{18,2},{3,19},{19,3},{4,20},{20... | collective-permute-start | bytes 1572872 | tf_op jit(solution)/shard_map/ppermute | solution.py:58
  24.6 0.0 copy-done.14
  24.6 0.8 broadcast_in_dim.6
  25.5 3.6 %all-to-all-start = ((bf16[16,8,2048]{2,1,0:T(8,128)(2,1)}), bf16[16,8,2048]{2,1,0:T(8,128)(2,1)S(1)}, u32[]{:S(2)}, u32[]{:S(2)}) async-start(bf16[16,8,2048]{2,1,0:T(8,128)(2,1)} %bitcast.4), calls=%async_computation | async-start | bytes 1048576 | tf_op jit(solution)/shard_map/all_to_all | solution.py:376
  29.1 1.2 %dynamic-slice_bitcast_fusion.block_ref = s32[16]{0:T(128)} fusion(s32[32,16]{1,0:T(8,128)} %constant.34.clone, s32[]{:T(128)S(6)} %select_n.10), kind=kLoop, calls=%fused_computation.20 | loop fusion | bytes 132 | tf_op jit(solution)/shard_map/squeeze | solution.py:471
  30.3 1.5 %collective-permute-done.5.refs_11_ = bf16[512,512]{1,0:T(8,128)(2,1)} collective-permute-done((bf16[512,512]{1,0:T(8,128)(2,1)S(1)}, bf16[512,512]{1,0:T(8,128)(2,1)}, u32[]{:S(2)}, u32[]{:S(2)}) %collective-permute-start.5) | collective-permute-done | bytes 524320 | tf_op jit(solution)/shard_map/ppermute | solution.py:54
  31.7 0.0 collective-permute-done.refs_3_.refs_4_.refs_5_.refs_2_
  31.7 2.2 %collective-permute-start.8 = (bf16[512,512]{1,0:T(8,128)(2,1)S(1)}, bf16[512,512]{1,0:T(8,128)(2,1)}, u32[]{:S(2)}, u32[]{:S(2)}) collective-permute-start(bf16[512,512]{1,0:T(8,128)(2,1)S(1)} %collective-permute-done.1.refs_7_), channel_id=1, source_target_pairs={{0,2},{1,3},{2,0},{3,1},{4,6},{5,7},{6,4},{7,5},{8,10},{9,11},{10,... | collective-permute-start | bytes 1572872 | tf_op jit(solution)/shard_map/ppermute | solution.py:54
  34.0 4.6 %collective-permute-done.4.refs_10_ = bf16[512,512]{1,0:T(8,128)(2,1)S(1)} collective-permute-done((bf16[512,512]{1,0:T(8,128)(2,1)S(1)}, bf16[512,512]{1,0:T(8,128)(2,1)S(1)}, u32[]{:S(2)}, u32[]{:S(2)}) %collective-permute-start.4) | collective-permute-done | bytes 524320 | tf_op jit(solution)/shard_map/ppermute | solution.py:50
  38.5 2.7 %collective-permute-start.7 = (bf16[512,512]{1,0:T(8,128)(2,1)S(1)}, bf16[512,512]{1,0:T(8,128)(2,1)S(1)}, u32[]{:S(2)}, u32[]{:S(2)}) collective-permute-start(bf16[512,512]{1,0:T(8,128)(2,1)S(1)} %collective-permute-done.1.refs_7_), channel_id=1, source_target_pairs={{0,4},{1,5},{2,6},{3,7},{4,12},{5,13},{6,14},{7,15},{12,8},{13,9},... | collective-permute-start | bytes 1572872 | tf_op jit(solution)/shard_map/ppermute | solution.py:50
  41.2 0.0 collective-permute-done.6.refs_5_
  41.3 0.0 collective-permute-start.9
  41.3 0.0 copy-done.15
  41.3 0.0 copy-done.16
  41.3 0.1 add_convert_fusion
  41.4 0.0 collective-permute-start.10
  41.4 1.1 collective-permute-done.10
  42.6 0.1 slice_convert_fusion
  42.6 0.0 copy-done.5
  42.7 10.6 %rows_1.1.refs_4_ = f32[1024,512]{1,0:T(8,128)} custom-call(s32[16]{0:T(128)} %dynamic-slice_bitcast_fusion.block_ref, bf16[512,8192]{1,0:T(8,128)(2,1)} %refs_2_.5, bf16[512,8192]{1,0:T(8,128)(2,1)} %refs_2_.5, bf16[512,8192]{1,0:T(8,128)(2,1)} %refs_2_.5, bf16[512,8192]{1,0:T(8,128)(2,1)} %collective-permute-done.refs_3_.refs_4_.refs_5_.refs_2_, ...), custom_call_target="tpu_custom_call" | custom-call | bytes 262144 | tf_op jit(solution)/shard_map/rows_1/pallas_call | solution.py:455
  53.2 0.0 collective-permute-done.8.refs_7_
  53.3 1.6 %collective-permute-start.12 = (bf16[512,512]{1,0:T(8,128)(2,1)}, bf16[512,512]{1,0:T(8,128)(2,1)S(1)}, u32[]{:S(2)}, u32[]{:S(2)}) collective-permute-start(bf16[512,512]{1,0:T(8,128)(2,1)} %copy-done.1), channel_id=1, source_target_pairs={{0,2},{1,3},{2,0},{3,1},{4,6},{5,7},{6,4},{7,5},{8,10},{9,11},{10,... | collective-permute-start | bytes 1572872 | tf_op jit(solution)/shard_map/ppermute | solution.py:54
  54.9 2.4 %collective-permute-done.7.refs_6_ = bf16[512,512]{1,0:T(8,128)(2,1)S(1)} collective-permute-done((bf16[512,512]{1,0:T(8,128)(2,1)S(1)}, bf16[512,512]{1,0:T(8,128)(2,1)S(1)}, u32[]{:S(2)}, u32[]{:S(2)}) %collective-permute-start.7) | collective-permute-done | bytes 524320 | tf_op jit(solution)/shard_map/ppermute | solution.py:50
  57.3 1.4 %collective-permute-start.11 = (bf16[512,512]{1,0:T(8,128)(2,1)}, bf16[512,512]{1,0:T(8,128)(2,1)S(1)}, u32[]{:S(2)}, u32[]{:S(2)}) collective-permute-start(bf16[512,512]{1,0:T(8,128)(2,1)} %copy-done.1), channel_id=1, source_target_pairs={{0,4},{1,5},{2,6},{3,7},{4,12},{5,13},{6,14},{7,15},{12,8},{13,9},... | collective-permute-start | bytes 1572872 | tf_op jit(solution)/shard_map/ppermute | solution.py:50
  58.7 0.0 collective-permute-done.9.refs_8_
  58.7 0.0 collective-permute-start.13
  58.7 0.8 copy-done.8
  59.5 0.1 pad_add_fusion.1
  59.6 0.0 all-to-all-done
  59.6 0.2 fusion
  59.8 0.6 copy.17
  60.5 9.2 %rows_2.1.refs_6_ = f32[1024,512]{1,0:T(8,128)} custom-call(s32[16]{0:T(128)} %dynamic-slice_bitcast_fusion.block_ref, bf16[512,8192]{1,0:T(8,128)(2,1)} %refs_2_.5, bf16[512,8192]{1,0:T(8,128)(2,1)} %refs_2_.5, bf16[512,8192]{1,0:T(8,128)(2,1)} %collective-permute-done.refs_3_.refs_4_.refs_5_.refs_2_, ...), custom_call_target="tpu_custom_call" | custom-call | bytes 262144 | tf_op jit(solution)/shard_map/rows_2/pallas_call | solution.py:455
  69.7 0.5 pad_add_fusion.slot_ref
  70.2 0.0 collective-permute-done.12.refs_8_
  70.3 0.6 collective-permute-done.11.refs_7_
  70.8 2.3 %collective-permute-start.16 = (bf16[512,512]{1,0:T(8,128)(2,1)S(1)}, bf16[512,512]{1,0:T(8,128)(2,1)S(1)}, u32[]{:S(2)}, u32[]{:S(2)}) collective-permute-start(bf16[512,512]{1,0:T(8,128)(2,1)S(1)} %collective-permute-done.12.refs_8_), channel_id=1, source_target_pairs={{0,4},{1,5},{2,6},{3,7},{4,12},{5,13},{6,14},{7,15},{12,8},{13,9},... | collective-permute-start | bytes 1572872 | tf_op jit(solution)/shard_map/ppermute | solution.py:50
  73.1 0.0 collective-permute-done.13.refs_9_
  73.1 10.2 %collective-permute-start.15 = (bf16[512,512]{1,0:T(8,128)(2,1)S(1)}, bf16[512,512]{1,0:T(8,128)(2,1)S(1)}, u32[]{:S(2)}, u32[]{:S(2)}) collective-permute-start(bf16[512,512]{1,0:T(8,128)(2,1)S(1)} %collective-permute-done.12.refs_8_), channel_id=1, source_target_pairs={{0,16},{16,0},{1,17},{17,1},{2,18},{18,2},{3,19},{19,3},{4,20},{20... | collective-permute-start | bytes 1572872 | tf_op jit(solution)/shard_map/ppermute | solution.py:58
  83.3 0.0 collective-permute-start.14
  83.3 1.0 copy.11.refs_8_
  84.3 7.6 %rows_3.1.refs_6_ = f32[1024,512]{1,0:T(8,128)} custom-call(s32[16]{0:T(128)} %dynamic-slice_bitcast_fusion.block_ref, bf16[512,8192]{1,0:T(8,128)(2,1)} %refs_2_.5, bf16[512,8192]{1,0:T(8,128)(2,1)} %refs_2_.5, bf16[512,8192]{1,0:T(8,128)(2,1)} %refs_2_.5, bf16[512,8192]{1,0:T(8,128)(2,1)} %collective-permute-done.refs_3_.refs_4_.refs_5_.refs_2_, ...), custom_call_target="tpu_custom_call" | custom-call | bytes 262144 | tf_op jit(solution)/shard_map/rows_3/pallas_call | solution.py:455
  91.9 0.0 collective-permute-done.16.refs_11_
  91.9 3.2 %collective-permute-done.15.refs_10_ = bf16[512,512]{1,0:T(8,128)(2,1)S(1)} collective-permute-done((bf16[512,512]{1,0:T(8,128)(2,1)S(1)}, bf16[512,512]{1,0:T(8,128)(2,1)S(1)}, u32[]{:S(2)}, u32[]{:S(2)}) %collective-permute-start.15) | collective-permute-done | bytes 524320 | tf_op jit(solution)/shard_map/ppermute | solution.py:58
  95.2 1.7 %collective-permute-done.14.refs_9_ = bf16[512,512]{1,0:T(8,128)(2,1)S(1)} collective-permute-done((bf16[512,512]{1,0:T(8,128)(2,1)}, bf16[512,512]{1,0:T(8,128)(2,1)S(1)}, u32[]{:S(2)}, u32[]{:S(2)}) %collective-permute-start.14) | collective-permute-done | bytes 524320 | tf_op jit(solution)/shard_map/ppermute | solution.py:54
  96.8 0.8 copy-done.13
  97.6 8.1 %rows_4.1 = bf16[16,3,16,128]{3,2,1,0:T(8,128)(2,1)} custom-call(s32[16]{0:T(128)} %dynamic-slice_bitcast_fusion.block_ref, s32[3,16]{1,0:T(4,128)} %pad_add_fusion.slot_ref, bf16[512,8192]{1,0:T(8,128)(2,1)} %refs_2_.5, bf16[512,8192]{1,0:T(8,128)(2,1)} %refs_2_.5, bf16[512,8192]{1,0:T(8,128)(2,1)} %refs_2_.5, ...), custom_call_target="tpu_custom_call" | custom-call | bytes 262144 | tf_op jit(solution)/shard_map/rows_4/pallas_call | solution.py:455
  105.7 3.8 %all-to-all-start.1 = ((bf16[16,3,16,128]{3,2,1,0:T(8,128)(2,1)}), bf16[16,3,16,128]{3,2,1,0:T(8,128)(2,1)S(1)}, u32[]{:S(2)}, u32[]{:S(2)}) async-start(bf16[16,3,16,128]{3,2,1,0:T(8,128)(2,1)} %rows_4.1), calls=%async_computation.1 | async-start | bytes 393216 | tf_op jit(solution)/shard_map/all_to_all | solution.py:521
  109.6 0.6 copy.16
  110.2 5.4 %resident.1 = (f32[8,32,128]{2,1,0:T(8,128)}, f32[32,128]{1,0:T(8,128)}, f32[32,128]{1,0:T(8,128)}) custom-call(s32[8]{0:T(128)} %length_ref, bf16[8,32,128]{2,1,0:T(8,128)(2,1)} %bitcast.34, bf16[8,256,1024]{2,1,0:T(8,128)(2,1)} %cache_ref.1), custom_call_target="tpu_custom_call" | custom-call | bytes 262144 | tf_op jit(solution)/shard_map/resident/pallas_call | solution.py:389
  115.6 3.0 %all-to-all-done.1.got_ref = bf16[16,3,16,128]{3,2,1,0:T(8,128)(2,1)S(1)} async-done(((bf16[16,3,16,128]{3,2,1,0:T(8,128)(2,1)}), bf16[16,3,16,128]{3,2,1,0:T(8,128)(2,1)S(1)}, u32[]{:S(2)}, u32[]{:S(2)}) %all-to-all-start.1) | async-done | bytes 196640 | tf_op jit(solution)/shard_map/all_to_all | solution.py:521
  118.6 0.7 copy-done
  119.2 3.3 %combine.1 = bf16[8,4096]{1,0:T(8,128)(2,1)} custom-call(bf16[16,3,16,128]{3,2,1,0:T(8,128)(2,1)} %copy-done, f32[8,32,128]{2,1,0:T(8,128)} %get-tuple-element.56.res_out_ref, f32[32,128]{1,0:T(8,128)} %get-tuple-element.57.res_top_ref, f32[32,128]{1,0:T(8,128)} %get-tuple-element.58.res_sum_ref), custom_call_target="tpu_custom_call" | custom-call | tf_op jit(solution)/shard_map/combine/pallas_call | solution.py:523
  (34 shorter events, 0.1 us)
Async XLA Ops:
  2.1 29.7 %collective-permute-start = (bf16[512,8192]{1,0:T(8,128)(2,1)}, bf16[512,8192]{1,0:T(8,128)(2,1)}, u32[]{:S(2)}, u32[]{:S(2)}) collective-permute-start(bf16[512,8192]{1,0:T(8,128)(2,1)} %refs_2_.5), channel_id=1, source_target_pairs={{0,1},{1,0},{2,3},{3,2},{4,5},{5,4},{6,7},{7,6},{8,9},{9,8},{10,11... | collective-permute-start | bytes 25165832 | tf_op jit(solution)/shard_map/ppermute | solution.py:30
  2.5 15.3 %collective-permute-start.2 = (bf16[512,512]{1,0:T(8,128)(2,1)}, bf16[512,512]{1,0:T(8,128)(2,1)S(1)}, u32[]{:S(2)}, u32[]{:S(2)}) collective-permute-start(bf16[512,512]{1,0:T(8,128)(2,1)} %get-tuple-element.32.refs_6_), channel_id=1, source_target_pairs={{0,2},{1,3},{2,0},{3,1},{4,6},{5,7},{6,4},{7,5},{8,10},{9,11},{10,... | collective-permute-start | bytes 1572872 | tf_op jit(solution)/shard_map/ppermute | solution.py:54
  5.1 19.5 %copy-start.14 = (bf16[8,4096]{1,0:T(8,128)(2,1)S(1)}, bf16[8,4096]{1,0:T(8,128)(2,1)}, u32[]{:S(2)}) copy-start(bf16[8,4096]{1,0:T(8,128)(2,1)} %param.12) | copy-start | bytes 196612
  5.1 36.2 %copy-start.15 = (s32[8]{0:T(128)S(1)}, s32[8]{0:T(128)}, u32[]{:S(2)}) copy-start(s32[8]{0:T(128)} %param.11) | copy-start | bytes 100
  5.1 36.2 %copy-start.16 = (s32[8]{0:T(128)S(1)}, s32[8]{0:T(128)}, u32[]{:S(2)}) copy-start(s32[8]{0:T(128)} %param.10) | copy-start | bytes 100
  5.1 12.8 %collective-permute-start.3 = (bf16[512,512]{1,0:T(8,128)(2,1)}, bf16[512,512]{1,0:T(8,128)(2,1)S(1)}, u32[]{:S(2)}, u32[]{:S(2)}) collective-permute-start(bf16[512,512]{1,0:T(8,128)(2,1)} %get-tuple-element.34), channel_id=1, source_target_pairs={{0,1},{1,0},{2,3},{3,2},{4,5},{5,4},{6,7},{7,6},{8,9},{9,8},{10,11... | collective-permute-start | bytes 1572872 | tf_op jit(solution)/shard_map/ppermute | solution.py:30
  5.3 15.3 %collective-permute-start.1 = (bf16[512,512]{1,0:T(8,128)(2,1)}, bf16[512,512]{1,0:T(8,128)(2,1)S(1)}, u32[]{:S(2)}, u32[]{:S(2)}) collective-permute-start(bf16[512,512]{1,0:T(8,128)(2,1)} %get-tuple-element.32.refs_6_), channel_id=1, source_target_pairs={{0,4},{1,5},{2,6},{3,7},{4,12},{5,13},{6,14},{7,15},{12,8},{13,9},... | collective-permute-start | bytes 1572872 | tf_op jit(solution)/shard_map/ppermute | solution.py:50
  17.9 24.8 %copy-start.5 = (bf16[512,512]{1,0:T(8,128)(2,1)}, bf16[512,512]{1,0:T(8,128)(2,1)S(1)}, u32[]{:S(2)}) copy-start(bf16[512,512]{1,0:T(8,128)(2,1)S(1)} %collective-permute-done.2.refs_8_) | copy-start | bytes 1572868
  17.9 16.1 %copy-start.6 = (bf16[512,512]{1,0:T(8,128)(2,1)}, bf16[512,512]{1,0:T(8,128)(2,1)S(1)}, u32[]{:S(2)}) copy-start(bf16[512,512]{1,0:T(8,128)(2,1)S(1)} %collective-permute-done.3.refs_9_) | copy-start | bytes 1572868
  17.9 13.9 %collective-permute-start.5 = (bf16[512,512]{1,0:T(8,128)(2,1)S(1)}, bf16[512,512]{1,0:T(8,128)(2,1)}, u32[]{:S(2)}, u32[]{:S(2)}) collective-permute-start(bf16[512,512]{1,0:T(8,128)(2,1)S(1)} %collective-permute-done.3.refs_9_), channel_id=1, source_target_pairs={{0,2},{1,3},{2,0},{3,1},{4,6},{5,7},{6,4},{7,5},{8,10},{9,11},{10,... | collective-permute-start | bytes 1572872 | tf_op jit(solution)/shard_map/ppermute | solution.py:54
  20.5 22.1 %copy-start.4 = (bf16[512,512]{1,0:T(8,128)(2,1)}, bf16[512,512]{1,0:T(8,128)(2,1)S(1)}, u32[]{:S(2)}) copy-start(bf16[512,512]{1,0:T(8,128)(2,1)S(1)} %collective-permute-done.1.refs_7_) | copy-start | bytes 1572868
  20.5 18.0 %collective-permute-start.4 = (bf16[512,512]{1,0:T(8,128)(2,1)S(1)}, bf16[512,512]{1,0:T(8,128)(2,1)S(1)}, u32[]{:S(2)}, u32[]{:S(2)}) collective-permute-start(bf16[512,512]{1,0:T(8,128)(2,1)S(1)} %collective-permute-done.3.refs_9_), channel_id=1, source_target_pairs={{0,4},{1,5},{2,6},{3,7},{4,12},{5,13},{6,14},{7,15},{12,8},{13,9},... | collective-permute-start | bytes 1572872 | tf_op jit(solution)/shard_map/ppermute | solution.py:50
  21.4 19.8 %collective-permute-start.6 = (bf16[512,512]{1,0:T(8,128)(2,1)S(1)}, bf16[512,512]{1,0:T(8,128)(2,1)S(1)}, u32[]{:S(2)}, u32[]{:S(2)}) collective-permute-start(bf16[512,512]{1,0:T(8,128)(2,1)S(1)} %collective-permute-done.1.refs_7_), channel_id=1, source_target_pairs={{0,16},{16,0},{1,17},{17,1},{2,18},{18,2},{3,19},{19,3},{4,20},{20... | collective-permute-start | bytes 1572872 | tf_op jit(solution)/shard_map/ppermute | solution.py:58
  25.5 34.1 %all-to-all-start = ((bf16[16,8,2048]{2,1,0:T(8,128)(2,1)}), bf16[16,8,2048]{2,1,0:T(8,128)(2,1)S(1)}, u32[]{:S(2)}, u32[]{:S(2)}) async-start(bf16[16,8,2048]{2,1,0:T(8,128)(2,1)} %bitcast.4), calls=%async_computation | async-start | bytes 1048576 | tf_op jit(solution)/shard_map/all_to_all | solution.py:376
  31.7 21.5 %collective-permute-start.8 = (bf16[512,512]{1,0:T(8,128)(2,1)S(1)}, bf16[512,512]{1,0:T(8,128)(2,1)}, u32[]{:S(2)}, u32[]{:S(2)}) collective-permute-start(bf16[512,512]{1,0:T(8,128)(2,1)S(1)} %collective-permute-done.1.refs_7_), channel_id=1, source_target_pairs={{0,2},{1,3},{2,0},{3,1},{4,6},{5,7},{6,4},{7,5},{8,10},{9,11},{10,... | collective-permute-start | bytes 1572872 | tf_op jit(solution)/shard_map/ppermute | solution.py:54
  38.5 4.1 %copy-start.1 = (bf16[512,512]{1,0:T(8,128)(2,1)}, bf16[512,512]{1,0:T(8,128)(2,1)S(1)}, u32[]{:S(2)}) copy-start(bf16[512,512]{1,0:T(8,128)(2,1)S(1)} %collective-permute-done.4.refs_10_) | copy-start | bytes 1572868
  38.5 18.8 %collective-permute-start.7 = (bf16[512,512]{1,0:T(8,128)(2,1)S(1)}, bf16[512,512]{1,0:T(8,128)(2,1)S(1)}, u32[]{:S(2)}, u32[]{:S(2)}) collective-permute-start(bf16[512,512]{1,0:T(8,128)(2,1)S(1)} %collective-permute-done.1.refs_7_), channel_id=1, source_target_pairs={{0,4},{1,5},{2,6},{3,7},{4,12},{5,13},{6,14},{7,15},{12,8},{13,9},... | collective-permute-start | bytes 1572872 | tf_op jit(solution)/shard_map/ppermute | solution.py:50
  41.2 12.0 %copy-start.2 = (bf16[512,512]{1,0:T(8,128)(2,1)}, bf16[512,512]{1,0:T(8,128)(2,1)S(1)}, u32[]{:S(2)}) copy-start(bf16[512,512]{1,0:T(8,128)(2,1)S(1)} %collective-permute-done.6.refs_5_) | copy-start | bytes 1572868
  41.3 17.4 %collective-permute-start.9 = (bf16[512,512]{1,0:T(8,128)(2,1)S(1)}, bf16[512,512]{1,0:T(8,128)(2,1)S(1)}, u32[]{:S(2)}, u32[]{:S(2)}) collective-permute-start(bf16[512,512]{1,0:T(8,128)(2,1)S(1)} %collective-permute-done.4.refs_10_), channel_id=1, source_target_pairs={{0,16},{16,0},{1,17},{17,1},{2,18},{18,2},{3,19},{19,3},{4,20},{20... | collective-permute-start | bytes 1572872 | tf_op jit(solution)/shard_map/ppermute | solution.py:58
  41.4 1.2 collective-permute-start.10
  53.3 17.0 %collective-permute-start.12 = (bf16[512,512]{1,0:T(8,128)(2,1)}, bf16[512,512]{1,0:T(8,128)(2,1)S(1)}, u32[]{:S(2)}, u32[]{:S(2)}) collective-permute-start(bf16[512,512]{1,0:T(8,128)(2,1)} %copy-done.1), channel_id=1, source_target_pairs={{0,2},{1,3},{2,0},{3,1},{4,6},{5,7},{6,4},{7,5},{8,10},{9,11},{10,... | collective-permute-start | bytes 1572872 | tf_op jit(solution)/shard_map/ppermute | solution.py:54
  57.3 3.2 %copy-start.3 = (bf16[512,512]{1,0:T(8,128)(2,1)}, bf16[512,512]{1,0:T(8,128)(2,1)S(1)}, u32[]{:S(2)}) copy-start(bf16[512,512]{1,0:T(8,128)(2,1)S(1)} %collective-permute-done.7.refs_6_) | copy-start | bytes 1572868
  57.3 13.5 %collective-permute-start.11 = (bf16[512,512]{1,0:T(8,128)(2,1)}, bf16[512,512]{1,0:T(8,128)(2,1)S(1)}, u32[]{:S(2)}, u32[]{:S(2)}) collective-permute-start(bf16[512,512]{1,0:T(8,128)(2,1)} %copy-done.1), channel_id=1, source_target_pairs={{0,4},{1,5},{2,6},{3,7},{4,12},{5,13},{6,14},{7,15},{12,8},{13,9},... | collective-permute-start | bytes 1572872 | tf_op jit(solution)/shard_map/ppermute | solution.py:50
  58.7 0.8 copy-start.8
  58.7 14.4 %collective-permute-start.13 = (bf16[512,512]{1,0:T(8,128)(2,1)}, bf16[512,512]{1,0:T(8,128)(2,1)S(1)}, u32[]{:S(2)}, u32[]{:S(2)}) collective-permute-start(bf16[512,512]{1,0:T(8,128)(2,1)} %collective-permute-done.8.refs_7_), channel_id=1, source_target_pairs={{0,16},{16,0},{1,17},{17,1},{2,18},{18,2},{3,19},{19,3},{4,20},{20... | collective-permute-start | bytes 1572872 | tf_op jit(solution)/shard_map/ppermute | solution.py:58
  70.3 14.1 %copy-start.7 = (bf16[512,512]{1,0:T(8,128)(2,1)}, bf16[512,512]{1,0:T(8,128)(2,1)S(1)}, u32[]{:S(2)}) copy-start(bf16[512,512]{1,0:T(8,128)(2,1)S(1)} %collective-permute-done.12.refs_8_) | copy-start | bytes 1572868
  70.8 13.5 %copy-start.9 = (bf16[512,512]{1,0:T(8,128)(2,1)}, bf16[512,512]{1,0:T(8,128)(2,1)S(1)}, u32[]{:S(2)}) copy-start(bf16[512,512]{1,0:T(8,128)(2,1)S(1)} %collective-permute-done.11.refs_7_) | copy-start | bytes 1572868
  70.8 21.1 %collective-permute-start.16 = (bf16[512,512]{1,0:T(8,128)(2,1)S(1)}, bf16[512,512]{1,0:T(8,128)(2,1)S(1)}, u32[]{:S(2)}, u32[]{:S(2)}) collective-permute-start(bf16[512,512]{1,0:T(8,128)(2,1)S(1)} %collective-permute-done.12.refs_8_), channel_id=1, source_target_pairs={{0,4},{1,5},{2,6},{3,7},{4,12},{5,13},{6,14},{7,15},{12,8},{13,9},... | collective-permute-start | bytes 1572872 | tf_op jit(solution)/shard_map/ppermute | solution.py:50
  73.1 11.2 %copy-start.10 = (bf16[512,512]{1,0:T(8,128)(2,1)}, bf16[512,512]{1,0:T(8,128)(2,1)S(1)}, u32[]{:S(2)}) copy-start(bf16[512,512]{1,0:T(8,128)(2,1)S(1)} %collective-permute-done.13.refs_9_) | copy-start | bytes 1572868
  73.1 22.0 %collective-permute-start.15 = (bf16[512,512]{1,0:T(8,128)(2,1)S(1)}, bf16[512,512]{1,0:T(8,128)(2,1)S(1)}, u32[]{:S(2)}, u32[]{:S(2)}) collective-permute-start(bf16[512,512]{1,0:T(8,128)(2,1)S(1)} %collective-permute-done.12.refs_8_), channel_id=1, source_target_pairs={{0,16},{16,0},{1,17},{17,1},{2,18},{18,2},{3,19},{19,3},{4,20},{20... | collective-permute-start | bytes 1572872 | tf_op jit(solution)/shard_map/ppermute | solution.py:58
  83.3 13.5 %collective-permute-start.14 = (bf16[512,512]{1,0:T(8,128)(2,1)}, bf16[512,512]{1,0:T(8,128)(2,1)S(1)}, u32[]{:S(2)}, u32[]{:S(2)}) collective-permute-start(bf16[512,512]{1,0:T(8,128)(2,1)} %copy-done.3), channel_id=1, source_target_pairs={{0,2},{1,3},{2,0},{3,1},{4,6},{5,7},{6,4},{7,5},{8,10},{9,11},{10,... | collective-permute-start | bytes 1572872 | tf_op jit(solution)/shard_map/ppermute | solution.py:54
  91.9 4.9 %copy-start.11 = (bf16[512,512]{1,0:T(8,128)(2,1)}, bf16[512,512]{1,0:T(8,128)(2,1)S(1)}, u32[]{:S(2)}) copy-start(bf16[512,512]{1,0:T(8,128)(2,1)S(1)} %collective-permute-done.16.refs_11_) | copy-start | bytes 1572868
  95.2 1.7 %copy-start.12 = (bf16[512,512]{1,0:T(8,128)(2,1)}, bf16[512,512]{1,0:T(8,128)(2,1)S(1)}, u32[]{:S(2)}) copy-start(bf16[512,512]{1,0:T(8,128)(2,1)S(1)} %collective-permute-done.15.refs_10_) | copy-start | bytes 1572868
  96.8 0.8 copy-start.13
  105.7 12.8 %all-to-all-start.1 = ((bf16[16,3,16,128]{3,2,1,0:T(8,128)(2,1)}), bf16[16,3,16,128]{3,2,1,0:T(8,128)(2,1)S(1)}, u32[]{:S(2)}, u32[]{:S(2)}) async-start(bf16[16,3,16,128]{3,2,1,0:T(8,128)(2,1)} %rows_4.1), calls=%async_computation.1 | async-start | bytes 393216 | tf_op jit(solution)/shard_map/all_to_all | solution.py:521
  118.6 0.7 copy-start

commit v9 on v8

--- a/solution.py
+++ b/solution.py
@@ -77,9 +77,11 @@
                     out.append(chip * 2 + (core ^ other))
                 return out
 
-            one = blocks(0, 0) + blocks(0, 1)
-            two_a, two_b, three_a, three_b = blocks(1, 0), blocks(1, 1), blocks(2, 0), blocks(2, 1)
-            table.append(one + two_a + two_b + three_a + three_b)
+            def both(step):
+                return [block for pair in zip(blocks(step, 0), blocks(step, 1)) for block in pair]
+
+            three = both(2)
+            table.append(both(0) + both(1) + [three[0], three[2], three[3], three[1]])
     return np.array(table, np.int32)
 
 
@@ -104,9 +106,9 @@
     depth = count * rows
     copies = [
         pltpu.make_async_copy(
-            piece_refs[which].at[pl.ds(start, rows)], weight.at[pl.ds(i * rows, rows)], sems.at[i]
+            piece_refs[which].at[pl.ds(start, size)], weight.at[pl.ds(place, size)], sems.at[i]
         )
-        for i, (which, start) in enumerate(layout)
+        for i, (which, start, size, place) in enumerate(layout)
     ]
 
     @pl.when((step == 0) & (half == 0))
@@ -114,12 +116,13 @@
         for copy in copies:
             copy.start()
 
-    for i in range(0, len(copies), count):
-
-        @pl.when((step == i // count) & (half == 0))
+    for i in range(weight.shape[0] // depth):
+
+        @pl.when((step == i) & (half == 0))
         def _():
-            for copy in copies[i : i + count]:
-                copy.wait()
+            for copy, (_, _, _, place) in zip(copies, layout):
+                if place // depth == i:
+                    copy.wait()
 
     if carry_ref is not None:
         carried = pltpu.make_async_copy(carry_ref, carry, sems.at[len(layout)])
@@ -340,7 +343,7 @@
         name="split",
     )(core.reshape(1), kv_weight, kv_weight)
     taken = swap_core(give)
-    swapped_states, _ = lax.optimization_barrier((prompt_states, keep))
+    swapped_states, _ = lax.optimization_barrier((prompt_states, taken))
     other = swap_core(swapped_states)
 
     def square_sums(tied):
@@ -413,12 +416,15 @@
 
     def product(blocks, base, count, pieces, carry, name, last=None):
         arrays, layout = [], []
-        for array, start in pieces:
-            at = [i for i, known in enumerate(arrays) if known is array]
-            if not at:
-                arrays.append(array)
-                at = [len(arrays) - 1]
-            layout.append((at[0], start))
+        for index, piece in enumerate(pieces):
+            place = index * rows_dev
+            for array, start, rows in piece:
+                at = [i for i, known in enumerate(arrays) if known is array]
+                if not at:
+                    arrays.append(array)
+                    at = [len(arrays) - 1]
+                layout.append((at[0], start, rows, place))
+                place += rows
         steps = len(pieces) // count
 
         def token_spec(k):
@@ -459,7 +465,7 @@
                 grid=(steps, 2),
                 in_specs=in_specs + [anywhere] * len(arrays),
                 out_specs=out_specs,
-                scratch_shapes=scratch + [pltpu.SemaphoreType.DMA((len(pieces) + 1,))],
+                scratch_shapes=scratch + [pltpu.SemaphoreType.DMA((len(layout) + 1,))],
             ),
             out_shape=out_shape,
             compiler_params=pltpu.CompilerParams(vmem_limit_bytes=60 * 2**20),
@@ -471,39 +477,36 @@
         blocks = jnp.array(block_table())[lax.axis_index("replica") * 16 + section]
 
         def starts(*arrays):
-            return [(array, 0) for array in arrays]
+            return [[(array, 0, rows_dev)] for array in arrays]
 
         tie = lax.optimization_barrier
-        a_behind, a_own_y = along_ring(keep), across_y(keep)
-
-        squares = square_sums(keep)
-
-        b_behind = along_ring(tie((taken, a_behind, squares))[0])
-        b_own_y = across_y(tie((taken, a_own_y, squares))[0])
-        a_ahead = across_replica(a_behind)
-        all_q = gather_queries((squares, a_own_y))
-
-        a_opposite = along_ring(tie((a_behind, b_behind, other))[0])
-        a_behind_y = across_y(tie((a_behind, b_own_y, other))[0])
-        b_ahead = across_replica(tie((b_behind, a_ahead, other))[0])
-        factor, owners, rows = swap_small(tie((squares, a_ahead))[0])
-        ones = starts(keep, a_behind, a_own_y, taken, b_behind, b_own_y)
-        total = product(blocks, 0, 3, ones, None, "rows_1")
-
-        b_opposite = along_ring(tie((b_behind, a_opposite, total))[0])
-        b_behind_y = across_y(tie((b_behind, a_behind_y, total))[0])
-        a_ahead_y = across_replica(tie((a_behind_y, b_ahead, total))[0])
-        all_q, owners, rows, _ = tie((all_q, owners, rows, a_opposite))
+
+        def both(array):
+            return [[(array, half, rows_dev)] for half in (0, rows_dev)]
+
+        own = jnp.concatenate([keep, taken], axis=0)
+        behind, own_y = along_ring(own), across_y(own)
+        squares = square_sums(own)
+
+        source, squares, _ = tie((behind, squares, own_y))
+        opposite, behind_y, ahead = along_ring(source), across_y(source), across_replica(source)
+        total = product(blocks, 0, 2, both(own) + both(behind) + both(own_y), None, "rows_1")
+        factor, owners, rows = swap_small(squares)
+        all_q = gather_queries(squares)
+
+        cut = rows_dev + rows_dev // 2
+        source, source_y, source_x, total, owners, rows, all_q = tie(
+            (behind_y, opposite, ahead, total, owners, rows, all_q)
+        )
+        opposite_y_b = along_ring(source[rows_dev:])
+        opposite_y_a = across_y(source_y[:rows_dev])
+        ahead_y_x = across_replica(source[:cut])
+        ahead_y_y = across_y(source_x[cut:])
         image_q, slot = place_images(all_q, owners, rows)
-        twos = starts(a_ahead, a_opposite, a_behind_y, b_ahead)
-        total, image_q, slot = tie((product(blocks, 6, 2, twos, total, "rows_2"), image_q, slot))
-
-        a_opposite_y = across_y(tie((a_opposite, b_behind_y, total))[0])
-        b_opposite_y = along_ring(tie((b_behind_y, b_opposite, total))[0])
-        b_ahead_y = across_replica(tie((b_behind_y, a_ahead_y, total))[0])
-        total = product(blocks, 10, 3, starts(b_opposite, b_behind_y, a_ahead_y), total, "rows_3")
-        lasts = starts(a_opposite_y, b_ahead_y, b_opposite_y)
-        slots = product(blocks, 13, 3, lasts, total, "rows_4", last=(image_q, slot, factor))
+        total = product(blocks, 6, 2, both(ahead) + both(opposite) + both(behind_y), total, "rows_2")
+        ahead_y_b = [(ahead_y_x, rows_dev, cut - rows_dev), (ahead_y_y, 0, 2 * rows_dev - cut)]
+        lasts = starts(ahead_y_x, opposite_y_a, opposite_y_b) + [ahead_y_b]
+        slots = product(blocks, 12, 2, lasts, total, "rows_3", last=(image_q, slot, factor))
         length, slots = tie((context_length, slots))
         res_out, res_top, res_sum = resident(length)
     else:
@@ -514,9 +517,9 @@
         a = gather_plain(keep)
         b = gather_plain(taken)
         chips = jnp.array([chip for chip, _, _ in a], jnp.int32)
-        total = product(chips * 2 + core, 0, 2, [piece[1:] for piece in a], None, "rows_a")
+        total = product(chips * 2 + core, 0, 2, [[(array, start, rows_dev)] for _, array, start in a], None, "rows_a")
         slots = product(
-            chips * 2 + 1 - core, 0, 2, [piece[1:] for piece in b], total, "rows_b", last=(image_q, slot, factor)
+            chips * 2 + 1 - core, 0, 2, [[(array, start, rows_dev)] for _, array, start in b], total, "rows_b", last=(image_q, slot, factor)
         )
     got = lax.all_to_all(slots, "section", split_axis=0, concat_axis=0, tiled=True)
 

time: 123 us -> 125 us (1.016)
  waiting for transfers between devices: 21.3 us -> 35 us
  starting transfers between devices: 38.4 us -> 26.1 us
  local copies, waits for them, and re-layouts: 6.73 us -> 9.54 us
  Pallas kernels: 53.8 us -> 51 us
    all_to_all x1, waiting for transfers between devices: 0.01 us -> 12.1 us  [gather_queries(): lax.all_to_all(send_q, 'section', split_axis=0, concat_axis=0, tiled=True)]
    ppermute x4 -> x2, starting transfers between devices: 13.4 us -> 3.68 us  [across_replica(): return lax.ppermute(x, 'replica', [(0, 1), (1, 0)])]
    ppermute x5 -> x3, waiting for transfers between devices: 8.49 us -> 14.6 us  [along_ring(): return lax.ppermute(x, ('replica', 'section'), perm)]
    ppermute x4 -> x2, waiting for transfers between devices: 3.25 us -> 0.01 us  [across_replica(): return lax.ppermute(x, 'replica', [(0, 1), (1, 0)])]
    ppermute x5 -> x4, starting transfers between devices: 8.2 us -> 5.27 us  [across_y(): return lax.ppermute(x, 'section', [(i, i ^ 2) for i in range(16)])]
    ppermute x5 -> x4, waiting for transfers between devices: 5.43 us -> 2.65 us  [across_y(): return lax.ppermute(x, 'section', [(i, i ^ 2) for i in range(16)])]
    pallas_call x4 -> x3, Pallas kernels: 35.4 us -> 32.7 us  [product(): pl.pallas_call(body, grid_spec=pltpu.PrefetchScalarGridSpec(num_scalar_pr...]
    slice x0 -> x4, local copies, waits for them, and re-layouts: none -> 2.66 us  [the longest x1 0.97 us: per_device(): ahead_y_y = across_y(source_x[cut:])]
  transfers between devices with their start and end apart: 19 -> 14, of which waited for: 10 -> 7; matrix products, arithmetic and copies ran while one was open for 5% -> 8% of each run, Pallas kernels for 33% -> 29%
where the time goes in v9:
time: 125 us; the launch traced here: 124 us
  Pallas kernels  51 us (41%)
  waiting for transfers between devices  35 us (28%)
  starting transfers between devices  26.1 us (21%)
  local copies, waits for them, and re-layouts  9.54 us (8%)
  other arithmetic  1.94 us (2%)
    pallas_call x3, Pallas kernels, product(): pl.pallas_call(body, grid_spec=pltpu.PrefetchScalarGridSpec(num_scalar_pr...  32.7 us
    ppermute x3, waiting for transfers between devices, along_ring(): return lax.ppermute(x, ('replica', 'section'), perm)  14.6 us
    all_to_all x1, waiting for transfers between devices, gather_queries(): lax.all_to_all(send_q, 'section', split_axis=0, concat_axis=0, tiled=True)  12.1 us
    pallas_call x1, Pallas kernels, square_sums(): pl.pallas_call(square_kernel, grid=(8,), in_specs=[pl.BlockSpec((tokens /...  7.6 us
    ppermute x3, starting transfers between devices, along_ring(): return lax.ppermute(x, ('replica', 'section'), perm)  7.33 us
    pallas_call x1, Pallas kernels, resident(): pl.pallas_call(resident_kernel, grid_spec=pltpu.PrefetchScalarGridSpec(nu...  5.36 us
    ppermute x4, starting transfers between devices, across_y(): return lax.ppermute(x, 'section', [(i, i ^ 2) for i in range(16)])  5.27 us
    all_to_all x1, starting transfers between devices, per_device(): lax.all_to_all(slots, 'section', split_axis=0, concat_axis=0, tiled=True)  5.07 us
  transfers between devices with their start and end apart: 14, of which 7 were waited for; matrix products, arithmetic and copies ran while one was open for 8% of the time, Pallas kernels for 29%

profile of v9, /device:TPU:0, one launch (start us, length us, event | category | flops | bytes accessed | tf_op | source)
XLA Modules:
  0.0 124.0 jit_solution(6687783090277938487)
XLA Ops:
  0.0 2.0 %split.1 = (bf16[512,512]{1,0:T(8,128)(2,1)}, bf16[512,512]{1,0:T(8,128)(2,1)}) custom-call(s32[1]{0:T(128)} %bitcast.1.core_ref, bf16[512,1024]{1,0:T(8,128)(2,1)} %give_in.1, bf16[512,1024]{1,0:T(8,128)(2,1)} %give_in.1), custom_call_target="tpu_custom_call" | custom-call | bytes 262144 | tf_op jit(solution)/shard_map/split/pallas_call | solution.py:330
  2.1 0.5 collective-permute-start
  2.5 1.7 %collective-permute-done = bf16[512,512]{1,0:T(8,128)(2,1)S(1)} collective-permute-done((bf16[512,512]{1,0:T(8,128)(2,1)}, bf16[512,512]{1,0:T(8,128)(2,1)S(1)}, u32[]{:S(2)}, u32[]{:S(2)}) %collective-permute-start) | collective-permute-done | bytes 524320 | tf_op jit(solution)/shard_map/ppermute | solution.py:30
  4.3 0.4 collective-permute-start.6
  4.6 1.1 constant_dynamic-update-slice_fusion.1
  5.8 0.0 copy-start.2
  5.8 0.0 copy-start.5
  5.8 0.0 copy-start.6
  5.8 0.0 copy-start.7
  5.8 2.8 %collective-permute-start.1 = (bf16[1024,512]{1,0:T(8,128)(2,1)S(1)}, bf16[1024,512]{1,0:T(8,128)(2,1)}, u32[]{:S(2)}, u32[]{:S(2)}) collective-permute-start(bf16[1024,512]{1,0:T(8,128)(2,1)S(1)} %constant_dynamic-update-slice_fusion.refs_4_), channel_id=1, source_target_pairs={{0,4},{1,5},{2,6},{3,7},{4,12},{5,13},{6,14},{7,15},{12,8},{13,9},... | collective-permute-start | bytes 3145736 | tf_op jit(solution)/shard_map/ppermute | solution.py:50
  8.6 1.5 %collective-permute-start.2 = (bf16[1024,512]{1,0:T(8,128)(2,1)S(1)}, bf16[1024,512]{1,0:T(8,128)(2,1)}, u32[]{:S(2)}, u32[]{:S(2)}) collective-permute-start(bf16[1024,512]{1,0:T(8,128)(2,1)S(1)} %constant_dynamic-update-slice_fusion.refs_4_), channel_id=1, source_target_pairs={{0,2},{1,3},{2,0},{3,1},{4,6},{5,7},{6,4},{7,5},{8,10},{9,11},{10,... | collective-permute-start | bytes 3145736 | tf_op jit(solution)/shard_map/ppermute | solution.py:54
  10.1 7.6 %squares.1 = f32[512,1]{1,0:T(8,128)} custom-call(bf16[512,8192]{1,0:T(8,128)(2,1)} %refs_1_.5), custom_call_target="tpu_custom_call" | custom-call | bytes 262144 | tf_op jit(solution)/shard_map/squares/pallas_call | solution.py:351
  17.7 0.0 copy-done.2
  17.7 1.1 reduce
  18.8 14.6 %collective-permute-done.1.refs_5_ = bf16[1024,512]{1,0:T(8,128)(2,1)} collective-permute-done((bf16[1024,512]{1,0:T(8,128)(2,1)S(1)}, bf16[1024,512]{1,0:T(8,128)(2,1)}, u32[]{:S(2)}, u32[]{:S(2)}) %collective-permute-start.1) | collective-permute-done | bytes 1048608 | tf_op jit(solution)/shard_map/ppermute | solution.py:50
  33.4 0.4 collective-permute-done.2.refs_6_
  33.8 1.5 %collective-permute-start.3 = (bf16[1024,512]{1,0:T(8,128)(2,1)}, bf16[1024,512]{1,0:T(8,128)(2,1)S(1)}, u32[]{:S(2)}, u32[]{:S(2)}) collective-permute-start(bf16[1024,512]{1,0:T(8,128)(2,1)} %collective-permute-done.1.refs_5_), channel_id=1, source_target_pairs={{0,2},{1,3},{2,0},{3,1},{4,6},{5,7},{6,4},{7,5},{8,10},{9,11},{10,... | collective-permute-start | bytes 3145736 | tf_op jit(solution)/shard_map/ppermute | solution.py:54
  35.3 2.6 %collective-permute-start.4 = (bf16[1024,512]{1,0:T(8,128)(2,1)}, bf16[1024,512]{1,0:T(8,128)(2,1)S(1)}, u32[]{:S(2)}, u32[]{:S(2)}) collective-permute-start(bf16[1024,512]{1,0:T(8,128)(2,1)} %collective-permute-done.1.refs_5_), channel_id=1, source_target_pairs={{0,4},{1,5},{2,6},{3,7},{4,12},{5,13},{6,14},{7,15},{12,8},{13,9},... | collective-permute-start | bytes 3145736 | tf_op jit(solution)/shard_map/ppermute | solution.py:50
  37.9 1.5 %collective-permute-start.5 = (bf16[1024,512]{1,0:T(8,128)(2,1)}, bf16[1024,512]{1,0:T(8,128)(2,1)}, u32[]{:S(2)}, u32[]{:S(2)}) collective-permute-start(bf16[1024,512]{1,0:T(8,128)(2,1)} %collective-permute-done.1.refs_5_), channel_id=1, source_target_pairs={{0,16},{16,0},{1,17},{17,1},{2,18},{18,2},{3,19},{19,3},{4,20},{20... | collective-permute-start | bytes 3145736 | tf_op jit(solution)/shard_map/ppermute | solution.py:58
  39.4 0.0 copy-done.5
  39.4 0.8 broadcast_in_dim.6
  40.3 3.6 %all-to-all-start = ((bf16[16,8,2048]{2,1,0:T(8,128)(2,1)}), bf16[16,8,2048]{2,1,0:T(8,128)(2,1)S(1)}, u32[]{:S(2)}, u32[]{:S(2)}) async-start(bf16[16,8,2048]{2,1,0:T(8,128)(2,1)} %bitcast.6), calls=%async_computation | async-start | bytes 1048576 | tf_op jit(solution)/shard_map/all_to_all | solution.py:379
  43.9 1.2 dynamic-slice_bitcast_fusion.block_ref
  45.1 0.0 copy-done.6
  45.1 0.0 copy-done.7
  45.1 0.1 add_convert_fusion
  45.2 0.3 collective-permute-start.7
  45.5 0.9 collective-permute-done.7
  46.4 0.1 slice_convert_fusion
  46.4 0.1 pad_add_fusion.1
  46.5 0.0 collective-permute-done.6.refs_2_.refs_3_
  46.5 11.2 %rows_1.1.refs_4_ = f32[1024,512]{1,0:T(8,128)} custom-call(s32[16]{0:T(128)} %dynamic-slice_bitcast_fusion.block_ref, bf16[512,8192]{1,0:T(8,128)(2,1)} %refs_1_.5, bf16[512,8192]{1,0:T(8,128)(2,1)} %refs_1_.5, bf16[512,8192]{1,0:T(8,128)(2,1)} %collective-permute-done.6.refs_2_.refs_3_, bf16[512,8192]{1,0:T(8,128)(2,1)} %collective-permute-done.6.refs_2_.refs_3_, ...), custom_call_target="tpu_custom_call" | custom-call | bytes 262144 | tf_op jit(solution)/shard_map/rows_1/pallas_call | solution.py:461
  57.8 12.1 %all-to-all-done = bf16[16,8,2048]{2,1,0:T(8,128)(2,1)S(1)} async-done(((bf16[16,8,2048]{2,1,0:T(8,128)(2,1)}), bf16[16,8,2048]{2,1,0:T(8,128)(2,1)S(1)}, u32[]{:S(2)}, u32[]{:S(2)}) %all-to-all-start) | async-done | bytes 524320 | tf_op jit(solution)/shard_map/all_to_all | solution.py:379
  69.9 0.0 collective-permute-done.3.refs_7_
  69.9 0.0 collective-permute-done.4.refs_6_
  69.9 0.0 copy-start.1
  69.9 0.0 collective-permute-done.5.refs_5_
  69.9 0.1 slice.28
  70.0 2.2 %collective-permute-start.8 = (bf16[768,512]{1,0:T(8,128)(2,1)S(1)}, bf16[768,512]{1,0:T(8,128)(2,1)}, u32[]{:S(2)}, u32[]{:S(2)}) collective-permute-start(bf16[768,512]{1,0:T(8,128)(2,1)S(1)} %slice.28), channel_id=1, source_target_pairs={{0,16},{16,0},{1,17},{17,1},{2,18},{18,2},{3,19},{19,3},{4,20},{20... | collective-permute-start | bytes 2359304 | tf_op jit(solution)/shard_map/ppermute | solution.py:58
  72.2 0.8 slice.30
  73.0 2.0 %collective-permute-start.10 = (bf16[512,512]{1,0:T(8,128)(2,1)}, bf16[512,512]{1,0:T(8,128)(2,1)}, u32[]{:S(2)}, u32[]{:S(2)}) collective-permute-start(bf16[512,512]{1,0:T(8,128)(2,1)} %slice.30), channel_id=1, source_target_pairs={{0,4},{1,5},{2,6},{3,7},{4,12},{5,13},{6,14},{7,15},{12,8},{13,9},... | collective-permute-start | bytes 1572872 | tf_op jit(solution)/shard_map/ppermute | solution.py:50
  75.0 0.8 slice.29
  75.8 2.2 %collective-permute-start.9 = (bf16[512,512]{1,0:T(8,128)(2,1)}, bf16[512,512]{1,0:T(8,128)(2,1)}, u32[]{:S(2)}, u32[]{:S(2)}) collective-permute-start(bf16[512,512]{1,0:T(8,128)(2,1)} %slice.29), channel_id=1, source_target_pairs={{0,2},{1,3},{2,0},{3,1},{4,6},{5,7},{6,4},{7,5},{8,10},{9,11},{10,... | collective-permute-start | bytes 1572872 | tf_op jit(solution)/shard_map/ppermute | solution.py:54
  78.0 1.0 copy.11.refs_6_
  79.0 1.0 slice.31
  80.0 0.1 collective-permute-start.11
  80.1 0.2 fusion
  80.3 0.6 copy.17
  80.9 0.0 copy-done
  81.0 0.0 copy-done.1
  81.0 11.7 %rows_2.1.refs_4_ = f32[1024,512]{1,0:T(8,128)} custom-call(s32[16]{0:T(128)} %dynamic-slice_bitcast_fusion.block_ref, bf16[512,8192]{1,0:T(8,128)(2,1)} %refs_1_.5, bf16[512,8192]{1,0:T(8,128)(2,1)} %refs_1_.5, bf16[512,8192]{1,0:T(8,128)(2,1)} %collective-permute-done.6.refs_2_.refs_3_, bf16[512,8192]{1,0:T(8,128)(2,1)} %collective-permute-done.6.refs_2_.refs_3_, ...), custom_call_target="tpu_custom_call" | custom-call | bytes 262144 | tf_op jit(solution)/shard_map/rows_2/pallas_call | solution.py:461
  92.6 0.6 pad_add_fusion.slot_ref
  93.2 2.2 %collective-permute-done.11.refs_10_ = bf16[256,512]{1,0:T(8,128)(2,1)S(1)} collective-permute-done((bf16[256,512]{1,0:T(8,128)(2,1)S(1)}, bf16[256,512]{1,0:T(8,128)(2,1)S(1)}, u32[]{:S(2)}, u32[]{:S(2)}) %collective-permute-start.11) | collective-permute-done | bytes 262176 | tf_op jit(solution)/shard_map/ppermute | solution.py:54
  95.4 0.0 collective-permute-done.10.refs_9_
  95.4 0.0 collective-permute-done.9.refs_8_
  95.5 0.0 collective-permute-done.8.refs_7_
  95.5 0.7 copy-done.4
  96.1 9.8 %rows_3.1 = bf16[16,3,16,128]{3,2,1,0:T(8,128)(2,1)} custom-call(s32[16]{0:T(128)} %dynamic-slice_bitcast_fusion.block_ref, s32[3,16]{1,0:T(4,128)} %pad_add_fusion.slot_ref, bf16[512,8192]{1,0:T(8,128)(2,1)} %refs_1_.5, bf16[512,8192]{1,0:T(8,128)(2,1)} %refs_1_.5, bf16[512,8192]{1,0:T(8,128)(2,1)} %collective-permute-done.6.refs_2_.refs_3_, ...), custom_call_target="tpu_custom_call" | custom-call | bytes 262144 | tf_op jit(solution)/shard_map/rows_3/pallas_call | solution.py:461
  106.0 5.1 %all-to-all-start.1 = ((bf16[16,3,16,128]{3,2,1,0:T(8,128)(2,1)}), bf16[16,3,16,128]{3,2,1,0:T(8,128)(2,1)S(1)}, u32[]{:S(2)}, u32[]{:S(2)}) async-start(bf16[16,3,16,128]{3,2,1,0:T(8,128)(2,1)} %rows_3.1), calls=%async_computation.1 | async-start | bytes 393216 | tf_op jit(solution)/shard_map/all_to_all | solution.py:524
  111.0 0.6 copy.16
  111.7 5.4 %resident.1 = (f32[8,32,128]{2,1,0:T(8,128)}, f32[32,128]{1,0:T(8,128)}, f32[32,128]{1,0:T(8,128)}) custom-call(s32[8]{0:T(128)} %length_ref, bf16[8,32,128]{2,1,0:T(8,128)(2,1)} %bitcast.34, bf16[8,256,1024]{2,1,0:T(8,128)(2,1)} %cache_ref.1), custom_call_target="tpu_custom_call" | custom-call | bytes 262144 | tf_op jit(solution)/shard_map/resident/pallas_call | solution.py:392
  117.0 3.0 %all-to-all-done.1.got_ref = bf16[16,3,16,128]{3,2,1,0:T(8,128)(2,1)S(1)} async-done(((bf16[16,3,16,128]{3,2,1,0:T(8,128)(2,1)}), bf16[16,3,16,128]{3,2,1,0:T(8,128)(2,1)S(1)}, u32[]{:S(2)}, u32[]{:S(2)}) %all-to-all-start.1) | async-done | bytes 196640 | tf_op jit(solution)/shard_map/all_to_all | solution.py:524
  120.0 0.7 copy-done.3
  120.7 3.3 %combine.1 = bf16[8,4096]{1,0:T(8,128)(2,1)} custom-call(bf16[16,3,16,128]{3,2,1,0:T(8,128)(2,1)} %copy-done.3, f32[8,32,128]{2,1,0:T(8,128)} %get-tuple-element.40.res_out_ref, f32[32,128]{1,0:T(8,128)} %get-tuple-element.41.res_top_ref, f32[32,128]{1,0:T(8,128)} %get-tuple-element.42.res_sum_ref), custom_call_target="tpu_custom_call" | custom-call | tf_op jit(solution)/shard_map/combine/pallas_call | solution.py:526
  (11 shorter events, 0.1 us)
Async XLA Ops:
  2.1 2.2 %collective-permute-start = (bf16[512,512]{1,0:T(8,128)(2,1)}, bf16[512,512]{1,0:T(8,128)(2,1)S(1)}, u32[]{:S(2)}, u32[]{:S(2)}) collective-permute-start(bf16[512,512]{1,0:T(8,128)(2,1)} %get-tuple-element.25), channel_id=1, source_target_pairs={{0,1},{1,0},{2,3},{3,2},{4,5},{5,4},{6,7},{7,6},{8,9},{9,8},{10,11... | collective-permute-start | bytes 1572872 | tf_op jit(solution)/shard_map/ppermute | solution.py:30
  4.3 42.3 %collective-permute-start.6 = (bf16[512,8192]{1,0:T(8,128)(2,1)}, bf16[512,8192]{1,0:T(8,128)(2,1)}, u32[]{:S(2)}, u32[]{:S(2)}) collective-permute-start(bf16[512,8192]{1,0:T(8,128)(2,1)} %refs_1_.5), channel_id=1, source_target_pairs={{0,1},{1,0},{2,3},{3,2},{4,5},{5,4},{6,7},{7,6},{8,9},{9,8},{10,11... | collective-permute-start | bytes 25165832 | tf_op jit(solution)/shard_map/ppermute | solution.py:30
  5.8 11.9 %copy-start.2 = (bf16[1024,512]{1,0:T(8,128)(2,1)}, bf16[1024,512]{1,0:T(8,128)(2,1)S(1)}, u32[]{:S(2)}) copy-start(bf16[1024,512]{1,0:T(8,128)(2,1)S(1)} %constant_dynamic-update-slice_fusion.refs_4_) | copy-start | bytes 3145732
  5.8 33.7 %copy-start.5 = (bf16[8,4096]{1,0:T(8,128)(2,1)S(1)}, bf16[8,4096]{1,0:T(8,128)(2,1)}, u32[]{:S(2)}) copy-start(bf16[8,4096]{1,0:T(8,128)(2,1)} %param.12) | copy-start | bytes 196612
  5.8 39.3 %copy-start.6 = (s32[8]{0:T(128)S(1)}, s32[8]{0:T(128)}, u32[]{:S(2)}) copy-start(s32[8]{0:T(128)} %param.11) | copy-start | bytes 100
  5.8 39.3 %copy-start.7 = (s32[8]{0:T(128)S(1)}, s32[8]{0:T(128)}, u32[]{:S(2)}) copy-start(s32[8]{0:T(128)} %param.10) | copy-start | bytes 100
  5.8 27.6 %collective-permute-start.1 = (bf16[1024,512]{1,0:T(8,128)(2,1)S(1)}, bf16[1024,512]{1,0:T(8,128)(2,1)}, u32[]{:S(2)}, u32[]{:S(2)}) collective-permute-start(bf16[1024,512]{1,0:T(8,128)(2,1)S(1)} %constant_dynamic-update-slice_fusion.refs_4_), channel_id=1, source_target_pairs={{0,4},{1,5},{2,6},{3,7},{4,12},{5,13},{6,14},{7,15},{12,8},{13,9},... | collective-permute-start | bytes 3145736 | tf_op jit(solution)/shard_map/ppermute | solution.py:50
  8.6 25.2 %collective-permute-start.2 = (bf16[1024,512]{1,0:T(8,128)(2,1)S(1)}, bf16[1024,512]{1,0:T(8,128)(2,1)}, u32[]{:S(2)}, u32[]{:S(2)}) collective-permute-start(bf16[1024,512]{1,0:T(8,128)(2,1)S(1)} %constant_dynamic-update-slice_fusion.refs_4_), channel_id=1, source_target_pairs={{0,2},{1,3},{2,0},{3,1},{4,6},{5,7},{6,4},{7,5},{8,10},{9,11},{10,... | collective-permute-start | bytes 3145736 | tf_op jit(solution)/shard_map/ppermute | solution.py:54
  33.8 36.1 %collective-permute-start.3 = (bf16[1024,512]{1,0:T(8,128)(2,1)}, bf16[1024,512]{1,0:T(8,128)(2,1)S(1)}, u32[]{:S(2)}, u32[]{:S(2)}) collective-permute-start(bf16[1024,512]{1,0:T(8,128)(2,1)} %collective-permute-done.1.refs_5_), channel_id=1, source_target_pairs={{0,2},{1,3},{2,0},{3,1},{4,6},{5,7},{6,4},{7,5},{8,10},{9,11},{10,... | collective-permute-start | bytes 3145736 | tf_op jit(solution)/shard_map/ppermute | solution.py:54
  35.3 34.6 %collective-permute-start.4 = (bf16[1024,512]{1,0:T(8,128)(2,1)}, bf16[1024,512]{1,0:T(8,128)(2,1)S(1)}, u32[]{:S(2)}, u32[]{:S(2)}) collective-permute-start(bf16[1024,512]{1,0:T(8,128)(2,1)} %collective-permute-done.1.refs_5_), channel_id=1, source_target_pairs={{0,4},{1,5},{2,6},{3,7},{4,12},{5,13},{6,14},{7,15},{12,8},{13,9},... | collective-permute-start | bytes 3145736 | tf_op jit(solution)/shard_map/ppermute | solution.py:50
  37.9 32.0 %collective-permute-start.5 = (bf16[1024,512]{1,0:T(8,128)(2,1)}, bf16[1024,512]{1,0:T(8,128)(2,1)}, u32[]{:S(2)}, u32[]{:S(2)}) collective-permute-start(bf16[1024,512]{1,0:T(8,128)(2,1)} %collective-permute-done.1.refs_5_), channel_id=1, source_target_pairs={{0,16},{16,0},{1,17},{17,1},{2,18},{18,2},{3,19},{19,3},{4,20},{20... | collective-permute-start | bytes 3145736 | tf_op jit(solution)/shard_map/ppermute | solution.py:58
  40.3 29.6 %all-to-all-start = ((bf16[16,8,2048]{2,1,0:T(8,128)(2,1)}), bf16[16,8,2048]{2,1,0:T(8,128)(2,1)S(1)}, u32[]{:S(2)}, u32[]{:S(2)}) async-start(bf16[16,8,2048]{2,1,0:T(8,128)(2,1)} %bitcast.6), calls=%async_computation | async-start | bytes 1048576 | tf_op jit(solution)/shard_map/all_to_all | solution.py:379
  45.2 1.2 collective-permute-start.7
  69.9 11.0 %copy-start = (bf16[1024,512]{1,0:T(8,128)(2,1)}, bf16[1024,512]{1,0:T(8,128)(2,1)S(1)}, u32[]{:S(2)}) copy-start(bf16[1024,512]{1,0:T(8,128)(2,1)S(1)} %collective-permute-done.3.refs_7_) | copy-start | bytes 3145732
  69.9 11.0 %copy-start.1 = (bf16[1024,512]{1,0:T(8,128)(2,1)}, bf16[1024,512]{1,0:T(8,128)(2,1)S(1)}, u32[]{:S(2)}) copy-start(bf16[1024,512]{1,0:T(8,128)(2,1)S(1)} %collective-permute-done.4.refs_6_) | copy-start | bytes 3145732
  70.0 25.5 %collective-permute-start.8 = (bf16[768,512]{1,0:T(8,128)(2,1)S(1)}, bf16[768,512]{1,0:T(8,128)(2,1)}, u32[]{:S(2)}, u32[]{:S(2)}) collective-permute-start(bf16[768,512]{1,0:T(8,128)(2,1)S(1)} %slice.28), channel_id=1, source_target_pairs={{0,16},{16,0},{1,17},{17,1},{2,18},{18,2},{3,19},{19,3},{4,20},{20... | collective-permute-start | bytes 2359304 | tf_op jit(solution)/shard_map/ppermute | solution.py:58
  73.0 22.4 %collective-permute-start.10 = (bf16[512,512]{1,0:T(8,128)(2,1)}, bf16[512,512]{1,0:T(8,128)(2,1)}, u32[]{:S(2)}, u32[]{:S(2)}) collective-permute-start(bf16[512,512]{1,0:T(8,128)(2,1)} %slice.30), channel_id=1, source_target_pairs={{0,4},{1,5},{2,6},{3,7},{4,12},{5,13},{6,14},{7,15},{12,8},{13,9},... | collective-permute-start | bytes 1572872 | tf_op jit(solution)/shard_map/ppermute | solution.py:50
  75.8 19.6 %collective-permute-start.9 = (bf16[512,512]{1,0:T(8,128)(2,1)}, bf16[512,512]{1,0:T(8,128)(2,1)}, u32[]{:S(2)}, u32[]{:S(2)}) collective-permute-start(bf16[512,512]{1,0:T(8,128)(2,1)} %slice.29), channel_id=1, source_target_pairs={{0,2},{1,3},{2,0},{3,1},{4,6},{5,7},{6,4},{7,5},{8,10},{9,11},{10,... | collective-permute-start | bytes 1572872 | tf_op jit(solution)/shard_map/ppermute | solution.py:54
  80.0 15.5 %collective-permute-start.11 = (bf16[256,512]{1,0:T(8,128)(2,1)S(1)}, bf16[256,512]{1,0:T(8,128)(2,1)S(1)}, u32[]{:S(2)}, u32[]{:S(2)}) collective-permute-start(bf16[256,512]{1,0:T(8,128)(2,1)S(1)} %slice.31), channel_id=1, source_target_pairs={{0,2},{1,3},{2,0},{3,1},{4,6},{5,7},{6,4},{7,5},{8,10},{9,11},{10,... | collective-permute-start | bytes 786440 | tf_op jit(solution)/shard_map/ppermute | solution.py:54
  95.4 0.7 copy-start.4
  106.0 14.1 %all-to-all-start.1 = ((bf16[16,3,16,128]{3,2,1,0:T(8,128)(2,1)}), bf16[16,3,16,128]{3,2,1,0:T(8,128)(2,1)S(1)}, u32[]{:S(2)}, u32[]{:S(2)}) async-start(bf16[16,3,16,128]{3,2,1,0:T(8,128)(2,1)} %rows_3.1), calls=%async_computation.1 | async-start | bytes 393216 | tf_op jit(solution)/shard_map/all_to_all | solution.py:524
  120.0 0.7 copy-start.3

commit v10 on v9

--- a/solution.py
+++ b/solution.py
@@ -41,9 +41,9 @@
 RING = [0, 1, 3, 2]
 
 
-def along_ring(x):
+def along_ring(x, sign=1):
     perm = []
-    for rep, way in ((0, 1), (1, -1)):
+    for rep, way in ((0, sign), (1, -sign)):
         for p in range(4):
             for low in range(4):
                 perm.append((rep * 16 + RING[p] * 4 + low, rep * 16 + RING[(p + way) % 4] * 4 + low))
@@ -81,7 +81,11 @@
                 return [block for pair in zip(blocks(step, 0), blocks(step, 1)) for block in pair]
 
             three = both(2)
-            table.append(both(0) + both(1) + [three[0], three[2], three[3], three[1]])
+            places = [0] * 8
+            for i, name in enumerate(("own", "behind", "ahead", "opposite")):
+                chip = RING[ring[name] % 4] * 2
+                places[chip + y], places[chip + 1 - y] = i, 4 + i
+            table.append(both(0) + both(1) + [three[0], three[2], three[3], three[1]] + places)
     return np.array(table, np.int32)
 
 
@@ -100,8 +104,8 @@
 
 
 def accumulate(layout, token_refs, piece_refs, weight, total, sems, carry_ref=None, carry=None):
-    step, half = pl.program_id(0), pl.program_id(1)
-    tokens, rows = token_refs[0].shape
+    step = pl.program_id(0)
+    rows = token_refs[0].shape[1]
     count = len(token_refs) // 2
     depth = count * rows
     copies = [
@@ -110,49 +114,46 @@
         )
         for i, (which, start, size, place) in enumerate(layout)
     ]
-
-    @pl.when((step == 0) & (half == 0))
+    carried = []
+    if carry_ref is not None:
+        carried = [pltpu.make_async_copy(carry_ref, carry, sems.at[len(layout)])]
+
+    @pl.when(step == 0)
     def _():
-        for copy in copies:
+        for copy in copies + carried:
             copy.start()
 
     for i in range(weight.shape[0] // depth):
 
-        @pl.when((step == i) & (half == 0))
+        @pl.when(step == i)
         def _():
             for copy, (_, _, _, place) in zip(copies, layout):
                 if place // depth == i:
                     copy.wait()
 
+    states = jnp.concatenate(
+        [
+            jnp.concatenate([ref[...] for ref in token_refs[side * count : (side + 1) * count]], axis=1)
+            for side in range(2)
+        ],
+        axis=0,
+    )
+    block = weight[pl.ds(pl.multiple_of(step * depth, depth), depth), :]
+    product = jnp.dot(states, block, preferred_element_type=jnp.float32)
+
+    @pl.when(step == 0)
+    def _():
+        total[...] = product
+
+    @pl.when(step > 0)
+    def _():
+        total[...] += product
+
     if carry_ref is not None:
-        carried = pltpu.make_async_copy(carry_ref, carry, sems.at[len(layout)])
-
-        @pl.when((step == 0) & (half == 0))
+
+        @pl.when(step == pl.num_programs(0) - 1)
         def _():
-            carried.start()
-
-    for side in range(2):
-
-        @pl.when(half == side)
-        def _():
-            states = jnp.concatenate([ref[...] for ref in token_refs[side * count : (side + 1) * count]], axis=1)
-            block = weight[pl.ds(pl.multiple_of(step * depth, depth), depth), :]
-            product = jnp.dot(states, block, preferred_element_type=jnp.float32)
-            rows_of_side = pl.ds(side * tokens, tokens)
-
-            @pl.when(step == 0)
-            def _():
-                total[rows_of_side, :] = product
-
-            @pl.when(step > 0)
-            def _():
-                total[rows_of_side, :] += product
-
-    if carry_ref is not None:
-
-        @pl.when((step == pl.num_programs(0) - 1) & (half == 1))
-        def _():
-            carried.wait()
+            carried[0].wait()
             total[...] += carry[...]
 
 
@@ -181,13 +182,13 @@
     slots_ref, weight, carry, total, summed, stats, sems = refs[-7:]
     images = query_ref.shape[1] // GROUP
 
-    @pl.when((pl.program_id(0) == 0) & (pl.program_id(1) == 0))
+    @pl.when(pl.program_id(0) == 0)
     def _():
         slots_ref[...] = jnp.zeros_like(slots_ref)
 
     accumulate(layout, token_refs, piece_refs, weight, total, sems, carry_ref, carry)
 
-    @pl.when((pl.program_id(0) == pl.num_programs(0) - 1) & (pl.program_id(1) == 1))
+    @pl.when(pl.program_id(0) == pl.num_programs(0) - 1)
     def _():
         tokens = total.shape[0]
         queries = query_ref.shape[1]
@@ -370,17 +371,15 @@
         rows = jnp.concatenate([image_row, got[at : at + images].astype(jnp.int32)])
         return factor, owners, rows
 
-    def gather_queries(tied):
-        mine, _ = lax.optimization_barrier((queries, tied))
-        send_q = mine.reshape(decode_rows, 2, HALF_QH * HD).transpose(1, 0, 2)
-        send_q = jnp.broadcast_to(send_q[None], (n // 2, 2, decode_rows, HALF_QH * HD)).reshape(
-            n, decode_rows, HALF_QH * HD
+    query_halves = queries.reshape(decode_rows, 2, HALF_QH * HD)
+    keep_q = jnp.where(core == 0, query_halves[:, 0], query_halves[:, 1])
+    give_q = jnp.where(core == 0, query_halves[:, 1], query_halves[:, 0])
+
+    def place_images(all_q, owners, rows, chip_place):
+        chip_of = jnp.sum(
+            jnp.where(owners[:, None] // 2 == jnp.arange(n // 2)[None, :], chip_place[None, :], 0), axis=1
         )
-        all_q = lax.all_to_all(send_q, "section", split_axis=0, concat_axis=0, tiled=True)
-        return all_q.reshape(n * decode_rows, HALF_QH * HD)
-
-    def place_images(all_q, owners, rows):
-        target = owners * decode_rows + rows
+        target = chip_of * (2 * decode_rows) + (owners % 2 ^ core) * decode_rows + rows
         pick = (target[:, None] == jnp.arange(n * decode_rows)[None, :]).astype(jnp.bfloat16)
         image_q = jnp.dot(pick, all_q, preferred_element_type=jnp.float32).astype(jnp.bfloat16)
         image_q = image_q.reshape(2 * images, HALF_KVH, GROUP, HD).transpose(1, 0, 2, 3)
@@ -428,7 +427,7 @@
         steps = len(pieces) // count
 
         def token_spec(k):
-            return pl.BlockSpec((tokens, rows_dev), lambda i, half, block_ref, *_: (0, block_ref[base + count * i + k]))
+            return pl.BlockSpec((tokens, rows_dev), lambda i, block_ref, *_: (0, block_ref[base + count * i + k]))
 
         anywhere = pl.BlockSpec(memory_space=pl.ANY)
         in_specs = [token_spec(k) for k in range(count)] * 2
@@ -462,7 +461,7 @@
             body,
             grid_spec=pltpu.PrefetchScalarGridSpec(
                 num_scalar_prefetch=len(scalars),
-                grid=(steps, 2),
+                grid=(steps,),
                 in_specs=in_specs + [anywhere] * len(arrays),
                 out_specs=out_specs,
                 scratch_shapes=scratch + [pltpu.SemaphoreType.DMA((len(layout) + 1,))],
@@ -474,7 +473,8 @@
         )(*scalars, *inputs, *arrays)
 
     if n == 16 and lax.axis_size("replica") == 2:
-        blocks = jnp.array(block_table())[lax.axis_index("replica") * 16 + section]
+        table = block_table()
+        blocks = jnp.array(table)[lax.axis_index("replica") * 16 + section]
 
         def starts(*arrays):
             return [[(array, 0, rows_dev)] for array in arrays]
@@ -487,22 +487,26 @@
         own = jnp.concatenate([keep, taken], axis=0)
         behind, own_y = along_ring(own), across_y(own)
         squares = square_sums(own)
-
-        source, squares, _ = tie((behind, squares, own_y))
+        own_q = jnp.concatenate([keep_q, swap_core(tie((give_q, taken))[0])], axis=0)
+        behind_q, ahead_q = along_ring(own_q), along_ring(own_q, -1)
+
+        source, squares, source_q, _ = tie((behind, squares, behind_q, (own_y, ahead_q)))
         opposite, behind_y, ahead = along_ring(source), across_y(source), across_replica(source)
+        opposite_q = along_ring(source_q)
         total = product(blocks, 0, 2, both(own) + both(behind) + both(own_y), None, "rows_1")
-        factor, owners, rows = swap_small(squares)
-        all_q = gather_queries(squares)
+        factor, owners, rows = swap_small(tie((squares, opposite_q))[0])
+        ring_q = jnp.concatenate([own_q, behind_q, ahead_q, opposite_q], axis=0)
 
         cut = rows_dev + rows_dev // 2
-        source, source_y, source_x, total, owners, rows, all_q = tie(
-            (behind_y, opposite, ahead, total, owners, rows, all_q)
+        source, source_y, source_x, total, owners, rows, ring_q = tie(
+            (behind_y, opposite, ahead, total, owners, rows, ring_q)
         )
+        all_q = jnp.concatenate([ring_q, across_y(ring_q)], axis=0)
         opposite_y_b = along_ring(source[rows_dev:])
         opposite_y_a = across_y(source_y[:rows_dev])
         ahead_y_x = across_replica(source[:cut])
         ahead_y_y = across_y(source_x[cut:])
-        image_q, slot = place_images(all_q, owners, rows)
+        image_q, slot = place_images(all_q, owners, rows, blocks[16:])
         total = product(blocks, 6, 2, both(ahead) + both(opposite) + both(behind_y), total, "rows_2")
         ahead_y_b = [(ahead_y_x, rows_dev, cut - rows_dev), (ahead_y_y, 0, 2 * rows_dev - cut)]
         lasts = starts(ahead_y_x, opposite_y_a, opposite_y_b) + [ahead_y_b]
@@ -513,7 +517,10 @@
         res_out, res_top, res_sum = resident(context_length)
         squares = square_sums(taken)
         factor, owners, rows = swap_small(squares)
-        image_q, slot = place_images(gather_queries(squares), owners, rows)
+        chip_q = jnp.concatenate([keep_q, swap_core(give_q)], axis=0)
+        groups = [list(range(side, n, 2)) for side in range(2)]
+        all_q = lax.all_gather(chip_q, "section", axis=0, tiled=True, axis_index_groups=groups)
+        image_q, slot = place_images(all_q, owners, rows, jnp.arange(n // 2))
         a = gather_plain(keep)
         b = gather_plain(taken)
         chips = jnp.array([chip for chip, _, _ in a], jnp.int32)

time: 125 us -> 136 us (1.088)
  waiting for transfers between devices: 35 us -> 45 us
  Pallas kernels: 51 us -> 46.1 us
  other arithmetic: 1.94 us -> 4.89 us
  local copies, waits for them, and re-layouts: 9.54 us -> 12.4 us
    ppermute x3 -> x6, waiting for transfers between devices: 14.6 us -> 33.6 us  [along_ring(): return lax.ppermute(x, ('replica', 'section'), perm)]
    all_to_all x1 -> x0, waiting for transfers between devices: 12.1 us -> none  [gather_queries(): lax.all_to_all(send_q, 'section', split_axis=0, concat_axis=0, tiled=True)]
    pallas_call x3, Pallas kernels: 32.7 us -> 27.8 us  [product(): pl.pallas_call(body, grid_spec=pltpu.PrefetchScalarGridSpec(num_scalar_pr...]
    all_to_all x1 -> x0, starting transfers between devices: 3.57 us -> none  [gather_queries(): lax.all_to_all(send_q, 'section', split_axis=0, concat_axis=0, tiled=True)]
    ppermute x4 -> x5, waiting for transfers between devices: 2.65 us -> 6.16 us  [across_y(): return lax.ppermute(x, 'section', [(i, i ^ 2) for i in range(16)])]
    ppermute x3 -> x6, starting transfers between devices: 7.33 us -> 9.71 us  [along_ring(): return lax.ppermute(x, ('replica', 'section'), perm)]
    unnamed x19 -> x26, local copies, waits for them, and re-layouts: 3.13 us -> 5.2 us
    unnamed x0 -> x1, other arithmetic: none -> 1.39 us
  transfers between devices with their start and end apart: 14 -> 18, of which waited for: 7 -> 7; matrix products, arithmetic and copies ran while one was open for 8% -> 11% of each run, Pallas kernels for 29% -> 24%
where the time goes in v10:
time: 136 us; the launch traced here: 135 us
  Pallas kernels  46.1 us (34%)
  waiting for transfers between devices  45 us (33%)
  starting transfers between devices  25.3 us (19%)
  local copies, waits for them, and re-layouts  12.4 us (9%)
  other arithmetic  4.89 us (4%)
    ppermute x6, waiting for transfers between devices, along_ring(): return lax.ppermute(x, ('replica', 'section'), perm)  33.6 us
    pallas_call x3, Pallas kernels, product(): pl.pallas_call(body, grid_spec=pltpu.PrefetchScalarGridSpec(num_scalar_pr...  27.8 us
    ppermute x6, starting transfers between devices, along_ring(): return lax.ppermute(x, ('replica', 'section'), perm)  9.71 us
    pallas_call x1, Pallas kernels, square_sums(): pl.pallas_call(square_kernel, grid=(8,), in_specs=[pl.BlockSpec((tokens /...  7.61 us
    ppermute x5, waiting for transfers between devices, across_y(): return lax.ppermute(x, 'section', [(i, i ^ 2) for i in range(16)])  6.16 us
    ppermute x5, starting transfers between devices, across_y(): return lax.ppermute(x, 'section', [(i, i ^ 2) for i in range(16)])  5.57 us
    pallas_call x1, Pallas kernels, resident(): pl.pallas_call(resident_kernel, grid_spec=pltpu.PrefetchScalarGridSpec(nu...  5.36 us
    all_to_all x1, starting transfers between devices, per_device(): lax.all_to_all(slots, 'section', split_axis=0, concat_axis=0, tiled=True)  5.25 us
  transfers between devices with their start and end apart: 18, of which 7 were waited for; matrix products, arithmetic and copies ran while one was open for 11% of the time, Pallas kernels for 24%

profile of v10, /device:TPU:0, one launch (start us, length us, event | category | flops | bytes accessed | tf_op | source)
XLA Modules:
  0.0 135.2 jit_solution(7494142992608873328)
XLA Ops:
  0.0 2.1 %split.1 = (bf16[512,512]{1,0:T(8,128)(2,1)}, bf16[512,512]{1,0:T(8,128)(2,1)}) custom-call(s32[1]{0:T(128)} %bitcast.1.core_ref, bf16[512,1024]{1,0:T(8,128)(2,1)} %give_in.1, bf16[512,1024]{1,0:T(8,128)(2,1)} %give_in.1), custom_call_target="tpu_custom_call" | custom-call | bytes 262144 | tf_op jit(solution)/shard_map/split/pallas_call | solution.py:331
  2.1 0.5 collective-permute-start
  2.5 1.7 %collective-permute-done = bf16[512,512]{1,0:T(8,128)(2,1)S(1)} collective-permute-done((bf16[512,512]{1,0:T(8,128)(2,1)}, bf16[512,512]{1,0:T(8,128)(2,1)S(1)}, u32[]{:S(2)}, u32[]{:S(2)}) %collective-permute-start) | collective-permute-done | bytes 524320 | tf_op jit(solution)/shard_map/ppermute | solution.py:30
  4.3 0.4 collective-permute-start.9
  4.6 0.7 add_convert_fusion
  5.4 1.1 constant_dynamic-update-slice_fusion.1
  6.5 0.8 select_bitcast_fusion
  7.3 1.4 %constant_dynamic-update-slice_fusion.6 = (bf16[64,2048]{1,0:T(8,128)(2,1)}, bf16[8,2048]{1,0:T(8,128)(2,1)S(1)}) fusion(bf16[8,2,2048]{2,0,1:T(8,128)(2,1)} %bitcast.35, pred[]{:T(512)S(6)} %eq.18), kind=kLoop, calls=%fused_computation.16 | loop fusion | flops 16383 | bytes 131073
  8.7 2.8 %collective-permute-start.1 = (bf16[1024,512]{1,0:T(8,128)(2,1)S(1)}, bf16[1024,512]{1,0:T(8,128)(2,1)}, u32[]{:S(2)}, u32[]{:S(2)}) collective-permute-start(bf16[1024,512]{1,0:T(8,128)(2,1)S(1)} %constant_dynamic-update-slice_fusion.refs_4_), channel_id=1, source_target_pairs={{0,4},{1,5},{2,6},{3,7},{4,12},{5,13},{6,14},{7,15},{12,8},{13,9},... | collective-permute-start | bytes 3145736 | tf_op jit(solution)/shard_map/ppermute | solution.py:50
  11.5 1.5 %collective-permute-start.4 = (bf16[1024,512]{1,0:T(8,128)(2,1)S(1)}, bf16[1024,512]{1,0:T(8,128)(2,1)}, u32[]{:S(2)}, u32[]{:S(2)}) collective-permute-start(bf16[1024,512]{1,0:T(8,128)(2,1)S(1)} %constant_dynamic-update-slice_fusion.refs_4_), channel_id=1, source_target_pairs={{0,2},{1,3},{2,0},{3,1},{4,6},{5,7},{6,4},{7,5},{8,10},{9,11},{10,... | collective-permute-start | bytes 3145736 | tf_op jit(solution)/shard_map/ppermute | solution.py:54
  13.0 1.2 constant_dynamic-slice_fusion
  14.2 0.1 slice_bitcast_fusion.1
  14.2 0.0 collective-permute-start.2
  14.2 0.0 copy-start.8
  14.3 0.0 copy-start.9
  14.3 7.6 %squares.1 = f32[512,1]{1,0:T(8,128)} custom-call(bf16[512,8192]{1,0:T(8,128)(2,1)} %refs_1_.5), custom_call_target="tpu_custom_call" | custom-call | bytes 262144 | tf_op jit(solution)/shard_map/squares/pallas_call | solution.py:352
  21.9 1.1 reduce
  23.0 2.6 %collective-permute-start.3 = (bf16[16,2048]{1,0:T(8,128)(2,1)S(1)}, bf16[16,2048]{1,0:T(8,128)(2,1)S(1)}, u32[]{:S(2)}, u32[]{:S(2)}) collective-permute-start(bf16[16,2048]{1,0:T(8,128)(2,1)S(1)} %pad_maximum_fusion), channel_id=1, source_target_pairs={{0,4},{1,5},{2,6},{3,7},{4,12},{5,13},{6,14},{7,15},{12,8},{13,9},... | collective-permute-start | bytes 196616 | tf_op jit(solution)/shard_map/ppermute | solution.py:50
  25.6 0.3 collective-permute-start.5
  26.0 0.6 constant_dynamic-update-slice_fusion.5
  26.6 11.1 %collective-permute-done.3 = bf16[16,2048]{1,0:T(8,128)(2,1)S(1)} collective-permute-done((bf16[16,2048]{1,0:T(8,128)(2,1)S(1)}, bf16[16,2048]{1,0:T(8,128)(2,1)S(1)}, u32[]{:S(2)}, u32[]{:S(2)}) %collective-permute-start.3) | collective-permute-done | bytes 65568 | tf_op jit(solution)/shard_map/ppermute | solution.py:50
  37.7 0.6 constant_dynamic-update-slice_fusion.4
  38.3 0.7 collective-permute-done.5
  39.0 0.0 collective-permute-done.1.refs_5_
  39.0 1.6 %collective-permute-start.6 = (bf16[1024,512]{1,0:T(8,128)(2,1)}, bf16[1024,512]{1,0:T(8,128)(2,1)S(1)}, u32[]{:S(2)}, u32[]{:S(2)}) collective-permute-start(bf16[1024,512]{1,0:T(8,128)(2,1)} %collective-permute-done.1.refs_5_), channel_id=1, source_target_pairs={{0,2},{1,3},{2,0},{3,1},{4,6},{5,7},{6,4},{7,5},{8,10},{9,11},{10,... | collective-permute-start | bytes 3145736 | tf_op jit(solution)/shard_map/ppermute | solution.py:54
  40.6 1.7 %collective-permute-start.7 = (bf16[1024,512]{1,0:T(8,128)(2,1)}, bf16[1024,512]{1,0:T(8,128)(2,1)S(1)}, u32[]{:S(2)}, u32[]{:S(2)}) collective-permute-start(bf16[1024,512]{1,0:T(8,128)(2,1)} %collective-permute-done.1.refs_5_), channel_id=1, source_target_pairs={{0,4},{1,5},{2,6},{3,7},{4,12},{5,13},{6,14},{7,15},{12,8},{13,9},... | collective-permute-start | bytes 3145736 | tf_op jit(solution)/shard_map/ppermute | solution.py:50
  42.2 2.3 %collective-permute-start.8 = (bf16[1024,512]{1,0:T(8,128)(2,1)}, bf16[1024,512]{1,0:T(8,128)(2,1)S(1)}, u32[]{:S(2)}, u32[]{:S(2)}) collective-permute-start(bf16[1024,512]{1,0:T(8,128)(2,1)} %collective-permute-done.1.refs_5_), channel_id=1, source_target_pairs={{0,16},{16,0},{1,17},{17,1},{2,18},{18,2},{3,19},{19,3},{4,20},{20... | collective-permute-start | bytes 3145736 | tf_op jit(solution)/shard_map/ppermute | solution.py:58
  44.5 0.9 collective-permute-start.10
  45.5 0.6 constant_dynamic-update-slice_fusion.3
  46.1 21.8 %collective-permute-done.10 = bf16[16,2048]{1,0:T(8,128)(2,1)S(1)} collective-permute-done((bf16[16,2048]{1,0:T(8,128)(2,1)S(1)}, bf16[16,2048]{1,0:T(8,128)(2,1)S(1)}, u32[]{:S(2)}, u32[]{:S(2)}) %collective-permute-start.10) | collective-permute-done | bytes 65568 | tf_op jit(solution)/shard_map/ppermute | solution.py:50
  67.9 0.0 collective-permute-start.11
  67.9 0.6 constant_dynamic-update-slice_fusion.2
  68.5 0.5 collective-permute-done.11
  69.1 1.1 copy.13.refs_6_
  70.1 0.1 slice_convert_fusion
  70.2 0.1 pad_add_fusion.1
  70.3 0.0 collective-permute-done.9.refs_2_.refs_3_
  70.3 9.3 %rows_1.1.refs_4_ = f32[1024,512]{1,0:T(8,128)} custom-call(s32[24]{0:T(128)} %get-tuple-element.50.block_ref, bf16[512,8192]{1,0:T(8,128)(2,1)} %refs_1_.5, bf16[512,8192]{1,0:T(8,128)(2,1)} %refs_1_.5, bf16[512,8192]{1,0:T(8,128)(2,1)} %collective-permute-done.9.refs_2_.refs_3_, bf16[512,8192]{1,0:T(8,128)(2,1)} %collective-permute-done.9.refs_2_.refs_3_, ...), custom_call_target="tpu_custom_call" | custom-call | bytes 262144 | tf_op jit(solution)/shard_map/rows_1/pallas_call | solution.py:460
  79.7 0.0 collective-permute-done.7.refs_6_
  79.7 1.0 slice.43
  80.7 1.0 slice.45
  81.7 0.5 collective-permute-start.12
  82.2 1.6 %collective-permute-start.13 = (bf16[768,512]{1,0:T(8,128)(2,1)}, bf16[768,512]{1,0:T(8,128)(2,1)}, u32[]{:S(2)}, u32[]{:S(2)}) collective-permute-start(bf16[768,512]{1,0:T(8,128)(2,1)} %slice.43), channel_id=1, source_target_pairs={{0,16},{16,0},{1,17},{17,1},{2,18},{18,2},{3,19},{19,3},{4,20},{20... | collective-permute-start | bytes 2359304 | tf_op jit(solution)/shard_map/ppermute | solution.py:58
  83.9 0.8 slice.44
  84.7 1.5 %collective-permute-start.14 = (bf16[512,512]{1,0:T(8,128)(2,1)}, bf16[512,512]{1,0:T(8,128)(2,1)S(1)}, u32[]{:S(2)}, u32[]{:S(2)}) collective-permute-start(bf16[512,512]{1,0:T(8,128)(2,1)} %slice.44), channel_id=1, source_target_pairs={{0,2},{1,3},{2,0},{3,1},{4,6},{5,7},{6,4},{7,5},{8,10},{9,11},{10,... | collective-permute-start | bytes 1572872 | tf_op jit(solution)/shard_map/ppermute | solution.py:54
  86.2 1.3 collective-permute-start.15
  87.5 0.7 slice.46
  88.3 0.5 collective-permute-start.16
  88.8 0.1 select_reduce_fusion
  88.9 9.6 %rows_2.1.refs_4_ = f32[1024,512]{1,0:T(8,128)} custom-call(s32[24]{0:T(128)} %get-tuple-element.50.block_ref, bf16[512,8192]{1,0:T(8,128)(2,1)} %refs_1_.5, bf16[512,8192]{1,0:T(8,128)(2,1)} %refs_1_.5, bf16[512,8192]{1,0:T(8,128)(2,1)} %collective-permute-done.9.refs_2_.refs_3_, bf16[512,8192]{1,0:T(8,128)(2,1)} %collective-permute-done.9.refs_2_.refs_3_, ...), custom_call_target="tpu_custom_call" | custom-call | bytes 262144 | tf_op jit(solution)/shard_map/rows_2/pallas_call | solution.py:460
  98.5 0.6 pad_add_fusion.slot_ref
  99.1 1.3 fusion
  100.4 0.6 copy.19
  101.0 6.1 %collective-permute-done.16.refs_10_ = bf16[256,512]{1,0:T(8,128)(2,1)S(1)} collective-permute-done((bf16[256,512]{1,0:T(8,128)(2,1)}, bf16[256,512]{1,0:T(8,128)(2,1)S(1)}, u32[]{:S(2)}, u32[]{:S(2)}) %collective-permute-start.16) | collective-permute-done | bytes 262176 | tf_op jit(solution)/shard_map/ppermute | solution.py:54
  107.2 0.0 collective-permute-done.14.refs_8_
  107.2 0.7 copy-done.7
  107.9 0.2 copy-done.6
  108.1 8.9 %rows_3.1 = bf16[16,3,16,128]{3,2,1,0:T(8,128)(2,1)} custom-call(s32[24]{0:T(128)} %get-tuple-element.50.block_ref, s32[3,16]{1,0:T(4,128)} %pad_add_fusion.slot_ref, bf16[512,8192]{1,0:T(8,128)(2,1)} %refs_1_.5, bf16[512,8192]{1,0:T(8,128)(2,1)} %refs_1_.5, bf16[512,8192]{1,0:T(8,128)(2,1)} %collective-permute-done.9.refs_2_.refs_3_, ...), custom_call_target="tpu_custom_call" | custom-call | bytes 262144 | tf_op jit(solution)/shard_map/rows_3/pallas_call | solution.py:460
  117.0 5.2 %all-to-all-start = ((bf16[16,3,16,128]{3,2,1,0:T(8,128)(2,1)}), bf16[16,3,16,128]{3,2,1,0:T(8,128)(2,1)S(1)}, u32[]{:S(2)}, u32[]{:S(2)}) async-start(bf16[16,3,16,128]{3,2,1,0:T(8,128)(2,1)} %rows_3.1), calls=%async_computation | async-start | bytes 393216 | tf_op jit(solution)/shard_map/all_to_all | solution.py:531
  122.2 0.6 copy.18
  122.9 5.4 %resident.1 = (f32[8,32,128]{2,1,0:T(8,128)}, f32[32,128]{1,0:T(8,128)}, f32[32,128]{1,0:T(8,128)}) custom-call(s32[8]{0:T(128)} %length_ref, bf16[8,32,128]{2,1,0:T(8,128)(2,1)} %bitcast.38, bf16[8,256,1024]{2,1,0:T(8,128)(2,1)} %cache_ref.1), custom_call_target="tpu_custom_call" | custom-call | bytes 262144 | tf_op jit(solution)/shard_map/resident/pallas_call | solution.py:391
  128.2 3.0 %all-to-all-done.got_ref = bf16[16,3,16,128]{3,2,1,0:T(8,128)(2,1)S(1)} async-done(((bf16[16,3,16,128]{3,2,1,0:T(8,128)(2,1)}), bf16[16,3,16,128]{3,2,1,0:T(8,128)(2,1)S(1)}, u32[]{:S(2)}, u32[]{:S(2)}) %all-to-all-start) | async-done | bytes 196640 | tf_op jit(solution)/shard_map/all_to_all | solution.py:531
  131.2 0.7 copy-done.4
  131.9 3.3 %combine.1 = bf16[8,4096]{1,0:T(8,128)(2,1)} custom-call(bf16[16,3,16,128]{3,2,1,0:T(8,128)(2,1)} %copy-done.4, f32[8,32,128]{2,1,0:T(8,128)} %get-tuple-element.44.res_out_ref, f32[32,128]{1,0:T(8,128)} %get-tuple-element.45.res_top_ref, f32[32,128]{1,0:T(8,128)} %get-tuple-element.46.res_sum_ref), custom_call_target="tpu_custom_call" | custom-call | tf_op jit(solution)/shard_map/combine/pallas_call | solution.py:533
  (32 shorter events, 0.2 us)
Async XLA Ops:
  2.1 2.2 %collective-permute-start = (bf16[512,512]{1,0:T(8,128)(2,1)}, bf16[512,512]{1,0:T(8,128)(2,1)S(1)}, u32[]{:S(2)}, u32[]{:S(2)}) collective-permute-start(bf16[512,512]{1,0:T(8,128)(2,1)} %get-tuple-element.27), channel_id=1, source_target_pairs={{0,1},{1,0},{2,3},{3,2},{4,5},{5,4},{6,7},{7,6},{8,9},{9,8},{10,11... | collective-permute-start | bytes 1572872 | tf_op jit(solution)/shard_map/ppermute | solution.py:30
  4.3 66.0 %collective-permute-start.9 = (bf16[512,8192]{1,0:T(8,128)(2,1)}, bf16[512,8192]{1,0:T(8,128)(2,1)}, u32[]{:S(2)}, u32[]{:S(2)}) collective-permute-start(bf16[512,8192]{1,0:T(8,128)(2,1)} %refs_1_.5), channel_id=1, source_target_pairs={{0,1},{1,0},{2,3},{3,2},{4,5},{5,4},{6,7},{7,6},{8,9},{9,8},{10,11... | collective-permute-start | bytes 25165832 | tf_op jit(solution)/shard_map/ppermute | solution.py:30
  8.7 13.2 %copy-start.2 = (bf16[1024,512]{1,0:T(8,128)(2,1)}, bf16[1024,512]{1,0:T(8,128)(2,1)S(1)}, u32[]{:S(2)}) copy-start(bf16[1024,512]{1,0:T(8,128)(2,1)S(1)} %constant_dynamic-update-slice_fusion.refs_4_) | copy-start | bytes 3145732
  8.7 30.3 %collective-permute-start.1 = (bf16[1024,512]{1,0:T(8,128)(2,1)S(1)}, bf16[1024,512]{1,0:T(8,128)(2,1)}, u32[]{:S(2)}, u32[]{:S(2)}) collective-permute-start(bf16[1024,512]{1,0:T(8,128)(2,1)S(1)} %constant_dynamic-update-slice_fusion.refs_4_), channel_id=1, source_target_pairs={{0,4},{1,5},{2,6},{3,7},{4,12},{5,13},{6,14},{7,15},{12,8},{13,9},... | collective-permute-start | bytes 3145736 | tf_op jit(solution)/shard_map/ppermute | solution.py:50
  11.5 27.5 %collective-permute-start.4 = (bf16[1024,512]{1,0:T(8,128)(2,1)S(1)}, bf16[1024,512]{1,0:T(8,128)(2,1)}, u32[]{:S(2)}, u32[]{:S(2)}) collective-permute-start(bf16[1024,512]{1,0:T(8,128)(2,1)S(1)} %constant_dynamic-update-slice_fusion.refs_4_), channel_id=1, source_target_pairs={{0,2},{1,3},{2,0},{3,1},{4,6},{5,7},{6,4},{7,5},{8,10},{9,11},{10,... | collective-permute-start | bytes 3145736 | tf_op jit(solution)/shard_map/ppermute | solution.py:54
  14.2 8.7 %collective-permute-start.2 = (bf16[8,2048]{1,0:T(8,128)(2,1)S(1)}, bf16[8,2048]{1,0:T(8,128)(2,1)S(1)}, u32[]{:S(2)}, u32[]{:S(2)}) collective-permute-start(bf16[8,2048]{1,0:T(8,128)(2,1)S(1)} %select_bitcast_fusion), channel_id=1, source_target_pairs={{0,1},{1,0},{2,3},{3,2},{4,5},{5,4},{6,7},{7,6},{8,9},{9,8},{10,11... | collective-permute-start | bytes 98312 | tf_op jit(solution)/shard_map/ppermute | solution.py:30
  14.2 56.0 %copy-start.8 = (s32[8]{0:T(128)S(1)}, s32[8]{0:T(128)}, u32[]{:S(2)}) copy-start(s32[8]{0:T(128)} %param.11) | copy-start | bytes 100
  14.3 56.0 %copy-start.9 = (s32[8]{0:T(128)S(1)}, s32[8]{0:T(128)}, u32[]{:S(2)}) copy-start(s32[8]{0:T(128)} %param.10) | copy-start | bytes 100
  23.0 14.7 %collective-permute-start.3 = (bf16[16,2048]{1,0:T(8,128)(2,1)S(1)}, bf16[16,2048]{1,0:T(8,128)(2,1)S(1)}, u32[]{:S(2)}, u32[]{:S(2)}) collective-permute-start(bf16[16,2048]{1,0:T(8,128)(2,1)S(1)} %pad_maximum_fusion), channel_id=1, source_target_pairs={{0,4},{1,5},{2,6},{3,7},{4,12},{5,13},{6,14},{7,15},{12,8},{13,9},... | collective-permute-start | bytes 196616 | tf_op jit(solution)/shard_map/ppermute | solution.py:50
  25.6 13.3 %collective-permute-start.5 = (bf16[16,2048]{1,0:T(8,128)(2,1)S(1)}, bf16[16,2048]{1,0:T(8,128)(2,1)S(1)}, u32[]{:S(2)}, u32[]{:S(2)}) collective-permute-start(bf16[16,2048]{1,0:T(8,128)(2,1)S(1)} %pad_maximum_fusion), channel_id=1, source_target_pairs={{0,8},{1,9},{2,10},{3,11},{4,0},{5,1},{6,2},{7,3},{12,4},{13,5},{1... | collective-permute-start | bytes 196616 | tf_op jit(solution)/shard_map/ppermute | solution.py:50
  39.0 40.7 %collective-permute-start.6 = (bf16[1024,512]{1,0:T(8,128)(2,1)}, bf16[1024,512]{1,0:T(8,128)(2,1)S(1)}, u32[]{:S(2)}, u32[]{:S(2)}) collective-permute-start(bf16[1024,512]{1,0:T(8,128)(2,1)} %collective-permute-done.1.refs_5_), channel_id=1, source_target_pairs={{0,2},{1,3},{2,0},{3,1},{4,6},{5,7},{6,4},{7,5},{8,10},{9,11},{10,... | collective-permute-start | bytes 3145736 | tf_op jit(solution)/shard_map/ppermute | solution.py:54
  40.6 39.1 %collective-permute-start.7 = (bf16[1024,512]{1,0:T(8,128)(2,1)}, bf16[1024,512]{1,0:T(8,128)(2,1)S(1)}, u32[]{:S(2)}, u32[]{:S(2)}) collective-permute-start(bf16[1024,512]{1,0:T(8,128)(2,1)} %collective-permute-done.1.refs_5_), channel_id=1, source_target_pairs={{0,4},{1,5},{2,6},{3,7},{4,12},{5,13},{6,14},{7,15},{12,8},{13,9},... | collective-permute-start | bytes 3145736 | tf_op jit(solution)/shard_map/ppermute | solution.py:50
  42.2 37.4 %collective-permute-start.8 = (bf16[1024,512]{1,0:T(8,128)(2,1)}, bf16[1024,512]{1,0:T(8,128)(2,1)S(1)}, u32[]{:S(2)}, u32[]{:S(2)}) collective-permute-start(bf16[1024,512]{1,0:T(8,128)(2,1)} %collective-permute-done.1.refs_5_), channel_id=1, source_target_pairs={{0,16},{16,0},{1,17},{17,1},{2,18},{18,2},{3,19},{19,3},{4,20},{20... | collective-permute-start | bytes 3145736 | tf_op jit(solution)/shard_map/ppermute | solution.py:58
  44.5 23.4 %collective-permute-start.10 = (bf16[16,2048]{1,0:T(8,128)(2,1)S(1)}, bf16[16,2048]{1,0:T(8,128)(2,1)S(1)}, u32[]{:S(2)}, u32[]{:S(2)}) collective-permute-start(bf16[16,2048]{1,0:T(8,128)(2,1)S(1)} %collective-permute-done.3), channel_id=1, source_target_pairs={{0,4},{1,5},{2,6},{3,7},{4,12},{5,13},{6,14},{7,15},{12,8},{13,9},... | collective-permute-start | bytes 196616 | tf_op jit(solution)/shard_map/ppermute | solution.py:50
  67.9 1.2 collective-permute-start.11
  79.7 9.2 %copy-start = (bf16[1024,512]{1,0:T(8,128)(2,1)}, bf16[1024,512]{1,0:T(8,128)(2,1)S(1)}, u32[]{:S(2)}) copy-start(bf16[1024,512]{1,0:T(8,128)(2,1)S(1)} %collective-permute-done.6.refs_7_) | copy-start | bytes 3145732
  79.7 9.2 %copy-start.1 = (bf16[1024,512]{1,0:T(8,128)(2,1)}, bf16[1024,512]{1,0:T(8,128)(2,1)S(1)}, u32[]{:S(2)}) copy-start(bf16[1024,512]{1,0:T(8,128)(2,1)S(1)} %collective-permute-done.7.refs_6_) | copy-start | bytes 3145732
  79.7 9.2 %copy-start.3 = (bf16[1024,512]{1,0:T(8,128)(2,1)}, bf16[1024,512]{1,0:T(8,128)(2,1)S(1)}, u32[]{:S(2)}) copy-start(bf16[1024,512]{1,0:T(8,128)(2,1)S(1)} %collective-permute-done.8.refs_5_) | copy-start | bytes 3145732
  81.7 17.4 %collective-permute-start.12 = (bf16[64,2048]{1,0:T(8,128)(2,1)}, bf16[64,2048]{1,0:T(8,128)(2,1)}, u32[]{:S(2)}, u32[]{:S(2)}) collective-permute-start(bf16[64,2048]{1,0:T(8,128)(2,1)} %constant_dynamic-update-slice_fusion.2), channel_id=1, source_target_pairs={{0,2},{1,3},{2,0},{3,1},{4,6},{5,7},{6,4},{7,5},{8,10},{9,11},{10,... | collective-permute-start | bytes 786440 | tf_op jit(solution)/shard_map/ppermute | solution.py:54
  82.2 25.0 %collective-permute-start.13 = (bf16[768,512]{1,0:T(8,128)(2,1)}, bf16[768,512]{1,0:T(8,128)(2,1)}, u32[]{:S(2)}, u32[]{:S(2)}) collective-permute-start(bf16[768,512]{1,0:T(8,128)(2,1)} %slice.43), channel_id=1, source_target_pairs={{0,16},{16,0},{1,17},{17,1},{2,18},{18,2},{3,19},{19,3},{4,20},{20... | collective-permute-start | bytes 2359304 | tf_op jit(solution)/shard_map/ppermute | solution.py:58
  84.7 22.5 %collective-permute-start.14 = (bf16[512,512]{1,0:T(8,128)(2,1)}, bf16[512,512]{1,0:T(8,128)(2,1)S(1)}, u32[]{:S(2)}, u32[]{:S(2)}) collective-permute-start(bf16[512,512]{1,0:T(8,128)(2,1)} %slice.44), channel_id=1, source_target_pairs={{0,2},{1,3},{2,0},{3,1},{4,6},{5,7},{6,4},{7,5},{8,10},{9,11},{10,... | collective-permute-start | bytes 1572872 | tf_op jit(solution)/shard_map/ppermute | solution.py:54
  86.2 21.0 %collective-permute-start.15 = (bf16[512,512]{1,0:T(8,128)(2,1)}, bf16[512,512]{1,0:T(8,128)(2,1)}, u32[]{:S(2)}, u32[]{:S(2)}) collective-permute-start(bf16[512,512]{1,0:T(8,128)(2,1)} %slice.45), channel_id=1, source_target_pairs={{0,4},{1,5},{2,6},{3,7},{4,12},{5,13},{6,14},{7,15},{12,8},{13,9},... | collective-permute-start | bytes 1572872 | tf_op jit(solution)/shard_map/ppermute | solution.py:50
  88.3 18.9 %collective-permute-start.16 = (bf16[256,512]{1,0:T(8,128)(2,1)}, bf16[256,512]{1,0:T(8,128)(2,1)S(1)}, u32[]{:S(2)}, u32[]{:S(2)}) collective-permute-start(bf16[256,512]{1,0:T(8,128)(2,1)} %slice.46), channel_id=1, source_target_pairs={{0,2},{1,3},{2,0},{3,1},{4,6},{5,7},{6,4},{7,5},{8,10},{9,11},{10,... | collective-permute-start | bytes 786440 | tf_op jit(solution)/shard_map/ppermute | solution.py:54
  107.2 0.7 copy-start.7
  107.2 0.9 copy-start.6
  108.1 14.1 %copy-start.5 = (bf16[8,4096]{1,0:T(8,128)(2,1)S(1)}, bf16[8,4096]{1,0:T(8,128)(2,1)}, u32[]{:S(2)}) copy-start(bf16[8,4096]{1,0:T(8,128)(2,1)} %param.12) | copy-start | bytes 196612
  117.0 14.3 %all-to-all-start = ((bf16[16,3,16,128]{3,2,1,0:T(8,128)(2,1)}), bf16[16,3,16,128]{3,2,1,0:T(8,128)(2,1)S(1)}, u32[]{:S(2)}, u32[]{:S(2)}) async-start(bf16[16,3,16,128]{3,2,1,0:T(8,128)(2,1)} %rows_3.1), calls=%async_computation | async-start | bytes 393216 | tf_op jit(solution)/shard_map/all_to_all | solution.py:531
  131.2 0.7 copy-start.4

commit v11 on v10

--- a/solution.py
+++ b/solution.py
@@ -344,8 +344,8 @@
         name="split",
     )(core.reshape(1), kv_weight, kv_weight)
     taken = swap_core(give)
-    swapped_states, _ = lax.optimization_barrier((prompt_states, taken))
-    other = swap_core(swapped_states)
+    def swap_tokens(tied):
+        return swap_core(lax.optimization_barrier((prompt_states, tied))[0])
 
     def square_sums(tied):
         states, _ = lax.optimization_barrier((prompt_states, tied))
@@ -413,7 +413,7 @@
             name="resident",
         )(length, queries.reshape(decode_rows, QH, HD), cache)
 
-    def product(blocks, base, count, pieces, carry, name, last=None):
+    def product(other, blocks, base, count, pieces, carry, name, last=None):
         arrays, layout = [], []
         for index, piece in enumerate(pieces):
             place = index * rows_dev
@@ -484,37 +484,41 @@
         def both(array):
             return [[(array, half, rows_dev)] for half in (0, rows_dev)]
 
-        own = jnp.concatenate([keep, taken], axis=0)
-        behind, own_y = along_ring(own), across_y(own)
-        squares = square_sums(own)
-        own_q = jnp.concatenate([keep_q, swap_core(tie((give_q, taken))[0])], axis=0)
-        behind_q, ahead_q = along_ring(own_q), along_ring(own_q, -1)
-
-        source, squares, source_q, _ = tie((behind, squares, behind_q, (own_y, ahead_q)))
-        opposite, behind_y, ahead = along_ring(source), across_y(source), across_replica(source)
-        opposite_q = along_ring(source_q)
-        total = product(blocks, 0, 2, both(own) + both(behind) + both(own_y), None, "rows_1")
-        factor, owners, rows = swap_small(tie((squares, opposite_q))[0])
+        own_q = jnp.concatenate([keep_q, swap_core(give_q)], axis=0)
+        behind_q, ahead_q, opposite_q = (along_ring(own_q, way) for way in (1, -1, 2))
         ring_q = jnp.concatenate([own_q, behind_q, ahead_q, opposite_q], axis=0)
-
-        cut = rows_dev + rows_dev // 2
-        source, source_y, source_x, total, owners, rows, ring_q = tie(
-            (behind_y, opposite, ahead, total, owners, rows, ring_q)
+        a_own_y = across_y(keep)
+        source_a, source_b, source_q = tie((keep, taken, ring_q))
+        a_behind = along_ring(source_a)
+        b_behind, b_own_y = along_ring(source_b), across_y(source_b)
+        other = swap_tokens((taken, source_q))
+        squares = square_sums(taken)
+
+        source, squares, _ = tie((a_behind, squares, a_own_y))
+        a_ahead, a_opposite, a_behind_y = across_replica(source), along_ring(source), across_y(source)
+        source, squares, _ = tie((b_behind, squares, (b_own_y, a_ahead)))
+        b_ahead, b_opposite, b_behind_y = across_replica(source), along_ring(source), across_y(source)
+        ones = starts(keep, taken, a_behind, b_behind, a_own_y, b_own_y)
+        total = product(other, blocks, 0, 2, ones, None, "rows_1")
+
+        source_y, source, source_q, squares, total, _ = tie(
+            (a_behind_y, a_opposite, ring_q, squares, total, b_ahead)
         )
-        all_q = jnp.concatenate([ring_q, across_y(ring_q)], axis=0)
-        opposite_y_b = along_ring(source[rows_dev:])
-        opposite_y_a = across_y(source_y[:rows_dev])
-        ahead_y_x = across_replica(source[:cut])
-        ahead_y_y = across_y(source_x[cut:])
+        a_ahead_y, a_opposite_y = across_replica(source_y), across_y(source)
+        all_q = jnp.concatenate([ring_q, across_y(source_q)], axis=0)
+        source, squares, total, _ = tie((b_behind_y, squares, total, (b_opposite, a_ahead_y)))
+        b_ahead_y, b_opposite_y = across_replica(source), along_ring(source)
+        factor, owners, rows = swap_small(squares)
         image_q, slot = place_images(all_q, owners, rows, blocks[16:])
-        total = product(blocks, 6, 2, both(ahead) + both(opposite) + both(behind_y), total, "rows_2")
-        ahead_y_b = [(ahead_y_x, rows_dev, cut - rows_dev), (ahead_y_y, 0, 2 * rows_dev - cut)]
-        lasts = starts(ahead_y_x, opposite_y_a, opposite_y_b) + [ahead_y_b]
-        slots = product(blocks, 12, 2, lasts, total, "rows_3", last=(image_q, slot, factor))
+        twos = starts(a_ahead, b_ahead, a_opposite, b_opposite, a_behind_y, b_behind_y)
+        total = product(other, blocks, 6, 2, twos, total, "rows_2")
+        lasts = starts(a_ahead_y, a_opposite_y, b_opposite_y, b_ahead_y)
+        slots = product(other, blocks, 12, 2, lasts, total, "rows_3", last=(image_q, slot, factor))
         length, slots = tie((context_length, slots))
         res_out, res_top, res_sum = resident(length)
     else:
         res_out, res_top, res_sum = resident(context_length)
+        other = swap_tokens(taken)
         squares = square_sums(taken)
         factor, owners, rows = swap_small(squares)
         chip_q = jnp.concatenate([keep_q, swap_core(give_q)], axis=0)
@@ -524,9 +528,9 @@
         a = gather_plain(keep)
         b = gather_plain(taken)
         chips = jnp.array([chip for chip, _, _ in a], jnp.int32)
-        total = product(chips * 2 + core, 0, 2, [[(array, start, rows_dev)] for _, array, start in a], None, "rows_a")
+        total = product(other, chips * 2 + core, 0, 2, [[(array, start, rows_dev)] for _, array, start in a], None, "rows_a")
         slots = product(
-            chips * 2 + 1 - core, 0, 2, [[(array, start, rows_dev)] for _, array, start in b], total, "rows_b", last=(image_q, slot, factor)
+            other, chips * 2 + 1 - core, 0, 2, [[(array, start, rows_dev)] for _, array, start in b], total, "rows_b", last=(image_q, slot, factor)
         )
     got = lax.all_to_all(slots, "section", split_axis=0, concat_axis=0, tiled=True)
 

time: 136 us -> 126 us (0.926)
  waiting for transfers between devices: 45 us -> 32.1 us
  starting transfers between devices: 25.3 us -> 34.4 us
  local copies, waits for them, and re-layouts: 12.4 us -> 8.25 us
    ppermute x6 -> x8, waiting for transfers between devices: 33.6 us -> 14.9 us  [along_ring(): return lax.ppermute(x, ('replica', 'section'), perm)]
    ppermute x4, waiting for transfers between devices: 2.29 us -> 8.98 us  [swap_core(): return lax.ppermute(x, 'section', [(i, i ^ 1) for i in range(n)])]
    ppermute x5 -> x6, waiting for transfers between devices: 6.16 us -> 0.02 us  [across_y(): return lax.ppermute(x, 'section', [(i, i ^ 2) for i in range(16)])]
    ppermute x2 -> x4, waiting for transfers between devices: 0.01 us -> 5.28 us  [across_replica(): return lax.ppermute(x, 'replica', [(0, 1), (1, 0)])]
    ppermute x2 -> x4, starting transfers between devices: 3.93 us -> 9.06 us  [across_replica(): return lax.ppermute(x, 'replica', [(0, 1), (1, 0)])]
    ppermute x5 -> x6, starting transfers between devices: 5.57 us -> 9.44 us  [across_y(): return lax.ppermute(x, 'section', [(i, i ^ 2) for i in range(16)])]
    slice x4 -> x0, local copies, waits for them, and re-layouts: 3.58 us -> none  [the longest x1 1.03 us: per_device(): ahead_y_x = across_replica(source[:cut])]
    all_to_all x1, starting transfers between devices: 5.25 us -> 3.53 us  [per_device(): lax.all_to_all(slots, 'section', split_axis=0, concat_axis=0, tiled=True)]
  transfers between devices with their start and end apart: 18 -> 23, of which waited for: 7 -> 9; matrix products, arithmetic and copies ran while one was open for 11% -> 9% of each run, Pallas kernels for 24% -> 26%
where the time goes in v11:
time: 126 us; the launch traced here: 125 us
  Pallas kernels  46.1 us (37%)
  starting transfers between devices  34.4 us (27%)
  waiting for transfers between devices  32.1 us (25%)
  local copies, waits for them, and re-layouts  8.25 us (7%)
  other arithmetic  3.68 us (3%)
    pallas_call x3, Pallas kernels, product(): pl.pallas_call(body, grid_spec=pltpu.PrefetchScalarGridSpec(num_scalar_pr...  27.8 us
    ppermute x8, waiting for transfers between devices, along_ring(): return lax.ppermute(x, ('replica', 'section'), perm)  14.9 us
    ppermute x8, starting transfers between devices, along_ring(): return lax.ppermute(x, ('replica', 'section'), perm)  11.3 us
    ppermute x6, starting transfers between devices, across_y(): return lax.ppermute(x, 'section', [(i, i ^ 2) for i in range(16)])  9.44 us
    ppermute x4, starting transfers between devices, across_replica(): return lax.ppermute(x, 'replica', [(0, 1), (1, 0)])  9.06 us
    ppermute x4, waiting for transfers between devices, swap_core(): return lax.ppermute(x, 'section', [(i, i ^ 1) for i in range(n)])  8.98 us
    pallas_call x1, Pallas kernels, square_sums(): pl.pallas_call(square_kernel, grid=(8,), in_specs=[pl.BlockSpec((tokens /...  7.59 us
    pallas_call x1, Pallas kernels, resident(): pl.pallas_call(resident_kernel, grid_spec=pltpu.PrefetchScalarGridSpec(nu...  5.37 us
  transfers between devices with their start and end apart: 23, of which 9 were waited for; matrix products, arithmetic and copies ran while one was open for 9% of the time, Pallas kernels for 26%

profile of v11, /device:TPU:0, one launch (start us, length us, event | category | flops | bytes accessed | tf_op | source)
XLA Modules:
  0.0 125.0 jit_solution(1610862746424296730)
XLA Ops:
  0.0 2.1 %split.1 = (bf16[512,512]{1,0:T(8,128)(2,1)}, bf16[512,512]{1,0:T(8,128)(2,1)}) custom-call(s32[1]{0:T(128)} %bitcast.1.core_ref, bf16[512,1024]{1,0:T(8,128)(2,1)} %give_in.1, bf16[512,1024]{1,0:T(8,128)(2,1)} %give_in.1), custom_call_target="tpu_custom_call" | custom-call | bytes 262144 | tf_op jit(solution)/shard_map/split/pallas_call | solution.py:331
  2.1 0.5 collective-permute-start
  2.5 1.7 %collective-permute-done.refs_5_ = bf16[512,512]{1,0:T(8,128)(2,1)S(1)} collective-permute-done((bf16[512,512]{1,0:T(8,128)(2,1)}, bf16[512,512]{1,0:T(8,128)(2,1)S(1)}, u32[]{:S(2)}, u32[]{:S(2)}) %collective-permute-start) | collective-permute-done | bytes 524320 | tf_op jit(solution)/shard_map/ppermute | solution.py:30
  4.3 0.4 collective-permute-start.13
  4.6 0.8 select_bitcast_fusion
  5.4 0.2 collective-permute-start.1
  5.6 2.8 %collective-permute-start.7 = (bf16[512,512]{1,0:T(8,128)(2,1)}, bf16[512,512]{1,0:T(8,128)(2,1)S(1)}, u32[]{:S(2)}, u32[]{:S(2)}) collective-permute-start(bf16[512,512]{1,0:T(8,128)(2,1)} %get-tuple-element.30.refs_4_), channel_id=1, source_target_pairs={{0,2},{1,3},{2,0},{3,1},{4,6},{5,7},{6,4},{7,5},{8,10},{9,11},{10,... | collective-permute-start | bytes 1572872 | tf_op jit(solution)/shard_map/ppermute | solution.py:54
  8.4 0.8 constant_dynamic-update-slice_fusion.10
  9.2 0.6 constant_dynamic-update-slice_fusion.4
  9.8 7.2 %collective-permute-done.1 = bf16[8,2048]{1,0:T(8,128)(2,1)S(1)} collective-permute-done((bf16[8,2048]{1,0:T(8,128)(2,1)S(1)}, bf16[8,2048]{1,0:T(8,128)(2,1)S(1)}, u32[]{:S(2)}, u32[]{:S(2)}) %collective-permute-start.1) | collective-permute-done | bytes 32800 | tf_op jit(solution)/shard_map/ppermute | solution.py:30
  17.1 2.7 %collective-permute-start.2 = (bf16[16,2048]{1,0:T(8,128)(2,1)S(1)}, bf16[16,2048]{1,0:T(8,128)(2,1)S(1)}, u32[]{:S(2)}, u32[]{:S(2)}) collective-permute-start(bf16[16,2048]{1,0:T(8,128)(2,1)S(1)} %pad_maximum_fusion), channel_id=1, source_target_pairs={{0,4},{1,5},{2,6},{3,7},{4,12},{5,13},{6,14},{7,15},{12,8},{13,9},... | collective-permute-start | bytes 196616 | tf_op jit(solution)/shard_map/ppermute | solution.py:50
  19.8 1.1 collective-permute-start.3
  20.9 3.9 %collective-permute-start.4 = (bf16[16,2048]{1,0:T(8,128)(2,1)S(1)}, bf16[16,2048]{1,0:T(8,128)(2,1)S(1)}, u32[]{:S(2)}, u32[]{:S(2)}) collective-permute-start(bf16[16,2048]{1,0:T(8,128)(2,1)S(1)} %pad_maximum_fusion), channel_id=1, source_target_pairs={{0,12},{1,13},{2,14},{3,15},{4,8},{5,9},{6,10},{7,11},{12,0},{13,1... | collective-permute-start | bytes 196616 | tf_op jit(solution)/shard_map/ppermute | solution.py:50
  24.7 0.6 constant_dynamic-update-slice_fusion.9
  25.4 0.6 constant_dynamic-update-slice_fusion.8
  26.0 0.6 constant_dynamic-update-slice_fusion.7
  26.6 1.7 %collective-permute-done.4 = bf16[16,2048]{1,0:T(8,128)(2,1)S(1)} collective-permute-done((bf16[16,2048]{1,0:T(8,128)(2,1)S(1)}, bf16[16,2048]{1,0:T(8,128)(2,1)S(1)}, u32[]{:S(2)}, u32[]{:S(2)}) %collective-permute-start.4) | collective-permute-done | bytes 65568 | tf_op jit(solution)/shard_map/ppermute | solution.py:50
  28.3 0.6 constant_dynamic-update-slice_fusion.6
  28.9 1.2 collective-permute-start.6
  30.1 1.9 %collective-permute-start.5 = (bf16[512,512]{1,0:T(8,128)(2,1)S(1)}, bf16[512,512]{1,0:T(8,128)(2,1)}, u32[]{:S(2)}, u32[]{:S(2)}) collective-permute-start(bf16[512,512]{1,0:T(8,128)(2,1)S(1)} %collective-permute-done.refs_5_), channel_id=1, source_target_pairs={{0,4},{1,5},{2,6},{3,7},{4,12},{5,13},{6,14},{7,15},{12,8},{13,9},... | collective-permute-start | bytes 1572872 | tf_op jit(solution)/shard_map/ppermute | solution.py:50
  32.1 1.5 %collective-permute-start.8 = (bf16[512,512]{1,0:T(8,128)(2,1)S(1)}, bf16[512,512]{1,0:T(8,128)(2,1)}, u32[]{:S(2)}, u32[]{:S(2)}) collective-permute-start(bf16[512,512]{1,0:T(8,128)(2,1)S(1)} %collective-permute-done.refs_5_), channel_id=1, source_target_pairs={{0,2},{1,3},{2,0},{3,1},{4,6},{5,7},{6,4},{7,5},{8,10},{9,11},{10,... | collective-permute-start | bytes 1572872 | tf_op jit(solution)/shard_map/ppermute | solution.py:54
  33.6 7.6 %squares.1 = f32[512,1]{1,0:T(8,128)} custom-call(bf16[512,8192]{1,0:T(8,128)(2,1)} %refs_1_.5), custom_call_target="tpu_custom_call" | custom-call | bytes 262144 | tf_op jit(solution)/shard_map/squares/pallas_call | solution.py:352
  41.2 1.1 reduce
  42.3 2.7 %collective-permute-done.6.refs_6_ = bf16[512,512]{1,0:T(8,128)(2,1)} collective-permute-done((bf16[512,512]{1,0:T(8,128)(2,1)}, bf16[512,512]{1,0:T(8,128)(2,1)}, u32[]{:S(2)}, u32[]{:S(2)}) %collective-permute-start.6) | collective-permute-done | bytes 524320 | tf_op jit(solution)/shard_map/ppermute | solution.py:50
  45.0 0.9 collective-permute-start.9
  45.9 1.5 %collective-permute-start.11 = (bf16[512,512]{1,0:T(8,128)(2,1)}, bf16[512,512]{1,0:T(8,128)(2,1)S(1)}, u32[]{:S(2)}, u32[]{:S(2)}) collective-permute-start(bf16[512,512]{1,0:T(8,128)(2,1)} %collective-permute-done.6.refs_6_), channel_id=1, source_target_pairs={{0,2},{1,3},{2,0},{3,1},{4,6},{5,7},{6,4},{7,5},{8,10},{9,11},{10,... | collective-permute-start | bytes 1572872 | tf_op jit(solution)/shard_map/ppermute | solution.py:54
  47.5 7.0 %collective-permute-done.5.refs_7_ = bf16[512,512]{1,0:T(8,128)(2,1)} collective-permute-done((bf16[512,512]{1,0:T(8,128)(2,1)S(1)}, bf16[512,512]{1,0:T(8,128)(2,1)}, u32[]{:S(2)}, u32[]{:S(2)}) %collective-permute-start.5) | collective-permute-done | bytes 524320 | tf_op jit(solution)/shard_map/ppermute | solution.py:50
  54.4 0.0 collective-permute-done.8.refs_9_
  54.4 1.1 collective-permute-done.9.refs_5_
  55.5 3.2 %collective-permute-start.14 = (bf16[512,512]{1,0:T(8,128)(2,1)}, bf16[512,512]{1,0:T(8,128)(2,1)}, u32[]{:S(2)}, u32[]{:S(2)}) collective-permute-start(bf16[512,512]{1,0:T(8,128)(2,1)} %collective-permute-done.5.refs_7_), channel_id=1, source_target_pairs={{0,16},{16,0},{1,17},{17,1},{2,18},{18,2},{3,19},{19,3},{4,20},{20... | collective-permute-start | bytes 1572872 | tf_op jit(solution)/shard_map/ppermute | solution.py:58
  58.8 1.2 constant_dynamic-slice_fusion
  60.0 1.5 %collective-permute-start.10 = (bf16[512,512]{1,0:T(8,128)(2,1)}, bf16[512,512]{1,0:T(8,128)(2,1)S(1)}, u32[]{:S(2)}, u32[]{:S(2)}) collective-permute-start(bf16[512,512]{1,0:T(8,128)(2,1)} %collective-permute-done.5.refs_7_), channel_id=1, source_target_pairs={{0,2},{1,3},{2,0},{3,1},{4,6},{5,7},{6,4},{7,5},{8,10},{9,11},{10,... | collective-permute-start | bytes 1572872 | tf_op jit(solution)/shard_map/ppermute | solution.py:54
  61.5 0.0 copy-start.10
  61.5 0.0 copy-start.11
  61.5 9.4 %rows_1.1.refs_4_ = f32[1024,512]{1,0:T(8,128)} custom-call(s32[24]{0:T(128)} %get-tuple-element.62.block_ref, bf16[512,8192]{1,0:T(8,128)(2,1)} %refs_1_.5, bf16[512,8192]{1,0:T(8,128)(2,1)} %refs_1_.5, bf16[512,8192]{1,0:T(8,128)(2,1)} %collective-permute-done.13.refs_2_.refs_3_, bf16[512,8192]{1,0:T(8,128)(2,1)} %collective-permute-done.13.refs_2_.refs_3_, ...), custom_call_target="tpu_custom_call" | custom-call | bytes 262144 | tf_op jit(solution)/shard_map/rows_1/pallas_call | solution.py:460
  71.0 0.0 collective-permute-done.14.refs_6_
  71.0 2.3 %collective-permute-start.16 = (bf16[512,512]{1,0:T(8,128)(2,1)S(1)}, bf16[512,512]{1,0:T(8,128)(2,1)S(1)}, u32[]{:S(2)}, u32[]{:S(2)}) collective-permute-start(bf16[512,512]{1,0:T(8,128)(2,1)S(1)} %collective-permute-done.11.refs_9_), channel_id=1, source_target_pairs={{0,16},{16,0},{1,17},{17,1},{2,18},{18,2},{3,19},{19,3},{4,20},{20... | collective-permute-start | bytes 1572872 | tf_op jit(solution)/shard_map/ppermute | solution.py:58
  73.3 0.1 slice_bitcast_fusion.1
  73.4 0.5 collective-permute-start.18
  73.9 0.1 add_convert_fusion
  74.0 1.5 %collective-permute-start.19 = (bf16[512,512]{1,0:T(8,128)(2,1)S(1)}, bf16[512,512]{1,0:T(8,128)(2,1)S(1)}, u32[]{:S(2)}, u32[]{:S(2)}) collective-permute-start(bf16[512,512]{1,0:T(8,128)(2,1)S(1)} %collective-permute-done.12.refs_7_), channel_id=1, source_target_pairs={{0,2},{1,3},{2,0},{3,1},{4,6},{5,7},{6,4},{7,5},{8,10},{9,11},{10,... | collective-permute-start | bytes 1572872 | tf_op jit(solution)/shard_map/ppermute | solution.py:54
  75.5 0.0 collective-permute-done.10.refs_10_
  75.5 3.5 %collective-permute-done.15.refs_8_ = bf16[512,512]{1,0:T(8,128)(2,1)} collective-permute-done((bf16[512,512]{1,0:T(8,128)(2,1)}, bf16[512,512]{1,0:T(8,128)(2,1)}, u32[]{:S(2)}, u32[]{:S(2)}) %collective-permute-start.15) | collective-permute-done | bytes 524320 | tf_op jit(solution)/shard_map/ppermute | solution.py:50
  79.0 4.2 %collective-permute-done.16.refs_7_ = bf16[512,512]{1,0:T(8,128)(2,1)S(1)} collective-permute-done((bf16[512,512]{1,0:T(8,128)(2,1)S(1)}, bf16[512,512]{1,0:T(8,128)(2,1)S(1)}, u32[]{:S(2)}, u32[]{:S(2)}) %collective-permute-start.16) | collective-permute-done | bytes 524320 | tf_op jit(solution)/shard_map/ppermute | solution.py:58
  83.2 0.1 collective-permute-start.17
  83.3 0.5 collective-permute-start.20
  83.8 2.6 %collective-permute-start.21 = (bf16[512,512]{1,0:T(8,128)(2,1)S(1)}, bf16[512,512]{1,0:T(8,128)(2,1)}, u32[]{:S(2)}, u32[]{:S(2)}) collective-permute-start(bf16[512,512]{1,0:T(8,128)(2,1)S(1)} %collective-permute-done.10.refs_10_), channel_id=1, source_target_pairs={{0,16},{16,0},{1,17},{17,1},{2,18},{18,2},{3,19},{19,3},{4,20},{20... | collective-permute-start | bytes 1572872 | tf_op jit(solution)/shard_map/ppermute | solution.py:58
  86.4 9.6 %rows_2.1.refs_4_ = f32[1024,512]{1,0:T(8,128)} custom-call(s32[24]{0:T(128)} %get-tuple-element.62.block_ref, bf16[512,8192]{1,0:T(8,128)(2,1)} %refs_1_.5, bf16[512,8192]{1,0:T(8,128)(2,1)} %refs_1_.5, bf16[512,8192]{1,0:T(8,128)(2,1)} %collective-permute-done.13.refs_2_.refs_3_, bf16[512,8192]{1,0:T(8,128)(2,1)} %collective-permute-done.13.refs_2_.refs_3_, ...), custom_call_target="tpu_custom_call" | custom-call | bytes 262144 | tf_op jit(solution)/shard_map/rows_2/pallas_call | solution.py:460
  96.0 0.1 slice_convert_fusion.1
  96.1 0.1 and_select_fusion.1
  96.2 0.1 select_reduce_fusion
  96.3 1.1 copy.13.refs_6_
  97.3 0.1 fusion.7
  97.4 0.2 fusion
  97.7 0.6 copy.19
  98.3 0.6 pad_add_fusion.slot_ref
  98.9 0.8 copy-done.9
  99.7 8.8 %rows_3.1 = bf16[16,3,16,128]{3,2,1,0:T(8,128)(2,1)} custom-call(s32[24]{0:T(128)} %get-tuple-element.62.block_ref, s32[3,16]{1,0:T(4,128)} %pad_add_fusion.slot_ref, bf16[512,8192]{1,0:T(8,128)(2,1)} %refs_1_.5, bf16[512,8192]{1,0:T(8,128)(2,1)} %refs_1_.5, bf16[512,8192]{1,0:T(8,128)(2,1)} %collective-permute-done.13.refs_2_.refs_3_, ...), custom_call_target="tpu_custom_call" | custom-call | bytes 262144 | tf_op jit(solution)/shard_map/rows_3/pallas_call | solution.py:460
  108.6 3.5 %all-to-all-start = ((bf16[16,3,16,128]{3,2,1,0:T(8,128)(2,1)}), bf16[16,3,16,128]{3,2,1,0:T(8,128)(2,1)S(1)}, u32[]{:S(2)}, u32[]{:S(2)}) async-start(bf16[16,3,16,128]{3,2,1,0:T(8,128)(2,1)} %rows_3.1), calls=%async_computation | async-start | bytes 393216 | tf_op jit(solution)/shard_map/all_to_all | solution.py:535
  112.1 0.6 copy.18
  112.8 5.4 %resident.1 = (f32[8,32,128]{2,1,0:T(8,128)}, f32[32,128]{1,0:T(8,128)}, f32[32,128]{1,0:T(8,128)}) custom-call(s32[8]{0:T(128)} %length_ref, bf16[8,32,128]{2,1,0:T(8,128)(2,1)} %bitcast.40, bf16[8,256,1024]{2,1,0:T(8,128)(2,1)} %cache_ref.1), custom_call_target="tpu_custom_call" | custom-call | bytes 262144 | tf_op jit(solution)/shard_map/resident/pallas_call | solution.py:391
  118.1 2.9 %all-to-all-done.got_ref = bf16[16,3,16,128]{3,2,1,0:T(8,128)(2,1)S(1)} async-done(((bf16[16,3,16,128]{3,2,1,0:T(8,128)(2,1)}), bf16[16,3,16,128]{3,2,1,0:T(8,128)(2,1)S(1)}, u32[]{:S(2)}, u32[]{:S(2)}) %all-to-all-start) | async-done | bytes 196640 | tf_op jit(solution)/shard_map/all_to_all | solution.py:535
  121.1 0.7 copy-done
  121.8 3.3 %combine.1 = bf16[8,4096]{1,0:T(8,128)(2,1)} custom-call(bf16[16,3,16,128]{3,2,1,0:T(8,128)(2,1)} %copy-done, f32[8,32,128]{2,1,0:T(8,128)} %get-tuple-element.46.res_out_ref, f32[32,128]{1,0:T(8,128)} %get-tuple-element.47.res_top_ref, f32[32,128]{1,0:T(8,128)} %get-tuple-element.48.res_sum_ref), custom_call_target="tpu_custom_call" | custom-call | tf_op jit(solution)/shard_map/combine/pallas_call | solution.py:537
  (41 shorter events, 0.1 us)
Async XLA Ops:
  2.1 2.2 %collective-permute-start = (bf16[512,512]{1,0:T(8,128)(2,1)}, bf16[512,512]{1,0:T(8,128)(2,1)S(1)}, u32[]{:S(2)}, u32[]{:S(2)}) collective-permute-start(bf16[512,512]{1,0:T(8,128)(2,1)} %get-tuple-element.28), channel_id=1, source_target_pairs={{0,1},{1,0},{2,3},{3,2},{4,5},{5,4},{6,7},{7,6},{8,9},{9,8},{10,11... | collective-permute-start | bytes 1572872 | tf_op jit(solution)/shard_map/ppermute | solution.py:30
  4.3 36.9 %copy-start.2 = (bf16[512,512]{1,0:T(8,128)(2,1)}, bf16[512,512]{1,0:T(8,128)(2,1)S(1)}, u32[]{:S(2)}) copy-start(bf16[512,512]{1,0:T(8,128)(2,1)S(1)} %collective-permute-done.refs_5_) | copy-start | bytes 1572868
  4.3 57.2 %collective-permute-start.13 = (bf16[512,8192]{1,0:T(8,128)(2,1)}, bf16[512,8192]{1,0:T(8,128)(2,1)}, u32[]{:S(2)}, u32[]{:S(2)}) collective-permute-start(bf16[512,8192]{1,0:T(8,128)(2,1)} %refs_1_.5), channel_id=1, source_target_pairs={{0,1},{1,0},{2,3},{3,2},{4,5},{5,4},{6,7},{7,6},{8,9},{9,8},{10,11... | collective-permute-start | bytes 25165832 | tf_op jit(solution)/shard_map/ppermute | solution.py:30
  5.4 11.6 %collective-permute-start.1 = (bf16[8,2048]{1,0:T(8,128)(2,1)S(1)}, bf16[8,2048]{1,0:T(8,128)(2,1)S(1)}, u32[]{:S(2)}, u32[]{:S(2)}) collective-permute-start(bf16[8,2048]{1,0:T(8,128)(2,1)S(1)} %select_bitcast_fusion), channel_id=1, source_target_pairs={{0,1},{1,0},{2,3},{3,2},{4,5},{5,4},{6,7},{7,6},{8,9},{9,8},{10,11... | collective-permute-start | bytes 98312 | tf_op jit(solution)/shard_map/ppermute | solution.py:30
  5.6 36.6 %collective-permute-start.7 = (bf16[512,512]{1,0:T(8,128)(2,1)}, bf16[512,512]{1,0:T(8,128)(2,1)S(1)}, u32[]{:S(2)}, u32[]{:S(2)}) collective-permute-start(bf16[512,512]{1,0:T(8,128)(2,1)} %get-tuple-element.30.refs_4_), channel_id=1, source_target_pairs={{0,2},{1,3},{2,0},{3,1},{4,6},{5,7},{6,4},{7,5},{8,10},{9,11},{10,... | collective-permute-start | bytes 1572872 | tf_op jit(solution)/shard_map/ppermute | solution.py:54
  17.1 8.3 %collective-permute-start.2 = (bf16[16,2048]{1,0:T(8,128)(2,1)S(1)}, bf16[16,2048]{1,0:T(8,128)(2,1)S(1)}, u32[]{:S(2)}, u32[]{:S(2)}) collective-permute-start(bf16[16,2048]{1,0:T(8,128)(2,1)S(1)} %pad_maximum_fusion), channel_id=1, source_target_pairs={{0,4},{1,5},{2,6},{3,7},{4,12},{5,13},{6,14},{7,15},{12,8},{13,9},... | collective-permute-start | bytes 196616 | tf_op jit(solution)/shard_map/ppermute | solution.py:50
  19.8 6.2 %collective-permute-start.3 = (bf16[16,2048]{1,0:T(8,128)(2,1)S(1)}, bf16[16,2048]{1,0:T(8,128)(2,1)S(1)}, u32[]{:S(2)}, u32[]{:S(2)}) collective-permute-start(bf16[16,2048]{1,0:T(8,128)(2,1)S(1)} %pad_maximum_fusion), channel_id=1, source_target_pairs={{0,8},{1,9},{2,10},{3,11},{4,0},{5,1},{6,2},{7,3},{12,4},{13,5},{1... | collective-permute-start | bytes 196616 | tf_op jit(solution)/shard_map/ppermute | solution.py:50
  20.9 7.4 %collective-permute-start.4 = (bf16[16,2048]{1,0:T(8,128)(2,1)S(1)}, bf16[16,2048]{1,0:T(8,128)(2,1)S(1)}, u32[]{:S(2)}, u32[]{:S(2)}) collective-permute-start(bf16[16,2048]{1,0:T(8,128)(2,1)S(1)} %pad_maximum_fusion), channel_id=1, source_target_pairs={{0,12},{1,13},{2,14},{3,15},{4,8},{5,9},{6,10},{7,11},{12,0},{13,1... | collective-permute-start | bytes 196616 | tf_op jit(solution)/shard_map/ppermute | solution.py:50
  28.9 16.1 %collective-permute-start.6 = (bf16[512,512]{1,0:T(8,128)(2,1)}, bf16[512,512]{1,0:T(8,128)(2,1)}, u32[]{:S(2)}, u32[]{:S(2)}) collective-permute-start(bf16[512,512]{1,0:T(8,128)(2,1)} %get-tuple-element.30.refs_4_), channel_id=1, source_target_pairs={{0,4},{1,5},{2,6},{3,7},{4,12},{5,13},{6,14},{7,15},{12,8},{13,9},... | collective-permute-start | bytes 1572872 | tf_op jit(solution)/shard_map/ppermute | solution.py:50
  30.1 24.3 %collective-permute-start.5 = (bf16[512,512]{1,0:T(8,128)(2,1)S(1)}, bf16[512,512]{1,0:T(8,128)(2,1)}, u32[]{:S(2)}, u32[]{:S(2)}) collective-permute-start(bf16[512,512]{1,0:T(8,128)(2,1)S(1)} %collective-permute-done.refs_5_), channel_id=1, source_target_pairs={{0,4},{1,5},{2,6},{3,7},{4,12},{5,13},{6,14},{7,15},{12,8},{13,9},... | collective-permute-start | bytes 1572872 | tf_op jit(solution)/shard_map/ppermute | solution.py:50
  32.1 22.4 %collective-permute-start.8 = (bf16[512,512]{1,0:T(8,128)(2,1)S(1)}, bf16[512,512]{1,0:T(8,128)(2,1)}, u32[]{:S(2)}, u32[]{:S(2)}) collective-permute-start(bf16[512,512]{1,0:T(8,128)(2,1)S(1)} %collective-permute-done.refs_5_), channel_id=1, source_target_pairs={{0,2},{1,3},{2,0},{3,1},{4,6},{5,7},{6,4},{7,5},{8,10},{9,11},{10,... | collective-permute-start | bytes 1572872 | tf_op jit(solution)/shard_map/ppermute | solution.py:54
  42.3 19.2 %copy-start.4 = (bf16[512,512]{1,0:T(8,128)(2,1)}, bf16[512,512]{1,0:T(8,128)(2,1)S(1)}, u32[]{:S(2)}) copy-start(bf16[512,512]{1,0:T(8,128)(2,1)S(1)} %collective-permute-done.7.refs_8_) | copy-start | bytes 1572868
  45.0 10.5 %collective-permute-start.9 = (bf16[512,512]{1,0:T(8,128)(2,1)}, bf16[512,512]{1,0:T(8,128)(2,1)S(1)}, u32[]{:S(2)}, u32[]{:S(2)}) collective-permute-start(bf16[512,512]{1,0:T(8,128)(2,1)} %collective-permute-done.6.refs_6_), channel_id=1, source_target_pairs={{0,16},{16,0},{1,17},{17,1},{2,18},{18,2},{3,19},{19,3},{4,20},{20... | collective-permute-start | bytes 1572872 | tf_op jit(solution)/shard_map/ppermute | solution.py:58
  45.9 25.0 %collective-permute-start.11 = (bf16[512,512]{1,0:T(8,128)(2,1)}, bf16[512,512]{1,0:T(8,128)(2,1)S(1)}, u32[]{:S(2)}, u32[]{:S(2)}) collective-permute-start(bf16[512,512]{1,0:T(8,128)(2,1)} %collective-permute-done.6.refs_6_), channel_id=1, source_target_pairs={{0,2},{1,3},{2,0},{3,1},{4,6},{5,7},{6,4},{7,5},{8,10},{9,11},{10,... | collective-permute-start | bytes 1572872 | tf_op jit(solution)/shard_map/ppermute | solution.py:54
  54.4 16.5 %collective-permute-start.12 = (bf16[512,512]{1,0:T(8,128)(2,1)}, bf16[512,512]{1,0:T(8,128)(2,1)S(1)}, u32[]{:S(2)}, u32[]{:S(2)}) collective-permute-start(bf16[512,512]{1,0:T(8,128)(2,1)} %collective-permute-done.6.refs_6_), channel_id=1, source_target_pairs={{0,4},{1,5},{2,6},{3,7},{4,12},{5,13},{6,14},{7,15},{12,8},{13,9},... | collective-permute-start | bytes 1572872 | tf_op jit(solution)/shard_map/ppermute | solution.py:50
  55.5 15.4 %copy-start.6 = (bf16[512,512]{1,0:T(8,128)(2,1)}, bf16[512,512]{1,0:T(8,128)(2,1)S(1)}, u32[]{:S(2)}) copy-start(bf16[512,512]{1,0:T(8,128)(2,1)S(1)} %collective-permute-done.9.refs_5_) | copy-start | bytes 1572868
  55.5 15.4 %collective-permute-start.14 = (bf16[512,512]{1,0:T(8,128)(2,1)}, bf16[512,512]{1,0:T(8,128)(2,1)}, u32[]{:S(2)}, u32[]{:S(2)}) collective-permute-start(bf16[512,512]{1,0:T(8,128)(2,1)} %collective-permute-done.5.refs_7_), channel_id=1, source_target_pairs={{0,16},{16,0},{1,17},{17,1},{2,18},{18,2},{3,19},{19,3},{4,20},{20... | collective-permute-start | bytes 1572872 | tf_op jit(solution)/shard_map/ppermute | solution.py:58
  60.0 15.6 %collective-permute-start.10 = (bf16[512,512]{1,0:T(8,128)(2,1)}, bf16[512,512]{1,0:T(8,128)(2,1)S(1)}, u32[]{:S(2)}, u32[]{:S(2)}) collective-permute-start(bf16[512,512]{1,0:T(8,128)(2,1)} %collective-permute-done.5.refs_7_), channel_id=1, source_target_pairs={{0,2},{1,3},{2,0},{3,1},{4,6},{5,7},{6,4},{7,5},{8,10},{9,11},{10,... | collective-permute-start | bytes 1572872 | tf_op jit(solution)/shard_map/ppermute | solution.py:54
  61.5 17.5 %collective-permute-start.15 = (bf16[512,512]{1,0:T(8,128)(2,1)}, bf16[512,512]{1,0:T(8,128)(2,1)}, u32[]{:S(2)}, u32[]{:S(2)}) collective-permute-start(bf16[512,512]{1,0:T(8,128)(2,1)} %collective-permute-done.5.refs_7_), channel_id=1, source_target_pairs={{0,4},{1,5},{2,6},{3,7},{4,12},{5,13},{6,14},{7,15},{12,8},{13,9},... | collective-permute-start | bytes 1572872 | tf_op jit(solution)/shard_map/ppermute | solution.py:50
  61.5 12.4 %copy-start.10 = (s32[8]{0:T(128)S(1)}, s32[8]{0:T(128)}, u32[]{:S(2)}) copy-start(s32[8]{0:T(128)} %param.11) | copy-start | bytes 100
  61.5 12.4 %copy-start.11 = (s32[8]{0:T(128)S(1)}, s32[8]{0:T(128)}, u32[]{:S(2)}) copy-start(s32[8]{0:T(128)} %param.10) | copy-start | bytes 100
  70.9 15.5 %copy-start.7 = (bf16[512,512]{1,0:T(8,128)(2,1)}, bf16[512,512]{1,0:T(8,128)(2,1)S(1)}, u32[]{:S(2)}) copy-start(bf16[512,512]{1,0:T(8,128)(2,1)S(1)} %collective-permute-done.11.refs_9_) | copy-start | bytes 1572868
  71.0 15.4 %copy-start.3 = (bf16[512,512]{1,0:T(8,128)(2,1)}, bf16[512,512]{1,0:T(8,128)(2,1)S(1)}, u32[]{:S(2)}) copy-start(bf16[512,512]{1,0:T(8,128)(2,1)S(1)} %collective-permute-done.12.refs_7_) | copy-start | bytes 1572868
  71.0 12.2 %collective-permute-start.16 = (bf16[512,512]{1,0:T(8,128)(2,1)S(1)}, bf16[512,512]{1,0:T(8,128)(2,1)S(1)}, u32[]{:S(2)}, u32[]{:S(2)}) collective-permute-start(bf16[512,512]{1,0:T(8,128)(2,1)S(1)} %collective-permute-done.11.refs_9_), channel_id=1, source_target_pairs={{0,16},{16,0},{1,17},{17,1},{2,18},{18,2},{3,19},{19,3},{4,20},{20... | collective-permute-start | bytes 1572872 | tf_op jit(solution)/shard_map/ppermute | solution.py:58
  73.4 9.9 %collective-permute-start.18 = (bf16[64,2048]{1,0:T(8,128)(2,1)}, bf16[64,2048]{1,0:T(8,128)(2,1)S(1)}, u32[]{:S(2)}, u32[]{:S(2)}) collective-permute-start(bf16[64,2048]{1,0:T(8,128)(2,1)} %get-tuple-element.41), channel_id=1, source_target_pairs={{0,2},{1,3},{2,0},{3,1},{4,6},{5,7},{6,4},{7,5},{8,10},{9,11},{10,... | collective-permute-start | bytes 786440 | tf_op jit(solution)/shard_map/ppermute | solution.py:54
  74.0 24.9 %collective-permute-start.19 = (bf16[512,512]{1,0:T(8,128)(2,1)S(1)}, bf16[512,512]{1,0:T(8,128)(2,1)S(1)}, u32[]{:S(2)}, u32[]{:S(2)}) collective-permute-start(bf16[512,512]{1,0:T(8,128)(2,1)S(1)} %collective-permute-done.12.refs_7_), channel_id=1, source_target_pairs={{0,2},{1,3},{2,0},{3,1},{4,6},{5,7},{6,4},{7,5},{8,10},{9,11},{10,... | collective-permute-start | bytes 1572872 | tf_op jit(solution)/shard_map/ppermute | solution.py:54
  75.5 10.9 %copy-start.5 = (bf16[512,512]{1,0:T(8,128)(2,1)}, bf16[512,512]{1,0:T(8,128)(2,1)S(1)}, u32[]{:S(2)}) copy-start(bf16[512,512]{1,0:T(8,128)(2,1)S(1)} %collective-permute-done.10.refs_10_) | copy-start | bytes 1572868
  83.2 12.8 %copy-start.8 = (bf16[512,512]{1,0:T(8,128)(2,1)}, bf16[512,512]{1,0:T(8,128)(2,1)S(1)}, u32[]{:S(2)}) copy-start(bf16[512,512]{1,0:T(8,128)(2,1)S(1)} %collective-permute-done.16.refs_7_) | copy-start | bytes 1572868
  83.2 12.8 %collective-permute-start.17 = (f32[8,128]{1,0:T(8,128)S(1)}, f32[8,128]{1,0:T(8,128)S(1)}, u32[]{:S(2)}, u32[]{:S(2)}) collective-permute-start(f32[8,128]{1,0:T(8,128)S(1)} %fusion.2), channel_id=1, source_target_pairs={{0,1},{1,0},{2,3},{3,2},{4,5},{5,4},{6,7},{7,6},{8,9},{9,8},{10,11... | collective-permute-start | bytes 12296 | tf_op jit(solution)/shard_map/ppermute | solution.py:30
  83.3 15.6 %collective-permute-start.20 = (bf16[512,512]{1,0:T(8,128)(2,1)S(1)}, bf16[512,512]{1,0:T(8,128)(2,1)}, u32[]{:S(2)}, u32[]{:S(2)}) collective-permute-start(bf16[512,512]{1,0:T(8,128)(2,1)S(1)} %collective-permute-done.10.refs_10_), channel_id=1, source_target_pairs={{0,4},{1,5},{2,6},{3,7},{4,12},{5,13},{6,14},{7,15},{12,8},{13,9},... | collective-permute-start | bytes 1572872 | tf_op jit(solution)/shard_map/ppermute | solution.py:50
  83.8 15.1 %collective-permute-start.21 = (bf16[512,512]{1,0:T(8,128)(2,1)S(1)}, bf16[512,512]{1,0:T(8,128)(2,1)}, u32[]{:S(2)}, u32[]{:S(2)}) collective-permute-start(bf16[512,512]{1,0:T(8,128)(2,1)S(1)} %collective-permute-done.10.refs_10_), channel_id=1, source_target_pairs={{0,16},{16,0},{1,17},{17,1},{2,18},{18,2},{3,19},{19,3},{4,20},{20... | collective-permute-start | bytes 1572872 | tf_op jit(solution)/shard_map/ppermute | solution.py:58
  98.9 0.8 copy-start.9
  99.7 12.4 %copy-start.1 = (bf16[8,4096]{1,0:T(8,128)(2,1)S(1)}, bf16[8,4096]{1,0:T(8,128)(2,1)}, u32[]{:S(2)}) copy-start(bf16[8,4096]{1,0:T(8,128)(2,1)} %param.12) | copy-start | bytes 196612
  108.6 12.5 %all-to-all-start = ((bf16[16,3,16,128]{3,2,1,0:T(8,128)(2,1)}), bf16[16,3,16,128]{3,2,1,0:T(8,128)(2,1)S(1)}, u32[]{:S(2)}, u32[]{:S(2)}) async-start(bf16[16,3,16,128]{3,2,1,0:T(8,128)(2,1)} %rows_3.1), calls=%async_computation | async-start | bytes 393216 | tf_op jit(solution)/shard_map/all_to_all | solution.py:535
  121.1 0.7 copy-start

commit v12 on v11

--- a/solution.py
+++ b/solution.py
@@ -486,12 +486,11 @@
 
         own_q = jnp.concatenate([keep_q, swap_core(give_q)], axis=0)
         behind_q, ahead_q, opposite_q = (along_ring(own_q, way) for way in (1, -1, 2))
-        ring_q = jnp.concatenate([own_q, behind_q, ahead_q, opposite_q], axis=0)
-        a_own_y = across_y(keep)
-        source_a, source_b, source_q = tie((keep, taken, ring_q))
+        a_own_y = across_y(tie((keep, own_q))[0])
+        source_a, source_b, behind_q, ahead_q, opposite_q = tie((keep, taken, behind_q, ahead_q, opposite_q))
         a_behind = along_ring(source_a)
         b_behind, b_own_y = along_ring(source_b), across_y(source_b)
-        other = swap_tokens((taken, source_q))
+        other = swap_tokens((taken, own_q))
         squares = square_sums(taken)
 
         source, squares, _ = tie((a_behind, squares, a_own_y))
@@ -501,6 +500,7 @@
         ones = starts(keep, taken, a_behind, b_behind, a_own_y, b_own_y)
         total = product(other, blocks, 0, 2, ones, None, "rows_1")
 
+        ring_q = jnp.concatenate([own_q, behind_q, ahead_q, opposite_q], axis=0)
         source_y, source, source_q, squares, total, _ = tie(
             (a_behind_y, a_opposite, ring_q, squares, total, b_ahead)
         )

time: 126 us -> 115 us (0.913)
  waiting for transfers between devices: 32.1 us -> 21.8 us
  starting transfers between devices: 34.4 us -> 32.8 us
    ppermute x4, waiting for transfers between devices: 8.98 us -> 1.26 us  [swap_core(): return lax.ppermute(x, 'section', [(i, i ^ 1) for i in range(n)])]
    ppermute x8, waiting for transfers between devices: 14.9 us -> 9.96 us  [along_ring(): return lax.ppermute(x, ('replica', 'section'), perm)]
    ppermute x4, waiting for transfers between devices: 5.28 us -> 7.61 us  [across_replica(): return lax.ppermute(x, 'replica', [(0, 1), (1, 0)])]
    ppermute x6, starting transfers between devices: 9.44 us -> 8.13 us  [across_y(): return lax.ppermute(x, 'section', [(i, i ^ 2) for i in range(16)])]
    unnamed x31 -> x35, local copies, waits for them, and re-layouts: 5.25 us -> 6.25 us
  transfers between devices with their start and end apart: 23 -> 23, of which waited for: 9 -> 8; matrix products, arithmetic and copies ran while one was open for 9% -> 9% of each run, Pallas kernels for 26% -> 30%
where the time goes in v12:
time: 115 us; the launch traced here: 114 us
  Pallas kernels  46.2 us (40%)
  starting transfers between devices  32.8 us (29%)
  waiting for transfers between devices  21.8 us (19%)
  local copies, waits for them, and re-layouts  9.18 us (8%)
  other arithmetic  3.66 us (3%)
    pallas_call x3, Pallas kernels, product(): pl.pallas_call(body, grid_spec=pltpu.PrefetchScalarGridSpec(num_scalar_pr...  27.8 us
    ppermute x8, starting transfers between devices, along_ring(): return lax.ppermute(x, ('replica', 'section'), perm)  12.2 us
    ppermute x8, waiting for transfers between devices, along_ring(): return lax.ppermute(x, ('replica', 'section'), perm)  9.96 us
    ppermute x4, starting transfers between devices, across_replica(): return lax.ppermute(x, 'replica', [(0, 1), (1, 0)])  8.22 us
    ppermute x6, starting transfers between devices, across_y(): return lax.ppermute(x, 'section', [(i, i ^ 2) for i in range(16)])  8.13 us
    ppermute x4, waiting for transfers between devices, across_replica(): return lax.ppermute(x, 'replica', [(0, 1), (1, 0)])  7.61 us
    pallas_call x1, Pallas kernels, square_sums(): pl.pallas_call(square_kernel, grid=(8,), in_specs=[pl.BlockSpec((tokens /...  7.59 us
    unnamed x35, local copies, waits for them, and re-layouts  6.25 us
  transfers between devices with their start and end apart: 23, of which 8 were waited for; matrix products, arithmetic and copies ran while one was open for 9% of the time, Pallas kernels for 30%

profile of v12, /device:TPU:0, one launch (start us, length us, event | category | flops | bytes accessed | tf_op | source)
XLA Modules:
  0.0 114.1 jit_solution(2521746797316017897)
XLA Ops:
  0.0 0.8 select_bitcast_fusion
  0.8 0.5 collective-permute-start.1
  1.2 2.1 %split.1 = (bf16[512,512]{1,0:T(8,128)(2,1)}, bf16[512,512]{1,0:T(8,128)(2,1)}) custom-call(s32[1]{0:T(128)} %bitcast.1.core_ref, bf16[512,1024]{1,0:T(8,128)(2,1)} %give_in.1, bf16[512,1024]{1,0:T(8,128)(2,1)} %give_in.1), custom_call_target="tpu_custom_call" | custom-call | bytes 262144 | tf_op jit(solution)/shard_map/split/pallas_call | solution.py:331
  3.3 0.1 collective-permute-start
  3.4 0.8 constant_dynamic-update-slice_fusion.10
  4.2 0.0 collective-permute-done.1
  4.2 1.2 %collective-permute-done.refs_5_ = bf16[512,512]{1,0:T(8,128)(2,1)S(1)} collective-permute-done((bf16[512,512]{1,0:T(8,128)(2,1)}, bf16[512,512]{1,0:T(8,128)(2,1)S(1)}, u32[]{:S(2)}, u32[]{:S(2)}) %collective-permute-start) | collective-permute-done | bytes 524320 | tf_op jit(solution)/shard_map/ppermute | solution.py:30
  5.4 0.1 collective-permute-start.13
  5.6 2.9 %collective-permute-start.2 = (bf16[16,2048]{1,0:T(8,128)(2,1)S(1)}, bf16[16,2048]{1,0:T(8,128)(2,1)S(1)}, u32[]{:S(2)}, u32[]{:S(2)}) collective-permute-start(bf16[16,2048]{1,0:T(8,128)(2,1)S(1)} %pad_maximum_fusion), channel_id=1, source_target_pairs={{0,4},{1,5},{2,6},{3,7},{4,12},{5,13},{6,14},{7,15},{12,8},{13,9},... | collective-permute-start | bytes 196616 | tf_op jit(solution)/shard_map/ppermute | solution.py:50
  8.5 1.0 collective-permute-start.3
  9.5 3.9 %collective-permute-start.4 = (bf16[16,2048]{1,0:T(8,128)(2,1)S(1)}, bf16[16,2048]{1,0:T(8,128)(2,1)S(1)}, u32[]{:S(2)}, u32[]{:S(2)}) collective-permute-start(bf16[16,2048]{1,0:T(8,128)(2,1)S(1)} %pad_maximum_fusion), channel_id=1, source_target_pairs={{0,12},{1,13},{2,14},{3,15},{4,8},{5,9},{6,10},{7,11},{12,0},{13,1... | collective-permute-start | bytes 196616 | tf_op jit(solution)/shard_map/ppermute | solution.py:50
  13.5 1.5 %collective-permute-start.7 = (bf16[512,512]{1,0:T(8,128)(2,1)}, bf16[512,512]{1,0:T(8,128)(2,1)S(1)}, u32[]{:S(2)}, u32[]{:S(2)}) collective-permute-start(bf16[512,512]{1,0:T(8,128)(2,1)} %get-tuple-element.37.refs_4_), channel_id=1, source_target_pairs={{0,2},{1,3},{2,0},{3,1},{4,6},{5,7},{6,4},{7,5},{8,10},{9,11},{10,... | collective-permute-start | bytes 1572872 | tf_op jit(solution)/shard_map/ppermute | solution.py:54
  15.0 0.0 collective-permute-done.3
  15.0 1.8 %collective-permute-done.4 = bf16[16,2048]{1,0:T(8,128)(2,1)S(1)} collective-permute-done((bf16[16,2048]{1,0:T(8,128)(2,1)S(1)}, bf16[16,2048]{1,0:T(8,128)(2,1)S(1)}, u32[]{:S(2)}, u32[]{:S(2)}) %collective-permute-start.4) | collective-permute-done | bytes 65568 | tf_op jit(solution)/shard_map/ppermute | solution.py:50
  16.8 1.2 %collective-permute-start.6 = (bf16[512,512]{1,0:T(8,128)(2,1)}, bf16[512,512]{1,0:T(8,128)(2,1)}, u32[]{:S(2)}, u32[]{:S(2)}) collective-permute-start(bf16[512,512]{1,0:T(8,128)(2,1)} %get-tuple-element.37.refs_4_), channel_id=1, source_target_pairs={{0,4},{1,5},{2,6},{3,7},{4,12},{5,13},{6,14},{7,15},{12,8},{13,9},... | collective-permute-start | bytes 1572872 | tf_op jit(solution)/shard_map/ppermute | solution.py:50
  18.0 2.2 %collective-permute-start.5 = (bf16[512,512]{1,0:T(8,128)(2,1)S(1)}, bf16[512,512]{1,0:T(8,128)(2,1)S(1)}, u32[]{:S(2)}, u32[]{:S(2)}) collective-permute-start(bf16[512,512]{1,0:T(8,128)(2,1)S(1)} %collective-permute-done.refs_5_), channel_id=1, source_target_pairs={{0,4},{1,5},{2,6},{3,7},{4,12},{5,13},{6,14},{7,15},{12,8},{13,9},... | collective-permute-start | bytes 1572872 | tf_op jit(solution)/shard_map/ppermute | solution.py:50
  20.2 1.5 %collective-permute-start.8 = (bf16[512,512]{1,0:T(8,128)(2,1)S(1)}, bf16[512,512]{1,0:T(8,128)(2,1)}, u32[]{:S(2)}, u32[]{:S(2)}) collective-permute-start(bf16[512,512]{1,0:T(8,128)(2,1)S(1)} %collective-permute-done.refs_5_), channel_id=1, source_target_pairs={{0,2},{1,3},{2,0},{3,1},{4,6},{5,7},{6,4},{7,5},{8,10},{9,11},{10,... | collective-permute-start | bytes 1572872 | tf_op jit(solution)/shard_map/ppermute | solution.py:54
  21.7 7.6 %squares.1 = f32[512,1]{1,0:T(8,128)} custom-call(bf16[512,8192]{1,0:T(8,128)(2,1)} %refs_1_.5), custom_call_target="tpu_custom_call" | custom-call | bytes 262144 | tf_op jit(solution)/shard_map/squares/pallas_call | solution.py:352
  29.3 1.1 reduce
  30.4 2.4 %collective-permute-done.6.refs_6_ = bf16[512,512]{1,0:T(8,128)(2,1)} collective-permute-done((bf16[512,512]{1,0:T(8,128)(2,1)}, bf16[512,512]{1,0:T(8,128)(2,1)}, u32[]{:S(2)}, u32[]{:S(2)}) %collective-permute-start.6) | collective-permute-done | bytes 524320 | tf_op jit(solution)/shard_map/ppermute | solution.py:50
  32.9 0.4 collective-permute-start.9
  33.3 1.2 %constant_dynamic-slice_fusion = (s32[1,24]{1,0:T(1,128)S(1)}, s32[24]{0:T(128)}) fusion(s32[32,24]{1,0:T(8,128)} %constant.54.clone, s32[]{:T(128)S(6)} %select_n.52), kind=kLoop, calls=%fused_computation.45 | loop fusion | bytes 292 | tf_op jit(solution)/shard_map/dynamic_slice | solution.py:477
  34.5 0.6 constant_dynamic-update-slice_fusion.4
  35.1 0.6 constant_dynamic-update-slice_fusion.9
  35.7 1.5 %collective-permute-start.11 = (bf16[512,512]{1,0:T(8,128)(2,1)}, bf16[512,512]{1,0:T(8,128)(2,1)}, u32[]{:S(2)}, u32[]{:S(2)}) collective-permute-start(bf16[512,512]{1,0:T(8,128)(2,1)} %collective-permute-done.6.refs_6_), channel_id=1, source_target_pairs={{0,2},{1,3},{2,0},{3,1},{4,6},{5,7},{6,4},{7,5},{8,10},{9,11},{10,... | collective-permute-start | bytes 1572872 | tf_op jit(solution)/shard_map/ppermute | solution.py:54
  37.2 4.5 %collective-permute-done.5.refs_7_ = bf16[512,512]{1,0:T(8,128)(2,1)S(1)} collective-permute-done((bf16[512,512]{1,0:T(8,128)(2,1)S(1)}, bf16[512,512]{1,0:T(8,128)(2,1)S(1)}, u32[]{:S(2)}, u32[]{:S(2)}) %collective-permute-start.5) | collective-permute-done | bytes 524320 | tf_op jit(solution)/shard_map/ppermute | solution.py:50
  41.7 1.2 %collective-permute-done.9.refs_5_ = bf16[512,512]{1,0:T(8,128)(2,1)S(1)} collective-permute-done((bf16[512,512]{1,0:T(8,128)(2,1)}, bf16[512,512]{1,0:T(8,128)(2,1)S(1)}, u32[]{:S(2)}, u32[]{:S(2)}) %collective-permute-start.9) | collective-permute-done | bytes 524320 | tf_op jit(solution)/shard_map/ppermute | solution.py:58
  42.9 3.4 %collective-permute-start.14 = (bf16[512,512]{1,0:T(8,128)(2,1)S(1)}, bf16[512,512]{1,0:T(8,128)(2,1)S(1)}, u32[]{:S(2)}, u32[]{:S(2)}) collective-permute-start(bf16[512,512]{1,0:T(8,128)(2,1)S(1)} %collective-permute-done.5.refs_7_), channel_id=1, source_target_pairs={{0,16},{16,0},{1,17},{17,1},{2,18},{18,2},{3,19},{19,3},{4,20},{20... | collective-permute-start | bytes 1572872 | tf_op jit(solution)/shard_map/ppermute | solution.py:58
  46.3 0.6 constant_dynamic-update-slice_fusion.8
  46.9 0.6 constant_dynamic-update-slice_fusion.7
  47.6 0.6 constant_dynamic-update-slice_fusion.6
  48.2 1.5 %collective-permute-start.10 = (bf16[512,512]{1,0:T(8,128)(2,1)S(1)}, bf16[512,512]{1,0:T(8,128)(2,1)S(1)}, u32[]{:S(2)}, u32[]{:S(2)}) collective-permute-start(bf16[512,512]{1,0:T(8,128)(2,1)S(1)} %collective-permute-done.5.refs_7_), channel_id=1, source_target_pairs={{0,2},{1,3},{2,0},{3,1},{4,6},{5,7},{6,4},{7,5},{8,10},{9,11},{10,... | collective-permute-start | bytes 1572872 | tf_op jit(solution)/shard_map/ppermute | solution.py:54
  49.7 0.0 copy-start.12
  49.7 0.0 copy-start.13
  49.7 9.4 %rows_1.1.refs_4_ = f32[1024,512]{1,0:T(8,128)} custom-call(s32[24]{0:T(128)} %get-tuple-element.72.block_ref, bf16[512,8192]{1,0:T(8,128)(2,1)} %refs_1_.5, bf16[512,8192]{1,0:T(8,128)(2,1)} %refs_1_.5, bf16[512,8192]{1,0:T(8,128)(2,1)} %collective-permute-done.13.refs_2_.refs_3_, bf16[512,8192]{1,0:T(8,128)(2,1)} %collective-permute-done.13.refs_2_.refs_3_, ...), custom_call_target="tpu_custom_call" | custom-call | bytes 262144 | tf_op jit(solution)/shard_map/rows_1/pallas_call | solution.py:460
  59.2 0.8 copy-done.9
  60.0 2.3 %collective-permute-start.16 = (bf16[512,512]{1,0:T(8,128)(2,1)}, bf16[512,512]{1,0:T(8,128)(2,1)S(1)}, u32[]{:S(2)}, u32[]{:S(2)}) collective-permute-start(bf16[512,512]{1,0:T(8,128)(2,1)} %collective-permute-done.11.refs_9_), channel_id=1, source_target_pairs={{0,16},{16,0},{1,17},{17,1},{2,18},{18,2},{3,19},{19,3},{4,20},{20... | collective-permute-start | bytes 1572872 | tf_op jit(solution)/shard_map/ppermute | solution.py:58
  62.3 0.1 slice_bitcast_fusion.1
  62.4 0.5 collective-permute-start.18
  62.9 0.1 add_convert_fusion
  63.0 1.5 %collective-permute-start.19 = (bf16[512,512]{1,0:T(8,128)(2,1)S(1)}, bf16[512,512]{1,0:T(8,128)(2,1)S(1)}, u32[]{:S(2)}, u32[]{:S(2)}) collective-permute-start(bf16[512,512]{1,0:T(8,128)(2,1)S(1)} %collective-permute-done.12.refs_7_), channel_id=1, source_target_pairs={{0,2},{1,3},{2,0},{3,1},{4,6},{5,7},{6,4},{7,5},{8,10},{9,11},{10,... | collective-permute-start | bytes 1572872 | tf_op jit(solution)/shard_map/ppermute | solution.py:54
  64.5 1.2 %collective-permute-done.15.refs_8_ = bf16[512,512]{1,0:T(8,128)(2,1)} collective-permute-done((bf16[512,512]{1,0:T(8,128)(2,1)S(1)}, bf16[512,512]{1,0:T(8,128)(2,1)}, u32[]{:S(2)}, u32[]{:S(2)}) %collective-permute-start.15) | collective-permute-done | bytes 524320 | tf_op jit(solution)/shard_map/ppermute | solution.py:50
  65.7 6.4 %collective-permute-done.16.refs_7_ = bf16[512,512]{1,0:T(8,128)(2,1)S(1)} collective-permute-done((bf16[512,512]{1,0:T(8,128)(2,1)}, bf16[512,512]{1,0:T(8,128)(2,1)S(1)}, u32[]{:S(2)}, u32[]{:S(2)}) %collective-permute-start.16) | collective-permute-done | bytes 524320 | tf_op jit(solution)/shard_map/ppermute | solution.py:58
  72.1 0.1 collective-permute-start.17
  72.2 0.9 collective-permute-start.20
  73.2 2.1 %collective-permute-start.21 = (bf16[512,512]{1,0:T(8,128)(2,1)S(1)}, bf16[512,512]{1,0:T(8,128)(2,1)}, u32[]{:S(2)}, u32[]{:S(2)}) collective-permute-start(bf16[512,512]{1,0:T(8,128)(2,1)S(1)} %collective-permute-done.10.refs_10_), channel_id=1, source_target_pairs={{0,16},{16,0},{1,17},{17,1},{2,18},{18,2},{3,19},{19,3},{4,20},{20... | collective-permute-start | bytes 1572872 | tf_op jit(solution)/shard_map/ppermute | solution.py:58
  75.3 9.6 %rows_2.1.refs_4_ = f32[1024,512]{1,0:T(8,128)} custom-call(s32[24]{0:T(128)} %get-tuple-element.72.block_ref, bf16[512,8192]{1,0:T(8,128)(2,1)} %refs_1_.5, bf16[512,8192]{1,0:T(8,128)(2,1)} %refs_1_.5, bf16[512,8192]{1,0:T(8,128)(2,1)} %collective-permute-done.13.refs_2_.refs_3_, bf16[512,8192]{1,0:T(8,128)(2,1)} %collective-permute-done.13.refs_2_.refs_3_, ...), custom_call_target="tpu_custom_call" | custom-call | bytes 262144 | tf_op jit(solution)/shard_map/rows_2/pallas_call | solution.py:460
  85.0 0.1 slice_convert_fusion.1
  85.0 0.1 and_select_fusion.1
  85.1 0.1 select_reduce_fusion
  85.2 1.0 copy.13.refs_6_
  86.2 0.1 fusion.7
  86.3 0.2 fusion
  86.6 0.6 copy.19
  87.2 0.6 pad_add_fusion.slot_ref
  87.8 0.8 copy-done.10
  88.6 0.2 copy-done.11
  88.8 8.9 %rows_3.1 = bf16[16,3,16,128]{3,2,1,0:T(8,128)(2,1)} custom-call(s32[24]{0:T(128)} %get-tuple-element.72.block_ref, s32[3,16]{1,0:T(4,128)} %pad_add_fusion.slot_ref, bf16[512,8192]{1,0:T(8,128)(2,1)} %refs_1_.5, bf16[512,8192]{1,0:T(8,128)(2,1)} %refs_1_.5, bf16[512,8192]{1,0:T(8,128)(2,1)} %collective-permute-done.13.refs_2_.refs_3_, ...), custom_call_target="tpu_custom_call" | custom-call | bytes 262144 | tf_op jit(solution)/shard_map/rows_3/pallas_call | solution.py:460
  97.7 3.5 %all-to-all-start = ((bf16[16,3,16,128]{3,2,1,0:T(8,128)(2,1)}), bf16[16,3,16,128]{3,2,1,0:T(8,128)(2,1)S(1)}, u32[]{:S(2)}, u32[]{:S(2)}) async-start(bf16[16,3,16,128]{3,2,1,0:T(8,128)(2,1)} %rows_3.1), calls=%async_computation | async-start | bytes 393216 | tf_op jit(solution)/shard_map/all_to_all | solution.py:535
  101.2 0.6 copy.18
  101.9 5.4 %resident.1 = (f32[8,32,128]{2,1,0:T(8,128)}, f32[32,128]{1,0:T(8,128)}, f32[32,128]{1,0:T(8,128)}) custom-call(s32[8]{0:T(128)} %length_ref, bf16[8,32,128]{2,1,0:T(8,128)(2,1)} %bitcast.40, bf16[8,256,1024]{2,1,0:T(8,128)(2,1)} %cache_ref.1), custom_call_target="tpu_custom_call" | custom-call | bytes 262144 | tf_op jit(solution)/shard_map/resident/pallas_call | solution.py:391
  107.2 3.0 %all-to-all-done.got_ref = bf16[16,3,16,128]{3,2,1,0:T(8,128)(2,1)S(1)} async-done(((bf16[16,3,16,128]{3,2,1,0:T(8,128)(2,1)}), bf16[16,3,16,128]{3,2,1,0:T(8,128)(2,1)S(1)}, u32[]{:S(2)}, u32[]{:S(2)}) %all-to-all-start) | async-done | bytes 196640 | tf_op jit(solution)/shard_map/all_to_all | solution.py:535
  110.2 0.7 copy-done
  110.8 3.3 %combine.1 = bf16[8,4096]{1,0:T(8,128)(2,1)} custom-call(bf16[16,3,16,128]{3,2,1,0:T(8,128)(2,1)} %copy-done, f32[8,32,128]{2,1,0:T(8,128)} %get-tuple-element.56.res_out_ref, f32[32,128]{1,0:T(8,128)} %get-tuple-element.57.res_top_ref, f32[32,128]{1,0:T(8,128)} %get-tuple-element.58.res_sum_ref), custom_call_target="tpu_custom_call" | custom-call | tf_op jit(solution)/shard_map/combine/pallas_call | solution.py:537
  (45 shorter events, 0.2 us)
Async XLA Ops:
  0.8 3.4 %collective-permute-start.1 = (bf16[8,2048]{1,0:T(8,128)(2,1)S(1)}, bf16[8,2048]{1,0:T(8,128)(2,1)S(1)}, u32[]{:S(2)}, u32[]{:S(2)}) collective-permute-start(bf16[8,2048]{1,0:T(8,128)(2,1)S(1)} %select_bitcast_fusion), channel_id=1, source_target_pairs={{0,1},{1,0},{2,3},{3,2},{4,5},{5,4},{6,7},{7,6},{8,9},{9,8},{10,11... | collective-permute-start | bytes 98312 | tf_op jit(solution)/shard_map/ppermute | solution.py:30
  3.3 2.1 %collective-permute-start = (bf16[512,512]{1,0:T(8,128)(2,1)}, bf16[512,512]{1,0:T(8,128)(2,1)S(1)}, u32[]{:S(2)}, u32[]{:S(2)}) collective-permute-start(bf16[512,512]{1,0:T(8,128)(2,1)} %get-tuple-element.33), channel_id=1, source_target_pairs={{0,1},{1,0},{2,3},{3,2},{4,5},{5,4},{6,7},{7,6},{8,9},{9,8},{10,11... | collective-permute-start | bytes 1572872 | tf_op jit(solution)/shard_map/ppermute | solution.py:30
  5.4 23.9 %copy-start.2 = (bf16[512,512]{1,0:T(8,128)(2,1)}, bf16[512,512]{1,0:T(8,128)(2,1)S(1)}, u32[]{:S(2)}) copy-start(bf16[512,512]{1,0:T(8,128)(2,1)S(1)} %collective-permute-done.refs_5_) | copy-start | bytes 1572868
  5.4 44.3 %collective-permute-start.13 = (bf16[512,8192]{1,0:T(8,128)(2,1)}, bf16[512,8192]{1,0:T(8,128)(2,1)}, u32[]{:S(2)}, u32[]{:S(2)}) collective-permute-start(bf16[512,8192]{1,0:T(8,128)(2,1)} %refs_1_.5), channel_id=1, source_target_pairs={{0,1},{1,0},{2,3},{3,2},{4,5},{5,4},{6,7},{7,6},{8,9},{9,8},{10,11... | collective-permute-start | bytes 25165832 | tf_op jit(solution)/shard_map/ppermute | solution.py:30
  5.6 9.4 %collective-permute-start.2 = (bf16[16,2048]{1,0:T(8,128)(2,1)S(1)}, bf16[16,2048]{1,0:T(8,128)(2,1)S(1)}, u32[]{:S(2)}, u32[]{:S(2)}) collective-permute-start(bf16[16,2048]{1,0:T(8,128)(2,1)S(1)} %pad_maximum_fusion), channel_id=1, source_target_pairs={{0,4},{1,5},{2,6},{3,7},{4,12},{5,13},{6,14},{7,15},{12,8},{13,9},... | collective-permute-start | bytes 196616 | tf_op jit(solution)/shard_map/ppermute | solution.py:50
  8.5 6.5 %collective-permute-start.3 = (bf16[16,2048]{1,0:T(8,128)(2,1)S(1)}, bf16[16,2048]{1,0:T(8,128)(2,1)S(1)}, u32[]{:S(2)}, u32[]{:S(2)}) collective-permute-start(bf16[16,2048]{1,0:T(8,128)(2,1)S(1)} %pad_maximum_fusion), channel_id=1, source_target_pairs={{0,8},{1,9},{2,10},{3,11},{4,0},{5,1},{6,2},{7,3},{12,4},{13,5},{1... | collective-permute-start | bytes 196616 | tf_op jit(solution)/shard_map/ppermute | solution.py:50
  9.5 7.3 %collective-permute-start.4 = (bf16[16,2048]{1,0:T(8,128)(2,1)S(1)}, bf16[16,2048]{1,0:T(8,128)(2,1)S(1)}, u32[]{:S(2)}, u32[]{:S(2)}) collective-permute-start(bf16[16,2048]{1,0:T(8,128)(2,1)S(1)} %pad_maximum_fusion), channel_id=1, source_target_pairs={{0,12},{1,13},{2,14},{3,15},{4,8},{5,9},{6,10},{7,11},{12,0},{13,1... | collective-permute-start | bytes 196616 | tf_op jit(solution)/shard_map/ppermute | solution.py:50
  13.5 16.9 %collective-permute-start.7 = (bf16[512,512]{1,0:T(8,128)(2,1)}, bf16[512,512]{1,0:T(8,128)(2,1)S(1)}, u32[]{:S(2)}, u32[]{:S(2)}) collective-permute-start(bf16[512,512]{1,0:T(8,128)(2,1)} %get-tuple-element.37.refs_4_), channel_id=1, source_target_pairs={{0,2},{1,3},{2,0},{3,1},{4,6},{5,7},{6,4},{7,5},{8,10},{9,11},{10,... | collective-permute-start | bytes 1572872 | tf_op jit(solution)/shard_map/ppermute | solution.py:54
  16.8 16.1 %collective-permute-start.6 = (bf16[512,512]{1,0:T(8,128)(2,1)}, bf16[512,512]{1,0:T(8,128)(2,1)}, u32[]{:S(2)}, u32[]{:S(2)}) collective-permute-start(bf16[512,512]{1,0:T(8,128)(2,1)} %get-tuple-element.37.refs_4_), channel_id=1, source_target_pairs={{0,4},{1,5},{2,6},{3,7},{4,12},{5,13},{6,14},{7,15},{12,8},{13,9},... | collective-permute-start | bytes 1572872 | tf_op jit(solution)/shard_map/ppermute | solution.py:50
  18.0 23.7 %collective-permute-start.5 = (bf16[512,512]{1,0:T(8,128)(2,1)S(1)}, bf16[512,512]{1,0:T(8,128)(2,1)S(1)}, u32[]{:S(2)}, u32[]{:S(2)}) collective-permute-start(bf16[512,512]{1,0:T(8,128)(2,1)S(1)} %collective-permute-done.refs_5_), channel_id=1, source_target_pairs={{0,4},{1,5},{2,6},{3,7},{4,12},{5,13},{6,14},{7,15},{12,8},{13,9},... | collective-permute-start | bytes 1572872 | tf_op jit(solution)/shard_map/ppermute | solution.py:50
  20.2 21.5 %collective-permute-start.8 = (bf16[512,512]{1,0:T(8,128)(2,1)S(1)}, bf16[512,512]{1,0:T(8,128)(2,1)}, u32[]{:S(2)}, u32[]{:S(2)}) collective-permute-start(bf16[512,512]{1,0:T(8,128)(2,1)S(1)} %collective-permute-done.refs_5_), channel_id=1, source_target_pairs={{0,2},{1,3},{2,0},{3,1},{4,6},{5,7},{6,4},{7,5},{8,10},{9,11},{10,... | collective-permute-start | bytes 1572872 | tf_op jit(solution)/shard_map/ppermute | solution.py:54
  30.4 19.3 %copy-start.6 = (bf16[512,512]{1,0:T(8,128)(2,1)}, bf16[512,512]{1,0:T(8,128)(2,1)S(1)}, u32[]{:S(2)}) copy-start(bf16[512,512]{1,0:T(8,128)(2,1)S(1)} %collective-permute-done.7.refs_8_) | copy-start | bytes 1572868
  32.9 10.0 %collective-permute-start.9 = (bf16[512,512]{1,0:T(8,128)(2,1)}, bf16[512,512]{1,0:T(8,128)(2,1)S(1)}, u32[]{:S(2)}, u32[]{:S(2)}) collective-permute-start(bf16[512,512]{1,0:T(8,128)(2,1)} %collective-permute-done.6.refs_6_), channel_id=1, source_target_pairs={{0,16},{16,0},{1,17},{17,1},{2,18},{18,2},{3,19},{19,3},{4,20},{20... | collective-permute-start | bytes 1572872 | tf_op jit(solution)/shard_map/ppermute | solution.py:58
  35.7 23.4 %collective-permute-start.11 = (bf16[512,512]{1,0:T(8,128)(2,1)}, bf16[512,512]{1,0:T(8,128)(2,1)}, u32[]{:S(2)}, u32[]{:S(2)}) collective-permute-start(bf16[512,512]{1,0:T(8,128)(2,1)} %collective-permute-done.6.refs_6_), channel_id=1, source_target_pairs={{0,2},{1,3},{2,0},{3,1},{4,6},{5,7},{6,4},{7,5},{8,10},{9,11},{10,... | collective-permute-start | bytes 1572872 | tf_op jit(solution)/shard_map/ppermute | solution.py:54
  41.7 8.0 %copy-start.7 = (bf16[512,512]{1,0:T(8,128)(2,1)}, bf16[512,512]{1,0:T(8,128)(2,1)S(1)}, u32[]{:S(2)}) copy-start(bf16[512,512]{1,0:T(8,128)(2,1)S(1)} %collective-permute-done.5.refs_7_) | copy-start | bytes 1572868
  41.7 17.5 %collective-permute-start.12 = (bf16[512,512]{1,0:T(8,128)(2,1)}, bf16[512,512]{1,0:T(8,128)(2,1)S(1)}, u32[]{:S(2)}, u32[]{:S(2)}) collective-permute-start(bf16[512,512]{1,0:T(8,128)(2,1)} %collective-permute-done.6.refs_6_), channel_id=1, source_target_pairs={{0,4},{1,5},{2,6},{3,7},{4,12},{5,13},{6,14},{7,15},{12,8},{13,9},... | collective-permute-start | bytes 1572872 | tf_op jit(solution)/shard_map/ppermute | solution.py:50
  42.9 16.2 %copy-start.4 = (bf16[512,512]{1,0:T(8,128)(2,1)}, bf16[512,512]{1,0:T(8,128)(2,1)S(1)}, u32[]{:S(2)}) copy-start(bf16[512,512]{1,0:T(8,128)(2,1)S(1)} %collective-permute-done.9.refs_5_) | copy-start | bytes 1572868
  42.9 16.3 %collective-permute-start.14 = (bf16[512,512]{1,0:T(8,128)(2,1)S(1)}, bf16[512,512]{1,0:T(8,128)(2,1)S(1)}, u32[]{:S(2)}, u32[]{:S(2)}) collective-permute-start(bf16[512,512]{1,0:T(8,128)(2,1)S(1)} %collective-permute-done.5.refs_7_), channel_id=1, source_target_pairs={{0,16},{16,0},{1,17},{17,1},{2,18},{18,2},{3,19},{19,3},{4,20},{20... | collective-permute-start | bytes 1572872 | tf_op jit(solution)/shard_map/ppermute | solution.py:58
  48.2 16.3 %collective-permute-start.10 = (bf16[512,512]{1,0:T(8,128)(2,1)S(1)}, bf16[512,512]{1,0:T(8,128)(2,1)S(1)}, u32[]{:S(2)}, u32[]{:S(2)}) collective-permute-start(bf16[512,512]{1,0:T(8,128)(2,1)S(1)} %collective-permute-done.5.refs_7_), channel_id=1, source_target_pairs={{0,2},{1,3},{2,0},{3,1},{4,6},{5,7},{6,4},{7,5},{8,10},{9,11},{10,... | collective-permute-start | bytes 1572872 | tf_op jit(solution)/shard_map/ppermute | solution.py:54
  49.7 16.0 %collective-permute-start.15 = (bf16[512,512]{1,0:T(8,128)(2,1)S(1)}, bf16[512,512]{1,0:T(8,128)(2,1)}, u32[]{:S(2)}, u32[]{:S(2)}) collective-permute-start(bf16[512,512]{1,0:T(8,128)(2,1)S(1)} %collective-permute-done.5.refs_7_), channel_id=1, source_target_pairs={{0,4},{1,5},{2,6},{3,7},{4,12},{5,13},{6,14},{7,15},{12,8},{13,9},... | collective-permute-start | bytes 1572872 | tf_op jit(solution)/shard_map/ppermute | solution.py:50
  49.7 13.1 %copy-start.12 = (s32[8]{0:T(128)S(1)}, s32[8]{0:T(128)}, u32[]{:S(2)}) copy-start(s32[8]{0:T(128)} %param.11) | copy-start | bytes 100
  49.7 13.1 %copy-start.13 = (s32[8]{0:T(128)S(1)}, s32[8]{0:T(128)}, u32[]{:S(2)}) copy-start(s32[8]{0:T(128)} %param.10) | copy-start | bytes 100
  59.2 16.2 %copy-start.3 = (bf16[512,512]{1,0:T(8,128)(2,1)}, bf16[512,512]{1,0:T(8,128)(2,1)S(1)}, u32[]{:S(2)}) copy-start(bf16[512,512]{1,0:T(8,128)(2,1)S(1)} %collective-permute-done.12.refs_7_) | copy-start | bytes 1572868
  59.2 0.9 copy-start.9
  60.0 12.1 %collective-permute-start.16 = (bf16[512,512]{1,0:T(8,128)(2,1)}, bf16[512,512]{1,0:T(8,128)(2,1)S(1)}, u32[]{:S(2)}, u32[]{:S(2)}) collective-permute-start(bf16[512,512]{1,0:T(8,128)(2,1)} %collective-permute-done.11.refs_9_), channel_id=1, source_target_pairs={{0,16},{16,0},{1,17},{17,1},{2,18},{18,2},{3,19},{19,3},{4,20},{20... | collective-permute-start | bytes 1572872 | tf_op jit(solution)/shard_map/ppermute | solution.py:58
  62.4 9.9 %collective-permute-start.18 = (bf16[64,2048]{1,0:T(8,128)(2,1)}, bf16[64,2048]{1,0:T(8,128)(2,1)S(1)}, u32[]{:S(2)}, u32[]{:S(2)}) collective-permute-start(bf16[64,2048]{1,0:T(8,128)(2,1)} %get-tuple-element.51), channel_id=1, source_target_pairs={{0,2},{1,3},{2,0},{3,1},{4,6},{5,7},{6,4},{7,5},{8,10},{9,11},{10,... | collective-permute-start | bytes 786440 | tf_op jit(solution)/shard_map/ppermute | solution.py:54
  63.0 24.8 %collective-permute-start.19 = (bf16[512,512]{1,0:T(8,128)(2,1)S(1)}, bf16[512,512]{1,0:T(8,128)(2,1)S(1)}, u32[]{:S(2)}, u32[]{:S(2)}) collective-permute-start(bf16[512,512]{1,0:T(8,128)(2,1)S(1)} %collective-permute-done.12.refs_7_), channel_id=1, source_target_pairs={{0,2},{1,3},{2,0},{3,1},{4,6},{5,7},{6,4},{7,5},{8,10},{9,11},{10,... | collective-permute-start | bytes 1572872 | tf_op jit(solution)/shard_map/ppermute | solution.py:54
  64.5 10.8 %copy-start.5 = (bf16[512,512]{1,0:T(8,128)(2,1)}, bf16[512,512]{1,0:T(8,128)(2,1)S(1)}, u32[]{:S(2)}) copy-start(bf16[512,512]{1,0:T(8,128)(2,1)S(1)} %collective-permute-done.10.refs_10_) | copy-start | bytes 1572868
  72.1 12.8 %copy-start.8 = (bf16[512,512]{1,0:T(8,128)(2,1)}, bf16[512,512]{1,0:T(8,128)(2,1)S(1)}, u32[]{:S(2)}) copy-start(bf16[512,512]{1,0:T(8,128)(2,1)S(1)} %collective-permute-done.16.refs_7_) | copy-start | bytes 1572868
  72.1 12.8 %collective-permute-start.17 = (f32[8,128]{1,0:T(8,128)S(1)}, f32[8,128]{1,0:T(8,128)S(1)}, u32[]{:S(2)}, u32[]{:S(2)}) collective-permute-start(f32[8,128]{1,0:T(8,128)S(1)} %fusion.2), channel_id=1, source_target_pairs={{0,1},{1,0},{2,3},{3,2},{4,5},{5,4},{6,7},{7,6},{8,9},{9,8},{10,11... | collective-permute-start | bytes 12296 | tf_op jit(solution)/shard_map/ppermute | solution.py:30
  72.2 15.6 %collective-permute-start.20 = (bf16[512,512]{1,0:T(8,128)(2,1)S(1)}, bf16[512,512]{1,0:T(8,128)(2,1)S(1)}, u32[]{:S(2)}, u32[]{:S(2)}) collective-permute-start(bf16[512,512]{1,0:T(8,128)(2,1)S(1)} %collective-permute-done.10.refs_10_), channel_id=1, source_target_pairs={{0,4},{1,5},{2,6},{3,7},{4,12},{5,13},{6,14},{7,15},{12,8},{13,9},... | collective-permute-start | bytes 1572872 | tf_op jit(solution)/shard_map/ppermute | solution.py:50
  73.2 14.6 %collective-permute-start.21 = (bf16[512,512]{1,0:T(8,128)(2,1)S(1)}, bf16[512,512]{1,0:T(8,128)(2,1)}, u32[]{:S(2)}, u32[]{:S(2)}) collective-permute-start(bf16[512,512]{1,0:T(8,128)(2,1)S(1)} %collective-permute-done.10.refs_10_), channel_id=1, source_target_pairs={{0,16},{16,0},{1,17},{17,1},{2,18},{18,2},{3,19},{19,3},{4,20},{20... | collective-permute-start | bytes 1572872 | tf_op jit(solution)/shard_map/ppermute | solution.py:58
  87.8 0.8 copy-start.10
  87.8 1.0 copy-start.11
  88.8 12.4 %copy-start.1 = (bf16[8,4096]{1,0:T(8,128)(2,1)S(1)}, bf16[8,4096]{1,0:T(8,128)(2,1)}, u32[]{:S(2)}) copy-start(bf16[8,4096]{1,0:T(8,128)(2,1)} %param.12) | copy-start | bytes 196612
  97.7 12.5 %all-to-all-start = ((bf16[16,3,16,128]{3,2,1,0:T(8,128)(2,1)}), bf16[16,3,16,128]{3,2,1,0:T(8,128)(2,1)S(1)}, u32[]{:S(2)}, u32[]{:S(2)}) async-start(bf16[16,3,16,128]{3,2,1,0:T(8,128)(2,1)} %rows_3.1), calls=%async_computation | async-start | bytes 393216 | tf_op jit(solution)/shard_map/all_to_all | solution.py:535
  110.2 0.7 copy-start

commit v13 on v12

--- a/solution.py
+++ b/solution.py
@@ -487,13 +487,13 @@
         own_q = jnp.concatenate([keep_q, swap_core(give_q)], axis=0)
         behind_q, ahead_q, opposite_q = (along_ring(own_q, way) for way in (1, -1, 2))
         a_own_y = across_y(tie((keep, own_q))[0])
-        source_a, source_b, behind_q, ahead_q, opposite_q = tie((keep, taken, behind_q, ahead_q, opposite_q))
-        a_behind = along_ring(source_a)
+        a_behind = along_ring(tie((keep, own_q))[0])
+        source_b, behind_q, ahead_q, opposite_q = tie((taken, behind_q, ahead_q, opposite_q))
         b_behind, b_own_y = along_ring(source_b), across_y(source_b)
         other = swap_tokens((taken, own_q))
-        squares = square_sums(taken)
-
-        source, squares, _ = tie((a_behind, squares, a_own_y))
+        squares = square_sums(a_behind)
+
+        source, _ = tie((a_behind, a_own_y))
         a_ahead, a_opposite, a_behind_y = across_replica(source), along_ring(source), across_y(source)
         source, squares, _ = tie((b_behind, squares, (b_own_y, a_ahead)))
         b_ahead, b_opposite, b_behind_y = across_replica(source), along_ring(source), across_y(source)

time: 115 us -> 119 us (1.035)
  waiting for transfers between devices: 21.8 us -> 24.5 us
  starting transfers between devices: 32.8 us -> 34.5 us
    ppermute x8, starting transfers between devices: 12.2 us -> 20.7 us  [along_ring(): return lax.ppermute(x, ('replica', 'section'), perm)]
    ppermute x4, starting transfers between devices: 8.22 us -> 2.18 us  [across_replica(): return lax.ppermute(x, 'replica', [(0, 1), (1, 0)])]
    ppermute x8, waiting for transfers between devices: 9.96 us -> 13.4 us  [along_ring(): return lax.ppermute(x, ('replica', 'section'), perm)]
    ppermute x4, waiting for transfers between devices: 7.61 us -> 5.75 us  [across_replica(): return lax.ppermute(x, 'replica', [(0, 1), (1, 0)])]
    unnamed x35 -> x33, local copies, waits for them, and re-layouts: 6.25 us -> 5.34 us
  transfers between devices with their start and end apart: 23 -> 23, of which waited for: 8 -> 9; matrix products, arithmetic and copies ran while one was open for 9% -> 9% of each run, Pallas kernels for 30% -> 29%
where the time goes in v13:
time: 119 us; the launch traced here: 118 us
  Pallas kernels  46.3 us (39%)
  starting transfers between devices  34.5 us (29%)
  waiting for transfers between devices  24.5 us (21%)
  local copies, waits for them, and re-layouts  8.36 us (7%)
  other arithmetic  3.67 us (3%)
    pallas_call x3, Pallas kernels, product(): pl.pallas_call(body, grid_spec=pltpu.PrefetchScalarGridSpec(num_scalar_pr...  28 us
    ppermute x8, starting transfers between devices, along_ring(): return lax.ppermute(x, ('replica', 'section'), perm)  20.7 us
    ppermute x8, waiting for transfers between devices, along_ring(): return lax.ppermute(x, ('replica', 'section'), perm)  13.4 us
    pallas_call x1, Pallas kernels, square_sums(): pl.pallas_call(square_kernel, grid=(8,), in_specs=[pl.BlockSpec((tokens /...  7.6 us
    ppermute x6, starting transfers between devices, across_y(): return lax.ppermute(x, 'section', [(i, i ^ 2) for i in range(16)])  7.17 us
    ppermute x4, waiting for transfers between devices, across_replica(): return lax.ppermute(x, 'replica', [(0, 1), (1, 0)])  5.75 us
    pallas_call x1, Pallas kernels, resident(): pl.pallas_call(resident_kernel, grid_spec=pltpu.PrefetchScalarGridSpec(nu...  5.38 us
    unnamed x33, local copies, waits for them, and re-layouts  5.34 us
  transfers between devices with their start and end apart: 23, of which 9 were waited for; matrix products, arithmetic and copies ran while one was open for 9% of the time, Pallas kernels for 29%

profile of v13, /device:TPU:0, one launch (start us, length us, event | category | flops | bytes accessed | tf_op | source)
XLA Modules:
  0.0 117.7 jit_solution(4717960304724045942)
XLA Ops:
  0.0 0.8 select_bitcast_fusion
  0.8 0.5 collective-permute-start.1
  1.2 2.1 %split.1 = (bf16[512,512]{1,0:T(8,128)(2,1)}, bf16[512,512]{1,0:T(8,128)(2,1)}) custom-call(s32[1]{0:T(128)} %bitcast.1.core_ref, bf16[512,1024]{1,0:T(8,128)(2,1)} %give_in.1, bf16[512,1024]{1,0:T(8,128)(2,1)} %give_in.1), custom_call_target="tpu_custom_call" | custom-call | bytes 262144 | tf_op jit(solution)/shard_map/split/pallas_call | solution.py:331
  3.3 0.1 collective-permute-start
  3.4 0.8 constant_dynamic-update-slice_fusion.10
  4.2 0.0 collective-permute-done.1
  4.2 1.2 %collective-permute-done.refs_5_ = bf16[512,512]{1,0:T(8,128)(2,1)S(1)} collective-permute-done((bf16[512,512]{1,0:T(8,128)(2,1)}, bf16[512,512]{1,0:T(8,128)(2,1)S(1)}, u32[]{:S(2)}, u32[]{:S(2)}) %collective-permute-start) | collective-permute-done | bytes 524320 | tf_op jit(solution)/shard_map/ppermute | solution.py:30
  5.4 0.1 collective-permute-start.13
  5.6 2.9 %collective-permute-start.6 = (bf16[512,512]{1,0:T(8,128)(2,1)}, bf16[512,512]{1,0:T(8,128)(2,1)S(1)}, u32[]{:S(2)}, u32[]{:S(2)}) collective-permute-start(bf16[512,512]{1,0:T(8,128)(2,1)} %get-tuple-element.33.refs_4_), channel_id=1, source_target_pairs={{0,4},{1,5},{2,6},{3,7},{4,12},{5,13},{6,14},{7,15},{12,8},{13,9},... | collective-permute-start | bytes 1572872 | tf_op jit(solution)/shard_map/ppermute | solution.py:50
  8.5 1.5 %collective-permute-start.8 = (bf16[512,512]{1,0:T(8,128)(2,1)}, bf16[512,512]{1,0:T(8,128)(2,1)S(1)}, u32[]{:S(2)}, u32[]{:S(2)}) collective-permute-start(bf16[512,512]{1,0:T(8,128)(2,1)} %get-tuple-element.33.refs_4_), channel_id=1, source_target_pairs={{0,2},{1,3},{2,0},{3,1},{4,6},{5,7},{6,4},{7,5},{8,10},{9,11},{10,... | collective-permute-start | bytes 1572872 | tf_op jit(solution)/shard_map/ppermute | solution.py:54
  10.0 2.6 %collective-permute-start.2 = (bf16[16,2048]{1,0:T(8,128)(2,1)S(1)}, bf16[16,2048]{1,0:T(8,128)(2,1)S(1)}, u32[]{:S(2)}, u32[]{:S(2)}) collective-permute-start(bf16[16,2048]{1,0:T(8,128)(2,1)S(1)} %pad_maximum_fusion), channel_id=1, source_target_pairs={{0,4},{1,5},{2,6},{3,7},{4,12},{5,13},{6,14},{7,15},{12,8},{13,9},... | collective-permute-start | bytes 196616 | tf_op jit(solution)/shard_map/ppermute | solution.py:50
  12.6 0.3 collective-permute-start.3
  13.0 10.5 %collective-permute-done.2 = bf16[16,2048]{1,0:T(8,128)(2,1)S(1)} collective-permute-done((bf16[16,2048]{1,0:T(8,128)(2,1)S(1)}, bf16[16,2048]{1,0:T(8,128)(2,1)S(1)}, u32[]{:S(2)}, u32[]{:S(2)}) %collective-permute-start.2) | collective-permute-done | bytes 65568 | tf_op jit(solution)/shard_map/ppermute | solution.py:50
  23.5 5.5 %collective-permute-start.4 = (bf16[16,2048]{1,0:T(8,128)(2,1)S(1)}, bf16[16,2048]{1,0:T(8,128)(2,1)S(1)}, u32[]{:S(2)}, u32[]{:S(2)}) collective-permute-start(bf16[16,2048]{1,0:T(8,128)(2,1)S(1)} %pad_maximum_fusion), channel_id=1, source_target_pairs={{0,12},{1,13},{2,14},{3,15},{4,8},{5,9},{6,10},{7,11},{12,0},{13,1... | collective-permute-start | bytes 196616 | tf_op jit(solution)/shard_map/ppermute | solution.py:50
  29.0 2.4 %collective-permute-done.4 = bf16[16,2048]{1,0:T(8,128)(2,1)S(1)} collective-permute-done((bf16[16,2048]{1,0:T(8,128)(2,1)S(1)}, bf16[16,2048]{1,0:T(8,128)(2,1)S(1)}, u32[]{:S(2)}, u32[]{:S(2)}) %collective-permute-start.4) | collective-permute-done | bytes 65568 | tf_op jit(solution)/shard_map/ppermute | solution.py:50
  31.4 0.0 collective-permute-start.5
  31.4 1.5 %collective-permute-start.7 = (bf16[512,512]{1,0:T(8,128)(2,1)S(1)}, bf16[512,512]{1,0:T(8,128)(2,1)}, u32[]{:S(2)}, u32[]{:S(2)}) collective-permute-start(bf16[512,512]{1,0:T(8,128)(2,1)S(1)} %collective-permute-done.refs_5_), channel_id=1, source_target_pairs={{0,2},{1,3},{2,0},{3,1},{4,6},{5,7},{6,4},{7,5},{8,10},{9,11},{10,... | collective-permute-start | bytes 1572872 | tf_op jit(solution)/shard_map/ppermute | solution.py:54
  32.9 0.0 collective-permute-done.8.refs_8_
  32.9 1.9 %collective-permute-start.9 = (bf16[512,512]{1,0:T(8,128)(2,1)S(1)}, bf16[512,512]{1,0:T(8,128)(2,1)S(1)}, u32[]{:S(2)}, u32[]{:S(2)}) collective-permute-start(bf16[512,512]{1,0:T(8,128)(2,1)S(1)} %collective-permute-done.6.refs_6_), channel_id=1, source_target_pairs={{0,16},{16,0},{1,17},{17,1},{2,18},{18,2},{3,19},{19,3},{4,20},{20... | collective-permute-start | bytes 1572872 | tf_op jit(solution)/shard_map/ppermute | solution.py:58
  34.8 1.3 %constant_dynamic-slice_fusion = (s32[1,24]{1,0:T(1,128)S(1)}, s32[24]{0:T(128)}) fusion(s32[32,24]{1,0:T(8,128)} %constant.54.clone, s32[]{:T(128)S(6)} %select_n.52), kind=kLoop, calls=%fused_computation.45 | loop fusion | bytes 292 | tf_op jit(solution)/shard_map/dynamic_slice | solution.py:477
  36.1 0.6 constant_dynamic-update-slice_fusion.4
  36.7 0.6 constant_dynamic-update-slice_fusion.9
  37.3 0.5 collective-permute-start.11
  37.8 7.6 %squares.1 = f32[512,1]{1,0:T(8,128)} custom-call(bf16[512,8192]{1,0:T(8,128)(2,1)} %refs_1_.5), custom_call_target="tpu_custom_call" | custom-call | bytes 262144 | tf_op jit(solution)/shard_map/squares/pallas_call | solution.py:352
  45.4 1.1 reduce
  46.5 3.1 %collective-permute-start.12 = (bf16[512,512]{1,0:T(8,128)(2,1)S(1)}, bf16[512,512]{1,0:T(8,128)(2,1)S(1)}, u32[]{:S(2)}, u32[]{:S(2)}) collective-permute-start(bf16[512,512]{1,0:T(8,128)(2,1)S(1)} %collective-permute-done.6.refs_6_), channel_id=1, source_target_pairs={{0,4},{1,5},{2,6},{3,7},{4,12},{5,13},{6,14},{7,15},{12,8},{13,9},... | collective-permute-start | bytes 1572872 | tf_op jit(solution)/shard_map/ppermute | solution.py:50
  49.6 0.1 collective-permute-start.14
  49.8 0.7 constant_dynamic-update-slice_fusion.8
  50.5 0.6 constant_dynamic-update-slice_fusion.7
  51.1 0.6 constant_dynamic-update-slice_fusion.6
  51.8 1.5 %collective-permute-start.10 = (bf16[512,512]{1,0:T(8,128)(2,1)}, bf16[512,512]{1,0:T(8,128)(2,1)S(1)}, u32[]{:S(2)}, u32[]{:S(2)}) collective-permute-start(bf16[512,512]{1,0:T(8,128)(2,1)} %collective-permute-done.5.refs_7_), channel_id=1, source_target_pairs={{0,2},{1,3},{2,0},{3,1},{4,6},{5,7},{6,4},{7,5},{8,10},{9,11},{10,... | collective-permute-start | bytes 1572872 | tf_op jit(solution)/shard_map/ppermute | solution.py:54
  53.3 0.0 collective-permute-done.13.refs_2_.refs_3_
  53.3 1.9 %collective-permute-start.15 = (bf16[512,512]{1,0:T(8,128)(2,1)}, bf16[512,512]{1,0:T(8,128)(2,1)}, u32[]{:S(2)}, u32[]{:S(2)}) collective-permute-start(bf16[512,512]{1,0:T(8,128)(2,1)} %collective-permute-done.5.refs_7_), channel_id=1, source_target_pairs={{0,4},{1,5},{2,6},{3,7},{4,12},{5,13},{6,14},{7,15},{12,8},{13,9},... | collective-permute-start | bytes 1572872 | tf_op jit(solution)/shard_map/ppermute | solution.py:50
  55.2 9.5 %rows_1.1.refs_4_ = f32[1024,512]{1,0:T(8,128)} custom-call(s32[24]{0:T(128)} %get-tuple-element.68.block_ref, bf16[512,8192]{1,0:T(8,128)(2,1)} %refs_1_.5, bf16[512,8192]{1,0:T(8,128)(2,1)} %refs_1_.5, bf16[512,8192]{1,0:T(8,128)(2,1)} %collective-permute-done.13.refs_2_.refs_3_, bf16[512,8192]{1,0:T(8,128)(2,1)} %collective-permute-done.13.refs_2_.refs_3_, ...), custom_call_target="tpu_custom_call" | custom-call | bytes 262144 | tf_op jit(solution)/shard_map/rows_1/pallas_call | solution.py:460
  64.7 0.0 collective-permute-done.11.refs_9_
  64.7 0.2 collective-permute-start.16
  64.9 0.1 slice_bitcast_fusion.1
  65.0 1.2 collective-permute-start.18
  66.1 0.1 add_convert_fusion
  66.2 0.9 collective-permute-start.19
  67.1 0.9 collective-permute-done.10.refs_10_
  68.0 0.5 collective-permute-done.15.refs_8_
  68.5 5.7 %collective-permute-done.16.refs_7_ = bf16[512,512]{1,0:T(8,128)(2,1)S(1)} collective-permute-done((bf16[512,512]{1,0:T(8,128)(2,1)}, bf16[512,512]{1,0:T(8,128)(2,1)S(1)}, u32[]{:S(2)}, u32[]{:S(2)}) %collective-permute-start.16) | collective-permute-done | bytes 524320 | tf_op jit(solution)/shard_map/ppermute | solution.py:58
  74.2 0.1 collective-permute-start.17
  74.3 0.1 collective-permute-done.18
  74.5 4.3 %collective-permute-start.20 = (bf16[512,512]{1,0:T(8,128)(2,1)S(1)}, bf16[512,512]{1,0:T(8,128)(2,1)}, u32[]{:S(2)}, u32[]{:S(2)}) collective-permute-start(bf16[512,512]{1,0:T(8,128)(2,1)S(1)} %collective-permute-done.10.refs_10_), channel_id=1, source_target_pairs={{0,4},{1,5},{2,6},{3,7},{4,12},{5,13},{6,14},{7,15},{12,8},{13,9},... | collective-permute-start | bytes 1572872 | tf_op jit(solution)/shard_map/ppermute | solution.py:50
  78.8 9.6 %rows_2.1.refs_4_ = f32[1024,512]{1,0:T(8,128)} custom-call(s32[24]{0:T(128)} %get-tuple-element.68.block_ref, bf16[512,8192]{1,0:T(8,128)(2,1)} %refs_1_.5, bf16[512,8192]{1,0:T(8,128)(2,1)} %refs_1_.5, bf16[512,8192]{1,0:T(8,128)(2,1)} %collective-permute-done.13.refs_2_.refs_3_, bf16[512,8192]{1,0:T(8,128)(2,1)} %collective-permute-done.13.refs_2_.refs_3_, ...), custom_call_target="tpu_custom_call" | custom-call | bytes 262144 | tf_op jit(solution)/shard_map/rows_2/pallas_call | solution.py:460
  88.5 0.1 slice_convert_fusion.1
  88.6 0.1 and_select_fusion.1
  88.6 0.1 select_reduce_fusion
  88.7 1.0 copy.13.refs_6_
  89.8 0.1 fusion.7
  89.8 0.2 fusion
  90.1 0.6 copy.19
  90.7 0.6 pad_add_fusion.slot_ref
  91.3 0.1 collective-permute-done.21.refs_10_
  91.4 0.7 copy-done.10
  92.2 8.9 %rows_3.1 = bf16[16,3,16,128]{3,2,1,0:T(8,128)(2,1)} custom-call(s32[24]{0:T(128)} %get-tuple-element.68.block_ref, s32[3,16]{1,0:T(4,128)} %pad_add_fusion.slot_ref, bf16[512,8192]{1,0:T(8,128)(2,1)} %refs_1_.5, bf16[512,8192]{1,0:T(8,128)(2,1)} %refs_1_.5, bf16[512,8192]{1,0:T(8,128)(2,1)} %collective-permute-done.13.refs_2_.refs_3_, ...), custom_call_target="tpu_custom_call" | custom-call | bytes 262144 | tf_op jit(solution)/shard_map/rows_3/pallas_call | solution.py:460
  101.0 3.8 %all-to-all-start = ((bf16[16,3,16,128]{3,2,1,0:T(8,128)(2,1)}), bf16[16,3,16,128]{3,2,1,0:T(8,128)(2,1)S(1)}, u32[]{:S(2)}, u32[]{:S(2)}) async-start(bf16[16,3,16,128]{3,2,1,0:T(8,128)(2,1)} %rows_3.1), calls=%async_computation | async-start | bytes 393216 | tf_op jit(solution)/shard_map/all_to_all | solution.py:535
  104.8 0.6 copy.18
  105.4 5.4 %resident.1 = (f32[8,32,128]{2,1,0:T(8,128)}, f32[32,128]{1,0:T(8,128)}, f32[32,128]{1,0:T(8,128)}) custom-call(s32[8]{0:T(128)} %length_ref, bf16[8,32,128]{2,1,0:T(8,128)(2,1)} %bitcast.40, bf16[8,256,1024]{2,1,0:T(8,128)(2,1)} %cache_ref.1), custom_call_target="tpu_custom_call" | custom-call | bytes 262144 | tf_op jit(solution)/shard_map/resident/pallas_call | solution.py:391
  110.8 3.0 %all-to-all-done.got_ref = bf16[16,3,16,128]{3,2,1,0:T(8,128)(2,1)S(1)} async-done(((bf16[16,3,16,128]{3,2,1,0:T(8,128)(2,1)}), bf16[16,3,16,128]{3,2,1,0:T(8,128)(2,1)S(1)}, u32[]{:S(2)}, u32[]{:S(2)}) %all-to-all-start) | async-done | bytes 196640 | tf_op jit(solution)/shard_map/all_to_all | solution.py:535
  113.8 0.7 copy-done
  114.5 3.3 %combine.1 = bf16[8,4096]{1,0:T(8,128)(2,1)} custom-call(bf16[16,3,16,128]{3,2,1,0:T(8,128)(2,1)} %copy-done, f32[8,32,128]{2,1,0:T(8,128)} %get-tuple-element.52.res_out_ref, f32[32,128]{1,0:T(8,128)} %get-tuple-element.53.res_top_ref, f32[32,128]{1,0:T(8,128)} %get-tuple-element.54.res_sum_ref), custom_call_target="tpu_custom_call" | custom-call | tf_op jit(solution)/shard_map/combine/pallas_call | solution.py:537
  (43 shorter events, 0.1 us)
Async XLA Ops:
  0.8 3.4 %collective-permute-start.1 = (bf16[8,2048]{1,0:T(8,128)(2,1)S(1)}, bf16[8,2048]{1,0:T(8,128)(2,1)S(1)}, u32[]{:S(2)}, u32[]{:S(2)}) collective-permute-start(bf16[8,2048]{1,0:T(8,128)(2,1)S(1)} %select_bitcast_fusion), channel_id=1, source_target_pairs={{0,1},{1,0},{2,3},{3,2},{4,5},{5,4},{6,7},{7,6},{8,9},{9,8},{10,11... | collective-permute-start | bytes 98312 | tf_op jit(solution)/shard_map/ppermute | solution.py:30
  3.3 2.1 %collective-permute-start = (bf16[512,512]{1,0:T(8,128)(2,1)}, bf16[512,512]{1,0:T(8,128)(2,1)S(1)}, u32[]{:S(2)}, u32[]{:S(2)}) collective-permute-start(bf16[512,512]{1,0:T(8,128)(2,1)} %get-tuple-element.30), channel_id=1, source_target_pairs={{0,1},{1,0},{2,3},{3,2},{4,5},{5,4},{6,7},{7,6},{8,9},{9,8},{10,11... | collective-permute-start | bytes 1572872 | tf_op jit(solution)/shard_map/ppermute | solution.py:30
  5.4 40.0 %copy-start.2 = (bf16[512,512]{1,0:T(8,128)(2,1)}, bf16[512,512]{1,0:T(8,128)(2,1)S(1)}, u32[]{:S(2)}) copy-start(bf16[512,512]{1,0:T(8,128)(2,1)S(1)} %collective-permute-done.refs_5_) | copy-start | bytes 1572868
  5.4 47.9 %collective-permute-start.13 = (bf16[512,8192]{1,0:T(8,128)(2,1)}, bf16[512,8192]{1,0:T(8,128)(2,1)}, u32[]{:S(2)}, u32[]{:S(2)}) collective-permute-start(bf16[512,8192]{1,0:T(8,128)(2,1)} %refs_1_.5), channel_id=1, source_target_pairs={{0,1},{1,0},{2,3},{3,2},{4,5},{5,4},{6,7},{7,6},{8,9},{9,8},{10,11... | collective-permute-start | bytes 25165832 | tf_op jit(solution)/shard_map/ppermute | solution.py:30
  5.6 27.3 %collective-permute-start.6 = (bf16[512,512]{1,0:T(8,128)(2,1)}, bf16[512,512]{1,0:T(8,128)(2,1)S(1)}, u32[]{:S(2)}, u32[]{:S(2)}) collective-permute-start(bf16[512,512]{1,0:T(8,128)(2,1)} %get-tuple-element.33.refs_4_), channel_id=1, source_target_pairs={{0,4},{1,5},{2,6},{3,7},{4,12},{5,13},{6,14},{7,15},{12,8},{13,9},... | collective-permute-start | bytes 1572872 | tf_op jit(solution)/shard_map/ppermute | solution.py:50
  8.5 24.4 %collective-permute-start.8 = (bf16[512,512]{1,0:T(8,128)(2,1)}, bf16[512,512]{1,0:T(8,128)(2,1)S(1)}, u32[]{:S(2)}, u32[]{:S(2)}) collective-permute-start(bf16[512,512]{1,0:T(8,128)(2,1)} %get-tuple-element.33.refs_4_), channel_id=1, source_target_pairs={{0,2},{1,3},{2,0},{3,1},{4,6},{5,7},{6,4},{7,5},{8,10},{9,11},{10,... | collective-permute-start | bytes 1572872 | tf_op jit(solution)/shard_map/ppermute | solution.py:54
  10.0 13.4 %collective-permute-start.2 = (bf16[16,2048]{1,0:T(8,128)(2,1)S(1)}, bf16[16,2048]{1,0:T(8,128)(2,1)S(1)}, u32[]{:S(2)}, u32[]{:S(2)}) collective-permute-start(bf16[16,2048]{1,0:T(8,128)(2,1)S(1)} %pad_maximum_fusion), channel_id=1, source_target_pairs={{0,4},{1,5},{2,6},{3,7},{4,12},{5,13},{6,14},{7,15},{12,8},{13,9},... | collective-permute-start | bytes 196616 | tf_op jit(solution)/shard_map/ppermute | solution.py:50
  12.6 16.3 %collective-permute-start.3 = (bf16[16,2048]{1,0:T(8,128)(2,1)S(1)}, bf16[16,2048]{1,0:T(8,128)(2,1)S(1)}, u32[]{:S(2)}, u32[]{:S(2)}) collective-permute-start(bf16[16,2048]{1,0:T(8,128)(2,1)S(1)} %pad_maximum_fusion), channel_id=1, source_target_pairs={{0,8},{1,9},{2,10},{3,11},{4,0},{5,1},{6,2},{7,3},{12,4},{13,5},{1... | collective-permute-start | bytes 196616 | tf_op jit(solution)/shard_map/ppermute | solution.py:50
  23.5 7.9 %collective-permute-start.4 = (bf16[16,2048]{1,0:T(8,128)(2,1)S(1)}, bf16[16,2048]{1,0:T(8,128)(2,1)S(1)}, u32[]{:S(2)}, u32[]{:S(2)}) collective-permute-start(bf16[16,2048]{1,0:T(8,128)(2,1)S(1)} %pad_maximum_fusion), channel_id=1, source_target_pairs={{0,12},{1,13},{2,14},{3,15},{4,8},{5,9},{6,10},{7,11},{12,0},{13,1... | collective-permute-start | bytes 196616 | tf_op jit(solution)/shard_map/ppermute | solution.py:50
  31.4 15.2 %collective-permute-start.5 = (bf16[512,512]{1,0:T(8,128)(2,1)S(1)}, bf16[512,512]{1,0:T(8,128)(2,1)}, u32[]{:S(2)}, u32[]{:S(2)}) collective-permute-start(bf16[512,512]{1,0:T(8,128)(2,1)S(1)} %collective-permute-done.refs_5_), channel_id=1, source_target_pairs={{0,4},{1,5},{2,6},{3,7},{4,12},{5,13},{6,14},{7,15},{12,8},{13,9},... | collective-permute-start | bytes 1572872 | tf_op jit(solution)/shard_map/ppermute | solution.py:50
  31.4 18.3 %collective-permute-start.7 = (bf16[512,512]{1,0:T(8,128)(2,1)S(1)}, bf16[512,512]{1,0:T(8,128)(2,1)}, u32[]{:S(2)}, u32[]{:S(2)}) collective-permute-start(bf16[512,512]{1,0:T(8,128)(2,1)S(1)} %collective-permute-done.refs_5_), channel_id=1, source_target_pairs={{0,2},{1,3},{2,0},{3,1},{4,6},{5,7},{6,4},{7,5},{8,10},{9,11},{10,... | collective-permute-start | bytes 1572872 | tf_op jit(solution)/shard_map/ppermute | solution.py:54
  32.9 13.6 %copy-start.4 = (bf16[512,512]{1,0:T(8,128)(2,1)}, bf16[512,512]{1,0:T(8,128)(2,1)S(1)}, u32[]{:S(2)}) copy-start(bf16[512,512]{1,0:T(8,128)(2,1)S(1)} %collective-permute-done.6.refs_6_) | copy-start | bytes 1572868
  32.9 12.5 %copy-start.6 = (bf16[512,512]{1,0:T(8,128)(2,1)}, bf16[512,512]{1,0:T(8,128)(2,1)S(1)}, u32[]{:S(2)}) copy-start(bf16[512,512]{1,0:T(8,128)(2,1)S(1)} %collective-permute-done.8.refs_8_) | copy-start | bytes 1572868
  32.9 16.7 %collective-permute-start.9 = (bf16[512,512]{1,0:T(8,128)(2,1)S(1)}, bf16[512,512]{1,0:T(8,128)(2,1)S(1)}, u32[]{:S(2)}, u32[]{:S(2)}) collective-permute-start(bf16[512,512]{1,0:T(8,128)(2,1)S(1)} %collective-permute-done.6.refs_6_), channel_id=1, source_target_pairs={{0,16},{16,0},{1,17},{17,1},{2,18},{18,2},{3,19},{19,3},{4,20},{20... | collective-permute-start | bytes 1572872 | tf_op jit(solution)/shard_map/ppermute | solution.py:58
  37.3 27.4 %collective-permute-start.11 = (bf16[512,512]{1,0:T(8,128)(2,1)S(1)}, bf16[512,512]{1,0:T(8,128)(2,1)}, u32[]{:S(2)}, u32[]{:S(2)}) collective-permute-start(bf16[512,512]{1,0:T(8,128)(2,1)S(1)} %collective-permute-done.6.refs_6_), channel_id=1, source_target_pairs={{0,2},{1,3},{2,0},{3,1},{4,6},{5,7},{6,4},{7,5},{8,10},{9,11},{10,... | collective-permute-start | bytes 1572872 | tf_op jit(solution)/shard_map/ppermute | solution.py:54
  46.5 18.2 %collective-permute-start.12 = (bf16[512,512]{1,0:T(8,128)(2,1)S(1)}, bf16[512,512]{1,0:T(8,128)(2,1)S(1)}, u32[]{:S(2)}, u32[]{:S(2)}) collective-permute-start(bf16[512,512]{1,0:T(8,128)(2,1)S(1)} %collective-permute-done.6.refs_6_), channel_id=1, source_target_pairs={{0,4},{1,5},{2,6},{3,7},{4,12},{5,13},{6,14},{7,15},{12,8},{13,9},... | collective-permute-start | bytes 1572872 | tf_op jit(solution)/shard_map/ppermute | solution.py:50
  49.6 15.0 %copy-start.5 = (bf16[512,512]{1,0:T(8,128)(2,1)}, bf16[512,512]{1,0:T(8,128)(2,1)S(1)}, u32[]{:S(2)}) copy-start(bf16[512,512]{1,0:T(8,128)(2,1)S(1)} %collective-permute-done.9.refs_5_) | copy-start | bytes 1572868
  49.6 15.1 %collective-permute-start.14 = (bf16[512,512]{1,0:T(8,128)(2,1)}, bf16[512,512]{1,0:T(8,128)(2,1)S(1)}, u32[]{:S(2)}, u32[]{:S(2)}) collective-permute-start(bf16[512,512]{1,0:T(8,128)(2,1)} %collective-permute-done.5.refs_7_), channel_id=1, source_target_pairs={{0,16},{16,0},{1,17},{17,1},{2,18},{18,2},{3,19},{19,3},{4,20},{20... | collective-permute-start | bytes 1572872 | tf_op jit(solution)/shard_map/ppermute | solution.py:58
  51.8 16.3 %collective-permute-start.10 = (bf16[512,512]{1,0:T(8,128)(2,1)}, bf16[512,512]{1,0:T(8,128)(2,1)S(1)}, u32[]{:S(2)}, u32[]{:S(2)}) collective-permute-start(bf16[512,512]{1,0:T(8,128)(2,1)} %collective-permute-done.5.refs_7_), channel_id=1, source_target_pairs={{0,2},{1,3},{2,0},{3,1},{4,6},{5,7},{6,4},{7,5},{8,10},{9,11},{10,... | collective-permute-start | bytes 1572872 | tf_op jit(solution)/shard_map/ppermute | solution.py:54
  53.3 15.2 %collective-permute-start.15 = (bf16[512,512]{1,0:T(8,128)(2,1)}, bf16[512,512]{1,0:T(8,128)(2,1)}, u32[]{:S(2)}, u32[]{:S(2)}) collective-permute-start(bf16[512,512]{1,0:T(8,128)(2,1)} %collective-permute-done.5.refs_7_), channel_id=1, source_target_pairs={{0,4},{1,5},{2,6},{3,7},{4,12},{5,13},{6,14},{7,15},{12,8},{13,9},... | collective-permute-start | bytes 1572872 | tf_op jit(solution)/shard_map/ppermute | solution.py:50
  55.2 11.0 %copy-start.11 = (s32[8]{0:T(128)S(1)}, s32[8]{0:T(128)}, u32[]{:S(2)}) copy-start(s32[8]{0:T(128)} %param.11) | copy-start | bytes 100
  55.2 11.0 %copy-start.12 = (s32[8]{0:T(128)S(1)}, s32[8]{0:T(128)}, u32[]{:S(2)}) copy-start(s32[8]{0:T(128)} %param.10) | copy-start | bytes 100
  64.7 14.1 %copy-start.3 = (bf16[512,512]{1,0:T(8,128)(2,1)}, bf16[512,512]{1,0:T(8,128)(2,1)S(1)}, u32[]{:S(2)}) copy-start(bf16[512,512]{1,0:T(8,128)(2,1)S(1)} %collective-permute-done.12.refs_7_) | copy-start | bytes 1572868
  64.7 14.1 %copy-start.9 = (bf16[512,512]{1,0:T(8,128)(2,1)}, bf16[512,512]{1,0:T(8,128)(2,1)S(1)}, u32[]{:S(2)}) copy-start(bf16[512,512]{1,0:T(8,128)(2,1)S(1)} %collective-permute-done.14.refs_6_) | copy-start | bytes 1572868
  64.7 9.5 %collective-permute-start.16 = (bf16[512,512]{1,0:T(8,128)(2,1)}, bf16[512,512]{1,0:T(8,128)(2,1)S(1)}, u32[]{:S(2)}, u32[]{:S(2)}) collective-permute-start(bf16[512,512]{1,0:T(8,128)(2,1)} %collective-permute-done.11.refs_9_), channel_id=1, source_target_pairs={{0,16},{16,0},{1,17},{17,1},{2,18},{18,2},{3,19},{19,3},{4,20},{20... | collective-permute-start | bytes 1572872 | tf_op jit(solution)/shard_map/ppermute | solution.py:58
  65.0 9.5 %collective-permute-start.18 = (bf16[64,2048]{1,0:T(8,128)(2,1)}, bf16[64,2048]{1,0:T(8,128)(2,1)S(1)}, u32[]{:S(2)}, u32[]{:S(2)}) collective-permute-start(bf16[64,2048]{1,0:T(8,128)(2,1)} %get-tuple-element.47), channel_id=1, source_target_pairs={{0,2},{1,3},{2,0},{3,1},{4,6},{5,7},{6,4},{7,5},{8,10},{9,11},{10,... | collective-permute-start | bytes 786440 | tf_op jit(solution)/shard_map/ppermute | solution.py:54
  66.2 25.1 %collective-permute-start.19 = (bf16[512,512]{1,0:T(8,128)(2,1)S(1)}, bf16[512,512]{1,0:T(8,128)(2,1)S(1)}, u32[]{:S(2)}, u32[]{:S(2)}) collective-permute-start(bf16[512,512]{1,0:T(8,128)(2,1)S(1)} %collective-permute-done.12.refs_7_), channel_id=1, source_target_pairs={{0,2},{1,3},{2,0},{3,1},{4,6},{5,7},{6,4},{7,5},{8,10},{9,11},{10,... | collective-permute-start | bytes 1572872 | tf_op jit(solution)/shard_map/ppermute | solution.py:54
  68.0 10.8 %copy-start.7 = (bf16[512,512]{1,0:T(8,128)(2,1)}, bf16[512,512]{1,0:T(8,128)(2,1)S(1)}, u32[]{:S(2)}) copy-start(bf16[512,512]{1,0:T(8,128)(2,1)S(1)} %collective-permute-done.10.refs_10_) | copy-start | bytes 1572868
  74.2 14.3 %copy-start.8 = (bf16[512,512]{1,0:T(8,128)(2,1)}, bf16[512,512]{1,0:T(8,128)(2,1)S(1)}, u32[]{:S(2)}) copy-start(bf16[512,512]{1,0:T(8,128)(2,1)S(1)} %collective-permute-done.16.refs_7_) | copy-start | bytes 1572868
  74.2 14.3 %collective-permute-start.17 = (f32[8,128]{1,0:T(8,128)S(1)}, f32[8,128]{1,0:T(8,128)S(1)}, u32[]{:S(2)}, u32[]{:S(2)}) collective-permute-start(f32[8,128]{1,0:T(8,128)S(1)} %fusion.2), channel_id=1, source_target_pairs={{0,1},{1,0},{2,3},{3,2},{4,5},{5,4},{6,7},{7,6},{8,9},{9,8},{10,11... | collective-permute-start | bytes 12296 | tf_op jit(solution)/shard_map/ppermute | solution.py:30
  74.5 16.9 %collective-permute-start.20 = (bf16[512,512]{1,0:T(8,128)(2,1)S(1)}, bf16[512,512]{1,0:T(8,128)(2,1)}, u32[]{:S(2)}, u32[]{:S(2)}) collective-permute-start(bf16[512,512]{1,0:T(8,128)(2,1)S(1)} %collective-permute-done.10.refs_10_), channel_id=1, source_target_pairs={{0,4},{1,5},{2,6},{3,7},{4,12},{5,13},{6,14},{7,15},{12,8},{13,9},... | collective-permute-start | bytes 1572872 | tf_op jit(solution)/shard_map/ppermute | solution.py:50
  78.8 12.6 %collective-permute-start.21 = (bf16[512,512]{1,0:T(8,128)(2,1)S(1)}, bf16[512,512]{1,0:T(8,128)(2,1)}, u32[]{:S(2)}, u32[]{:S(2)}) collective-permute-start(bf16[512,512]{1,0:T(8,128)(2,1)S(1)} %collective-permute-done.10.refs_10_), channel_id=1, source_target_pairs={{0,16},{16,0},{1,17},{17,1},{2,18},{18,2},{3,19},{19,3},{4,20},{20... | collective-permute-start | bytes 1572872 | tf_op jit(solution)/shard_map/ppermute | solution.py:58
  91.3 0.8 copy-start.10
  92.2 12.6 %copy-start.1 = (bf16[8,4096]{1,0:T(8,128)(2,1)S(1)}, bf16[8,4096]{1,0:T(8,128)(2,1)}, u32[]{:S(2)}) copy-start(bf16[8,4096]{1,0:T(8,128)(2,1)} %param.12) | copy-start | bytes 196612
  101.0 12.8 %all-to-all-start = ((bf16[16,3,16,128]{3,2,1,0:T(8,128)(2,1)}), bf16[16,3,16,128]{3,2,1,0:T(8,128)(2,1)S(1)}, u32[]{:S(2)}, u32[]{:S(2)}) async-start(bf16[16,3,16,128]{3,2,1,0:T(8,128)(2,1)} %rows_3.1), calls=%async_computation | async-start | bytes 393216 | tf_op jit(solution)/shard_map/all_to_all | solution.py:535
  113.8 0.7 copy-start
